TPU v7x, 32 devices: a whole 2x2x4 slice. The times are simulated.
32 devices in a mesh: pipe: 2 (over core), dp: 16 (over z, y, x).
Axes of the slice: x: 2, y: 2, z: 4, core: 2. Of those that a mesh axis runs over, the one named last changes fastest.
Arguments:
- patches: bfloat16 [64, 196, 384], P('dp'), may hold values from -6 to 6
- class_token: bfloat16 [64, 384], P('dp'), may hold values from -6 to 6
- keep_mask: int32 [64, 196], P('dp'), may hold values 0 or 1
- class_cotangent: bfloat16 [64, 384], P('dp'), may hold values from -6 to 6
- norm1_gain: bfloat16 [2, 384], P('pipe'), may hold values from 0.5 to 1.5
- norm1_bias: bfloat16 [2, 384], P('pipe'), may hold values from -1.75 to 1.75
- qkv_weight: bfloat16 [2, 384, 1152], P('pipe'), may hold values from -0.3125 to 0.3125
- qv_bias: bfloat16 [2, 768], P('pipe'), may hold values from -1.75 to 1.75
- mix_pre: bfloat16 [8, 8], replicated, may hold values from -2 to 2
- mix_post: bfloat16 [8, 8], replicated, may hold values from -2 to 2
- post_bias: bfloat16 [8], replicated, may hold values from -0.015625 to 0.015625
- proj_weight: bfloat16 [2, 384, 384], P('pipe'), may hold values from -3.5 to 3.5
- proj_bias: bfloat16 [2, 384], P('pipe'), may hold values from -1.75 to 1.75
- scale_attn: bfloat16 [2, 384], P('pipe'), may hold values from 0.3984375 to 1.1953125
- norm2_gain: bfloat16 [2, 384], P('pipe'), may hold values from 0.5 to 1.5
- norm2_bias: bfloat16 [2, 384], P('pipe'), may hold values from -1.75 to 1.75
- fc1_weight: bfloat16 [2, 384, 1536], P('pipe'), may hold values from -0.3125 to 0.3125
- fc1_bias: bfloat16 [2, 1536], P('pipe'), may hold values from -1.75 to 1.75
- fc2_weight: bfloat16 [2, 1536, 384], P('pipe'), may hold values from -0.15625 to 0.15625
- fc2_bias: bfloat16 [2, 384], P('pipe'), may hold values from -1.75 to 1.75
- scale_mlp: bfloat16 [2, 384], P('pipe'), may hold values from 0.3984375 to 1.1953125
Outputs:
- class_output: bfloat16 [64, 384], P('dp', 'pipe')
- patch_grad: float32 [64, 196, 384], P('dp', None, 'pipe')
- class_grad: bfloat16 [64, 384], P('dp', 'pipe')
- grad_norm1_gain: float32 [2, 384], P('pipe')
- grad_norm1_bias: float32 [2, 384], P('pipe')
- grad_qkv_weight: float32 [2, 384, 1152], P('pipe')
- grad_qv_bias: float32 [2, 768], P('pipe')
- grad_proj_weight: float32 [2, 384, 384], P('pipe')
- grad_proj_bias: float32 [2, 384], P('pipe')
- grad_scale_attn: float32 [2, 384], P('pipe')
- grad_norm2_gain: float32 [2, 384], P('pipe')
- grad_norm2_bias: float32 [2, 384], P('pipe')
- grad_fc1_weight: float32 [2, 384, 1536], P('pipe')
- grad_fc1_bias: float32 [2, 1536], P('pipe')
- grad_fc2_weight: float32 [2, 1536, 384], P('pipe')
- grad_fc2_bias: float32 [2, 384], P('pipe')
- grad_scale_mlp: float32 [2, 384], P('pipe')
- grad_mix_pre: float32 [8, 8], replicated
- grad_mix_post: float32 [8, 8], replicated
- grad_post_bias: float32 [8], replicated
All inputs are finite; a program needn't handle non-finite values. No bound on the sum of `keep_mask` on one device may be relied on, other than what follows from the above.
Results may differ from a plain program's by a relative error of at most 0.013.
Values may be sent and summed in bfloat16 or wider, within the bound.
No kernel may reach another device: no remote copies, remote signals or barrier semaphores. Data moves between devices by JAX's collectives and lax.ppermute only.
A program may use at most 256 MiB of HBM per device.

v0:
```python
import jax
import jax.numpy as jnp
from jax import lax
from jax.sharding import PartitionSpec as P

HEADS = 8
IMG_MB = 1
MICRO = 4


def passed_along(array, axis, by):
    length = lax.axis_size(axis)
    pairs = [(i, i + by) for i in range(length) if 0 <= i + by < length]
    return lax.ppermute(array, axis, pairs)


def layer_norm(tokens, norm_gain, norm_bias):
    average = jnp.mean(tokens, -1, keepdims=True)
    centred = tokens - average
    spread = jnp.mean(centred * centred, -1, keepdims=True)
    return centred * lax.rsqrt(spread + 1e-06) * norm_gain + norm_bias


def gelu_exact(inner_rows):
    return jax.nn.gelu(inner_rows, approximate=False)


def matmul(pattern, left_side, right_side):
    return jnp.einsum(pattern, left_side, right_side, preferred_element_type=jnp.float32)


def to_low(array):
    return array.astype(jnp.bfloat16)


def as_float(array):
    return array.astype(jnp.float32)


def feed_forward(section_params, middle):
    hidden, norm_two = jax.vjp(
        layer_norm, middle, as_float(section_params[7]), as_float(section_params[8])
    )
    inner_low = to_low(hidden)
    inner_rows = matmul("rd,df->rf", inner_low, section_params[9]) + as_float(section_params[10])
    active, gelu_back = jax.vjp(gelu_exact, inner_rows)
    active_low = to_low(active)
    outer_rows = matmul("rf,fd->rd", active_low, section_params[11]) + as_float(section_params[12])
    result = middle + as_float(section_params[13]) * outer_rows
    return (result, (norm_two, inner_low, gelu_back, active_low, outer_rows))


def feed_backward(section_params, kept_values, upper_grad):
    norm_two, inner_low, gelu_back, active_low, outer_rows = kept_values
    grad_scale_mlp = jnp.sum(upper_grad * outer_rows, axis=0)
    outer_grad = to_low(upper_grad * as_float(section_params[13]))
    grad_fc2_bias = jnp.sum(as_float(outer_grad), axis=0)
    grad_fc2 = matmul("rf,rd->fd", active_low, outer_grad)
    active_grad = matmul("rd,fd->rf", outer_grad, section_params[11])
    inner_grad = to_low(gelu_back(active_grad)[0])
    grad_fc1_bias = jnp.sum(as_float(inner_grad), axis=0)
    grad_fc1 = matmul("rd,rf->df", inner_low, inner_grad)
    hidden_grad = matmul("rf,df->rd", inner_grad, section_params[9])
    middle_part, grad_norm2_gain, grad_norm2_bias = norm_two(hidden_grad)
    return (
        upper_grad + middle_part,
        (
            grad_norm2_gain,
            grad_norm2_bias,
            grad_fc1,
            grad_fc1_bias,
            grad_fc2,
            grad_fc2_bias,
            grad_scale_mlp,
        ),
    )


def self_forward(section_params, mixing, patch_rows, keep_rows):
    images, length, model_width = patch_rows.shape
    head_dim = model_width // HEADS
    shape_heads = (images, length, HEADS, head_dim)
    tokens = as_float(patch_rows).reshape(images * length, model_width)
    hidden, norm_one = jax.vjp(
        layer_norm, tokens, as_float(section_params[0]), as_float(section_params[1])
    )
    hidden_low = to_low(hidden)
    joined = matmul("rd,de->re", hidden_low, section_params[2])
    bias_rows = as_float(section_params[3])
    queries = to_low(joined[:, :model_width] + bias_rows[:model_width]).reshape(shape_heads)
    key_rows = to_low(joined[:, model_width : 2 * model_width]).reshape(shape_heads)
    value_rows = to_low(joined[:, 2 * model_width :] + bias_rows[model_width:]).reshape(shape_heads)
    raw_scores = matmul("bihe,bjhe->bhij", queries, key_rows)
    positions = jnp.arange(length)
    allowed = (keep_rows[:, None, None, :] > 0) | (positions[:, None] == positions[None, :])[
        None, None
    ]

    def mixing_piece(raw_part, mix_first, mix_second, post_rows):
        mixed_scores = jnp.einsum(
            "hc,bcij->bhij",
            mix_first,
            raw_part * head_dim ** (-0.5),
            precision=lax.Precision.HIGHEST,
        )
        weights = jax.nn.softmax(jnp.where(allowed, mixed_scores, -1e30), axis=-1)
        spread_rows = jnp.einsum(
            "hc,bcij->bhij", mix_second, weights, precision=lax.Precision.HIGHEST
        )
        return spread_rows + post_rows[None, :, None, None] * allowed

    combined, mixing_back = jax.vjp(
        mixing_piece, raw_scores, as_float(mixing[0]), as_float(mixing[1]), as_float(mixing[2])
    )
    combined_low = to_low(combined)
    attended = to_low(matmul("bhij,bjhe->bihe", combined_low, value_rows)).reshape(
        images * length, model_width
    )
    branch = matmul("rd,de->re", attended, section_params[4]) + as_float(section_params[5])
    middle = tokens + as_float(section_params[6]) * branch
    result, feed_values = feed_forward(section_params, middle)
    kept_values = (
        norm_one,
        hidden_low,
        queries,
        key_rows,
        value_rows,
        mixing_back,
        combined_low,
        attended,
        branch,
        feed_values,
    )
    return (to_low(result).reshape(images, length, model_width), kept_values)


def self_backward(section_params, mixing, patch_rows, keep_rows, incoming):
    images, length, model_width = patch_rows.shape
    head_dim = model_width // HEADS
    sent_rows, kept_values = self_forward(section_params, mixing, patch_rows, keep_rows)
    (
        norm_one,
        hidden_low,
        queries,
        key_rows,
        value_rows,
        mixing_back,
        combined_low,
        attended,
        branch,
        feed_values,
    ) = kept_values
    upper_grad = as_float(incoming).reshape(images * length, model_width)
    middle_grad, feed_grads = feed_backward(section_params, feed_values, upper_grad)
    grad_scale_attn = jnp.sum(middle_grad * branch, axis=0)
    branch_grad = to_low(middle_grad * as_float(section_params[6]))
    grad_proj_bias = jnp.sum(as_float(branch_grad), axis=0)
    grad_proj = matmul("rd,re->de", attended, branch_grad)
    attended_grad = to_low(matmul("re,de->rd", branch_grad, section_params[4])).reshape(
        images, length, HEADS, head_dim
    )
    combined_grad = matmul("bihe,bjhe->bhij", attended_grad, value_rows)
    value_grad = to_low(matmul("bhij,bihe->bjhe", combined_low, attended_grad))
    raw_grad, grad_mix_pre, grad_mix_post, grad_post_bias = mixing_back(combined_grad)
    raw_low = to_low(raw_grad)
    query_grad = to_low(matmul("bhij,bjhe->bihe", raw_low, key_rows))
    key_grad = to_low(matmul("bhij,bihe->bjhe", raw_low, queries))
    flat_shape = (images * length, model_width)
    query_flat = query_grad.reshape(flat_shape)
    value_flat = value_grad.reshape(flat_shape)
    joined_grad = jnp.concatenate([query_flat, key_grad.reshape(flat_shape), value_flat], axis=1)
    grad_qv_bias = jnp.concatenate(
        [jnp.sum(as_float(query_flat), axis=0), jnp.sum(as_float(value_flat), axis=0)]
    )
    grad_qkv = matmul("rd,re->de", hidden_low, joined_grad)
    hidden_grad = matmul("re,de->rd", joined_grad, section_params[2])
    token_part, grad_norm1_gain, grad_norm1_bias = norm_one(hidden_grad)
    patch_part = (middle_grad + token_part).reshape(images, length, model_width)
    section_grads = (
        grad_norm1_gain,
        grad_norm1_bias,
        grad_qkv,
        grad_qv_bias,
        grad_proj,
        grad_proj_bias,
        grad_scale_attn,
    ) + feed_grads
    return (patch_part, section_grads, (grad_mix_pre, grad_mix_post, grad_post_bias))


def class_step(section_params, class_rows, patch_rows, keep_rows, cotangent):
    images, length, model_width = patch_rows.shape
    head_dim = model_width // HEADS
    token_heads = (images, length + 1, HEADS, head_dim)
    class_start = as_float(class_rows)
    tokens = jnp.concatenate([class_start[:, None, :], as_float(patch_rows)], axis=1)
    hidden, norm_one = jax.vjp(
        layer_norm, tokens, as_float(section_params[0]), as_float(section_params[1])
    )
    hidden_low = to_low(hidden)
    query_weight = section_params[2][:, :model_width]
    pair_weight = section_params[2][:, model_width:]
    bias_rows = as_float(section_params[3])
    queries = to_low(
        matmul("bd,de->be", hidden_low[:, 0], query_weight) + bias_rows[:model_width]
    ).reshape(images, HEADS, head_dim)
    joined = matmul("bpd,de->bpe", hidden_low, pair_weight)
    key_rows = to_low(joined[..., :model_width]).reshape(token_heads)
    value_rows = to_low(joined[..., model_width:] + bias_rows[model_width:]).reshape(token_heads)
    raw_scores = matmul("bhe,bjhe->bhj", queries, key_rows)
    allowed = jnp.concatenate([jnp.ones((images, 1), jnp.bool_), keep_rows > 0], axis=1)[:, None, :]

    def softmax_piece(raw_part):
        return jax.nn.softmax(jnp.where(allowed, raw_part * head_dim ** (-0.5), -1e30), axis=-1)

    weights, softmax_back = jax.vjp(softmax_piece, raw_scores)
    weights_low = to_low(weights)
    attended = to_low(matmul("bhj,bjhe->bhe", weights_low, value_rows)).reshape(images, model_width)
    branch = matmul("bd,de->be", attended, section_params[4]) + as_float(section_params[5])
    middle = class_start + as_float(section_params[6]) * branch
    result, feed_values = feed_forward(section_params, middle)
    middle_grad, feed_grads = feed_backward(section_params, feed_values, as_float(cotangent))
    grad_scale_attn = jnp.sum(middle_grad * branch, axis=0)
    branch_grad = to_low(middle_grad * as_float(section_params[6]))
    grad_proj_bias = jnp.sum(as_float(branch_grad), axis=0)
    grad_proj = matmul("bd,be->de", attended, branch_grad)
    attended_grad = to_low(matmul("be,de->bd", branch_grad, section_params[4])).reshape(
        images, HEADS, head_dim
    )
    weights_grad = matmul("bhe,bjhe->bhj", attended_grad, value_rows)
    value_grad = to_low(matmul("bhj,bhe->bjhe", weights_low, attended_grad)).reshape(
        images, length + 1, model_width
    )
    raw_low = to_low(softmax_back(weights_grad)[0])
    query_grad = to_low(matmul("bhj,bjhe->bhe", raw_low, key_rows)).reshape(images, model_width)
    key_grad = to_low(matmul("bhj,bhe->bjhe", raw_low, queries)).reshape(
        images, length + 1, model_width
    )
    pair_grad = jnp.concatenate([key_grad, value_grad], axis=2)
    grad_qv_bias = jnp.concatenate(
        [jnp.sum(as_float(query_grad), axis=0), jnp.sum(as_float(value_grad), axis=(0, 1))]
    )
    grad_qkv = jnp.concatenate(
        [
            matmul("bd,be->de", hidden_low[:, 0], query_grad),
            matmul("bpd,bpe->de", hidden_low, pair_grad),
        ],
        axis=1,
    )
    hidden_grad = matmul("bpe,de->bpd", pair_grad, pair_weight)
    hidden_grad = hidden_grad.at[:, 0].add(matmul("be,de->bd", query_grad, query_weight))
    token_part, grad_norm1_gain, grad_norm1_bias = norm_one(hidden_grad)
    class_part = middle_grad + token_part[:, 0]
    section_grads = (
        grad_norm1_gain,
        grad_norm1_bias,
        grad_qkv,
        grad_qv_bias,
        grad_proj,
        grad_proj_bias,
        grad_scale_attn,
    ) + feed_grads
    return (to_low(result), to_low(class_part), to_low(token_part[:, 1:]), section_grads)


def empty_outputs(micro_images, length, model_width, section_params, mixing):
    empty_rows = jnp.zeros((micro_images, length, model_width), jnp.bfloat16)
    empty_class = jnp.zeros((micro_images, model_width), jnp.bfloat16)
    empty_grad = jnp.zeros((micro_images, length, model_width), jnp.float32)
    section_zero = tuple((jnp.zeros(member.shape, jnp.float32) for member in section_params))
    mixing_zero = tuple((jnp.zeros(member.shape, jnp.float32) for member in mixing))
    return (empty_rows, empty_class, empty_class, empty_grad, section_zero, mixing_zero)


def local(
    patches,
    class_token,
    keep_mask,
    class_cotangent,
    norm1_gain,
    norm1_bias,
    qkv_weight,
    qv_bias,
    mix_pre,
    mix_post,
    post_bias,
    proj_weight,
    proj_bias,
    scale_attn,
    norm2_gain,
    norm2_bias,
    fc1_weight,
    fc1_bias,
    fc2_weight,
    fc2_bias,
    scale_mlp,
):
    stacked = (
        norm1_gain,
        norm1_bias,
        qkv_weight,
        qv_bias,
        proj_weight,
        proj_bias,
        scale_attn,
        norm2_gain,
        norm2_bias,
        fc1_weight,
        fc1_bias,
        fc2_weight,
        fc2_bias,
        scale_mlp,
    )
    mixing = (mix_pre, mix_post, post_bias)
    section_index = lax.axis_index("pipe")
    length = patches.shape[1]
    model_width = patches.shape[2]
    half_width = model_width // 2
    micro_images = IMG_MB
    micro_count = MICRO
    own_section = tuple((member[0] for member in stacked))
    first_rank = section_index == 0
    totals = tuple((jnp.zeros(member.shape, jnp.float32) for member in own_section))
    mixing_totals = tuple((jnp.zeros(member.shape, jnp.float32) for member in mixing))
    returned = jnp.zeros((micro_images, length, model_width), jnp.bfloat16)
    arrived = returned
    class_parts = []
    class_grad_parts = []
    patch_parts = []
    for step_index in range(micro_count + 1):
        ahead_index = step_index
        behind_index = step_index - 1
        if ahead_index < micro_count:
            ahead_rows = patches[ahead_index * micro_images : (ahead_index + 1) * micro_images]
            ahead_keep = keep_mask[ahead_index * micro_images : (ahead_index + 1) * micro_images]

            def forward_first():
                return self_forward(own_section, mixing, ahead_rows, ahead_keep)[0]

            def forward_other():
                return jnp.zeros_like(ahead_rows)

            leaving = lax.cond(first_rank, forward_first, forward_other)
            arrived = passed_along(leaving, "pipe", 1)

        def backward_first():
            if behind_index < 0:
                return empty_outputs(micro_images, length, model_width, own_section, mixing)
            previous = patches[behind_index * micro_images : (behind_index + 1) * micro_images]
            previous_keep = keep_mask[
                behind_index * micro_images : (behind_index + 1) * micro_images
            ]
            patch_part, section_grads, mixing_grads = self_backward(
                own_section, mixing, previous, previous_keep, returned
            )
            empty = empty_outputs(micro_images, length, model_width, own_section, mixing)
            return (empty[0], empty[1], empty[2], patch_part, section_grads, mixing_grads)

        def work_second():
            if ahead_index >= micro_count:
                return empty_outputs(micro_images, length, model_width, own_section, mixing)
            lower = ahead_index * micro_images
            upper = lower + micro_images
            class_result, class_part, sent_grad, section_grads = class_step(
                own_section,
                class_token[lower:upper],
                arrived,
                keep_mask[lower:upper],
                class_cotangent[lower:upper],
            )
            empty = empty_outputs(micro_images, length, model_width, own_section, mixing)
            return (sent_grad, class_result, class_part, empty[3], section_grads, empty[5])

        produced = lax.cond(first_rank, backward_first, work_second)
        sent_grad, class_result, class_part, patch_part, section_grads, mixing_grads = produced
        totals = tuple((total + grad for total, grad in zip(totals, section_grads)))
        mixing_totals = tuple((total + grad for total, grad in zip(mixing_totals, mixing_grads)))
        if behind_index >= 0:
            patch_parts.append(patch_part)
        if ahead_index < micro_count:
            returned, class_low, class_grad_low = passed_along(
                (sent_grad, class_result[:, :half_width], class_part[:, :half_width]), "pipe", -1
            )
            class_parts.append(jnp.where(first_rank, class_low, class_result[:, half_width:]))
            class_grad_parts.append(
                jnp.where(first_rank, class_grad_low, class_part[:, half_width:])
            )
    full_grad = jnp.concatenate(patch_parts, axis=0)
    moved_half = passed_along(full_grad[..., half_width:].astype(jnp.bfloat16), "pipe", 1).astype(
        jnp.float32
    )
    patch_out = jnp.where(first_rank, full_grad[..., :half_width], moved_half)
    class_out = jnp.concatenate(class_parts, axis=0)
    class_grad_out = jnp.concatenate(class_grad_parts, axis=0)
    summed = lax.psum(
        (
            totals[0],
            totals[1],
            totals[2],
            totals[3],
            totals[4],
            totals[5],
            totals[6],
            totals[7],
            totals[8],
            totals[9],
            totals[10],
            totals[11],
            totals[12],
            totals[13],
        ),
        "dp",
    )
    mixing_summed = lax.psum((mixing_totals[0], mixing_totals[1], mixing_totals[2]), ("pipe", "dp"))
    section_outs = tuple((member[None] for member in summed))
    return (
        class_out,
        patch_out,
        class_grad_out,
        section_outs[0],
        section_outs[1],
        section_outs[2],
        section_outs[3],
        section_outs[4],
        section_outs[5],
        section_outs[6],
        section_outs[7],
        section_outs[8],
        section_outs[9],
        section_outs[10],
        section_outs[11],
        section_outs[12],
        section_outs[13],
        mixing_summed[0],
        mixing_summed[1],
        mixing_summed[2],
    )


def solution(mesh):
    return jax.shard_map(
        local,
        mesh=mesh,
        in_specs=(
            P("dp", None, None),
            P("dp", None),
            P("dp", None),
            P("dp", None),
            P("pipe", None),
            P("pipe", None),
            P("pipe", None, None),
            P("pipe", None),
            P(),
            P(),
            P(),
            P("pipe", None, None),
            P("pipe", None),
            P("pipe", None),
            P("pipe", None),
            P("pipe", None),
            P("pipe", None, None),
            P("pipe", None),
            P("pipe", None, None),
            P("pipe", None),
            P("pipe", None),
        ),
        out_specs=(
            P("dp", "pipe"),
            P("dp", None, "pipe"),
            P("dp", "pipe"),
            P("pipe", None),
            P("pipe", None),
            P("pipe", None, None),
            P("pipe", None),
            P("pipe", None, None),
            P("pipe", None),
            P("pipe", None),
            P("pipe", None),
            P("pipe", None),
            P("pipe", None, None),
            P("pipe", None),
            P("pipe", None, None),
            P("pipe", None),
            P("pipe", None),
            P(),
            P(),
            P(),
        ),
        check_vma=False,
    )
```

profile of v0, /device:TPU:0, one launch (start us, length us, event | category | flops | bytes accessed | tf_op | source)
XLA Modules:
  0.0 616.5 jit_solution(18376750941637530039)
XLA Ops:
  14.3 18.4 %conditional.9 = (bf16[1,196,384]{2,1,0:T(8,128)(2,1)}) conditional(s32[]{:T(128)} %convert_element_type.1520, () %tuple.109, (bf16[4,196,384]{2,0,1:T(4,128)(2,1)}, bf16[384]{0:T(512)(128)(2,1)S(1)}, bf16[384]{0:T(512)(128)(2,1)S(1)}, bf16[384]{0:T(512)(128)(2,1)S(1)}, bf16[384,1152]{1,0:T(8,128)(2,1)}, /*index=5*/bf16[768]{0:T(1024)(128)(2,1)S(1)}, ...), branch_computations={%region_0.0_spmd, %region_1.8_spmd} | conditional | flops 837880896 | bytes 33467216 | solution.py:343
  20.6 3.0 fusion.11
  27.6 5.1 fusion.29
  34.7 18.9 %conditional.11 = (bf16[1,196,384]{2,1,0:T(8,128)(2,1)}) conditional(s32[]{:T(128)} %convert_element_type.1520, () %tuple.113, (bf16[4,196,384]{2,0,1:T(4,128)(2,1)}, bf16[384]{0:T(512)(128)(2,1)S(1)}, bf16[384]{0:T(512)(128)(2,1)S(1)}, bf16[384]{0:T(512)(128)(2,1)S(1)}, bf16[384,1152]{1,0:T(8,128)(2,1)}, /*index=5*/bf16[768]{0:T(1024)(128)(2,1)S(1)}, ...), branch_computations={%region_24.25_spmd, %region_25.32_spmd} | conditional | flops 837880896 | bytes 33467216 | solution.py:343
  41.4 3.0 fusion.185
  48.4 5.1 fusion.203
  55.5 10.1 %conditional.10 = (bf16[1,196,384]{2,1,0:T(8,128)(2,1)}, bf16[1,384]{1,0:T(2,128)(2,1)}, bf16[1,384]{1,0:T(2,128)(2,1)S(1)}, f32[384]{0:T(512)S(1)}, f32[384]{0:...) conditional(s32[]{:T(128)} %convert_element_type.1520, ...), branch_computations={%region_8.23_spmd, %region_23.24_spmd} | conditional | flops 362205568 | bytes 52824316 | solution.py:374
  67.0 19.0 %conditional.13 = (bf16[1,196,384]{2,1,0:T(8,128)(2,1)}) conditional(s32[]{:T(128)} %convert_element_type.1520, () %tuple.116, (bf16[4,196,384]{2,0,1:T(4,128)(2,1)}, bf16[384]{0:T(512)(128)(2,1)}, bf16[384]{0:T(512)(128)(2,1)}, bf16[384]{0:T(512)(128)(2,1)}, bf16[384,1152]{1,0:T(8,128)(2,1)}, /*index=5*/bf16[768]{0:T(1024)(128)(2,1)S(1)}, ...), branch_computations={%region_71.72_spmd, %region_72.79_spmd} | conditional | flops 837880896 | bytes 38321256 | solution.py:343
  75.4 2.9 fusion.445
  81.9 4.0 fusion.463
  86.0 3.5 collective-permute-start.5
  89.5 57.5 %conditional.12 = (bf16[1,196,384]{2,1,0:T(8,128)(2,1)}, bf16[1,384]{1,0:T(2,128)(2,1)S(1)}, bf16[1,384]{1,0:T(2,128)(2,1)S(1)}, f32[384]{0:T(512)S(1)}, f32[384...) conditional(s32[]{:T(128)} %convert_element_type.1520, ...), branch_computations={%region_32.47_spmd, %region_47.71_spmd} | conditional | flops 2482556928 | bytes 124973008 | solution.py:374
  98.9 2.4 fusion.364
  103.9 3.8 multiply_convert_fusion.7
  115.5 2.2 multiply_reduce_fusion.18
  117.7 4.4 fusion.376
  122.2 3.4 fusion.349
  125.7 4.6 fusion.375
  130.4 2.0 fusion.433
  132.4 2.3 fusion.363
  143.5 2.0 fusion.410
  148.4 18.5 %conditional.15 = (bf16[1,196,384]{2,1,0:T(8,128)(2,1)}) conditional(s32[]{:T(128)} %convert_element_type.1520, () %tuple.119, (bf16[4,196,384]{2,0,1:T(4,128)(2,1)}, bf16[384]{0:T(512)(128)(2,1)}, bf16[384]{0:T(512)(128)(2,1)}, bf16[384]{0:T(512)(128)(2,1)}, bf16[384,1152]{1,0:T(8,128)(2,1)}, /*index=5*/bf16[768]{0:T(1024)(128)(2,1)S(1)}, ...), branch_computations={%region_118.119_spmd, %region_119.126_spmd} | conditional | flops 837880896 | bytes 33504332 | solution.py:343
  154.8 2.9 fusion.705
  161.8 5.1 fusion.723
  168.8 60.8 %conditional.14 = (bf16[1,196,384]{2,1,0:T(8,128)(2,1)S(1)}, bf16[1,384]{1,0:T(2,128)(2,1)S(1)}, bf16[1,384]{1,0:T(2,128)(2,1)S(1)}, f32[384]{0:T(512)S(1)}, f32...) conditional(s32[]{:T(128)} %convert_element_type.1520, ...), branch_computations={%region_79.94_spmd, %region_94.118_spmd} | conditional | flops 2482556928 | bytes 124954320 | solution.py:374
  181.7 2.4 fusion.624
  186.7 3.8 multiply_convert_fusion.13
  198.4 2.3 multiply_reduce_fusion.32
  200.6 4.4 fusion.636
  205.1 3.5 fusion.609
  208.6 4.6 fusion.635
  213.3 2.0 fusion.693
  215.3 2.3 fusion.623
  226.4 2.1 fusion.670
  231.0 2.0 collective-permute-done.9
  233.0 56.7 %conditional.16 = (bf16[1,196,384]{2,1,0:T(8,128)(2,1)S(1)}, bf16[1,384]{1,0:T(2,128)(2,1)S(1)}, bf16[1,384]{1,0:T(2,128)(2,1)S(1)}, f32[384]{0:T(512)S(1)}, f32...) conditional(s32[]{:T(128)} %convert_element_type.1520, ...), branch_computations={%region_126.141_spmd, %region_141.165_spmd} | conditional | flops 2482556928 | bytes 124973008 | solution.py:374
  242.1 2.4 fusion.884
  247.0 3.8 multiply_convert_fusion.19
  258.7 2.2 multiply_reduce_fusion.46
  260.9 4.4 fusion.896
  265.4 3.4 fusion.869
  268.9 4.6 fusion.895
  273.6 2.0 fusion.953
  275.6 2.3 fusion.883
  286.8 2.1 fusion.930
  291.1 2.0 collective-permute-done.11
  293.1 53.3 %conditional.17 = (f32[384]{0:T(512)}, f32[384]{0:T(512)}, f32[384,1152]{1,0:T(8,128)S(1)}, f32[768]{0:T(1024)}, f32[384,384]{1,0:T(8,128)}, /*index=5*/f32[384]...) conditional(s32[]{:T(128)} %convert_element_type.1520, ...), branch_computations={%region_165.166_spmd, %region_166.190_spmd} | conditional | flops 2482556928 | bytes 125115784 | solution.py:374
  300.4 2.7 fusion.970
  305.7 3.8 multiply_convert_fusion.22
  317.3 2.3 multiply_reduce_fusion.51
  319.6 4.4 fusion.982
  324.0 3.4 fusion.955
  327.5 4.6 fusion.981
  332.2 2.0 fusion.1039
  334.1 2.3 fusion.969
  348.5 6.5 %add_bitcast_fusion.4 = f32[1,1536,384]{2,1,0:T(8,128)} fusion(f32[1536,384]{1,0:T(8,128)} %copy-done.67, f32[1536,384]{1,0:T(8,128)} %get-tuple-element.1074, f32[1536,384]{1,0:T(8,128)} %get-tuple-element.1073, f32[1536,384]{1,0:T(8,128)} %get-tuple-element.1071, f32[1536,384]{1,0:T(8,128)} %get-tuple-element.1072), kind=kLoop, calls=%fused_computation.1624 | loop fusion | flops 2359296 | bytes 14155776 | tf_op jit(solution)/shard_map/broadcast_in_dim | solution.py:415
  355.0 5.9 add_bitcast_fusion.5
  360.9 2.8 add_bitcast_fusion.7
  363.7 4.4 add_bitcast_fusion.6
  389.4 3.1 collective-permute-start.12
  398.5 45.8 %all-reduce = (f32[8,8]{1,0:T(8,128)}, f32[8,8]{1,0:T(8,128)}, f32[8]{0:T(128)}) all-reduce(f32[8,8]{1,0:T(8,128)S(1)} %get-tuple-element.2109, f32[8,8]{1,0:T(8,128)S(1)} %get-tuple-element.2108, f32[8]{0:T(128)S(1)} %add_add_fusion.32), channel_id=1, replica_groups=mesh['pipe'=2,'dp'=16] {'pipe','dp'}, use_global_device_ids=true, to_apply=%region_204.205 | all-reduce | flops 136 | bytes 1088 | tf_op jit(solution)/shard_map/psum | solution.py:414
  444.3 76.7 %all-reduce.1 = (f32[1,384]{1,0:T(1,128)}, f32[1,384]{1,0:T(1,128)}, f32[1,768]{1,0:T(1,128)}, f32[1,384]{1,0:T(1,128)}, f32[1,384]{1,0:T(1,128)}, /*index=5*/f3...) all-reduce(f32[1,384]{1,0:T(1,128)S(1)} %broadcast_in_dim.636, ...), channel_id=1, replica_groups=mesh['pipe'=2,'dp'=16] {'dp'}, use_global_device_ids=true, to_apply=%region_190.191 | all-reduce | flops 5376 | bytes 43008 | tf_op jit(solution)/shard_map/psum | solution.py:395
  521.9 79.9 %all-reduce.5.cloned.1.call-done = (f32[1,384,1152]{2,1,0:T(8,128)}, f32[1,384,384]{2,1,0:T(8,128)}, f32[1,384,1536]{2,1,0:T(8,128)}, f32[1,1536,384]{2,1,0:T(8,128)}) async-done(((f32[1,384,1152]{2,1,0:T(8,128)}, f32[1,384,384]{2,1,0:T(8,128)}, f32[1,384,1536]{2,1,0:T(8,128)}, f32[1,1536,384]{2,1,0:T(8,128)}), (f32[1,384,1152]{2,1,0:T(8,128)}, f32[1,384,384]{2,1,0:T(8,128)}, f32[1,384,1536]{2,1,0:T(8,128)}, ...) | async-done | bytes 7077904 | tf_op jit(solution)/shard_map/psum | solution.py:395
  601.8 2.9 copy.982
  (1320 shorter events, 215.7 us)
Async XLA Ops:
  7.2 594.6 %all-reduce.5.cloned.1.call-start = ((), (), s32[]{:S(2)}) async-start(), calls=%async_computation | async-start | bytes 14155776 | tf_op jit(solution)/shard_map/psum | solution.py:395
  8.0 47.5 %copy-start.165 = (bf16[1536]{0:T(1024)(128)(2,1)}, bf16[1536]{0:T(1024)(128)(2,1)S(1)}, u32[]{:S(2)}) copy-start(bf16[1536]{0:T(1024)(128)(2,1)S(1)} %reduce.232) | copy-start | bytes 9220
  9.4 46.1 %copy-start.261 = (bf16[384]{0:T(512)(128)(2,1)}, bf16[384]{0:T(512)(128)(2,1)S(1)}, u32[]{:S(2)}) copy-start(bf16[384]{0:T(512)(128)(2,1)S(1)} %reduce.224) | copy-start | bytes 2308
  10.1 45.4 %copy-start.303 = (bf16[384]{0:T(512)(128)(2,1)}, bf16[384]{0:T(512)(128)(2,1)S(1)}, u32[]{:S(2)}) copy-start(bf16[384]{0:T(512)(128)(2,1)S(1)} %reduce.225) | copy-start | bytes 2308
  10.8 44.7 %copy-start.313 = (bf16[384]{0:T(512)(128)(2,1)}, bf16[384]{0:T(512)(128)(2,1)S(1)}, u32[]{:S(2)}) copy-start(bf16[384]{0:T(512)(128)(2,1)S(1)} %reduce.226) | copy-start | bytes 2308
  11.5 44.0 %copy-start.331 = (bf16[384]{0:T(512)(128)(2,1)}, bf16[384]{0:T(512)(128)(2,1)S(1)}, u32[]{:S(2)}) copy-start(bf16[384]{0:T(512)(128)(2,1)S(1)} %reduce.228) | copy-start | bytes 2308
  12.2 43.3 %copy-start.271 = (bf16[384]{0:T(512)(128)(2,1)}, bf16[384]{0:T(512)(128)(2,1)S(1)}, u32[]{:S(2)}) copy-start(bf16[384]{0:T(512)(128)(2,1)S(1)} %reduce.229) | copy-start | bytes 2308
  12.9 42.6 %copy-start.251 = (bf16[384]{0:T(512)(128)(2,1)}, bf16[384]{0:T(512)(128)(2,1)S(1)}, u32[]{:S(2)}) copy-start(bf16[384]{0:T(512)(128)(2,1)S(1)} %reduce.230) | copy-start | bytes 2308
  13.6 41.9 %copy-start.323 = (bf16[384]{0:T(512)(128)(2,1)}, bf16[384]{0:T(512)(128)(2,1)S(1)}, u32[]{:S(2)}) copy-start(bf16[384]{0:T(512)(128)(2,1)S(1)} %reduce.231) | copy-start | bytes 2308
  14.3 41.2 %copy-start.339 = (bf16[384]{0:T(512)(128)(2,1)}, bf16[384]{0:T(512)(128)(2,1)S(1)}, u32[]{:S(2)}) copy-start(bf16[384]{0:T(512)(128)(2,1)S(1)} %reduce.233) | copy-start | bytes 2308
  32.7 22.8 %collective-permute-start = (bf16[1,196,384]{2,1,0:T(8,128)(2,1)}, bf16[1,196,384]{2,1,0:T(8,128)(2,1)}, u32[]{:S(2)}, u32[]{:S(2)}) collective-permute-start(bf16[1,196,384]{2,1,0:T(8,128)(2,1)} %get-tuple-element.2340), channel_id=1, source_target_pairs={{0,16},{1,17},{2,18},{3,19},{4,20},{5,21},{6,22},{7,23},{8,24},{9,... | collective-permute-start | bytes 451592 | tf_op jit(solution)/shard_map/ppermute | solution.py:14
  53.5 36.0 %collective-permute-start.2 = (bf16[1,196,384]{2,1,0:T(8,128)(2,1)}, bf16[1,196,384]{2,1,0:T(8,128)(2,1)}, u32[]{:S(2)}, u32[]{:S(2)}) collective-permute-start(bf16[1,196,384]{2,1,0:T(8,128)(2,1)} %get-tuple-element.2341), channel_id=1, source_target_pairs={{0,16},{1,17},{2,18},{3,19},{4,20},{5,21},{6,22},{7,23},{8,24},{9,... | collective-permute-start | bytes 451592 | tf_op jit(solution)/shard_map/ppermute | solution.py:14
  65.6 23.9 %collective-permute-start.3 = (bf16[1,196,384]{2,1,0:T(8,128)(2,1)}, bf16[1,196,384]{2,1,0:T(8,128)(2,1)S(1)}, u32[]{:S(2)}, u32[]{:S(2)}) collective-permute-start(bf16[1,196,384]{2,1,0:T(8,128)(2,1)} %get-tuple-element.1001), channel_id=1, source_target_pairs={{16,0},{17,1},{18,2},{19,3},{20,4},{21,5},{22,6},{23,7},{24,8},{25... | collective-permute-start | bytes 451592 | tf_op jit(solution)/shard_map/ppermute | solution.py:14
  86.0 82.9 %collective-permute-start.5 = (bf16[1,196,384]{2,1,0:T(8,128)(2,1)}, bf16[1,196,384]{2,1,0:T(8,128)(2,1)}, u32[]{:S(2)}, u32[]{:S(2)}) collective-permute-start(bf16[1,196,384]{2,1,0:T(8,128)(2,1)} %get-tuple-element.2342), channel_id=1, source_target_pairs={{0,16},{1,17},{2,18},{3,19},{4,20},{5,21},{6,22},{7,23},{8,24},{9,... | collective-permute-start | bytes 451592 | tf_op jit(solution)/shard_map/ppermute | solution.py:14
  147.1 21.8 %collective-permute-start.6 = (bf16[1,196,384]{2,1,0:T(8,128)(2,1)}, bf16[1,196,384]{2,1,0:T(8,128)(2,1)S(1)}, u32[]{:S(2)}, u32[]{:S(2)}) collective-permute-start(bf16[1,196,384]{2,1,0:T(8,128)(2,1)} %get-tuple-element.1003), channel_id=1, source_target_pairs={{16,0},{17,1},{18,2},{19,3},{20,4},{21,5},{22,6},{23,7},{24,8},{25... | collective-permute-start | bytes 451592 | tf_op jit(solution)/shard_map/ppermute | solution.py:14
  166.9 64.1 %collective-permute-start.8 = (bf16[1,196,384]{2,1,0:T(8,128)(2,1)}, bf16[1,196,384]{2,1,0:T(8,128)(2,1)}, u32[]{:S(2)}, u32[]{:S(2)}) collective-permute-start(bf16[1,196,384]{2,1,0:T(8,128)(2,1)} %get-tuple-element.2343), channel_id=1, source_target_pairs={{0,16},{1,17},{2,18},{3,19},{4,20},{5,21},{6,22},{7,23},{8,24},{9,... | collective-permute-start | bytes 451592 | tf_op jit(solution)/shard_map/ppermute | solution.py:14
  229.7 3.3 collective-permute-start.9
  289.8 3.3 collective-permute-start.11
  368.0 10.6 %copy-start.586 = (bf16[1,384]{1,0:T(2,128)(2,1)S(1)}, bf16[1,384]{1,0:T(2,128)(2,1)}, u32[]{:S(2)}) copy-start(bf16[1,384]{1,0:T(2,128)(2,1)} %copy-done.585) | copy-start | bytes 2308
  368.0 11.8 %copy-start.579 = (bf16[1,384]{1,0:T(2,128)(2,1)S(1)}, bf16[1,384]{1,0:T(2,128)(2,1)}, u32[]{:S(2)}) copy-start(bf16[1,384]{1,0:T(2,128)(2,1)} %copy-done.578) | copy-start | bytes 2308
  368.1 14.9 %copy-start.588 = (bf16[1,384]{1,0:T(2,128)(2,1)S(1)}, bf16[1,384]{1,0:T(2,128)(2,1)}, u32[]{:S(2)}) copy-start(bf16[1,384]{1,0:T(2,128)(2,1)} %copy-done.587) | copy-start | bytes 2308
  368.1 16.2 %copy-start.581 = (bf16[1,384]{1,0:T(2,128)(2,1)S(1)}, bf16[1,384]{1,0:T(2,128)(2,1)}, u32[]{:S(2)}) copy-start(bf16[1,384]{1,0:T(2,128)(2,1)} %copy-done.580) | copy-start | bytes 2308
  368.7 3.0 collective-permute-start.13
  370.0 3.0 collective-permute-start.1
  373.1 3.6 collective-permute-start.14
  375.5 3.0 collective-permute-start.4
  378.6 3.7 collective-permute-start.15
  379.9 3.0 collective-permute-start.7
  382.2 10.2 %copy-start.523 = (f32[768]{0:T(1024)S(1)}, f32[768]{0:T(1024)}, u32[]{:S(2)}) copy-start(f32[768]{0:T(1024)} %get-tuple-element.1032) | copy-start | bytes 9220
  382.2 10.2 %copy-start.524 = (f32[768]{0:T(1024)S(1)}, f32[768]{0:T(1024)}, u32[]{:S(2)}) copy-start(f32[768]{0:T(1024)} %get-tuple-element.1033) | copy-start | bytes 9220
  382.2 10.2 %copy-start.525 = (f32[768]{0:T(1024)S(1)}, f32[768]{0:T(1024)}, u32[]{:S(2)}) copy-start(f32[768]{0:T(1024)} %get-tuple-element.1034) | copy-start | bytes 9220
  382.3 10.2 %copy-start.526 = (f32[768]{0:T(1024)S(1)}, f32[768]{0:T(1024)}, u32[]{:S(2)}) copy-start(f32[768]{0:T(1024)} %get-tuple-element.1031) | copy-start | bytes 9220
  382.3 10.9 %copy-start.508 = (f32[384]{0:T(512)S(1)}, f32[384]{0:T(512)}, u32[]{:S(2)}) copy-start(f32[384]{0:T(512)} %get-tuple-element.1077) | copy-start | bytes 4612
  382.3 10.9 %copy-start.510 = (f32[384]{0:T(512)S(1)}, f32[384]{0:T(512)}, u32[]{:S(2)}) copy-start(f32[384]{0:T(512)} %get-tuple-element.1078) | copy-start | bytes 4612
  382.3 10.9 %copy-start.512 = (f32[384]{0:T(512)S(1)}, f32[384]{0:T(512)}, u32[]{:S(2)}) copy-start(f32[384]{0:T(512)} %get-tuple-element.1079) | copy-start | bytes 4612
  382.3 10.9 %copy-start.514 = (f32[384]{0:T(512)S(1)}, f32[384]{0:T(512)}, u32[]{:S(2)}) copy-start(f32[384]{0:T(512)} %get-tuple-element.1076) | copy-start | bytes 4612
  382.3 10.9 %copy-start.613 = (f32[384]{0:T(512)S(1)}, f32[384]{0:T(512)}, u32[]{:S(2)}) copy-start(f32[384]{0:T(512)} %copy-done.612) | copy-start | bytes 4612
  383.0 4.0 collective-permute-start.16
  384.3 3.3 collective-permute-start.10
  385.6 8.3 %copy-start.475 = (f32[384]{0:T(512)S(1)}, f32[384]{0:T(512)}, u32[]{:S(2)}) copy-start(f32[384]{0:T(512)} %get-tuple-element.1057) | copy-start | bytes 4612
  385.7 8.3 %copy-start.477 = (f32[384]{0:T(512)S(1)}, f32[384]{0:T(512)}, u32[]{:S(2)}) copy-start(f32[384]{0:T(512)} %get-tuple-element.1058) | copy-start | bytes 4612
  385.7 9.0 %copy-start.467 = (f32[384]{0:T(512)S(1)}, f32[384]{0:T(512)}, u32[]{:S(2)}) copy-start(f32[384]{0:T(512)} %get-tuple-element.1042) | copy-start | bytes 4612
  385.7 9.0 %copy-start.469 = (f32[384]{0:T(512)S(1)}, f32[384]{0:T(512)}, u32[]{:S(2)}) copy-start(f32[384]{0:T(512)} %get-tuple-element.1043) | copy-start | bytes 4612
  385.7 9.0 %copy-start.471 = (f32[384]{0:T(512)S(1)}, f32[384]{0:T(512)}, u32[]{:S(2)}) copy-start(f32[384]{0:T(512)} %get-tuple-element.1044) | copy-start | bytes 4612
  385.8 9.0 %copy-start.473 = (f32[384]{0:T(512)S(1)}, f32[384]{0:T(512)}, u32[]{:S(2)}) copy-start(f32[384]{0:T(512)} %get-tuple-element.1041) | copy-start | bytes 4612
  385.8 9.0 %copy-start.611 = (f32[384]{0:T(512)S(1)}, f32[384]{0:T(512)}, u32[]{:S(2)}) copy-start(f32[384]{0:T(512)} %get-tuple-element.1047) | copy-start | bytes 4612
  385.8 9.0 %copy-start.614 = (f32[384]{0:T(512)S(1)}, f32[384]{0:T(512)}, u32[]{:S(2)}) copy-start(f32[384]{0:T(512)} %get-tuple-element.1048) | copy-start | bytes 4612
  385.8 9.7 %copy-start.591 = (f32[384]{0:T(512)S(1)}, f32[384]{0:T(512)}, u32[]{:S(2)}) copy-start(f32[384]{0:T(512)} %get-tuple-element.1022) | copy-start | bytes 4612
  385.8 9.7 %copy-start.594 = (f32[384]{0:T(512)S(1)}, f32[384]{0:T(512)}, u32[]{:S(2)}) copy-start(f32[384]{0:T(512)} %copy-done.593) | copy-start | bytes 4612
  385.8 9.7 %copy-start.595 = (f32[384]{0:T(512)S(1)}, f32[384]{0:T(512)}, u32[]{:S(2)}) copy-start(f32[384]{0:T(512)} %get-tuple-element.1023) | copy-start | bytes 4612
  385.8 9.7 %copy-start.598 = (f32[384]{0:T(512)S(1)}, f32[384]{0:T(512)}, u32[]{:S(2)}) copy-start(f32[384]{0:T(512)} %copy-done.597) | copy-start | bytes 4612
  385.8 9.7 %copy-start.599 = (f32[384]{0:T(512)S(1)}, f32[384]{0:T(512)}, u32[]{:S(2)}) copy-start(f32[384]{0:T(512)} %get-tuple-element.1024) | copy-start | bytes 4612
  385.8 9.7 %copy-start.602 = (f32[384]{0:T(512)S(1)}, f32[384]{0:T(512)}, u32[]{:S(2)}) copy-start(f32[384]{0:T(512)} %copy-done.601) | copy-start | bytes 4612
  385.8 9.7 %copy-start.604 = (f32[384]{0:T(512)S(1)}, f32[384]{0:T(512)}, u32[]{:S(2)}) copy-start(f32[384]{0:T(512)} %copy-done.603) | copy-start | bytes 4612
  385.9 9.7 %copy-start.606 = (f32[384]{0:T(512)S(1)}, f32[384]{0:T(512)}, u32[]{:S(2)}) copy-start(f32[384]{0:T(512)} %copy-done.605) | copy-start | bytes 4612
  385.9 10.4 %copy-start.372 = (f32[1536]{0:T(1024)S(1)}, f32[1536]{0:T(1024)}, u32[]{:S(2)}) copy-start(f32[1536]{0:T(1024)} %get-tuple-element.1067) | copy-start | bytes 18436
  385.9 10.3 %copy-start.374 = (f32[1536]{0:T(1024)S(1)}, f32[1536]{0:T(1024)}, u32[]{:S(2)}) copy-start(f32[1536]{0:T(1024)} %get-tuple-element.1068) | copy-start | bytes 18436
  385.9 10.3 %copy-start.376 = (f32[1536]{0:T(1024)S(1)}, f32[1536]{0:T(1024)}, u32[]{:S(2)}) copy-start(f32[1536]{0:T(1024)} %get-tuple-element.1069) | copy-start | bytes 18436
  385.9 10.3 %copy-start.378 = (f32[1536]{0:T(1024)S(1)}, f32[1536]{0:T(1024)}, u32[]{:S(2)}) copy-start(f32[1536]{0:T(1024)} %get-tuple-element.1066) | copy-start | bytes 18436
  385.9 11.9 %copy-start.527 = (f32[8,8]{1,0:T(8,128)S(1)}, f32[8,8]{1,0:T(8,128)}, u32[]{:S(2)}) copy-start(f32[8,8]{1,0:T(8,128)} %get-tuple-element.1088) | copy-start | bytes 772
  385.9 11.9 %copy-start.528 = (f32[8,8]{1,0:T(8,128)S(1)}, f32[8,8]{1,0:T(8,128)}, u32[]{:S(2)}) copy-start(f32[8,8]{1,0:T(8,128)} %get-tuple-element.1092) | copy-start | bytes 772
  385.9 11.9 %copy-start.529 = (f32[8,8]{1,0:T(8,128)S(1)}, f32[8,8]{1,0:T(8,128)}, u32[]{:S(2)}) copy-start(f32[8,8]{1,0:T(8,128)} %get-tuple-element.1089) | copy-start | bytes 772
  385.9 11.9 %copy-start.530 = (f32[8,8]{1,0:T(8,128)S(1)}, f32[8,8]{1,0:T(8,128)}, u32[]{:S(2)}) copy-start(f32[8,8]{1,0:T(8,128)} %get-tuple-element.1093) | copy-start | bytes 772
  389.4 131.5 %collective-permute-start.12 = (bf16[4,196,192]{1,2,0:T(8,128)(2,1)S(1)}, bf16[4,196,192]{1,2,0:T(8,128)(2,1)S(1)}, u32[]{:S(2)}, u32[]{:S(2)}) collective-permute-start(bf16[4,196,192]{1,2,0:T(8,128)(2,1)S(1)} %slice.910), channel_id=1, source_target_pairs={{0,16},{1,17},{2,18},{3,19},{4,20},{5,21},{6,22},{7,23},{8,24},{9,... | collective-permute-start | bytes 903176 | tf_op jit(solution)/shard_map/ppermute | solution.py:14
  (379 other events, 911.2 us)
Sparse Core Ops, SparseCore 0:
  368.2 233.5 all-reduce.4
where the time goes:
time: 626 us; the launch traced here: 617 us
  matrix products  210 us (34%)
  blocking collectives  122 us (19%)
  waiting for transfers between devices  87.7 us (14%)
  local copies, waits for them, and re-layouts  74.7 us (12%)
  other arithmetic  66.6 us (11%)
  starting transfers between devices  27.9 us (4%)
  between operations  15.6 us (2%)
  loops' own time  11.6 us (2%)
    dot_general x92, matrix products, matmul(): jnp.einsum(pattern, left_side, right_side, preferred_element_type=jnp.flo...  115 us
    psum x1, waiting for transfers between devices, local(): lax.psum((totals[0], totals[1], totals[2], totals[3], totals[4], totals[5...  79.9 us
    psum x1, blocking collectives, local(): lax.psum((totals[0], totals[1], totals[2], totals[3], totals[4], totals[5...  76.7 us
    dot_general x16, matrix products, mixing_piece(): jnp.einsum('hc,bcij->bhij', mix_second, weights, precision=lax.Precision....  52.9 us
    psum x1, blocking collectives, local(): lax.psum((mixing_totals[0], mixing_totals[1], mixing_totals[2]), ('pipe',...  45.8 us
    dot_general x16, matrix products, mixing_piece(): jnp.einsum('hc,bcij->bhij', mix_first, raw_part * head_dim ** (-0.5), pre...  42 us
    ppermute x17, starting transfers between devices, passed_along(): return lax.ppermute(array, axis, pairs)  27.9 us
    cond x684, local copies, waits for them, and re-layouts  21.3 us
  transfers between devices with their start and end apart: 18, of which 7 were waited for; matrix products, arithmetic and copies ran while one was open for 29% of the time, Pallas kernels for 0%

commit v1 on v0

v1 whole, which is shorter than its diff:
```python
import jax
import jax.numpy as jnp
from jax import lax
from jax.experimental import pallas as pl
from jax.experimental.pallas import tpu as pltpu
from jax.sharding import PartitionSpec as P

HEADS = 8
IMGS = 2
VMEM_LIMIT = 48 * 1024 * 1024
LOG2E = 1.4426950408889634
F32 = jnp.float32
BF16 = jnp.bfloat16


def mm(left, right):
    return lax.dot_general(left, right, (((1,), (0,)), ((), ())), preferred_element_type=F32)


def mm_nt(left, right):
    return lax.dot_general(left, right, (((1,), (1,)), ((), ())), preferred_element_type=F32)


def mm_tn(left, right):
    return lax.dot_general(left, right, (((0,), (0,)), ((), ())), preferred_element_type=F32)


def normed(rows):
    centred = rows - jnp.mean(rows, -1, keepdims=True)
    scale = lax.rsqrt(jnp.mean(centred * centred, -1, keepdims=True) + 1e-06)
    return centred * scale, scale


def norm_back(normal, scale, grad):
    inner = jnp.mean(grad * normal, -1, keepdims=True)
    return (grad - jnp.mean(grad, -1, keepdims=True) - normal * inner) * scale


def col_sum(rows):
    return jnp.sum(rows, axis=0, keepdims=True)


def gelu_pair(rows):
    size = jnp.abs(rows)
    bell = jnp.exp2(rows * rows * (-0.5 * LOG2E))
    t = 1.0 / (1.0 + (0.3275911 * 0.7071067811865476) * size)
    poly = t * (0.254829592 + t * (-0.284496736 + t * (1.421413741 + t * (-1.453152027 + t * 1.061405429))))
    tail = 0.5 * poly * bell
    phi = jnp.where(rows < 0.0, tail, 1.0 - tail)
    return rows * phi, phi + rows * (bell * 0.3989422804014327)


def head_mask(rows, width):
    lane = lax.broadcasted_iota(jnp.int32, (rows, width), 1)
    head = lax.rem(lax.broadcasted_iota(jnp.int32, (rows, width), 0), HEADS)
    size = width // HEADS
    return (lane >= head * size) & (lane < head * size + size)


def chosen(is_first, first, other):
    return jnp.where(is_first, first, other)


def transposed(rows):
    return rows.T


def attention_forward(
    place, mix_pre, mix_post, rows_ref, keep_ref, vec_own, vec_got, w_own, w_got, bias_ref,
    att_ref, hid_ref, q_ref, k_ref, v_ref, pt_ref, w_ref, vs_ref,
):
    first = place[0] == 0
    width = rows_ref.shape[2]
    length = rows_ref.shape[1]
    lanes = q_ref.shape[1]
    size = width // HEADS

    @pl.when(first)
    def _():
        w_ref[...] = w_own[...]

    @pl.when(jnp.logical_not(first))
    def _():
        w_ref[...] = w_got[...]

    vec = chosen(first, vec_own[...].astype(F32), vec_got[...].astype(F32))
    scale = size ** (-0.5) * LOG2E
    pad_rows = jnp.zeros((lanes - length, width), BF16)
    same = lax.broadcasted_iota(jnp.int32, (length, lanes), 0) == lax.broadcasted_iota(jnp.int32, (length, lanes), 1)

    for b in range(IMGS):
        normal, _ = normed(rows_ref[b].astype(F32))
        hidden = (normal * vec[0:1] + vec[1:2]).astype(BF16)
        hid_ref[b] = hidden
        joined = mm(hidden, w_ref[...])
        queries = joined[:, :width] + vec[2:3]
        keys = joined[:, width : 2 * width]
        values = joined[:, 2 * width :] + vec[3:4]
        low_k = keys.astype(BF16)
        low_v = values.astype(BF16)
        q_ref[b, :length] = queries.astype(BF16)
        k_ref[b, :length] = low_k
        v_ref[b, :length] = low_v
        q_ref[b, length:] = pad_rows
        k_ref[b, length:] = pad_rows
        v_ref[b, length:] = pad_rows
        q_t = transposed(q_ref[b].astype(F32))
        v_t = transposed(v_ref[b].astype(F32))
        keep = keep_ref[b]
        allowed = (keep > 0.0) | same
        for h in range(HEADS):
            scaled_q = jnp.concatenate(
                [q_t[c * size : (c + 1) * size] * mix_pre[h, c] for c in range(HEADS)], axis=0
            ).astype(BF16)
            scores = jnp.where(allowed, mm(low_k, scaled_q) * scale, -1e30)
            top = jnp.max(scores, axis=0, keepdims=True)
            weights = jnp.exp2(scores - top)
            weights = weights * (1.0 / jnp.sum(weights, axis=0, keepdims=True))
            pt_ref[b, h * lanes : h * lanes + length] = weights.astype(BF16)
            pt_ref[b, h * lanes + length : (h + 1) * lanes] = jnp.zeros((lanes - length, lanes), BF16)
            vs_ref[:, h * lanes : (h + 1) * lanes] = jnp.concatenate(
                [v_t[c * size : (c + 1) * size] * mix_post[c, h] for c in range(HEADS)], axis=0
            ).astype(BF16)
        mixed = transposed(mm(vs_ref[...], pt_ref[b]))[:length]
        low_f = low_v.astype(F32)
        extra = bias_ref[...] * (col_sum(low_f * keep) + (1.0 - keep) * low_f)
        att_ref[b] = (mixed + extra).astype(BF16)


def block_copy(place, source, target, start, count):
    for n in range(count):
        at = position_block(place, start + n)
        target[n] = source[at]


def position_block(place, at):
    first_bit, second_bit = (at >> 3) & 1, (at >> 2) & 1
    rest = ((at >> 4) << 4) | ((at & 1) << 3) | (((at >> 1) & 1) << 2)
    x_first = rest | first_bit | (second_bit << 1)
    y_first = rest | second_bit | (first_bit << 1)
    flip = place[0] ^ (at >> 4)
    return jnp.where(flip == 0, x_first, y_first) ^ place[1]


def block_position(place, block):
    apart = block ^ place[1]
    x_bit, y_bit = apart & 1, (apart >> 1) & 1
    half = apart >> 4
    straight = (place[0] ^ half) == 0
    top = jnp.where(straight, (x_bit << 3) | (y_bit << 2), (y_bit << 3) | (x_bit << 2))
    return (half << 4) | top | (((apart >> 2) & 1) << 1) | ((apart >> 3) & 1)


def put_blocks(target, rows, start, wide):
    tall, across = 48, 384
    for rb in range(rows.shape[0] // tall):
        for cb in range(rows.shape[1] // across):
            block = rb * wide[0] + wide[1] + cb
            for k in range(3):
                piece = rows[rb * tall : (rb + 1) * tall, cb * across + k * 128 : cb * across + (k + 1) * 128]
                target[block, start + k * tall : start + (k + 1) * tall] = piece.astype(BF16)


def middle_kernel(
    place, att_ref, rows_ref, keep_rows, class_ref, cot_ref,
    vec_own, vec_got, p_own, p_got, f1_own, f1_got, f2_own, f2_got, w_own, w_got,
    send_ref, kept_ref, mg_ref, vec_out, vec_out1, class_out, factor_ref,
    p0_ref, f10, f20, p1_ref, f11, f21, w1_ref, act_ref, gp_ref, blocks,
):
    first = place[0] == 0
    length, width = rows_ref.shape[1], rows_ref.shape[2]
    flat = IMGS * length
    size = width // HEADS
    patches = 196

    @pl.when(first)
    def _():
        p0_ref[...] = p_own[...]
        f10[...] = f1_own[...]
        f20[...] = f2_own[...]
        p1_ref[...] = p_got[...]
        f11[...] = f1_got[...]
        f21[...] = f2_got[...]
        w1_ref[...] = w_got[...]

    @pl.when(jnp.logical_not(first))
    def _():
        p0_ref[...] = p_got[...]
        f10[...] = f1_got[...]
        f20[...] = f2_got[...]
        p1_ref[...] = p_own[...]
        f11[...] = f1_own[...]
        f21[...] = f2_own[...]
        w1_ref[...] = w_own[...]

    own, got = vec_own[...].astype(F32), vec_got[...].astype(F32)
    vec, vec1 = chosen(first, own, got), chosen(first, got, own)

    def wide_bias(v):
        return jnp.concatenate([v[8 + k : 9 + k] for k in range(4)], axis=1)

    branch = mm(att_ref[...].reshape(flat, width), p0_ref[...]) + vec[4:5]
    middle = rows_ref[...].reshape(flat, width).astype(F32) + vec[5:6] * branch
    normal, norm_scale = normed(middle)
    inner_low = (normal * vec[6:7] + vec[7:8]).astype(BF16)
    bias = wide_bias(vec)
    step = 384
    for k in range(4):
        cut = slice(k * step, (k + 1) * step)
        inner = mm(inner_low, f10[:, cut]) + bias[:, cut]
        active, slope = gelu_pair(inner)
        act_ref[:, cut] = active.astype(BF16)
        gp_ref[:, cut] = slope.astype(BF16)
    outer = mm(act_ref[...], f20[...]) + vec[12:13]
    sent = (middle + vec[13:14] * outer).astype(BF16).astype(F32)

    class_rows = class_ref[...].astype(F32)
    normal_c, _ = normed(class_rows)
    hidden_c = (normal_c * vec1[0:1] + vec1[1:2]).astype(BF16)
    query = (mm(hidden_c, w1_ref[:, :width]) + vec1[2:3]).astype(BF16).astype(F32)
    mask = head_mask(IMGS * HEADS, width)

    def spread(rows):
        both = jnp.concatenate(
            [jnp.broadcast_to(rows[b : b + 1], (HEADS, width)) for b in range(IMGS)], axis=0
        )
        return jnp.where(mask, both, 0.0)

    def gathered(rows):
        kept = jnp.where(mask, rows, 0.0)
        parts = [col_sum(kept[b * HEADS : (b + 1) * HEADS]) for b in range(IMGS)]
        return jnp.concatenate(parts + [jnp.zeros((8 - IMGS, width), F32)], axis=0)

    query_rows = mm_nt(spread(query).astype(BF16), w1_ref[:, width : 2 * width]).astype(BF16)
    at_row = lax.broadcasted_iota(jnp.int32, (length, width), 0)
    hiddens, normals, scales, probs, low_probs, sums, whs = [], [], [], [], [], [], []
    for b in range(IMGS):
        tokens = jnp.where(at_row == patches, class_rows[b : b + 1], sent[b * length : (b + 1) * length])
        n1, s1 = normed(tokens)
        h1 = (n1 * vec1[0:1] + vec1[1:2]).astype(BF16)
        scores = mm_nt(query_rows[b * HEADS : (b + 1) * HEADS], h1) * (size ** (-0.5) * LOG2E)
        scores = jnp.where(keep_rows[b : b + 1] > 0.0, scores, -1e30)
        weights = jnp.exp2(scores - jnp.max(scores, axis=-1, keepdims=True))
        weights = weights / jnp.sum(weights, axis=-1, keepdims=True)
        low = weights.astype(BF16)
        hiddens.append(h1)
        normals.append(n1)
        scales.append(s1)
        probs.append(weights)
        low_probs.append(low)
        sums.append(jnp.sum(low.astype(F32), axis=-1, keepdims=True))
        whs.append(mm(low, h1))
    wh = jnp.concatenate(whs, axis=0).astype(BF16)
    prob_sum = gathered(jnp.broadcast_to(jnp.concatenate(sums, axis=0), (IMGS * HEADS, width)))
    att1 = (gathered(mm(wh, w1_ref[:, 2 * width :])) + vec1[3:4] * prob_sum).astype(BF16)
    branch1 = mm(att1, p1_ref[...]) + vec1[4:5]
    middle1 = class_rows + vec1[5:6] * branch1
    normal2, scale2 = normed(middle1)
    inner1 = (normal2 * vec1[6:7] + vec1[7:8]).astype(BF16)
    active1, slope1 = gelu_pair(mm(inner1, f11[...]) + wide_bias(vec1))
    outer1 = mm(active1.astype(BF16), f21[...]) + vec1[12:13]
    class_result = middle1 + vec1[13:14] * outer1

    upper1 = cot_ref[...].astype(F32)
    og1 = (upper1 * vec1[13:14]).astype(BF16)
    ig1 = (mm_nt(og1, f21[...]) * slope1).astype(BF16)
    dh2 = mm_nt(ig1, f11[...])
    mg1 = upper1 + norm_back(normal2, scale2, dh2 * vec1[6:7])
    bg1 = (mg1 * vec1[5:6]).astype(BF16)
    da1 = mm_nt(bg1, p1_ref[...]).astype(BF16).astype(F32)
    value_rows = mm_nt(spread(da1).astype(BF16), w1_ref[:, 2 * width :]).astype(BF16)
    low_grads, gs = [], []
    for b in range(IMGS):
        part = slice(b * HEADS, (b + 1) * HEADS)
        dw = mm_nt(value_rows[part], hiddens[b])
        ds = probs[b] * (dw - jnp.sum(probs[b] * dw, axis=-1, keepdims=True))
        low = (ds * size ** (-0.5)).astype(BF16)
        low_grads.append(low)
        gs.append(mm(low, hiddens[b]))
    g_rows = jnp.concatenate(gs, axis=0).astype(BF16)
    dq1 = gathered(mm(g_rows, w1_ref[:, width : 2 * width])).astype(BF16)
    dclass = mm_nt(dq1, w1_ref[:, :width])
    uppers, class_grads = [], []
    n1g, n1b = jnp.zeros((1, width), F32), jnp.zeros((1, width), F32)
    for b in range(IMGS):
        part = slice(b * HEADS, (b + 1) * HEADS)
        left = jnp.concatenate([low_grads[b], low_probs[b]], axis=0)
        right = jnp.concatenate([query_rows[part], value_rows[part]], axis=0)
        dh1 = mm_tn(left, right)
        dh1 = jnp.where(at_row == patches, dh1 + dclass[b : b + 1], dh1)
        n1g = n1g + col_sum(dh1 * normals[b])
        n1b = n1b + col_sum(dh1)
        dtokens = norm_back(normals[b], scales[b], dh1 * vec1[0:1])
        class_grads.append(dtokens[patches : patches + 1] + mg1[b : b + 1])
        uppers.append(jnp.where(at_row < patches, dtokens, 0.0).astype(BF16).astype(F32))
    upper = jnp.concatenate(uppers, axis=0)
    blank = jnp.zeros((8 - IMGS, width), F32)
    class_out[0:8] = class_result
    class_out[8:16] = jnp.concatenate(class_grads + [blank], axis=0)
    ig1_sum = col_sum(ig1.astype(F32))
    vec_out1[...] = jnp.concatenate(
        [
            n1g,
            n1b,
            col_sum(dq1.astype(F32)),
            col_sum(da1 * prob_sum),
            col_sum(bg1.astype(F32)),
            col_sum(mg1 * branch1),
            col_sum(dh2 * normal2),
            col_sum(dh2),
        ]
        + [ig1_sum[:, k * width : (k + 1) * width] for k in range(4)]
        + [col_sum(og1.astype(F32)), col_sum(upper1 * outer1), jnp.zeros((2, width), F32)],
        axis=0,
    )
    pieces = [piece.astype(F32)[0:IMGS] for piece in (hidden_c, att1, bg1, inner1, og1)]
    vectors = jnp.concatenate(pieces + [jnp.zeros((16 - 5 * IMGS, width), F32)], axis=0).astype(BF16)
    for k in range(3):
        lanes = slice(k * 128, (k + 1) * 128)
        factor_ref[k * 48 : k * 48 + 16] = wh[:, lanes]
        factor_ref[k * 48 + 16 : k * 48 + 32] = g_rows[:, lanes]
        factor_ref[k * 48 + 32 : k * 48 + 48] = vectors[:, lanes]

    sm_grad = col_sum(upper * outer)
    og = (upper * vec[13:14]).astype(BF16)
    put_blocks(blocks, mm_tn(act_ref[...], og), 144, (1, 0))
    dh = jnp.zeros((flat, width), F32)
    fc1_sums = []
    for k in range(4):
        cut = slice(k * step, (k + 1) * step)
        ig = (mm_nt(og, f20[cut, :]) * gp_ref[:, cut].astype(F32)).astype(BF16)
        fc1_sums.append(col_sum(ig.astype(F32)))
        put_blocks(blocks, mm_tn(inner_low, ig), 0, (4, k))
        dh = dh + mm_nt(ig, f10[:, cut])
    mg = upper + norm_back(normal, norm_scale, dh * vec[6:7])
    mg_ref[...] = mg.reshape(IMGS, length, width)
    vec_out[...] = jnp.concatenate(
        [jnp.zeros((4, width), F32), jnp.zeros((1, width), F32), col_sum(mg * branch), col_sum(dh * normal), col_sum(dh)]
        + fc1_sums
        + [col_sum(og.astype(F32)), sm_grad, jnp.zeros((2, width), F32)],
        axis=0,
    )
    block_copy(place, blocks, kept_ref, 0, 16)
    block_copy(place, blocks, send_ref, 16, 16)


def attention_backward(
    place, mix_pre, mix_post, mg_ref, rows_ref, keep_ref, hid_ref, q_ref, k_ref, v_ref, pt_ref, att_ref,
    vec_in, vec_in1, vec_own, vec_got, w_own, w_got, p_own, p_got, bias_ref, pre_rows, post_rows,
    send_ref, kept_ref, own_half, other_half,
    w_ref, p_ref, dm_ref, ks_ref, da_ref, join_ref, bg_ref, blocks, tall_ref,
):
    first = place[0] == 0
    length, width = rows_ref.shape[1], rows_ref.shape[2]
    lanes = q_ref.shape[1]
    size = width // HEADS
    flat = IMGS * length
    root = size ** (-0.5)

    @pl.when(first)
    def _():
        w_ref[...] = w_own[...]
        p_ref[...] = p_own[...]

    @pl.when(jnp.logical_not(first))
    def _():
        w_ref[...] = w_got[...]
        p_ref[...] = p_got[...]

    vec = chosen(first, vec_own[...].astype(F32), vec_got[...].astype(F32))
    mg = mg_ref[...].reshape(flat, width)
    bg = (mg * vec[5:6]).astype(BF16)
    bg_ref[...] = bg
    pb_grad = col_sum(bg.astype(F32))
    put_blocks(blocks, mm_tn(att_ref[...].reshape(flat, width), bg), 0, (4, 3))
    pad_rows = jnp.zeros((lanes - length, width), BF16)
    pre_sum = jnp.zeros((HEADS, width), F32)
    post_sum = jnp.zeros((HEADS, width), F32)
    bias_sum = jnp.zeros((1, width), F32)
    for b in range(IMGS):
        da = mm_nt(bg_ref[b * length : (b + 1) * length], p_ref[...]).astype(BF16)
        da_ref[:length] = da
        da_ref[length:] = pad_rows
        da_t = transposed(da_ref[...].astype(F32))
        k_t = transposed(k_ref[b].astype(F32))
        low_v = v_ref[b, :length]
        val_f = low_v.astype(F32)
        key_f = k_ref[b, :length].astype(F32)
        da_f = da.astype(F32)
        keep = keep_ref[b]
        biased = da_f * bias_ref[...]
        dv = keep * col_sum(biased) + (1.0 - keep) * biased
        bias_sum = bias_sum + col_sum(da_f * (col_sum(val_f * keep) + (1.0 - keep) * val_f))
        post_parts = []
        for c in range(HEADS):
            scaled = jnp.concatenate(
                [da_t[h * size : (h + 1) * size] * mix_post[h, c] for h in range(HEADS)], axis=0
            ).astype(BF16)
            dp = mm(low_v, scaled)
            weights = pt_ref[b, c * lanes : c * lanes + length]
            w_f = weights.astype(F32)
            dm = w_f * (dp - col_sum(w_f * dp))
            dm_ref[c * lanes : c * lanes + length] = dm.astype(BF16)
            dm_ref[c * lanes + length : (c + 1) * lanes] = jnp.zeros((lanes - length, lanes), BF16)
            moved = mm(weights, da_ref[...])
            dv = dv + moved * post_rows[c : c + 1]
            post_parts.append(col_sum(moved * val_f))
            ks_ref[:, c * lanes : (c + 1) * lanes] = jnp.concatenate(
                [k_t[h * size : (h + 1) * size] * mix_pre[c, h] for h in range(HEADS)], axis=0
            ).astype(BF16)
        post_sum = post_sum + jnp.concatenate(post_parts, axis=0)
        dk = jnp.zeros((length, width), F32)
        pre_parts = []
        for h in range(HEADS):
            moved = mm(dm_ref[h * lanes : h * lanes + length], q_ref[b])
            dk = dk + moved * pre_rows[h : h + 1]
            pre_parts.append(col_sum(moved * key_f))
        pre_sum = pre_sum + jnp.concatenate(pre_parts, axis=0)
        dq = transposed(mm(ks_ref[...], dm_ref[...]))[:length] * root
        join_ref[b * length : (b + 1) * length, :width] = dq.astype(BF16)
        join_ref[b * length : (b + 1) * length, width : 2 * width] = (dk * root).astype(BF16)
        join_ref[b * length : (b + 1) * length, 2 * width :] = dv.astype(BF16)
    joined = join_ref[...]
    hidden = hid_ref[...].reshape(flat, width)
    for k in range(3):
        put_blocks(blocks, mm_tn(hidden, join_ref[:, k * width : (k + 1) * width]), 0, (4, k))
    dh = mm_nt(joined, w_ref[...])
    normal, norm_scale = normed(rows_ref[...].reshape(flat, width).astype(F32))
    patch = mg + norm_back(normal, norm_scale, dh * vec[0:1])
    half = width // 2
    low_half, high_half = patch[:, :half], patch[:, half:]
    own_half[...] = jnp.where(first, low_half, high_half).reshape(IMGS, length, half)
    other_half[...] = jnp.where(first, high_half, low_half).astype(BF16).reshape(IMGS, length, half)

    dq_sum = col_sum(join_ref[:, :width].astype(F32))
    dv_sum = col_sum(join_ref[:, 2 * width :].astype(F32))
    late = jnp.concatenate(
        [col_sum(dh * normal), col_sum(dh), dq_sum, dv_sum, pb_grad, jnp.zeros((11, width), F32)], axis=0
    )
    vec0 = vec_in[...] + late
    lane = lax.broadcasted_iota(jnp.int32, (width, 128), 1)
    feature = lax.broadcasted_iota(jnp.int32, (width, 128), 0)
    groups = jnp.where((feature >= lane * size) & (feature < lane * size + size), 1.0, 0.0)
    sums = jnp.concatenate([pre_sum * root, post_sum, bias_sum, jnp.zeros((7, width), F32)], axis=0)
    small = lax.dot_general(
        sums, groups, (((1,), (0,)), ((), ())), preferred_element_type=F32, precision=lax.Precision.HIGHEST
    )
    tall = jnp.concatenate(
        [vec0[:, k * 128 : (k + 1) * 128] for k in range(3)]
        + [vec_in1[:, k * 128 : (k + 1) * 128] for k in range(3)]
        + [small, jnp.zeros((8, 128), F32)],
        axis=0,
    )
    tall_ref[...] = tall
    filler = jnp.zeros((12, 128), F32)
    for n in range(32):
        blocks[n, 144:160] = jnp.concatenate([tall_ref[n * 4 : n * 4 + 4], filler], axis=0).astype(BF16)
    block_copy(place, blocks, kept_ref, 0, 16)
    block_copy(place, blocks, send_ref, 16, 16)


def unpack(place, mine, other, block, start):
    source = mine if block < 16 else other
    at = block_position(place, block) & 15
    return [source[at, start + k * 48 : start + (k + 1) * 48].astype(F32) for k in range(3)]


def fc_outputs(place, mine, other, factors, f1, f2, vec, fc1_out, fc2_out):
    width = f1.shape[0]

    @pl.when(place[0] == 0)
    def _():
        for block in range(32):
            rb, cb = block // 4, block % 4
            for k, piece in enumerate(unpack(place, mine, other, block, 0)):
                fc1_out[rb * 48 : (rb + 1) * 48, cb * 384 + k * 128 : cb * 384 + (k + 1) * 128] = piece
            for k, piece in enumerate(unpack(place, mine, other, block, 144)):
                fc2_out[block * 48 : (block + 1) * 48, k * 128 : (k + 1) * 128] = piece

    @pl.when(place[0] != 0)
    def _():
        bias = jnp.concatenate([vec[8 + k : 9 + k].astype(F32) for k in range(4)], axis=1)
        group = min(32, factors.shape[0])
        for n in range(factors.shape[0] // group):
            vectors = factor_rows(factors, slice(n * group, (n + 1) * group), 32, group)
            inner1, og1 = picked(vectors, 3, group), picked(vectors, 4, group)
            active, slope = gelu_pair(mm(inner1, f1[...]) + bias)
            ig1 = (mm_nt(og1, f2[...]) * slope).astype(BF16)
            fc1_part = mm_tn(inner1, ig1)
            fc2_part = mm_tn(active.astype(BF16), og1)
            fc1_out[...] = fc1_part if n == 0 else fc1_out[...] + fc1_part
            fc2_out[...] = fc2_part if n == 0 else fc2_out[...] + fc2_part


def factor_rows(factors, part, start, group):
    pieces = [factors[part, k * 48 + start : k * 48 + start + 16].reshape(group * 16, 128) for k in range(3)]
    return jnp.concatenate(pieces, axis=1)


def picked(vectors, kind, group):
    rows, cols = group * IMGS, group * 16
    row = lax.broadcasted_iota(jnp.int32, (rows, cols), 0)
    col = lax.broadcasted_iota(jnp.int32, (rows, cols), 1)
    wanted = (row >> 1) * 16 + kind * IMGS + (row & 1)
    return mm(jnp.where(col == wanted, 1.0, 0.0).astype(BF16), vectors).astype(BF16)


def qkv_outputs(place, mine, other, factors, w, p, vec, qkv_out, proj_out, vec_out, mix_out, tall_ref):
    width = p.shape[0]
    first = place[0] == 0
    for block in range(32):
        at = block_position(place, block) & 15
        here, there = mine[at, 144:160].astype(F32), other[at, 144:160].astype(F32)
        low = chosen(first, here, there) if block < 16 else chosen(first, there, here)
        tall_ref[block * 4 : block * 4 + 4] = low[0:4]
    for k in range(3):
        vec_out[:, k * 128 : (k + 1) * 128] = chosen(
            first, tall_ref[k * 16 : (k + 1) * 16], tall_ref[48 + k * 16 : 48 + (k + 1) * 16]
        )
    mix_out[...] = tall_ref[96:120]

    @pl.when(first)
    def _():
        for block in range(32):
            rb, cb = block // 4, block % 4
            for k, piece in enumerate(unpack(place, mine, other, block, 0)):
                rows = slice(rb * 48, (rb + 1) * 48)
                if cb < 3:
                    qkv_out[rows, cb * 384 + k * 128 : cb * 384 + (k + 1) * 128] = piece
                else:
                    proj_out[rows, k * 128 : (k + 1) * 128] = piece

    @pl.when(jnp.logical_not(first))
    def _():
        group = min(32, factors.shape[0])
        rows = group * IMGS * HEADS
        mask = head_mask(rows, width)
        spread = (
            lax.broadcasted_iota(jnp.int32, (rows, group * IMGS), 0) >> 3
            == lax.broadcasted_iota(jnp.int32, (rows, group * IMGS), 1)
        )
        spread = jnp.where(spread, 1.0, 0.0).astype(BF16)

        def expanded(vectors):
            return jnp.where(mask, mm(spread, vectors), 0.0).astype(BF16)

        for n in range(factors.shape[0] // group):
            part = slice(n * group, (n + 1) * group)
            wh, g, vectors = (factor_rows(factors, part, start, group) for start in (0, 16, 32))
            hidden_c, att1, bg1 = (picked(vectors, kind, group) for kind in range(3))
            query = (mm(hidden_c, w[:, :width]) + vec[2:3].astype(F32)).astype(BF16)
            da1 = mm_nt(bg1, p[...]).astype(BF16)
            chosen_g = jnp.where(mask, mm(g, w[:, width : 2 * width]), 0.0).astype(BF16)
            dq1 = mm_tn(spread, chosen_g).astype(BF16)
            parts = (mm_tn(hidden_c, dq1), mm_tn(g, expanded(query)), mm_tn(wh, expanded(da1)))
            for k, piece in enumerate(parts):
                cut = slice(k * width, (k + 1) * width)
                qkv_out[:, cut] = piece if n == 0 else qkv_out[:, cut] + piece
            piece = mm_tn(att1, bg1)
            proj_out[...] = piece if n == 0 else proj_out[...] + piece


VM = pl.BlockSpec(memory_space=pltpu.VMEM)
SM = pl.BlockSpec(memory_space=pltpu.SMEM)


def call(body, ins, outs, scratch, name, flops=0):
    specs = [SM if small else VM for small, _ in ins]
    return pl.pallas_call(
        body,
        out_shape=[jax.ShapeDtypeStruct(shape, kind) for shape, kind in outs],
        in_specs=specs,
        out_specs=[VM] * len(outs),
        scratch_shapes=[pltpu.VMEM(shape, kind) for shape, kind in scratch],
        compiler_params=pltpu.CompilerParams(vmem_limit_bytes=VMEM_LIMIT),
        cost_estimate=pl.CostEstimate(flops=flops, bytes_accessed=4000000, transcendentals=0),
        name=name,
    )(*[value for _, value in ins])


def swapped(array):
    return lax.ppermute(array, "pipe", [(0, 1), (1, 0)])


def core_pairs(dp, bits):
    return [
        (core * dp + i, core * dp + (i ^ bit)) for core, bit in enumerate(bits) for i in range(dp)
    ]


STEPS = ((1, 2), (2, 1), (4, 4), (8, 8))


def exchanged(array, bits):
    dp = lax.axis_size("dp")
    return lax.ppermute(array, ("pipe", "dp"), core_pairs(dp, bits))


def added(left, right):
    return (left.astype(F32) + right.astype(F32)).astype(BF16)


def scattered(kept, got):
    if lax.axis_size("dp") != 16:
        return lax.psum(added(kept, got).astype(F32), "dp").astype(BF16)
    count = kept.shape[0]
    for bits in STEPS:
        half = count // 2
        leaving = added(kept[half:count], got[half:count])
        kept = added(kept[:half], got[:half])
        got = exchanged(leaving, bits)
        count = half
    return added(kept, got)


def collected(blocks):
    if lax.axis_size("dp") != 16:
        return blocks
    for bits in STEPS[::-1]:
        blocks = jnp.concatenate([blocks, exchanged(blocks, bits)], axis=0)
    return blocks


def local(
    patches, class_token, keep_mask, class_cotangent, norm1_gain, norm1_bias, qkv_weight, qv_bias,
    mix_pre, mix_post, post_bias, proj_weight, proj_bias, scale_attn, norm2_gain, norm2_bias,
    fc1_weight, fc1_bias, fc2_weight, fc2_bias, scale_mlp,
):
    core = lax.axis_index("pipe")
    chip = lax.axis_index("dp")
    dp = lax.axis_size("dp")
    images, count, width = patches.shape
    hidden_width = fc1_weight.shape[2]
    length, lanes = 208, 256
    size = width // HEADS
    me = core * 16 + (chip if dp == 16 else 0)
    place = jnp.stack([core, me]).astype(jnp.int32)

    w_own, p_own, f1_own, f2_own = qkv_weight[0], proj_weight[0], fc1_weight[0], fc2_weight[0]
    w_got = swapped(w_own)
    vec_own = jnp.concatenate(
        [
            norm1_gain, norm1_bias, qv_bias.reshape(2, width), proj_bias, scale_attn, norm2_gain, norm2_bias,
            fc1_bias.reshape(4, width), fc2_bias, scale_mlp, jnp.zeros((2, width), BF16),
        ],
        axis=0,
    )
    vec_got = swapped(vec_own)
    p_got, f1_got, f2_got = swapped(p_own), swapped(f1_own), swapped(f2_own)

    def own_images(array):
        return lax.dynamic_slice_in_dim(array, core * IMGS, IMGS, 0)

    rows = jnp.pad(own_images(patches), ((0, 0), (0, length - count), (0, 0)))
    keep = own_images(keep_mask).astype(F32)
    keep_col = jnp.pad(keep, ((0, 0), (0, length - count)))[:, :, None]
    keep_row = jnp.pad(
        jnp.concatenate([keep, jnp.ones((IMGS, 1), F32)], axis=1), ((0, 8 - IMGS), (0, length - count - 1))
    )
    class_rows = jnp.pad(own_images(class_token), ((0, 8 - IMGS), (0, 0)))
    cot_rows = jnp.pad(own_images(class_cotangent), ((0, 8 - IMGS), (0, 0)))
    pre_f, post_f = mix_pre.astype(F32), mix_post.astype(F32)
    bias_row = jnp.repeat(post_bias.astype(F32), size)[None]
    pre_rows = jnp.repeat(pre_f, size, axis=1)
    post_rows = jnp.repeat(post_f.T, size, axis=1)

    token_shape = (IMGS, length, width)
    wide_shape = (IMGS, lanes, width)
    att, hid, queries, keys, values, probs = call(
        attention_forward,
        [(1, place), (1, pre_f), (1, post_f), (0, rows), (0, keep_col), (0, vec_own), (0, vec_got), (0, w_own),
         (0, w_got), (0, bias_row)],
        [(token_shape, BF16), (token_shape, BF16), (wide_shape, BF16), (wide_shape, BF16), (wide_shape, BF16),
         ((IMGS, HEADS * lanes, lanes), BF16)],
        [((width, 3 * width), BF16), ((width, HEADS * lanes), BF16)],
        "attention_forward",
    )
    flat = IMGS * length
    vec_shape = (16, width)
    send1, kept1, mg, vec0, vec1, class_out, factors = call(
        middle_kernel,
        [(1, place), (0, att), (0, rows), (0, keep_row), (0, class_rows), (0, cot_rows), (0, vec_own), (0, vec_got),
         (0, p_own), (0, p_got), (0, f1_own), (0, f1_got), (0, f2_own), (0, f2_got), (0, w_own), (0, w_got)],
        [((16, 288, 128), BF16), ((16, 288, 128), BF16), (token_shape, F32), (vec_shape, F32), (vec_shape, F32),
         ((16, width), F32), ((144, 128), BF16)],
        [((width, width), BF16), ((width, hidden_width), BF16), ((hidden_width, width), BF16),
         ((width, width), BF16), ((width, hidden_width), BF16), ((hidden_width, width), BF16),
         ((width, 3 * width), BF16), ((flat, hidden_width), BF16), ((flat, hidden_width), BF16),
         ((32, 288, 128), BF16)],
        "middle_kernel",
    )
    half = width // 2
    send2, kept2, own_half, other_half = call(
        attention_backward,
        [(1, place), (1, pre_f), (1, post_f), (0, mg), (0, rows), (0, keep_col), (0, hid), (0, queries), (0, keys),
         (0, values), (0, probs), (0, att), (0, vec0), (0, vec1), (0, vec_own), (0, vec_got), (0, w_own), (0, w_got),
         (0, p_own), (0, p_got), (0, bias_row), (0, pre_rows), (0, post_rows)],
        [((16, 160, 128), BF16), ((16, 160, 128), BF16), ((IMGS, length, half), F32), ((IMGS, length, half), BF16)],
        [((width, 3 * width), BF16), ((width, width), BF16), ((HEADS * lanes, lanes), BF16),
         ((width, HEADS * lanes), BF16), ((lanes, width), BF16), ((flat, 3 * width), BF16), ((flat, width), BF16),
         ((32, 160, 128), BF16), ((128, 128), F32)],
        "attention_backward",
    )

    class_low = class_out.astype(BF16)
    class_got = swapped(class_low)

    def halves(array):
        return jnp.where(core == 0, array[..., :half], array[..., half:])

    own_class, got_class = halves(class_low), halves(class_got)

    def image_order(own, got):
        return jnp.where(core == 0, jnp.concatenate([own, got], axis=0), jnp.concatenate([got, own], axis=0))

    class_result = image_order(own_class[0:IMGS], got_class[0:IMGS])
    class_grad = image_order(own_class[8 : 8 + IMGS], got_class[8 : 8 + IMGS])
    patch_out = image_order(own_half[:, :count], swapped(other_half)[:, :count].astype(F32))

    blocks1 = scattered(kept1, swapped(send1))
    if dp == 16:
        both = jnp.concatenate([blocks1, factors[None]], axis=1)
        both = collected(both)
        mine1, gathered_factors = both[:, :288], both[:, 288:]
    else:
        mine1, gathered_factors = blocks1, lax.all_gather(factors, "dp")
    other1 = swapped(mine1)
    all_factors = jnp.concatenate([gathered_factors, swapped(gathered_factors)], axis=0)
    mine2 = collected(scattered(kept2, swapped(send2)))
    other2 = swapped(mine2)

    fc1_out, fc2_out = call(
        fc_outputs,
        [(1, place), (0, mine1), (0, other1), (0, all_factors), (0, f1_own), (0, f2_own), (0, vec_own)],
        [((width, hidden_width), F32), ((hidden_width, width), F32)],
        [],
        "fc_outputs",
    )
    qkv_out, proj_out, vec_out, mix_out = call(
        qkv_outputs,
        [(1, place), (0, mine2), (0, other2), (0, all_factors), (0, w_own), (0, p_own), (0, vec_own)],
        [((width, 3 * width), F32), ((width, width), F32), (vec_shape, F32), ((24, 128), F32)],
        [((128, 128), F32)],
        "qkv_outputs",
    )
    return (
        class_result,
        patch_out,
        class_grad,
        vec_out[0:1],
        vec_out[1:2],
        qkv_out[None],
        vec_out[2:4].reshape(1, 2 * width),
        proj_out[None],
        vec_out[4:5],
        vec_out[5:6],
        vec_out[6:7],
        vec_out[7:8],
        fc1_out[None],
        vec_out[8:12].reshape(1, hidden_width),
        fc2_out[None],
        vec_out[12:13],
        vec_out[13:14],
        mix_out[0:8, 0:8],
        mix_out[8:16, 0:8].T,
        mix_out[16, 0:8],
    )


def solution(mesh):
    stacked = (P("pipe", None), P("pipe", None), P("pipe", None, None))
    row, _, cube = stacked
    return jax.shard_map(
        local,
        mesh=mesh,
        in_specs=(
            P("dp", None, None), P("dp", None), P("dp", None), P("dp", None),
            row, row, cube, row, P(), P(), P(), cube, row, row, row, row, cube, row, cube, row, row,
        ),
        out_specs=(
            P("dp", "pipe"), P("dp", None, "pipe"), P("dp", "pipe"),
            row, row, cube, row, cube, row, row, row, row, cube, row, cube, row, row, P(), P(), P(),
        ),
        check_vma=False,
    )
```

time: 626 us -> 171 us (0.27)
  the two profiles are of different devices: /device:TPU:0 before, /device:TPU:9 now
where the time goes in v1:
time: 171 us; the launch traced here: 170 us
  Pallas kernels  43.2 us (25%)
  local copies, waits for them, and re-layouts  39.9 us (23%)
  waiting for transfers between devices  36.6 us (21%)
  starting transfers between devices  34.5 us (20%)
  other arithmetic  14.3 us (8%)
    pallas_call x5, Pallas kernels, call(): pl.pallas_call(body, out_shape=[jax.ShapeDtypeStruct(shape, kind) for sha...  43.2 us
    ppermute x16, waiting for transfers between devices, exchanged(): return lax.ppermute(array, ('pipe', 'dp'), core_pairs(dp, bits))  36.5 us
    unnamed x97, local copies, waits for them, and re-layouts  26.6 us
    ppermute x16, starting transfers between devices, exchanged(): return lax.ppermute(array, ('pipe', 'dp'), core_pairs(dp, bits))  19 us
    ppermute x12, starting transfers between devices, swapped(): return lax.ppermute(array, 'pipe', [(0, 1), (1, 0)])  15.5 us
    convert_element_type x9, other arithmetic, added(): return (left.astype(F32) + right.astype(F32)).astype(BF16)  5.32 us
  transfers between devices with their start and end apart: 28, of which 11 were waited for; matrix products, arithmetic and copies ran while one was open for 20% of the time, Pallas kernels for 13%

profile of v1, /device:TPU:9, one launch (start us, length us, event | category | flops | bytes accessed | tf_op | source)
XLA Modules:
  0.0 169.6 jit_solution(15019333775082367586)
XLA Ops:
  0.7 0.7 collective-permute-start.3
  2.2 0.7 reduce.1
  3.0 1.5 concatenate.60.vec_own.vec
  6.2 0.7 constant_dynamic-slice_fusion
  7.8 1.3 convert_bitcast_fusion
  9.9 0.7 broadcast_in_dim.32
  12.2 5.4 %attention_forward.1 = (bf16[2,208,384]{2,1,0:T(8,128)(2,1)S(1)}, bf16[2,208,384]{2,1,0:T(8,128)(2,1)S(1)}, bf16[2,256,384]{2,1,0:T(8,128)(2,1)S(1)}, bf16[2,256...) custom-call(s32[2]{0:T(128)S(1)} %pad_add_fusion.place, ...), custom_call_target="tpu_custom_call" | custom-call | bytes 4000000 | tf_op jit(solution)/shard_map/attention_forward/pallas_call | solution.py:569
  17.6 0.7 copy-done.16
  18.4 0.7 copy-done.18
  19.1 0.7 copy-done.20
  19.9 0.7 copy-done.22
  20.7 0.7 copy-done.25
  22.1 16.3 %middle_kernel.1 = (bf16[16,288,128]{2,1,0:T(8,128)(2,1)}, bf16[16,288,128]{2,1,0:T(8,128)(2,1)S(1)}, f32[2,208,384]{2,1,0:T(8,128)S(1)}, f32[16,384]{1,0:T(8,12...) custom-call(s32[2]{0:T(128)S(1)} %copy-done.37, ...), custom_call_target="tpu_custom_call" | custom-call | bytes 4000000 | tf_op jit(solution)/shard_map/middle_kernel/pallas_call | solution.py:569
  38.4 1.0 copy-done.9
  39.4 0.8 copy-done.12
  42.2 0.8 copy.47
  43.1 0.8 broadcast_in_dim.33
  43.9 1.0 copy-done.8
  44.9 1.1 copy-done.13
  46.0 1.0 copy-done.17
  47.0 1.0 copy-done.19
  48.0 1.0 copy-done.21
  49.0 1.0 copy-done.23
  50.7 0.7 copy-done.33
  51.4 0.7 copy-done.35
  52.8 11.0 %attention_backward.1 = (bf16[16,160,128]{2,1,0:T(8,128)(2,1)}, bf16[16,160,128]{2,1,0:T(8,128)(2,1)S(1)}, f32[2,208,192]{2,1,0:T(8,128)S(1)}, bf16[2,208,192]{2,1,0:T(8,128)(2,1)S(1)}) custom-call(s32[2]{0:T(128)S(1)} %copy-done.38, f32[8,8]{1,0:T(8,128)S(1)} %convert_element_type.189.mix_pre, f32[8,8]{1,0:T(8,128)S(1)} %get-tuple-element.137.mix_post, ...), custom_call_target="tpu_custom_call" | custom-call | bytes 4000000 | tf_op jit(solution)/shard_map/attention_backward/pallas_call | solution.py:569
  64.3 2.4 %add_convert_fusion.1 = (bf16[8,288,128]{2,1,0:T(8,128)(2,1)S(1)}, bf16[8,288,128]{2,1,0:T(8,128)(2,1)}) fusion(bf16[16,288,128]{2,1,0:T(8,128)(2,1)} %collective-permute-done.17, bf16[16,288,128]{2,1,0:T(8,128)(2,1)S(1)} %copy-done.10), kind=kLoop, calls=%fused_computation.2 | loop fusion | flops 2359296 | bytes 3538944 | tf_op jit(solution)/shard_map/convert_element_type | solution.py:600
  66.6 1.2 collective-permute-start.18
  68.5 1.4 add_convert_fusion.3
  69.9 1.3 collective-permute-start.8
  71.2 4.8 %collective-permute-done.18 = bf16[8,288,128]{2,1,0:T(8,128)(2,1)} collective-permute-done((bf16[8,288,128]{2,1,0:T(8,128)(2,1)}, bf16[8,288,128]{2,1,0:T(8,128)(2,1)}, u32[]{:S(2)}, u32[]{:S(2)}) %collective-permute-start.18) | collective-permute-done | bytes 589856 | tf_op jit(solution)/shard_map/ppermute | solution.py:596
  76.0 1.2 add_convert_fusion.5
  77.2 1.3 collective-permute-start.19
  78.6 0.8 collective-permute-done.8
  79.5 1.3 collective-permute-start.9
  80.8 2.6 %collective-permute-done.19 = bf16[4,288,128]{2,1,0:T(8,128)(2,1)S(1)} collective-permute-done((bf16[4,288,128]{2,1,0:T(8,128)(2,1)S(1)}, bf16[4,288,128]{2,1,0:T(8,128)(2,1)S(1)}, u32[]{:S(2)}, u32[]{:S(2)}) %collective-permute-start.19) | collective-permute-done | bytes 294944 | tf_op jit(solution)/shard_map/ppermute | solution.py:596
  83.5 1.6 collective-permute-done.9
  85.2 2.3 %collective-permute-done.20 = bf16[2,288,128]{2,1,0:T(8,128)(2,1)S(1)} collective-permute-done((bf16[2,288,128]{2,1,0:T(8,128)(2,1)S(1)}, bf16[2,288,128]{2,1,0:T(8,128)(2,1)S(1)}, u32[]{:S(2)}, u32[]{:S(2)}) %collective-permute-start.20) | collective-permute-done | bytes 147488 | tf_op jit(solution)/shard_map/ppermute | solution.py:596
  87.5 2.4 %collective-permute-start.21 = (bf16[1,288,128]{2,1,0:T(8,128)(2,1)S(1)}, bf16[1,288,128]{2,1,0:T(8,128)(2,1)S(1)}, u32[]{:S(2)}, u32[]{:S(2)}) collective-permute-start(bf16[1,288,128]{2,1,0:T(8,128)(2,1)S(1)} %add_convert_fusion.13), channel_id=1, source_target_pairs={{0,8},{1,9},{2,10},{3,11},{4,12},{5,13},{6,14},{7,15},{8,0},{9,1},... | collective-permute-start | bytes 221192 | tf_op jit(solution)/shard_map/ppermute | solution.py:596
  89.9 1.6 collective-permute-start.11
  91.5 1.0 collective-permute-done.21
  93.2 2.1 %collective-permute-start.22 = (bf16[1,432,128]{2,1,0:T(8,128)(2,1)S(1)}, bf16[1,432,128]{2,1,0:T(8,128)(2,1)S(1)}, u32[]{:S(2)}, u32[]{:S(2)}) collective-permute-start(bf16[1,432,128]{2,1,0:T(8,128)(2,1)S(1)} %get-tuple-element.120), channel_id=1, source_target_pairs={{0,8},{1,9},{2,10},{3,11},{4,12},{5,13},{6,14},{7,15},{8,0},{9,1},... | collective-permute-start | bytes 331784 | tf_op jit(solution)/shard_map/ppermute | solution.py:596
  96.2 3.2 %collective-permute-done.22 = bf16[1,432,128]{2,1,0:T(8,128)(2,1)S(1)} collective-permute-done((bf16[1,432,128]{2,1,0:T(8,128)(2,1)S(1)}, bf16[1,432,128]{2,1,0:T(8,128)(2,1)S(1)}, u32[]{:S(2)}, u32[]{:S(2)}) %collective-permute-start.22) | collective-permute-done | bytes 110624 | tf_op jit(solution)/shard_map/ppermute | solution.py:596
  100.0 7.0 %collective-permute-start.6 = (bf16[2,208,192]{2,1,0:T(8,128)(2,1)S(1)}, bf16[2,208,192]{2,1,0:T(8,128)(2,1)S(1)}, u32[]{:S(2)}, u32[]{:S(2)}) collective-permute-start(bf16[2,208,192]{2,1,0:T(8,128)(2,1)S(1)} %copy-done.41), channel_id=1, source_target_pairs={{0,16},{16,0},{1,17},{17,1},{2,18},{18,2},{3,19},{19,3},{4,20},{20... | collective-permute-start | bytes 479240 | tf_op jit(solution)/shard_map/ppermute | solution.py:582
  107.0 1.8 %collective-permute-start.13 = (bf16[2,160,128]{2,1,0:T(8,128)(2,1)S(1)}, bf16[2,160,128]{2,1,0:T(8,128)(2,1)S(1)}, u32[]{:S(2)}, u32[]{:S(2)}) collective-permute-start(bf16[2,160,128]{2,1,0:T(8,128)(2,1)S(1)} %pad_maximum_fusion.7), channel_id=1, source_target_pairs={{0,4},{1,5},{2,6},{3,7},{4,0},{5,1},{6,2},{7,3},{8,12},{9,13},{10,... | collective-permute-start | bytes 245768 | tf_op jit(solution)/shard_map/ppermute | solution.py:596
  108.8 1.3 collective-permute-start.24
  110.1 1.6 collective-permute-done.13
  111.8 1.3 collective-permute-start.14
  113.0 3.0 %collective-permute-done.24 = bf16[4,432,128]{2,1,0:T(8,128)(2,1)S(1)} collective-permute-done((bf16[4,432,128]{2,1,0:T(8,128)(2,1)S(1)}, bf16[4,432,128]{2,1,0:T(8,128)(2,1)S(1)}, u32[]{:S(2)}, u32[]{:S(2)}) %collective-permute-start.24) | collective-permute-done | bytes 442400 | tf_op jit(solution)/shard_map/ppermute | solution.py:596
  116.1 1.3 collective-permute-start.25
  118.1 1.3 collective-permute-start.15
  121.3 15.0 %collective-permute-done.15 = bf16[8,160,128]{2,1,0:T(8,128)(2,1)S(1)} collective-permute-done((bf16[8,160,128]{2,1,0:T(8,128)(2,1)S(1)}, bf16[8,160,128]{2,1,0:T(8,128)(2,1)S(1)}, u32[]{:S(2)}, u32[]{:S(2)}) %collective-permute-start.15) | collective-permute-done | bytes 327712 | tf_op jit(solution)/shard_map/ppermute | solution.py:596
  136.4 0.7 constant_dynamic-update-slice_fusion.mine
  137.1 5.0 %collective-permute-start.16 = (bf16[16,160,128]{2,1,0:T(8,128)(2,1)}, bf16[16,160,128]{2,1,0:T(8,128)(2,1)}, u32[]{:S(2)}, u32[]{:S(2)}) collective-permute-start(bf16[16,160,128]{2,1,0:T(8,128)(2,1)} %constant_dynamic-update-slice_fusion.mine), channel_id=1, source_target_pairs={{0,16},{16,0},{1,17},{17,1},{2,18},{18,2},{3,19},{19,3},{4,20},{20... | collective-permute-start | bytes 1966088 | tf_op jit(solution)/shard_map/ppermute | solution.py:582
  143.5 0.8 constant_dynamic-update-slice_fusion.6
  144.3 1.0 constant_dynamic-update-slice_fusion.5
  145.3 1.9 %slice.265 = bf16[16,144,128]{2,1,0:T(8,128)(2,1)} slice(bf16[16,432,128]{2,1,0:T(8,128)(2,1)} %constant_dynamic-update-slice_fusion.5), slice={[0:16], [288:432], [0:128]} | slice | bytes 1179648 | tf_op jit(solution)/shard_map/slice | solution.py:724
  148.5 1.2 copy.49
  149.7 1.3 slice.266.mine
  151.7 1.3 pad_maximum_fusion.factors
  153.0 5.3 %qkv_outputs.1 = (f32[384,1152]{1,0:T(8,128)}, f32[384,384]{1,0:T(8,128)}, f32[16,384]{1,0:T(8,128)S(1)}, f32[24,128]{1,0:T(8,128)S(1)}) custom-call(s32[2]{0:T(128)S(1)} %copy-done.39, bf16[16,160,128]{2,1,0:T(8,128)(2,1)} %constant_dynamic-update-slice_fusion.mine, bf16[16,160,128]{2,1,0:T(8,128)(2,1)} %collective-permute-done.16.other, ...), custom_call_target="tpu_custom_call" | custom-call | bytes 4000000 | tf_op jit(solution)/shard_map/qkv_outputs/pallas_call | solution.py:569
  161.9 1.3 copy-done.4
  163.2 1.3 copy-done.5
  164.5 5.1 %fc_outputs.1 = (f32[384,1536]{1,0:T(8,128)}, f32[1536,384]{1,0:T(8,128)}) custom-call(s32[2]{0:T(128)S(1)} %copy-done.39, bf16[16,288,128]{2,1,0:T(8,128)(2,1)S(1)} %slice.266.mine, bf16[16,288,128]{2,1,0:T(8,128)(2,1)} %collective-permute-done.27.other, bf16[32,144,128]{2,1,0:T(8,128)(2,1)S(1)} %pad_maximum_fusion.factors, bf16[384,1536]{1,0:T(8,128)(2,1)S(1)} %bitcast.34, ...), custom_call_target="tpu_custom_call" | custom-call | bytes 4000000 | tf_op jit(solution)/shard_map/fc_outputs/pallas_call | solution.py:569
  (154 shorter events, 23.2 us)
Async XLA Ops:
  0.7 6.9 %copy-start = (bf16[4,196,384]{2,0,1:T(4,128)(2,1)S(1)}, bf16[4,196,384]{2,0,1:T(4,128)(2,1)}, u32[]{:S(2)}) copy-start(bf16[4,196,384]{2,0,1:T(4,128)(2,1)} %param.21) | copy-start | bytes 1806340
  0.7 11.5 %copy-start.1 = (bf16[1,384,1152]{2,1,0:T(8,128)(2,1)S(1)}, bf16[1,384,1152]{2,1,0:T(8,128)(2,1)}, u32[]{:S(2)}) copy-start(bf16[1,384,1152]{2,1,0:T(8,128)(2,1)} %param.27) | copy-start | bytes 2654212
  0.7 19.9 %collective-permute-start.3 = (bf16[384,1536]{1,0:T(8,128)(2,1)}, bf16[384,1536]{1,0:T(8,128)(2,1)}, u32[]{:S(2)}, u32[]{:S(2)}) collective-permute-start(bf16[384,1536]{1,0:T(8,128)(2,1)} %bitcast.32), channel_id=1, source_target_pairs={{0,16},{16,0},{1,17},{17,1},{2,18},{18,2},{3,19},{19,3},{4,20},{20... | collective-permute-start | bytes 3538952 | tf_op jit(solution)/shard_map/ppermute | solution.py:582
  1.4 19.2 %collective-permute-start.4 = (bf16[1536,384]{1,0:T(8,128)(2,1)}, bf16[1536,384]{1,0:T(8,128)(2,1)}, u32[]{:S(2)}, u32[]{:S(2)}) collective-permute-start(bf16[1536,384]{1,0:T(8,128)(2,1)} %bitcast.35), channel_id=1, source_target_pairs={{0,16},{16,0},{1,17},{17,1},{2,18},{18,2},{3,19},{19,3},{4,20},{20... | collective-permute-start | bytes 3538952 | tf_op jit(solution)/shard_map/ppermute | solution.py:582
  4.5 39.4 %copy-start.14 = (bf16[16,384]{1,0:T(8,128)(2,1)}, bf16[16,384]{1,0:T(8,128)(2,1)S(1)}, u32[]{:S(2)}) copy-start(bf16[16,384]{1,0:T(8,128)(2,1)S(1)} %concatenate.60.vec_own.vec) | copy-start | bytes 36868
  4.5 7.7 %collective-permute-start = (bf16[16,384]{1,0:T(8,128)(2,1)S(1)}, bf16[16,384]{1,0:T(8,128)(2,1)S(1)}, u32[]{:S(2)}, u32[]{:S(2)}) collective-permute-start(bf16[16,384]{1,0:T(8,128)(2,1)S(1)} %concatenate.60.vec_own.vec), channel_id=1, source_target_pairs={{0,16},{16,0},{1,17},{17,1},{2,18},{18,2},{3,19},{19,3},{4,20},{20... | collective-permute-start | bytes 36872 | tf_op jit(solution)/shard_map/ppermute | solution.py:582
  5.0 15.6 %collective-permute-start.2 = (bf16[384,384]{1,0:T(8,128)(2,1)}, bf16[384,384]{1,0:T(8,128)(2,1)S(1)}, u32[]{:S(2)}, u32[]{:S(2)}) collective-permute-start(bf16[384,384]{1,0:T(8,128)(2,1)} %bitcast.38), channel_id=1, source_target_pairs={{0,16},{16,0},{1,17},{17,1},{2,18},{18,2},{3,19},{19,3},{4,20},{20... | collective-permute-start | bytes 884744 | tf_op jit(solution)/shard_map/ppermute | solution.py:582
  5.1 7.1 %collective-permute-start.1 = (bf16[384,1152]{1,0:T(8,128)(2,1)}, bf16[384,1152]{1,0:T(8,128)(2,1)S(1)}, u32[]{:S(2)}, u32[]{:S(2)}) collective-permute-start(bf16[384,1152]{1,0:T(8,128)(2,1)} %bitcast.27), channel_id=1, source_target_pairs={{0,16},{16,0},{1,17},{17,1},{2,18},{18,2},{3,19},{19,3},{4,20},{20... | collective-permute-start | bytes 2654216 | tf_op jit(solution)/shard_map/ppermute | solution.py:582
  9.2 8.4 %copy-start.36 = (s32[2]{0:T(128)}, s32[2]{0:T(128)S(1)}, u32[]{:S(2)}) copy-start(s32[2]{0:T(128)S(1)} %pad_add_fusion.place) | copy-start | bytes 28
  12.0 8.6 %copy-start.6 = (bf16[1,384,384]{2,1,0:T(8,128)(2,1)S(1)}, bf16[1,384,384]{2,1,0:T(8,128)(2,1)}, u32[]{:S(2)}) copy-start(bf16[1,384,384]{2,1,0:T(8,128)(2,1)} %param.32) | copy-start | bytes 884740
  12.0 8.6 %copy-start.27 = (f32[8,208]{1,0:T(8,128)S(1)}, f32[8,208]{1,0:T(8,128)}, u32[]{:S(2)}) copy-start(f32[8,208]{1,0:T(8,128)} %select_select_fusion.keep_rows) | copy-start | bytes 19972
  12.1 8.6 %copy-start.28 = (bf16[8,384]{1,0:T(8,128)(2,1)S(1)}, bf16[8,384]{1,0:T(8,128)(2,1)}, u32[]{:S(2)}) copy-start(bf16[8,384]{1,0:T(8,128)(2,1)} %pad.24.cot_ref) | copy-start | bytes 18436
  12.1 8.6 %copy-start.29 = (bf16[8,384]{1,0:T(8,128)(2,1)S(1)}, bf16[8,384]{1,0:T(8,128)(2,1)}, u32[]{:S(2)}) copy-start(bf16[8,384]{1,0:T(8,128)(2,1)} %pad.23.class_ref) | copy-start | bytes 18436
  12.2 8.5 %copy-start.24 = (bf16[16,384]{1,0:T(8,128)(2,1)}, bf16[16,384]{1,0:T(8,128)(2,1)S(1)}, u32[]{:S(2)}) copy-start(bf16[16,384]{1,0:T(8,128)(2,1)S(1)} %collective-permute-done.vec_got) | copy-start | bytes 36868
  12.2 26.2 %copy-start.3 = (bf16[384,1152]{1,0:T(8,128)(2,1)}, bf16[384,1152]{1,0:T(8,128)(2,1)S(1)}, u32[]{:S(2)}) copy-start(bf16[384,1152]{1,0:T(8,128)(2,1)S(1)} %collective-permute-done.1.w_got) | copy-start | bytes 2654212
  17.6 0.7 copy-start.16
  18.4 0.7 copy-start.18
  19.1 0.7 copy-start.20
  19.9 0.7 copy-start.22
  20.6 17.8 %copy-start.7 = (bf16[2,208,384]{2,1,0:T(8,128)(2,1)}, bf16[2,208,384]{2,1,0:T(8,128)(2,1)S(1)}, u32[]{:S(2)}) copy-start(bf16[2,208,384]{2,1,0:T(8,128)(2,1)S(1)} %get-tuple-element.43.att_ref) | copy-start | bytes 958468
  20.7 0.7 copy-start.25
  38.4 1.0 copy-start.9
  39.4 0.8 copy-start.12
  42.1 22.2 %collective-permute-start.17 = (bf16[16,288,128]{2,1,0:T(8,128)(2,1)}, bf16[16,288,128]{2,1,0:T(8,128)(2,1)}, u32[]{:S(2)}, u32[]{:S(2)}) collective-permute-start(bf16[16,288,128]{2,1,0:T(8,128)(2,1)} %get-tuple-element.58), channel_id=1, source_target_pairs={{0,16},{16,0},{1,17},{17,1},{2,18},{18,2},{3,19},{19,3},{4,20},{20... | collective-permute-start | bytes 3538952 | tf_op jit(solution)/shard_map/ppermute | solution.py:582
  43.9 1.0 copy-start.8
  44.9 1.1 copy-start.13
  46.0 1.0 copy-start.17
  47.0 1.0 copy-start.19
  48.0 1.0 copy-start.21
  49.0 1.0 copy-start.23
  50.6 0.7 copy-start.33
  51.4 0.7 copy-start.35
  52.8 11.5 %copy-start.10 = (bf16[16,288,128]{2,1,0:T(8,128)(2,1)S(1)}, bf16[16,288,128]{2,1,0:T(8,128)(2,1)}, u32[]{:S(2)}) copy-start(bf16[16,288,128]{2,1,0:T(8,128)(2,1)} %copy-done.9) | copy-start | bytes 3538948
  63.8 2.8 %copy-start.11 = (bf16[16,160,128]{2,1,0:T(8,128)(2,1)}, bf16[16,160,128]{2,1,0:T(8,128)(2,1)S(1)}, u32[]{:S(2)}) copy-start(bf16[16,160,128]{2,1,0:T(8,128)(2,1)S(1)} %get-tuple-element.55) | copy-start | bytes 1966084
  63.8 2.8 %copy-start.40 = (bf16[2,208,192]{2,1,0:T(8,128)(2,1)}, bf16[2,208,192]{2,1,0:T(8,128)(2,1)S(1)}, u32[]{:S(2)}) copy-start(bf16[2,208,192]{2,1,0:T(8,128)(2,1)S(1)} %get-tuple-element.54) | copy-start | bytes 479236
  63.8 4.6 %collective-permute-start.7 = (bf16[16,160,128]{2,1,0:T(8,128)(2,1)}, bf16[16,160,128]{2,1,0:T(8,128)(2,1)}, u32[]{:S(2)}, u32[]{:S(2)}) collective-permute-start(bf16[16,160,128]{2,1,0:T(8,128)(2,1)} %get-tuple-element.56), channel_id=1, source_target_pairs={{0,16},{16,0},{1,17},{17,1},{2,18},{18,2},{3,19},{19,3},{4,20},{20... | collective-permute-start | bytes 1966088 | tf_op jit(solution)/shard_map/ppermute | solution.py:582
  64.3 3.6 %copy-start.31 = (f32[16,384]{1,0:T(8,128)S(1)}, f32[16,384]{1,0:T(8,128)}, u32[]{:S(2)}) copy-start(f32[16,384]{1,0:T(8,128)} %copy-done.30) | copy-start | bytes 73732
  66.6 9.3 %collective-permute-start.18 = (bf16[8,288,128]{2,1,0:T(8,128)(2,1)}, bf16[8,288,128]{2,1,0:T(8,128)(2,1)}, u32[]{:S(2)}, u32[]{:S(2)}) collective-permute-start(bf16[8,288,128]{2,1,0:T(8,128)(2,1)} %get-tuple-element.109), channel_id=1, source_target_pairs={{0,1},{1,0},{2,3},{3,2},{4,5},{5,4},{6,7},{7,6},{8,9},{9,8},{10,11... | collective-permute-start | bytes 1769480 | tf_op jit(solution)/shard_map/ppermute | solution.py:596
  67.9 42.2 %collective-permute-start.5 = (bf16[16,384]{1,0:T(8,128)(2,1)S(1)}, bf16[16,384]{1,0:T(8,128)(2,1)S(1)}, u32[]{:S(2)}, u32[]{:S(2)}) collective-permute-start(bf16[16,384]{1,0:T(8,128)(2,1)S(1)} %convert_element_type.193), channel_id=1, source_target_pairs={{0,16},{16,0},{1,17},{17,1},{2,18},{18,2},{3,19},{19,3},{4,20},{20... | collective-permute-start | bytes 36872 | tf_op jit(solution)/shard_map/ppermute | solution.py:582
  69.9 9.5 %collective-permute-start.8 = (bf16[8,160,128]{2,1,0:T(8,128)(2,1)S(1)}, bf16[8,160,128]{2,1,0:T(8,128)(2,1)S(1)}, u32[]{:S(2)}, u32[]{:S(2)}) collective-permute-start(bf16[8,160,128]{2,1,0:T(8,128)(2,1)S(1)} %get-tuple-element.111), channel_id=1, source_target_pairs={{0,1},{1,0},{2,3},{3,2},{4,5},{5,4},{6,7},{7,6},{8,9},{9,8},{10,11... | collective-permute-start | bytes 983048 | tf_op jit(solution)/shard_map/ppermute | solution.py:596
  77.2 6.1 %collective-permute-start.19 = (bf16[4,288,128]{2,1,0:T(8,128)(2,1)S(1)}, bf16[4,288,128]{2,1,0:T(8,128)(2,1)S(1)}, u32[]{:S(2)}, u32[]{:S(2)}) collective-permute-start(bf16[4,288,128]{2,1,0:T(8,128)(2,1)S(1)} %get-tuple-element.113), channel_id=1, source_target_pairs={{0,2},{1,3},{2,0},{3,1},{4,6},{5,7},{6,4},{7,5},{8,10},{9,11},{10,... | collective-permute-start | bytes 884744 | tf_op jit(solution)/shard_map/ppermute | solution.py:596
  79.5 5.6 %collective-permute-start.9 = (bf16[4,160,128]{2,1,0:T(8,128)(2,1)S(1)}, bf16[4,160,128]{2,1,0:T(8,128)(2,1)S(1)}, u32[]{:S(2)}, u32[]{:S(2)}) collective-permute-start(bf16[4,160,128]{2,1,0:T(8,128)(2,1)S(1)} %get-tuple-element.115), channel_id=1, source_target_pairs={{0,2},{1,3},{2,0},{3,1},{4,6},{5,7},{6,4},{7,5},{8,10},{9,11},{10,... | collective-permute-start | bytes 491528 | tf_op jit(solution)/shard_map/ppermute | solution.py:596
  83.3 16.6 %copy-start.41 = (bf16[2,208,192]{2,1,0:T(8,128)(2,1)S(1)}, bf16[2,208,192]{2,1,0:T(8,128)(2,1)}, u32[]{:S(2)}) copy-start(bf16[2,208,192]{2,1,0:T(8,128)(2,1)} %copy-done.40) | copy-start | bytes 479236
  83.4 4.1 %collective-permute-start.20 = (bf16[2,288,128]{2,1,0:T(8,128)(2,1)S(1)}, bf16[2,288,128]{2,1,0:T(8,128)(2,1)S(1)}, u32[]{:S(2)}, u32[]{:S(2)}) collective-permute-start(bf16[2,288,128]{2,1,0:T(8,128)(2,1)S(1)} %get-tuple-element.117), channel_id=1, source_target_pairs={{0,4},{1,5},{2,6},{3,7},{4,0},{5,1},{6,2},{7,3},{8,12},{9,13},{10,... | collective-permute-start | bytes 442376 | tf_op jit(solution)/shard_map/ppermute | solution.py:596
  85.1 4.8 %collective-permute-start.10 = (bf16[2,160,128]{2,1,0:T(8,128)(2,1)S(1)}, bf16[2,160,128]{2,1,0:T(8,128)(2,1)S(1)}, u32[]{:S(2)}, u32[]{:S(2)}) collective-permute-start(bf16[2,160,128]{2,1,0:T(8,128)(2,1)S(1)} %get-tuple-element.119), channel_id=1, source_target_pairs={{0,4},{1,5},{2,6},{3,7},{4,0},{5,1},{6,2},{7,3},{8,12},{9,13},{10,... | collective-permute-start | bytes 245768 | tf_op jit(solution)/shard_map/ppermute | solution.py:596
  87.5 5.0 %collective-permute-start.21 = (bf16[1,288,128]{2,1,0:T(8,128)(2,1)S(1)}, bf16[1,288,128]{2,1,0:T(8,128)(2,1)S(1)}, u32[]{:S(2)}, u32[]{:S(2)}) collective-permute-start(bf16[1,288,128]{2,1,0:T(8,128)(2,1)S(1)} %add_convert_fusion.13), channel_id=1, source_target_pairs={{0,8},{1,9},{2,10},{3,11},{4,12},{5,13},{6,14},{7,15},{8,0},{9,1},... | collective-permute-start | bytes 221192 | tf_op jit(solution)/shard_map/ppermute | solution.py:596
  89.9 5.5 %collective-permute-start.11 = (bf16[1,160,128]{2,1,0:T(8,128)(2,1)S(1)}, bf16[1,160,128]{2,1,0:T(8,128)(2,1)S(1)}, u32[]{:S(2)}, u32[]{:S(2)}) collective-permute-start(bf16[1,160,128]{2,1,0:T(8,128)(2,1)S(1)} %add_convert_fusion.16), channel_id=1, source_target_pairs={{0,8},{1,9},{2,10},{3,11},{4,12},{5,13},{6,14},{7,15},{8,0},{9,1},... | collective-permute-start | bytes 122888 | tf_op jit(solution)/shard_map/ppermute | solution.py:596
  93.2 6.2 %collective-permute-start.22 = (bf16[1,432,128]{2,1,0:T(8,128)(2,1)S(1)}, bf16[1,432,128]{2,1,0:T(8,128)(2,1)S(1)}, u32[]{:S(2)}, u32[]{:S(2)}) collective-permute-start(bf16[1,432,128]{2,1,0:T(8,128)(2,1)S(1)} %get-tuple-element.120), channel_id=1, source_target_pairs={{0,8},{1,9},{2,10},{3,11},{4,12},{5,13},{6,14},{7,15},{8,0},{9,1},... | collective-permute-start | bytes 331784 | tf_op jit(solution)/shard_map/ppermute | solution.py:596
  96.0 10.9 %collective-permute-start.12 = (bf16[1,160,128]{2,1,0:T(8,128)(2,1)S(1)}, bf16[1,160,128]{2,1,0:T(8,128)(2,1)S(1)}, u32[]{:S(2)}, u32[]{:S(2)}) collective-permute-start(bf16[1,160,128]{2,1,0:T(8,128)(2,1)S(1)} %get-tuple-element.107), channel_id=1, source_target_pairs={{0,8},{1,9},{2,10},{3,11},{4,12},{5,13},{6,14},{7,15},{8,0},{9,1},... | collective-permute-start | bytes 122888 | tf_op jit(solution)/shard_map/ppermute | solution.py:596
  99.4 9.3 %collective-permute-start.23 = (bf16[2,432,128]{2,1,0:T(8,128)(2,1)S(1)}, bf16[2,432,128]{2,1,0:T(8,128)(2,1)S(1)}, u32[]{:S(2)}, u32[]{:S(2)}) collective-permute-start(bf16[2,432,128]{2,1,0:T(8,128)(2,1)S(1)} %pad_maximum_fusion.4), channel_id=1, source_target_pairs={{0,4},{1,5},{2,6},{3,7},{4,0},{5,1},{6,2},{7,3},{8,12},{9,13},{10,... | collective-permute-start | bytes 663560 | tf_op jit(solution)/shard_map/ppermute | solution.py:596
  100.0 48.4 %collective-permute-start.6 = (bf16[2,208,192]{2,1,0:T(8,128)(2,1)S(1)}, bf16[2,208,192]{2,1,0:T(8,128)(2,1)S(1)}, u32[]{:S(2)}, u32[]{:S(2)}) collective-permute-start(bf16[2,208,192]{2,1,0:T(8,128)(2,1)S(1)} %copy-done.41), channel_id=1, source_target_pairs={{0,16},{16,0},{1,17},{17,1},{2,18},{18,2},{3,19},{19,3},{4,20},{20... | collective-permute-start | bytes 479240 | tf_op jit(solution)/shard_map/ppermute | solution.py:582
  107.0 4.8 %collective-permute-start.13 = (bf16[2,160,128]{2,1,0:T(8,128)(2,1)S(1)}, bf16[2,160,128]{2,1,0:T(8,128)(2,1)S(1)}, u32[]{:S(2)}, u32[]{:S(2)}) collective-permute-start(bf16[2,160,128]{2,1,0:T(8,128)(2,1)S(1)} %pad_maximum_fusion.7), channel_id=1, source_target_pairs={{0,4},{1,5},{2,6},{3,7},{4,0},{5,1},{6,2},{7,3},{8,12},{9,13},{10,... | collective-permute-start | bytes 245768 | tf_op jit(solution)/shard_map/ppermute | solution.py:596
  108.8 7.2 %collective-permute-start.24 = (bf16[4,432,128]{2,1,0:T(8,128)(2,1)S(1)}, bf16[4,432,128]{2,1,0:T(8,128)(2,1)S(1)}, u32[]{:S(2)}, u32[]{:S(2)}) collective-permute-start(bf16[4,432,128]{2,1,0:T(8,128)(2,1)S(1)} %pad_maximum_fusion.2), channel_id=1, source_target_pairs={{0,2},{1,3},{2,0},{3,1},{4,6},{5,7},{6,4},{7,5},{8,10},{9,11},{10,... | collective-permute-start | bytes 1327112 | tf_op jit(solution)/shard_map/ppermute | solution.py:596
  111.8 6.3 %collective-permute-start.14 = (bf16[4,160,128]{2,1,0:T(8,128)(2,1)S(1)}, bf16[4,160,128]{2,1,0:T(8,128)(2,1)S(1)}, u32[]{:S(2)}, u32[]{:S(2)}) collective-permute-start(bf16[4,160,128]{2,1,0:T(8,128)(2,1)S(1)} %pad_maximum_fusion.5), channel_id=1, source_target_pairs={{0,2},{1,3},{2,0},{3,1},{4,6},{5,7},{6,4},{7,5},{8,10},{9,11},{10,... | collective-permute-start | bytes 491528 | tf_op jit(solution)/shard_map/ppermute | solution.py:596
  116.1 28.2 %collective-permute-start.25 = (bf16[8,432,128]{2,1,0:T(8,128)(2,1)S(1)}, bf16[8,432,128]{2,1,0:T(8,128)(2,1)S(1)}, u32[]{:S(2)}, u32[]{:S(2)}) collective-permute-start(bf16[8,432,128]{2,1,0:T(8,128)(2,1)S(1)} %pad_maximum_fusion.1), channel_id=1, source_target_pairs={{0,1},{1,0},{2,3},{3,2},{4,5},{5,4},{6,7},{7,6},{8,9},{9,8},{10,11... | collective-permute-start | bytes 2654216 | tf_op jit(solution)/shard_map/ppermute | solution.py:596
  118.1 18.3 %collective-permute-start.15 = (bf16[8,160,128]{2,1,0:T(8,128)(2,1)S(1)}, bf16[8,160,128]{2,1,0:T(8,128)(2,1)S(1)}, u32[]{:S(2)}, u32[]{:S(2)}) collective-permute-start(bf16[8,160,128]{2,1,0:T(8,128)(2,1)S(1)} %pad_maximum_fusion.3), channel_id=1, source_target_pairs={{0,1},{1,0},{2,3},{3,2},{4,5},{5,4},{6,7},{7,6},{8,9},{9,8},{10,11... | collective-permute-start | bytes 983048 | tf_op jit(solution)/shard_map/ppermute | solution.py:596
  137.1 15.9 %collective-permute-start.16 = (bf16[16,160,128]{2,1,0:T(8,128)(2,1)}, bf16[16,160,128]{2,1,0:T(8,128)(2,1)}, u32[]{:S(2)}, u32[]{:S(2)}) collective-permute-start(bf16[16,160,128]{2,1,0:T(8,128)(2,1)} %constant_dynamic-update-slice_fusion.mine), channel_id=1, source_target_pairs={{0,16},{16,0},{1,17},{17,1},{2,18},{18,2},{3,19},{19,3},{4,20},{20... | collective-permute-start | bytes 1966088 | tf_op jit(solution)/shard_map/ppermute | solution.py:582
  147.2 4.5 %collective-permute-start.26 = (bf16[16,144,128]{2,1,0:T(8,128)(2,1)}, bf16[16,144,128]{2,1,0:T(8,128)(2,1)}, u32[]{:S(2)}, u32[]{:S(2)}) collective-permute-start(bf16[16,144,128]{2,1,0:T(8,128)(2,1)} %slice.265), channel_id=1, source_target_pairs={{0,16},{16,0},{1,17},{17,1},{2,18},{18,2},{3,19},{19,3},{4,20},{20... | collective-permute-start | bytes 1769480 | tf_op jit(solution)/shard_map/ppermute | solution.py:582
  151.0 2.0 %copy-start.2 = (bf16[1,384,1152]{2,1,0:T(8,128)(2,1)S(1)}, bf16[1,384,1152]{2,1,0:T(8,128)(2,1)}, u32[]{:S(2)}) copy-start(bf16[1,384,1152]{2,1,0:T(8,128)(2,1)} %param.27) | copy-start | bytes 2654212
  151.1 2.0 %copy-start.15 = (bf16[16,384]{1,0:T(8,128)(2,1)S(1)}, bf16[16,384]{1,0:T(8,128)(2,1)}, u32[]{:S(2)}) copy-start(bf16[16,384]{1,0:T(8,128)(2,1)} %copy-done.14) | copy-start | bytes 36868
  151.1 2.0 %copy-start.39 = (s32[2]{0:T(128)S(1)}, s32[2]{0:T(128)}, u32[]{:S(2)}) copy-start(s32[2]{0:T(128)} %copy-done.36) | copy-start | bytes 28
  151.1 10.8 %collective-permute-start.27 = (bf16[16,288,128]{2,1,0:T(8,128)(2,1)S(1)}, bf16[16,288,128]{2,1,0:T(8,128)(2,1)}, u32[]{:S(2)}, u32[]{:S(2)}) collective-permute-start(bf16[16,288,128]{2,1,0:T(8,128)(2,1)S(1)} %slice.266.mine), channel_id=1, source_target_pairs={{0,16},{16,0},{1,17},{17,1},{2,18},{18,2},{3,19},{19,3},{4,20},{20... | collective-permute-start | bytes 3538952 | tf_op jit(solution)/shard_map/ppermute | solution.py:582
  161.9 1.3 copy-start.4
  163.2 1.3 copy-start.5
  (6 other events, 3.8 us)

commit v2 on v1

v2 whole, which is shorter than its diff:
```python
import jax
import jax.numpy as jnp
from jax import lax
from jax.experimental import pallas as pl
from jax.experimental.pallas import tpu as pltpu
from jax.sharding import PartitionSpec as P

HEADS = 8
IMGS = 2
LIMIT_P, LIMIT_A, LIMIT_B, LIMIT_C, LIMIT_D, LIMIT_E = 60, 24, 24, 24, 24, 24
LOG2E = 1.4426950408889634
F32 = jnp.float32
BF16 = jnp.bfloat16


def mm(left, right):
    return lax.dot_general(left, right, (((1,), (0,)), ((), ())), preferred_element_type=F32)


def mm_nt(left, right):
    return lax.dot_general(left, right, (((1,), (1,)), ((), ())), preferred_element_type=F32)


def mm_tn(left, right):
    return lax.dot_general(left, right, (((0,), (0,)), ((), ())), preferred_element_type=F32)


def normed(rows):
    centred = rows - jnp.mean(rows, -1, keepdims=True)
    scale = lax.rsqrt(jnp.mean(centred * centred, -1, keepdims=True) + 1e-06)
    return centred * scale, scale


def norm_back(normal, scale, grad):
    inner = jnp.mean(grad * normal, -1, keepdims=True)
    return (grad - jnp.mean(grad, -1, keepdims=True) - normal * inner) * scale


def col_sum(rows):
    return jnp.sum(rows, axis=0, keepdims=True)


def gelu_pair(rows):
    phi = 0.5 + 0.5 * lax.erf(rows * 0.7071067811865476)
    return rows * phi, phi + rows * (jnp.exp2(rows * rows * (-0.5 * LOG2E)) * 0.3989422804014327)


def head_mask(rows, width):
    lane = lax.broadcasted_iota(jnp.int32, (rows, width), 1)
    head = lax.rem(lax.broadcasted_iota(jnp.int32, (rows, width), 0), HEADS)
    size = width // HEADS
    return (lane >= head * size) & (lane < head * size + size)


def chosen(is_first, first, other):
    return jnp.where(is_first, first, other)


def transposed(rows):
    return rows.T


def own_place():
    core = lax.axis_index("pipe")
    return core, core * 16 + (lax.axis_index("dp") if lax.axis_size("dp") == 16 else 0)


def fetch(first, own, got, target, sem):
    @pl.when(first)
    def _():
        pltpu.make_async_copy(own, target, sem).start()

    @pl.when(jnp.logical_not(first))
    def _():
        pltpu.make_async_copy(got, target, sem).start()

    return pltpu.make_async_copy(own, target, sem)


def own_images(first, rows):
    return chosen(first, rows[0:IMGS], rows[IMGS : 2 * IMGS])


def token_rows(rows_ref):
    rows = rows_ref[pl.ds(lax.axis_index("pipe") * IMGS, IMGS)]
    return rows.reshape(-1, rows.shape[2])


def keep_columns(first, mask_ref, scratch):
    scratch[...] = jnp.zeros_like(scratch)
    scratch[0:IMGS, 0 : mask_ref.shape[1]] = own_images(first, mask_ref[...].astype(F32))
    return scratch[...].T


def prepare(*refs):
    sources, (vec_ref, pre_ref, post_ref, bias_ref), held, sems = refs[:13], refs[13:17], refs[17:30], refs[30]
    copies = [pltpu.make_async_copy(*pair, sems.at[n]) for n, pair in enumerate(zip(sources, held))]
    for copy in copies:
        copy.start()
    for copy in copies:
        copy.wait()
    n1g, n1b, qvb, pb, sa, n2g, n2b, f1b, f2b, sm, pre, post, post_bias = held
    width = n1g.shape[1]
    rows = [n1g[...], n1b[...], qvb[:, :width], qvb[:, width:], pb[...], sa[...], n2g[...], n2b[...]]
    rows += [f1b[:, k * width : (k + 1) * width] for k in range(4)] + [f2b[...], sm[...]]
    rows = [row.astype(F32) for row in rows] + [jnp.zeros((2, width), F32)]
    vec_ref[...] = jnp.concatenate(rows, axis=0).astype(BF16)
    spread = jnp.where(head_mask(HEADS, width), 1.0, 0.0).astype(BF16)
    pre_ref[...] = mm(pre[...], spread)
    post_ref[...] = mm_tn(post[...], spread)
    bias_ref[...] = mm(post_bias[...], spread)


def attention_forward(
    mixing, rows_ref, mask_ref, vec_own, vec_got, w_own, w_got, bias_ref,
    att_ref, hid_ref, q_ref, k_ref, v_ref, pt_ref, w_ref, vs_ref, keep_ref, sems,
):
    first = lax.axis_index("pipe") == 0
    weights_copy = fetch(first, w_own, w_got, w_ref, sems.at[0])
    width = rows_ref.shape[2]
    length = rows_ref.shape[1]
    lanes = q_ref.shape[1]
    size = width // HEADS
    keeps = keep_columns(first, mask_ref, keep_ref)

    vec = chosen(first, vec_own[...].astype(F32), vec_got[...].astype(F32))
    scale = size ** (-0.5) * LOG2E
    pad_rows = jnp.zeros((lanes - length, width), BF16)
    same = lax.broadcasted_iota(jnp.int32, (length, lanes), 0) == lax.broadcasted_iota(jnp.int32, (length, lanes), 1)

    for b in range(IMGS):
        normal, _ = normed(rows_ref[lax.axis_index("pipe") * IMGS + b].astype(F32))
        hidden = (normal * vec[0:1] + vec[1:2]).astype(BF16)
        hid_ref[b] = hidden
        if b == 0:
            weights_copy.wait()
        joined = mm(hidden, w_ref[...])
        queries = joined[:, :width] + vec[2:3]
        keys = joined[:, width : 2 * width]
        values = joined[:, 2 * width :] + vec[3:4]
        low_k = keys.astype(BF16)
        low_v = values.astype(BF16)
        q_ref[b, :length] = queries.astype(BF16)
        k_ref[b, :length] = low_k
        v_ref[b, :length] = low_v
        q_ref[b, length:] = pad_rows
        k_ref[b, length:] = pad_rows
        v_ref[b, length:] = pad_rows
        q_t = transposed(q_ref[b].astype(F32))
        v_t = transposed(v_ref[b].astype(F32))
        keep = keeps[:length, b : b + 1]
        allowed = (keep > 0.0) | same
        for h in range(HEADS):
            scaled_q = jnp.concatenate(
                [q_t[c * size : (c + 1) * size] * mixing[0, h, c] for c in range(HEADS)], axis=0
            ).astype(BF16)
            scores = jnp.where(allowed, mm(low_k, scaled_q) * scale, -1e30)
            top = jnp.max(scores, axis=0, keepdims=True)
            weights = jnp.exp2(scores - top)
            weights = weights * (1.0 / jnp.sum(weights, axis=0, keepdims=True))
            pt_ref[b, h * lanes : h * lanes + length] = weights.astype(BF16)
            pt_ref[b, h * lanes + length : (h + 1) * lanes] = jnp.zeros((lanes - length, lanes), BF16)
            vs_ref[:, h * lanes : (h + 1) * lanes] = jnp.concatenate(
                [v_t[c * size : (c + 1) * size] * mixing[1, c, h] for c in range(HEADS)], axis=0
            ).astype(BF16)
        mixed = transposed(mm(vs_ref[...], pt_ref[b]))[:length]
        low_f = low_v.astype(F32)
        extra = bias_ref[...] * (col_sum(low_f * keep) + (1.0 - keep) * low_f)
        att_ref[b] = (mixed + extra).astype(BF16)


def block_copy(source, target, start, count):
    for n in range(count):
        target[n] = source[position_block(start + n)]


def position_block(at):
    core, me = own_place()
    first_bit, second_bit = (at >> 3) & 1, (at >> 2) & 1
    rest = ((at >> 4) << 4) | ((at & 1) << 3) | (((at >> 1) & 1) << 2)
    x_first = rest | first_bit | (second_bit << 1)
    y_first = rest | second_bit | (first_bit << 1)
    return jnp.where(core == (at >> 4), x_first, y_first) ^ me


def block_position(block):
    core, me = own_place()
    apart = block ^ me
    x_bit, y_bit = apart & 1, (apart >> 1) & 1
    half = apart >> 4
    top = jnp.where(core == half, (x_bit << 3) | (y_bit << 2), (y_bit << 3) | (x_bit << 2))
    return (half << 4) | top | (((apart >> 2) & 1) << 1) | ((apart >> 3) & 1)


def put_blocks(target, rows, start, wide):
    tall, across = 48, 384
    for rb in range(rows.shape[0] // tall):
        for cb in range(rows.shape[1] // across):
            block = rb * wide[0] + wide[1] + cb
            for k in range(3):
                piece = rows[rb * tall : (rb + 1) * tall, cb * across + k * 128 : cb * across + (k + 1) * 128]
                target[block, start + k * tall : start + (k + 1) * tall] = piece.astype(BF16)


def middle_kernel(
    att_ref, rows_ref, mask_ref, class_ref, cot_ref,
    vec_own, vec_got, p_own, p_got, f1_own, f1_got, f2_own, f2_got, w_own, w_got,
    send_ref, kept_ref, mg_ref, vec_out, vec_out1, class_own, class_other, factor_ref,
    p0_ref, f10, f20, p1_ref, f11, f21, w1_ref, act_ref, gp_ref, blocks, keep_ref, sems,
):
    first = lax.axis_index("pipe") == 0
    p0_copy = fetch(first, p_own, p_got, p0_ref, sems.at[0])
    f10_copy = fetch(first, f1_own, f1_got, f10, sems.at[1])
    f20_copy = fetch(first, f2_own, f2_got, f20, sems.at[2])
    w1_copy = fetch(first, w_got, w_own, w1_ref, sems.at[3])
    p1_copy = fetch(first, p_got, p_own, p1_ref, sems.at[4])
    f11_copy = fetch(first, f1_got, f1_own, f11, sems.at[5])
    f21_copy = fetch(first, f2_got, f2_own, f21, sems.at[6])
    length, width = rows_ref.shape[1], rows_ref.shape[2]
    flat = IMGS * length
    size = width // HEADS
    patches = mask_ref.shape[1]
    keep_ref[...] = jnp.zeros_like(keep_ref)
    keep_ref[0:IMGS, 0:patches] = own_images(first, mask_ref[...].astype(F32))
    keep_rows = keep_ref[0:IMGS, :length]
    keep_lane = lax.broadcasted_iota(jnp.int32, (IMGS, length), 1)
    keep_rows = jnp.where(keep_lane == patches, 1.0, keep_rows)

    own, got = vec_own[...].astype(F32), vec_got[...].astype(F32)
    vec, vec1 = chosen(first, own, got), chosen(first, got, own)

    def wide_bias(v):
        return jnp.concatenate([v[8 + k : 9 + k] for k in range(4)], axis=1)

    p0_copy.wait()
    branch = mm(att_ref[...].reshape(flat, width), p0_ref[...]) + vec[4:5]
    middle = token_rows(rows_ref).astype(F32) + vec[5:6] * branch
    normal, norm_scale = normed(middle)
    inner_low = (normal * vec[6:7] + vec[7:8]).astype(BF16)
    bias = wide_bias(vec)
    step = 384
    f10_copy.wait()
    for k in range(4):
        cut = slice(k * step, (k + 1) * step)
        inner = mm(inner_low, f10[:, cut]) + bias[:, cut]
        active, slope = gelu_pair(inner)
        act_ref[:, cut] = active.astype(BF16)
        gp_ref[:, cut] = slope.astype(BF16)
    f20_copy.wait()
    outer = mm(act_ref[...], f20[...]) + vec[12:13]
    sent = (middle + vec[13:14] * outer).astype(BF16).astype(F32)

    blank = jnp.zeros((8 - IMGS, width), F32)
    class_rows = jnp.concatenate([own_images(first, class_ref[...].astype(F32)), blank], axis=0)
    w1_copy.wait()
    normal_c, _ = normed(class_rows)
    hidden_c = (normal_c * vec1[0:1] + vec1[1:2]).astype(BF16)
    query = (mm(hidden_c, w1_ref[:, :width]) + vec1[2:3]).astype(BF16).astype(F32)
    mask = head_mask(IMGS * HEADS, width)

    def spread(rows):
        both = jnp.concatenate(
            [jnp.broadcast_to(rows[b : b + 1], (HEADS, width)) for b in range(IMGS)], axis=0
        )
        return jnp.where(mask, both, 0.0)

    def gathered(rows):
        kept = jnp.where(mask, rows, 0.0)
        parts = [col_sum(kept[b * HEADS : (b + 1) * HEADS]) for b in range(IMGS)]
        return jnp.concatenate(parts + [jnp.zeros((8 - IMGS, width), F32)], axis=0)

    query_rows = mm_nt(spread(query).astype(BF16), w1_ref[:, width : 2 * width]).astype(BF16)
    at_row = lax.broadcasted_iota(jnp.int32, (length, width), 0)
    hiddens, normals, scales, probs, low_probs, sums, whs = [], [], [], [], [], [], []
    for b in range(IMGS):
        tokens = jnp.where(at_row == patches, class_rows[b : b + 1], sent[b * length : (b + 1) * length])
        n1, s1 = normed(tokens)
        h1 = (n1 * vec1[0:1] + vec1[1:2]).astype(BF16)
        scores = mm_nt(query_rows[b * HEADS : (b + 1) * HEADS], h1) * (size ** (-0.5) * LOG2E)
        scores = jnp.where(keep_rows[b : b + 1] > 0.0, scores, -1e30)
        weights = jnp.exp2(scores - jnp.max(scores, axis=-1, keepdims=True))
        weights = weights / jnp.sum(weights, axis=-1, keepdims=True)
        low = weights.astype(BF16)
        hiddens.append(h1)
        normals.append(n1)
        scales.append(s1)
        probs.append(weights)
        low_probs.append(low)
        sums.append(jnp.sum(low.astype(F32), axis=-1, keepdims=True))
        whs.append(mm(low, h1))
    wh = jnp.concatenate(whs, axis=0).astype(BF16)
    prob_sum = gathered(jnp.broadcast_to(jnp.concatenate(sums, axis=0), (IMGS * HEADS, width)))
    att1 = (gathered(mm(wh, w1_ref[:, 2 * width :])) + vec1[3:4] * prob_sum).astype(BF16)
    p1_copy.wait()
    branch1 = mm(att1, p1_ref[...]) + vec1[4:5]
    middle1 = class_rows + vec1[5:6] * branch1
    normal2, scale2 = normed(middle1)
    inner1 = (normal2 * vec1[6:7] + vec1[7:8]).astype(BF16)
    f11_copy.wait()
    f21_copy.wait()
    active1, slope1 = gelu_pair(mm(inner1, f11[...]) + wide_bias(vec1))
    outer1 = mm(active1.astype(BF16), f21[...]) + vec1[12:13]
    class_result = middle1 + vec1[13:14] * outer1

    upper1 = jnp.concatenate([own_images(first, cot_ref[...].astype(F32)), blank], axis=0)
    og1 = (upper1 * vec1[13:14]).astype(BF16)
    ig1 = (mm_nt(og1, f21[...]) * slope1).astype(BF16)
    dh2 = mm_nt(ig1, f11[...])
    mg1 = upper1 + norm_back(normal2, scale2, dh2 * vec1[6:7])
    bg1 = (mg1 * vec1[5:6]).astype(BF16)
    da1 = mm_nt(bg1, p1_ref[...]).astype(BF16).astype(F32)
    value_rows = mm_nt(spread(da1).astype(BF16), w1_ref[:, 2 * width :]).astype(BF16)
    low_grads, gs = [], []
    for b in range(IMGS):
        part = slice(b * HEADS, (b + 1) * HEADS)
        dw = mm_nt(value_rows[part], hiddens[b])
        ds = probs[b] * (dw - jnp.sum(probs[b] * dw, axis=-1, keepdims=True))
        low = (ds * size ** (-0.5)).astype(BF16)
        low_grads.append(low)
        gs.append(mm(low, hiddens[b]))
    g_rows = jnp.concatenate(gs, axis=0).astype(BF16)
    dq1 = gathered(mm(g_rows, w1_ref[:, width : 2 * width])).astype(BF16)
    dclass = mm_nt(dq1, w1_ref[:, :width])
    uppers, class_grads = [], []
    n1g, n1b = jnp.zeros((1, width), F32), jnp.zeros((1, width), F32)
    for b in range(IMGS):
        part = slice(b * HEADS, (b + 1) * HEADS)
        left = jnp.concatenate([low_grads[b], low_probs[b]], axis=0)
        right = jnp.concatenate([query_rows[part], value_rows[part]], axis=0)
        dh1 = mm_tn(left, right)
        dh1 = jnp.where(at_row == patches, dh1 + dclass[b : b + 1], dh1)
        n1g = n1g + col_sum(dh1 * normals[b])
        n1b = n1b + col_sum(dh1)
        dtokens = norm_back(normals[b], scales[b], dh1 * vec1[0:1])
        class_grads.append(dtokens[patches : patches + 1] + mg1[b : b + 1])
        uppers.append(jnp.where(at_row < patches, dtokens, 0.0).astype(BF16).astype(F32))
    upper = jnp.concatenate(uppers, axis=0)
    class_rows = jnp.concatenate([class_result] + class_grads + [blank], axis=0)
    low_half, high_half = class_rows[:, : width // 2], class_rows[:, width // 2 :]
    class_own[...] = chosen(first, low_half, high_half).astype(BF16)
    class_other[...] = chosen(first, high_half, low_half).astype(BF16)
    ig1_sum = col_sum(ig1.astype(F32))
    vec_out1[...] = jnp.concatenate(
        [
            n1g,
            n1b,
            col_sum(dq1.astype(F32)),
            col_sum(da1 * prob_sum),
            col_sum(bg1.astype(F32)),
            col_sum(mg1 * branch1),
            col_sum(dh2 * normal2),
            col_sum(dh2),
        ]
        + [ig1_sum[:, k * width : (k + 1) * width] for k in range(4)]
        + [col_sum(og1.astype(F32)), col_sum(upper1 * outer1), jnp.zeros((2, width), F32)],
        axis=0,
    )
    pieces = [piece.astype(F32)[0:IMGS] for piece in (hidden_c, att1, bg1, inner1, og1)]
    vectors = jnp.concatenate(pieces + [jnp.zeros((16 - 5 * IMGS, width), F32)], axis=0).astype(BF16)
    for k in range(3):
        lanes = slice(k * 128, (k + 1) * 128)
        factor_ref[k * 48 : k * 48 + 16] = wh[:, lanes]
        factor_ref[k * 48 + 16 : k * 48 + 32] = g_rows[:, lanes]
        factor_ref[k * 48 + 32 : k * 48 + 48] = vectors[:, lanes]

    sm_grad = col_sum(upper * outer)
    og = (upper * vec[13:14]).astype(BF16)
    put_blocks(blocks, mm_tn(act_ref[...], og), 144, (1, 0))
    dh = jnp.zeros((flat, width), F32)
    fc1_sums = []
    for k in range(4):
        cut = slice(k * step, (k + 1) * step)
        ig = (mm_nt(og, f20[cut, :]) * gp_ref[:, cut].astype(F32)).astype(BF16)
        fc1_sums.append(col_sum(ig.astype(F32)))
        put_blocks(blocks, mm_tn(inner_low, ig), 0, (4, k))
        dh = dh + mm_nt(ig, f10[:, cut])
    mg = upper + norm_back(normal, norm_scale, dh * vec[6:7])
    mg_ref[...] = mg.reshape(IMGS, length, width)
    vec_out[...] = jnp.concatenate(
        [jnp.zeros((4, width), F32), jnp.zeros((1, width), F32), col_sum(mg * branch), col_sum(dh * normal), col_sum(dh)]
        + fc1_sums
        + [col_sum(og.astype(F32)), sm_grad, jnp.zeros((2, width), F32)],
        axis=0,
    )
    block_copy(blocks, kept_ref, 0, 16)
    block_copy(blocks, send_ref, 16, 16)


def attention_backward(
    b, mixing, mg_ref, mask_ref, q_ref, k_ref, v_ref, pt_ref, vec_own, vec_got, p_own, p_got, bias_ref,
    pre_rows, post_rows, join_ref, sum_ref, p_ref, dm_ref, ks_ref, da_ref, keep_ref, sems,
):
    first = lax.axis_index("pipe") == 0
    p_copy = fetch(first, p_own, p_got, p_ref, sems.at[0])
    length, width = mg_ref.shape[1], mg_ref.shape[2]
    lanes = q_ref.shape[1]
    size = width // HEADS
    root = size ** (-0.5)
    scale_row = chosen(first, vec_own[5:6].astype(F32), vec_got[5:6].astype(F32))
    bg = (mg_ref[b] * scale_row).astype(BF16)
    keep = keep_columns(first, mask_ref, keep_ref)[:length, b : b + 1]
    p_copy.wait()
    da = mm_nt(bg, p_ref[...]).astype(BF16)
    da_ref[:length] = da
    da_ref[length:] = jnp.zeros((lanes - length, width), BF16)
    da_t = transposed(da_ref[...].astype(F32))
    k_t = transposed(k_ref[b].astype(F32))
    low_v = v_ref[b, :length]
    val_f = low_v.astype(F32)
    key_f = k_ref[b, :length].astype(F32)
    da_f = da.astype(F32)
    biased = da_f * bias_ref[...]
    dv = keep * col_sum(biased) + (1.0 - keep) * biased
    bias_sum = col_sum(da_f * (col_sum(val_f * keep) + (1.0 - keep) * val_f))
    post_parts = []
    for c in range(HEADS):
        scaled = jnp.concatenate(
            [da_t[h * size : (h + 1) * size] * mixing[1, h, c] for h in range(HEADS)], axis=0
        ).astype(BF16)
        dp = mm(low_v, scaled)
        weights = pt_ref[b, c * lanes : c * lanes + length]
        w_f = weights.astype(F32)
        dm = w_f * (dp - col_sum(w_f * dp))
        dm_ref[c * lanes : c * lanes + length] = dm.astype(BF16)
        dm_ref[c * lanes + length : (c + 1) * lanes] = jnp.zeros((lanes - length, lanes), BF16)
        moved = mm(weights, da_ref[...])
        dv = dv + moved * post_rows[c : c + 1]
        post_parts.append(col_sum(moved * val_f))
        ks_ref[:, c * lanes : (c + 1) * lanes] = jnp.concatenate(
            [k_t[h * size : (h + 1) * size] * mixing[0, c, h] for h in range(HEADS)], axis=0
        ).astype(BF16)
    dk = jnp.zeros((length, width), F32)
    pre_parts = []
    for h in range(HEADS):
        moved = mm(dm_ref[h * lanes : h * lanes + length], q_ref[b])
        dk = dk + moved * pre_rows[h : h + 1]
        pre_parts.append(col_sum(moved * key_f))
    dq = transposed(mm(ks_ref[...], dm_ref[...]))[:length] * root
    join_ref[:, :width] = dq.astype(BF16)
    join_ref[:, width : 2 * width] = (dk * root).astype(BF16)
    join_ref[:, 2 * width :] = dv.astype(BF16)
    sum_ref[...] = jnp.concatenate(
        [part * root for part in pre_parts] + post_parts + [bias_sum, jnp.zeros((7, width), F32)], axis=0
    )


def input_gradients(
    mg_ref, rows_ref, hid_ref, att_ref, join0, join1, sum0, sum1, vec_in, vec_in1, vec_own, vec_got, w_own, w_got,
    class_other,
    send_ref, kept_ref, own_half, other_half, w_ref, join_ref, blocks, tall_ref, sems,
):
    first = lax.axis_index("pipe") == 0
    w_copy = fetch(first, w_own, w_got, w_ref, sems.at[0])
    length, width = rows_ref.shape[1], rows_ref.shape[2]
    size = width // HEADS
    flat = IMGS * length
    vec = chosen(first, vec_own[...].astype(F32), vec_got[...].astype(F32))
    mg = mg_ref[...].reshape(flat, width)
    bg = (mg * vec[5:6]).astype(BF16)
    pb_grad = col_sum(bg.astype(F32))
    put_blocks(blocks, mm_tn(att_ref[...].reshape(flat, width), bg), 0, (4, 3))
    join_ref[:length] = join0[...]
    join_ref[length:] = join1[...]
    hidden = hid_ref[...].reshape(flat, width)
    for k in range(3):
        put_blocks(blocks, mm_tn(hidden, join_ref[:, k * width : (k + 1) * width]), 0, (4, k))
    w_copy.wait()
    dh = mm_nt(join_ref[...], w_ref[...])
    normal, norm_scale = normed(token_rows(rows_ref).astype(F32))
    patch = mg + norm_back(normal, norm_scale, dh * vec[0:1])
    half = width // 2
    low_half, high_half = patch[:, :half], patch[:, half:]
    own_rows, other_rows = chosen(first, low_half, high_half), chosen(first, high_half, low_half)
    for b in range(IMGS):
        own_half[b] = transposed(own_rows[b * length : (b + 1) * length])
        other_half[b, :half] = transposed(other_rows[b * length : (b + 1) * length]).astype(BF16)
        other_half[b, half:] = jnp.zeros((16, length), BF16)
    other_half[0, half:, :half] = class_other[...]

    dq_sum = col_sum(join_ref[:, :width].astype(F32))
    dv_sum = col_sum(join_ref[:, 2 * width :].astype(F32))
    late = jnp.concatenate(
        [col_sum(dh * normal), col_sum(dh), dq_sum, dv_sum, pb_grad, jnp.zeros((11, width), F32)], axis=0
    )
    vec0 = vec_in[...] + late
    lane = lax.broadcasted_iota(jnp.int32, (width, 128), 1)
    feature = lax.broadcasted_iota(jnp.int32, (width, 128), 0)
    groups = jnp.where((feature >= lane * size) & (feature < lane * size + size), 1.0, 0.0)
    small = lax.dot_general(
        sum0[...] + sum1[...], groups, (((1,), (0,)), ((), ())),
        preferred_element_type=F32, precision=lax.Precision.HIGHEST,
    )
    tall_ref[...] = jnp.concatenate(
        [vec0[:, k * 128 : (k + 1) * 128] for k in range(3)]
        + [vec_in1[:, k * 128 : (k + 1) * 128] for k in range(3)]
        + [small, jnp.zeros((8, 128), F32)],
        axis=0,
    )
    filler = jnp.zeros((12, 128), F32)
    for n in range(32):
        blocks[n, 144:160] = jnp.concatenate([tall_ref[n * 4 : n * 4 + 4], filler], axis=0).astype(BF16)
    block_copy(blocks, kept_ref, 0, 16)
    block_copy(blocks, send_ref, 16, 16)


def assemble(own_half, half_got, class_own, patch_out, class_out, class_grad):
    first = lax.axis_index("pipe") == 0
    half, count = patch_out.shape[1:]
    for b in range(IMGS):
        mine, theirs = own_half[b, :, :count], half_got[b, :half, :count].astype(F32)
        patch_out[b] = chosen(first, mine, theirs)
        patch_out[IMGS + b] = chosen(first, theirs, mine)
    mine, theirs = class_own[...].astype(F32), half_got[0, half:, :half].astype(F32)
    for at, out in ((0, class_out), (8, class_grad)):
        pair = mine[at : at + IMGS], theirs[at : at + IMGS]
        rows = jnp.concatenate([chosen(first, *pair), chosen(first, *pair[::-1])], axis=0)
        out[...] = rows.astype(BF16)


def join_pieces(low, high, target):
    target[0:8] = low[:, : target.shape[1]]
    target[8:16] = high[:, : target.shape[1]]


def unpack(mine, other, block, start):
    source = mine if block < 16 else other
    at = block_position(block) & 15
    return [source[at, start + k * 48 : start + (k + 1) * 48].astype(F32) for k in range(3)]


def class_gradients(*refs):
    factor_refs = refs[:-19]
    w_in, p_in, f1_in, f2_in, vec, *outs = refs[-19:-10]
    w, p, f1, f2, factors, *held, sems = refs[-10:]
    width = p.shape[0]

    @pl.when(lax.axis_index("pipe") != 0)
    def _():
        copies = [
            pltpu.make_async_copy(source, target, sems.at[n])
            for n, (source, target) in enumerate(((f1_in, f1), (f2_in, f2), (w_in, w), (p_in, p)))
        ]
        for copy in copies:
            copy.start()
        join_factors(factor_refs, factors)
        group = min(32, factors.shape[0])
        rows = group * IMGS * HEADS
        mask = head_mask(rows, width)
        spread = (
            lax.broadcasted_iota(jnp.int32, (rows, group * IMGS), 0) >> 3
            == lax.broadcasted_iota(jnp.int32, (rows, group * IMGS), 1)
        )
        spread = jnp.where(spread, 1.0, 0.0).astype(BF16)
        bias = jnp.concatenate([vec[8 + k : 9 + k].astype(F32) for k in range(4)], axis=1)
        for copy in copies:
            copy.wait()

        def expanded(vectors):
            return jnp.where(mask, mm(spread, vectors), 0.0).astype(BF16)

        def put(n, at, target, cut, piece):
            target[:, cut] = piece if n == 0 else target[:, cut] + piece
            if n == factors.shape[0] // group - 1:
                done.append(pltpu.make_async_copy(target.at[:, cut], outs[at].at[:, cut], sems.at[4 + len(done)]))
                done[-1].start()

        done = []
        whole = slice(0, width)
        for n in range(factors.shape[0] // group):
            part = slice(n * group, (n + 1) * group)
            wh, g, vectors = (factor_rows(factors, part, start, group) for start in (0, 16, 32))
            hidden_c, att1, bg1, inner1, og1 = (picked(vectors, kind, group) for kind in range(5))
            active, slope = gelu_pair(mm(inner1, f1[...]) + bias)
            ig1 = (mm_nt(og1, f2[...]) * slope).astype(BF16)
            put(n, 3, held[3], whole, mm_tn(active.astype(BF16), og1))
            put(n, 2, held[2], slice(0, f1.shape[1]), mm_tn(inner1, ig1))
            query = (mm(hidden_c, w[:, :width]) + vec[2:3].astype(F32)).astype(BF16)
            da1 = mm_nt(bg1, p[...]).astype(BF16)
            chosen_g = jnp.where(mask, mm(g, w[:, width : 2 * width]), 0.0).astype(BF16)
            dq1 = mm_tn(spread, chosen_g).astype(BF16)
            put(n, 1, held[1], whole, mm_tn(att1, bg1))
            parts = (mm_tn(hidden_c, dq1), mm_tn(g, expanded(query)), mm_tn(wh, expanded(da1)))
            for k, piece in enumerate(parts):
                put(n, 0, held[0], slice(k * width, (k + 1) * width), piece)
        for copy in done:
            copy.wait()


def fc_outputs(mine_low, mine_high, other_low, other_high, fc1_in, fc2_in, fc1_out, fc2_out, mine, other, fc1, fc2, sems):
    del fc1_in, fc2_in

    @pl.when(lax.axis_index("pipe") == 0)
    def _():
        join_pieces(mine_low, mine_high, mine)
        join_pieces(other_low, other_high, other)
        copies = []
        for rb in range(8):
            for cb in range(4):
                block = rb * 4 + cb
                for k, piece in enumerate(unpack(mine, other, block, 0)):
                    fc1[rb * 48 : (rb + 1) * 48, cb * 384 + k * 128 : cb * 384 + (k + 1) * 128] = piece
                for k, piece in enumerate(unpack(mine, other, block, 144)):
                    fc2[block * 48 : (block + 1) * 48, k * 128 : (k + 1) * 128] = piece
            for n, (source, target, tall) in enumerate(((fc1, fc1_out, 48), (fc2, fc2_out, 192))):
                rows = pl.ds(rb * tall, tall)
                copies.append(pltpu.make_async_copy(source.at[rows], target.at[rows], sems.at[rb * 2 + n]))
                copies[-1].start()
        for copy in copies:
            copy.wait()


def join_factors(pieces, factors):
    at = 0
    for piece in pieces:
        count, start = piece.shape[0], piece.shape[1] - 144
        factors[at : at + count] = piece[:, start:]
        at += count


def factor_rows(factors, part, start, group):
    pieces = [factors[part, k * 48 + start : k * 48 + start + 16].reshape(group * 16, 128) for k in range(3)]
    return jnp.concatenate(pieces, axis=1)


def picked(vectors, kind, group):
    rows, cols = group * IMGS, group * 16
    row = lax.broadcasted_iota(jnp.int32, (rows, cols), 0)
    col = lax.broadcasted_iota(jnp.int32, (rows, cols), 1)
    wanted = (row >> 1) * 16 + kind * IMGS + (row & 1)
    return mm(jnp.where(col == wanted, 1.0, 0.0).astype(BF16), vectors).astype(BF16)


def qkv_outputs(mine_low, mine_high, other_low, other_high, qkv_in, proj_in, *refs):
    del qkv_in, proj_in
    qkv_out, proj_out = refs[:2]
    vec_outs, (pre_out, post_out, bias_out, mine, other, tall_ref, qkv, proj, sems) = refs[2:12], refs[12:]
    first = lax.axis_index("pipe") == 0
    width = proj_out.shape[0]
    join_pieces(mine_low, mine_high, mine)
    join_pieces(other_low, other_high, other)

    @pl.when(first)
    def _():
        for rb in range(8):
            rows = slice(rb * 48, (rb + 1) * 48)
            for cb in range(4):
                for k, piece in enumerate(unpack(mine, other, rb * 4 + cb, 0)):
                    if cb < 3:
                        qkv[rows, cb * 384 + k * 128 : cb * 384 + (k + 1) * 128] = piece
                    else:
                        proj[rows, k * 128 : (k + 1) * 128] = piece
            rows = pl.ds(rb * 48, 48)
            pltpu.make_async_copy(qkv.at[rows], qkv_out.at[rows], sems.at[rb]).start()
            pltpu.make_async_copy(proj.at[rows], proj_out.at[rows], sems.at[8 + rb]).start()

    for block in range(32):
        at = block_position(block) & 15
        here, there = mine[at, 144:160].astype(F32), other[at, 144:160].astype(F32)
        low = chosen(first, here, there) if block < 16 else chosen(first, there, here)
        tall_ref[block * 4 : block * 4 + 4] = low[0:4]
    rows = [
        chosen(first, tall_ref[k * 16 : (k + 1) * 16], tall_ref[48 + k * 16 : 48 + (k + 1) * 16]) for k in range(3)
    ]
    rows = jnp.concatenate(rows, axis=1)
    at = 0
    for out in vec_outs:
        for k in range(out.shape[1] // width):
            out[:, k * width : (k + 1) * width] = rows[at : at + 1]
            at += 1
    pre_out[...] = tall_ref[96:104, 0:HEADS]
    post_out[...] = tall_ref[104:112].T[0:HEADS]
    bias_out[...] = tall_ref[112:113, 0:HEADS]

    @pl.when(first)
    def _():
        for rb in range(8):
            rows = pl.ds(rb * 48, 48)
            pltpu.make_async_copy(qkv.at[rows], qkv_out.at[rows], sems.at[rb]).wait()
            pltpu.make_async_copy(proj.at[rows], proj_out.at[rows], sems.at[8 + rb]).wait()


VM = pl.BlockSpec(memory_space=pltpu.VMEM)
SM = pl.BlockSpec(memory_space=pltpu.SMEM)
HB = pl.BlockSpec(memory_space=pltpu.HBM)


def call(body, ins, outs, scratch, name, limit, sems=0, far=0, aliases=None):
    return pl.pallas_call(
        body,
        out_shape=[jax.ShapeDtypeStruct(shape, kind) for shape, kind in outs],
        in_specs=[spec for spec, _ in ins],
        out_specs=[HB] * far + [VM] * (len(outs) - far),
        scratch_shapes=[pltpu.VMEM(shape, kind) for shape, kind in scratch]
        + ([pltpu.SemaphoreType.DMA((sems,))] if sems else []),
        compiler_params=pltpu.CompilerParams(vmem_limit_bytes=limit * 1024 * 1024),
        cost_estimate=pl.CostEstimate(flops=0, bytes_accessed=1, transcendentals=0),
        input_output_aliases=aliases or {},
        name=name,
    )(*[value for _, value in ins])


def swapped(array):
    return lax.ppermute(array, "pipe", [(0, 1), (1, 0)])


def core_pairs(dp, bits):
    return [
        (core * dp + i, core * dp + (i ^ bit)) for core, bit in enumerate(bits) for i in range(dp)
    ]


def exchanged(array, bits):
    dp = lax.axis_size("dp")
    return lax.ppermute(array, ("pipe", "dp"), core_pairs(dp, bits))


def total(pieces, start, stop):
    parts = [piece[start:stop].astype(F32) for piece in pieces]
    return sum(parts[1:], parts[0]).astype(BF16)


def after(arrays, *others):
    return lax.optimization_barrier((arrays, others))[0]


NEAR, FAR = (4, 4), (8, 8)
LONG = (("halve", (1, 2)), ("halve", (2, 1)), ("halve", NEAR), ("swap", FAR), ("collect", NEAR), ("collect", (2, 1)), ("collect", (1, 2)))
SHORT = (("halve", (1, 2)), ("halve", (2, 1)), ("swap", NEAR), ("swap", FAR), ("collect", (2, 1)), ("collect", (1, 2)))
GATHER = (("collect", FAR), ("collect", NEAR), ("collect", (2, 1)), ("collect", (1, 2)))


class Stream:
    def __init__(self, pieces, steps):
        self.pieces, self.steps, self.at = list(pieces), steps, 0
        self.whole = lax.axis_size("dp") == 16
        self.leaving = self.pieces[0]

    def wait(self, *others):
        self.pieces = list(after(tuple(self.pieces), *others))

    def step(self):
        if not self.whole:
            return
        kind, bits = self.steps[self.at]
        self.at += 1
        count = min(piece.shape[0] for piece in self.pieces)
        if kind == "halve":
            self.leaving = total(self.pieces, count // 2, count)
            self.pieces = [piece[: count // 2] for piece in self.pieces] + [exchanged(self.leaving, bits)]
        elif kind == "swap":
            run = 1 if bits == FAR else 2
            starts = [at ^ run for at in range(0, count, run)]
            self.leaving = jnp.concatenate([total(self.pieces, at, at + run) for at in starts], axis=0)
            self.pieces = [total(self.pieces, 0, count), exchanged(self.leaving, bits)]
            if self.steps[self.at][0] == "collect":
                self.pieces = [total(self.pieces, 0, count)]
        else:
            self.leaving = jnp.concatenate(self.pieces, axis=0) if len(self.pieces) > 1 else self.pieces[0]
            self.pieces = [self.leaving, exchanged(self.leaving, bits)]

    def halves(self):
        if self.whole:
            return self.pieces
        whole = lax.psum(total(self.pieces, 0, 16).astype(F32), "dp").astype(BF16)
        return whole[:8], whole[8:]


def local(
    patches, class_token, keep_mask, class_cotangent, norm1_gain, norm1_bias, qkv_weight, qv_bias,
    mix_pre, mix_post, post_bias, proj_weight, proj_bias, scale_attn, norm2_gain, norm2_bias,
    fc1_weight, fc1_bias, fc2_weight, fc2_bias, scale_mlp,
):
    dp = lax.axis_size("dp")
    images, count, width = patches.shape
    hidden_width = fc1_weight.shape[2]
    length, lanes = 208, 256
    half = width // 2
    flat = IMGS * length

    w_own, p_own, f1_own, f2_own = qkv_weight[0], proj_weight[0], fc1_weight[0], fc2_weight[0]
    w_got = swapped(w_own)
    small = (
        norm1_gain, norm1_bias, qv_bias, proj_bias, scale_attn, norm2_gain, norm2_bias, fc1_bias, fc2_bias, scale_mlp,
        mix_pre, mix_post, post_bias[None],
    )
    vec_own, pre_rows, post_rows, bias_row = call(
        prepare,
        [(HB, array) for array in small],
        [((16, width), BF16), ((HEADS, width), F32), ((HEADS, width), F32), ((1, width), F32)],
        [(array.shape, BF16) for array in small],
        "prepare",
        LIMIT_P,
        sems=13,
    )
    vec_got = swapped(vec_own)
    p_late, f1_late, f2_late = after((p_own, f1_own, f2_own), w_got)
    p_got, f1_got, f2_got = swapped(p_late), swapped(f1_late), swapped(f2_late)
    mixing = jnp.stack([mix_pre, mix_post]).astype(F32)
    rows = jnp.pad(patches, ((0, 0), (0, length - count), (0, 0)))

    token_shape = (IMGS, length, width)
    wide_shape = (IMGS, lanes, width)
    keep_scratch = ((8, lanes), F32)
    att, hid, queries, keys, values, probs = call(
        attention_forward,
        [(SM, mixing), (VM, rows), (VM, keep_mask), (VM, vec_own), (VM, vec_got), (HB, w_own), (HB, w_got),
         (VM, bias_row)],
        [(token_shape, BF16), (token_shape, BF16), (wide_shape, BF16), (wide_shape, BF16), (wide_shape, BF16),
         ((IMGS, HEADS * lanes, lanes), BF16)],
        [((width, 3 * width), BF16), ((width, HEADS * lanes), BF16), keep_scratch],
        "attention_forward",
        LIMIT_A,
        sems=1,
    )
    vec_shape = (16, width)
    send1, kept1, mg, vec0, vec1, class_own, class_other, factors = call(
        middle_kernel,
        [(VM, att), (VM, rows), (VM, keep_mask), (VM, class_token), (VM, class_cotangent), (VM, vec_own),
         (VM, vec_got), (HB, p_own), (HB, p_got), (HB, f1_own), (HB, f1_got), (HB, f2_own), (HB, f2_got), (HB, w_own),
         (HB, w_got)],
        [((16, 288, 128), BF16), ((16, 288, 128), BF16), (token_shape, F32), (vec_shape, F32), (vec_shape, F32),
         ((16, half), BF16), ((16, half), BF16), ((144, 128), BF16)],
        [((width, width), BF16), ((width, hidden_width), BF16), ((hidden_width, width), BF16),
         ((width, width), BF16), ((width, hidden_width), BF16), ((hidden_width, width), BF16),
         ((width, 3 * width), BF16), ((flat, hidden_width), BF16), ((flat, hidden_width), BF16),
         ((32, 288, 128), BF16), keep_scratch],
        "middle_kernel",
        LIMIT_B,
        sems=7,
    )

    def image_backward(b, mg):
        return call(
            lambda *refs: attention_backward(b, *refs),
            [(SM, mixing), (VM, mg), (VM, keep_mask), (VM, queries), (VM, keys), (VM, values), (VM, probs),
             (VM, vec_own), (VM, vec_got), (HB, p_own), (HB, p_got), (VM, bias_row), (VM, pre_rows), (VM, post_rows)],
            [((length, 3 * width), BF16), ((24, width), F32)],
            [((width, width), BF16), ((HEADS * lanes, lanes), BF16), ((width, HEADS * lanes), BF16),
             ((lanes, width), BF16), keep_scratch],
            f"attention_backward_{b}",
            LIMIT_C,
            sems=1,
        )

    got1 = swapped(send1)
    stream1, shared = Stream((kept1, got1), LONG), Stream((factors[None],), GATHER)
    join0, sum0 = image_backward(0, mg)
    stream1.wait(join0)
    stream1.step()
    join1, sum1 = image_backward(1, after(mg, stream1.leaving))
    mg = after(mg, join1)
    send2, kept2, own_half, other_half = call(
        input_gradients,
        [(VM, mg), (VM, rows), (VM, hid), (VM, att), (VM, join0), (VM, join1), (VM, sum0), (VM, sum1), (VM, vec0),
         (VM, vec1), (VM, vec_own), (VM, vec_got), (HB, w_own), (HB, w_got), (VM, class_other)],
        [((16, 160, 128), BF16), ((16, 160, 128), BF16), ((IMGS, half, length), F32), ((IMGS, half + 16, length), BF16)],
        [((width, 3 * width), BF16), ((flat, 3 * width), BF16), ((32, 160, 128), BF16), ((128, 128), F32)],
        "input_gradients",
        LIMIT_C,
        sems=1,
    )
    got2, half_got = swapped(send2), swapped(other_half)
    patch_out, class_result, class_grad = call(
        assemble,
        [(VM, own_half), (VM, half_got), (VM, class_own)],
        [((2 * IMGS, half, count), F32), ((2 * IMGS, half), BF16), ((2 * IMGS, half), BF16)],
        [],
        "assemble",
        LIMIT_C,
    )

    def turn(*streams):
        for stream in streams:
            turn.last = stream.wait(*turn.last) or (stream.step(), stream.leaving)[1:]

    turn.last = (kept2,)
    stream2 = Stream((kept2, got2), SHORT)
    turn(stream1, stream2)
    stream1.wait(half_got)
    turn(stream1, stream2, shared, stream1, stream2, shared, stream1, stream2, shared, stream1, shared, stream2, stream1)
    stream2.wait(patch_out, class_result, class_grad)
    turn(stream2)
    if dp == 16:
        factor_parts = after(tuple(shared.pieces), stream2.leaving)
    else:
        factor_parts = (lax.all_gather(factors, "dp"),)
    factor_parts += tuple(swapped(part) for part in factor_parts)
    low1, high1 = stream1.halves()
    matrices = [((width, 3 * width), F32), ((width, width), F32), ((width, hidden_width), F32), ((hidden_width, width), F32)]
    qkv1, proj1, fc11, fc21 = call(
        class_gradients,
        [(VM, part) for part in factor_parts]
        + [(HB, w_own), (HB, p_own), (HB, f1_own), (HB, f2_own), (VM, vec_own)],
        matrices,
        [(shape, BF16) for shape, _ in matrices] + [((2 * dp, 144, 128), BF16)] + matrices,
        "class_gradients",
        LIMIT_E,
        sems=10,
        far=4,
    )
    low1_other, high1 = swapped(low1), after(high1, fc11)
    high1_other = swapped(high1)
    low2, high2 = stream2.halves()
    low2_other = swapped(low2)
    fc1_out, fc2_out = call(
        fc_outputs,
        [(VM, low1), (VM, high1), (VM, low1_other), (VM, high1_other), (HB, fc11), (HB, fc21)],
        matrices[2:],
        [((16, 288, 128), BF16), ((16, 288, 128), BF16)] + matrices[2:],
        "fc_outputs",
        LIMIT_D,
        sems=16,
        far=2,
        aliases={4: 0, 5: 1},
    )
    high2 = after(high2, fc1_out)
    high2_other = swapped(high2)
    qkv_out, proj_out, *small_outs = call(
        qkv_outputs,
        [(VM, low2), (VM, high2), (VM, low2_other), (VM, high2_other), (HB, qkv1), (HB, proj1)],
        matrices[:2]
        + [((1, size * width), F32) for size in (1, 1, 2, 1, 1, 1, 1, 4, 1, 1)]
        + [((HEADS, HEADS), F32), ((HEADS, HEADS), F32), ((1, HEADS), F32)],
        [((16, 160, 128), BF16), ((16, 160, 128), BF16), ((128, 128), F32)] + matrices[:2],
        "qkv_outputs",
        LIMIT_D,
        sems=16,
        far=2,
        aliases={4: 0, 5: 1},
    )
    n1g, n1b, qvb, pb, sa, n2g, n2b, f1b, f2b, sm, pre, post, bias = small_outs
    return (
        class_result, patch_out.transpose(0, 2, 1), class_grad, n1g, n1b, qkv_out[None], qvb, proj_out[None], pb, sa, n2g, n2b,
        fc1_out[None], f1b, fc2_out[None], f2b, sm, pre, post, bias[0],
    )


def solution(mesh):
    stacked = (P("pipe", None), P("pipe", None), P("pipe", None, None))
    row, _, cube = stacked
    return jax.shard_map(
        local,
        mesh=mesh,
        in_specs=(
            P("dp", None, None), P("dp", None), P("dp", None), P("dp", None),
            row, row, cube, row, P(), P(), P(), cube, row, row, row, row, cube, row, cube, row, row,
        ),
        out_specs=(
            P("dp", "pipe"), P("dp", None, "pipe"), P("dp", "pipe"),
            row, row, cube, row, cube, row, row, row, row, cube, row, cube, row, row, P(), P(), P(),
        ),
        check_vma=False,
    )
```

time: 171 us -> 107 us (0.63)
  the two profiles are of different devices: /device:TPU:9 before, /device:TPU:0 now
where the time goes in v2:
time: 107 us; the launch traced here: 106 us
  Pallas kernels  36.4 us (34%)
  starting transfers between devices  35.1 us (33%)
  waiting for transfers between devices  29.4 us (27%)
  other arithmetic  1.83 us (2%)
  local copies, waits for them, and re-layouts  1.82 us (2%)
  between operations  1.36 us (1%)
    pallas_call x10, Pallas kernels, call(): pl.pallas_call(body, out_shape=[jax.ShapeDtypeStruct(shape, kind) for sha...  36.4 us
    ppermute x17, starting transfers between devices, exchanged(): return lax.ppermute(array, ('pipe', 'dp'), core_pairs(dp, bits))  30.5 us
    ppermute x17, waiting for transfers between devices, exchanged(): return lax.ppermute(array, ('pipe', 'dp'), core_pairs(dp, bits))  23.8 us
    ppermute x14, waiting for transfers between devices, swapped(): return lax.ppermute(array, 'pipe', [(0, 1), (1, 0)])  5.66 us
    ppermute x14, starting transfers between devices, swapped(): return lax.ppermute(array, 'pipe', [(0, 1), (1, 0)])  4.56 us
  transfers between devices with their start and end apart: 31, of which 14 were waited for; matrix products, arithmetic and copies ran while one was open for 3% of the time, Pallas kernels for 20%

profile of v2, /device:TPU:0, one launch (start us, length us, event | category | flops | bytes accessed | tf_op | source)
XLA Modules:
  0.0 105.9 jit_solution(14558608580791661926)
XLA Ops:
  0.7 0.5 collective-permute-start.1
  1.2 2.3 %collective-permute-done.1.w_got = bf16[384,1152]{1,0:T(8,128)(2,1)S(1)} collective-permute-done((bf16[384,1152]{1,0:T(8,128)(2,1)}, bf16[384,1152]{1,0:T(8,128)(2,1)S(1)}, u32[]{:S(2)}, u32[]{:S(2)}) %collective-permute-start.1) | collective-permute-done | bytes 884768 | tf_op jit(solution)/shard_map/ppermute | solution.py:703
  3.4 0.4 collective-permute-start.3
  3.8 0.1 collective-permute-start.4
  4.0 0.4 collective-permute-start.2
  4.3 1.7 %prepare.1 = (bf16[16,384]{1,0:T(8,128)(2,1)}, f32[8,384]{1,0:T(8,128)}, f32[8,384]{1,0:T(8,128)}, f32[1,384]{1,0:T(1,128)}) custom-call(bf16[1,384]{1,0:T(2,128)(2,1)} %refs_0_.1, bf16[1,384]{1,0:T(2,128)(2,1)} %refs_1_.1, bf16[1,768]{1,0:T(2,128)(2,1)} %refs_2_.3, bf16[1,384]{1,0:T(2,128)(2,1)} %refs_3_.1, bf16[1,384]{1,0:T(2,128)(2,1)} %refs_4_.1, ...), custom_call_target="tpu_custom_call" | custom-call | bytes 1 | tf_op jit(solution)/shard_map/prepare/pallas_call | solution.py:688
  6.0 0.2 collective-permute-start
  6.2 0.7 maximum_convert_fusion.mixing.refs_0_
  7.0 1.2 %copy.45 = bf16[4,196,384]{2,1,0:T(8,128)(2,1)S(1)} copy(bf16[4,196,384]{2,0,1:T(4,128)(2,1)} %param.21) | data formatting | bytes 1204224 | tf_op args[0]
  8.3 0.3 collective-permute-done.vec_got.refs_8_
  8.7 4.6 %attention_forward.1 = (bf16[2,208,384]{2,1,0:T(8,128)(2,1)S(1)}, bf16[2,208,384]{2,1,0:T(8,128)(2,1)S(1)}, bf16[2,256,384]{2,1,0:T(8,128)(2,1)S(1)}, bf16[2,256...) custom-call(f32[2,8,8]{2,1,0:T(8,128)S(1)} %maximum_convert_fusion.mixing.refs_0_, ...), custom_call_target="tpu_custom_call" | custom-call | bytes 1 | tf_op jit(solution)/shard_map/attention_forward/pallas_call | solution.py:688
  13.4 13.2 %middle_kernel.1 = (bf16[16,288,128]{2,1,0:T(8,128)(2,1)S(1)}, bf16[16,288,128]{2,1,0:T(8,128)(2,1)S(1)}, f32[2,208,384]{2,1,0:T(8,128)S(1)}, f32[16,384]{1,0:T(...) custom-call(bf16[2,208,384]{2,1,0:T(8,128)(2,1)S(1)} %get-tuple-elem, ...), custom_call_target="tpu_custom_call" | custom-call | bytes 1 | tf_op jit(solution)/shard_map/middle_kernel/pallas_call | solution.py:688
  26.6 0.4 collective-permute-start.5
  27.0 3.8 %attention_backward_0.1 = (bf16[208,1152]{1,0:T(8,128)(2,1)S(1)}, f32[24,384]{1,0:T(8,128)S(1)}) custom-call(f32[2,8,8]{2,1,0:T(8,128)S(1)} %maximum_convert_fusion.mixing.refs_0_, f32[2,208,384]{2,1,0:T(8,128)S(1)} %get-tuple-element.145.refs_1_.mg_ref, s32[4,196]{1,0:T(4,128)S(1)} %copy-done.5, bf16[2,256,384]{2,1,0:T(8,128)(2,1)S(1)} %get-tuple-element.134.refs_3_, ...), custom_call_target="tpu_custom_call" | custom-call | bytes 1 | tf_op jit(solution)/shard_map/attention_backward_0/pallas_call | solution.py:688
  30.9 0.2 add_convert_fusion
  31.0 2.7 %collective-permute-start.8 = (bf16[8,288,128]{2,1,0:T(8,128)(2,1)S(1)}, bf16[8,288,128]{2,1,0:T(8,128)(2,1)S(1)}, u32[]{:S(2)}, u32[]{:S(2)}) collective-permute-start(bf16[8,288,128]{2,1,0:T(8,128)(2,1)S(1)} %add_convert_fusion), channel_id=1, source_target_pairs={{0,1},{1,0},{2,3},{3,2},{4,5},{5,4},{6,7},{7,6},{8,9},{9,8},{10,11... | collective-permute-start | bytes 1769480 | tf_op jit(solution)/shard_map/ppermute | solution.py:714
  33.7 4.0 %attention_backward_1.1 = (bf16[208,1152]{1,0:T(8,128)(2,1)S(1)}, f32[24,384]{1,0:T(8,128)S(1)}) custom-call(f32[2,8,8]{2,1,0:T(8,128)S(1)} %maximum_convert_fusion.mixing.refs_0_, f32[2,208,384]{2,1,0:T(8,128)S(1)} %get-tuple-element.145.refs_1_.mg_ref, s32[4,196]{1,0:T(4,128)S(1)} %copy-done.5, bf16[2,256,384]{2,1,0:T(8,128)(2,1)S(1)} %get-tuple-element.134.refs_3_, ...), custom_call_target="tpu_custom_call" | custom-call | bytes 1 | tf_op jit(solution)/shard_map/attention_backward_1/pallas_call | solution.py:688
  37.8 3.3 %input_gradients.1 = (bf16[16,160,128]{2,1,0:T(8,128)(2,1)S(1)}, bf16[16,160,128]{2,1,0:T(8,128)(2,1)S(1)}, f32[2,192,208]{2,1,0:T(8,128)S(1)}, bf16[2,208,208]{2,1,0:T(8,128)(2,1)S(1)}) custom-call(f32[2,208,384]{2,1,0:T(8,128)S(1)} %get-tuple-element.145.refs_1_.mg_ref, bf16[4,208,384]{2,1,0:T(8,128)(2,1)S(1)} %pad.4.rows_ref, ...), custom_call_target="tpu_custom_call" | custom-call | bytes 1 | tf_op jit(solution)/shard_map/input_gradients/pallas_call | solution.py:688
  41.0 0.2 collective-permute-start.7
  41.3 0.5 collective-permute-start.6
  41.8 0.1 add_convert_fusion.2
  41.9 1.9 %collective-permute-start.10 = (bf16[4,288,128]{2,1,0:T(8,128)(2,1)S(1)}, bf16[4,288,128]{2,1,0:T(8,128)(2,1)S(1)}, u32[]{:S(2)}, u32[]{:S(2)}) collective-permute-start(bf16[4,288,128]{2,1,0:T(8,128)(2,1)S(1)} %add_convert_fusion.2), channel_id=1, source_target_pairs={{0,2},{1,3},{2,0},{3,1},{4,6},{5,7},{6,4},{7,5},{8,10},{9,11},{10,... | collective-permute-start | bytes 884744 | tf_op jit(solution)/shard_map/ppermute | solution.py:714
  43.8 0.1 add_convert_fusion.1
  43.9 1.6 %collective-permute-start.9 = (bf16[8,160,128]{2,1,0:T(8,128)(2,1)S(1)}, bf16[8,160,128]{2,1,0:T(8,128)(2,1)S(1)}, u32[]{:S(2)}, u32[]{:S(2)}) collective-permute-start(bf16[8,160,128]{2,1,0:T(8,128)(2,1)S(1)} %add_convert_fusion.1), channel_id=1, source_target_pairs={{0,1},{1,0},{2,3},{3,2},{4,5},{5,4},{6,7},{7,6},{8,9},{9,8},{10,11... | collective-permute-start | bytes 983048 | tf_op jit(solution)/shard_map/ppermute | solution.py:714
  45.6 5.7 %collective-permute-done.10 = bf16[4,288,128]{2,1,0:T(8,128)(2,1)S(1)} collective-permute-done((bf16[4,288,128]{2,1,0:T(8,128)(2,1)S(1)}, bf16[4,288,128]{2,1,0:T(8,128)(2,1)S(1)}, u32[]{:S(2)}, u32[]{:S(2)}) %collective-permute-start.10) | collective-permute-done | bytes 294944 | tf_op jit(solution)/shard_map/ppermute | solution.py:714
  51.5 0.1 add_convert_fusion.9
  51.5 2.2 %collective-permute-start.12 = (bf16[2,288,128]{2,1,0:T(8,128)(2,1)S(1)}, bf16[2,288,128]{2,1,0:T(8,128)(2,1)S(1)}, u32[]{:S(2)}, u32[]{:S(2)}) collective-permute-start(bf16[2,288,128]{2,1,0:T(8,128)(2,1)S(1)} %add_convert_fusion.9), channel_id=1, source_target_pairs={{0,4},{1,5},{2,6},{3,7},{4,0},{5,1},{6,2},{7,3},{8,12},{9,13},{10,... | collective-permute-start | bytes 442376 | tf_op jit(solution)/shard_map/ppermute | solution.py:714
  53.8 0.1 add_convert_fusion.6
  53.9 1.6 %collective-permute-start.11 = (bf16[4,160,128]{2,1,0:T(8,128)(2,1)S(1)}, bf16[4,160,128]{2,1,0:T(8,128)(2,1)S(1)}, u32[]{:S(2)}, u32[]{:S(2)}) collective-permute-start(bf16[4,160,128]{2,1,0:T(8,128)(2,1)S(1)} %add_convert_fusion.6), channel_id=1, source_target_pairs={{0,2},{1,3},{2,0},{3,1},{4,6},{5,7},{6,4},{7,5},{8,10},{9,11},{10,... | collective-permute-start | bytes 491528 | tf_op jit(solution)/shard_map/ppermute | solution.py:714
  55.5 2.6 %collective-permute-start.15 = (bf16[1,144,128]{2,1,0:T(8,128)(2,1)S(1)}, bf16[1,144,128]{2,1,0:T(8,128)(2,1)S(1)}, u32[]{:S(2)}, u32[]{:S(2)}) collective-permute-start(bf16[1,144,128]{2,1,0:T(8,128)(2,1)S(1)} %bitcast.30), channel_id=1, source_target_pairs={{0,8},{1,9},{2,10},{3,11},{4,12},{5,13},{6,14},{7,15},{8,0},{9,1},... | collective-permute-start | bytes 110600 | tf_op jit(solution)/shard_map/ppermute | solution.py:714
  58.1 0.1 add_convert_fusion.13
  58.3 2.3 %collective-permute-start.14 = (bf16[2,288,128]{2,1,0:T(8,128)(2,1)S(1)}, bf16[2,288,128]{2,1,0:T(8,128)(2,1)S(1)}, u32[]{:S(2)}, u32[]{:S(2)}) collective-permute-start(bf16[2,288,128]{2,1,0:T(8,128)(2,1)S(1)} %pad_maximum_fusion.2), channel_id=1, source_target_pairs={{0,8},{1,9},{2,10},{3,11},{4,12},{5,13},{6,14},{7,15},{8,0},{9,1},... | collective-permute-start | bytes 442376 | tf_op jit(solution)/shard_map/ppermute | solution.py:714
  60.6 0.1 add_convert_fusion.11
  60.7 1.2 %collective-permute-start.13 = (bf16[4,160,128]{2,1,0:T(8,128)(2,1)S(1)}, bf16[4,160,128]{2,1,0:T(8,128)(2,1)S(1)}, u32[]{:S(2)}, u32[]{:S(2)}) collective-permute-start(bf16[4,160,128]{2,1,0:T(8,128)(2,1)S(1)} %pad_maximum_fusion), channel_id=1, source_target_pairs={{0,4},{1,5},{2,6},{3,7},{4,0},{5,1},{6,2},{7,3},{8,12},{9,13},{10,... | collective-permute-start | bytes 491528 | tf_op jit(solution)/shard_map/ppermute | solution.py:714
  61.9 0.9 collective-permute-done.15
  62.8 0.1 collective-permute-start.17
  62.9 0.1 add_convert_fusion.5
  63.0 3.9 %collective-permute-done.14 = bf16[2,288,128]{2,1,0:T(8,128)(2,1)S(1)} collective-permute-done((bf16[2,288,128]{2,1,0:T(8,128)(2,1)S(1)}, bf16[2,288,128]{2,1,0:T(8,128)(2,1)S(1)}, u32[]{:S(2)}, u32[]{:S(2)}) %collective-permute-start.14) | collective-permute-done | bytes 147488 | tf_op jit(solution)/shard_map/ppermute | solution.py:714
  66.9 0.1 add_convert_fusion.7
  67.1 0.1 collective-permute-start.19
  67.2 0.5 collective-permute-done.13
  67.7 2.1 %collective-permute-start.16 = (bf16[4,160,128]{2,1,0:T(8,128)(2,1)S(1)}, bf16[4,160,128]{2,1,0:T(8,128)(2,1)S(1)}, u32[]{:S(2)}, u32[]{:S(2)}) collective-permute-start(bf16[4,160,128]{2,1,0:T(8,128)(2,1)S(1)} %pad_maximum_fusion.1), channel_id=1, source_target_pairs={{0,8},{1,9},{2,10},{3,11},{4,12},{5,13},{6,14},{7,15},{8,0},{9,1},... | collective-permute-start | bytes 491528 | tf_op jit(solution)/shard_map/ppermute | solution.py:714
  69.8 2.9 %collective-permute-start.18 = (bf16[4,144,128]{2,1,0:T(8,128)(2,1)S(1)}, bf16[4,144,128]{2,1,0:T(8,128)(2,1)S(1)}, u32[]{:S(2)}, u32[]{:S(2)}) collective-permute-start(bf16[4,144,128]{2,1,0:T(8,128)(2,1)S(1)} %constant_dynamic-update-slice_fusion.2), channel_id=1, source_target_pairs={{0,2},{1,3},{2,0},{3,1},{4,6},{5,7},{6,4},{7,5},{8,10},{9,11},{10,... | collective-permute-start | bytes 442376 | tf_op jit(solution)/shard_map/ppermute | solution.py:714
  72.7 1.5 %collective-permute-done.19 = bf16[2,288,128]{2,1,0:T(8,128)(2,1)S(1)} collective-permute-done((bf16[2,288,128]{2,1,0:T(8,128)(2,1)S(1)}, bf16[2,288,128]{2,1,0:T(8,128)(2,1)S(1)}, u32[]{:S(2)}, u32[]{:S(2)}) %collective-permute-start.19) | collective-permute-done | bytes 147488 | tf_op jit(solution)/shard_map/ppermute | solution.py:714
  74.3 0.1 collective-permute-start.21
  74.4 2.1 %collective-permute-done.18 = bf16[4,144,128]{2,1,0:T(8,128)(2,1)S(1)} collective-permute-done((bf16[4,144,128]{2,1,0:T(8,128)(2,1)S(1)}, bf16[4,144,128]{2,1,0:T(8,128)(2,1)S(1)}, u32[]{:S(2)}, u32[]{:S(2)}) %collective-permute-start.18) | collective-permute-done | bytes 147488 | tf_op jit(solution)/shard_map/ppermute | solution.py:714
  76.5 2.4 %collective-permute-start.24 = (bf16[8,144,128]{2,1,0:T(8,128)(2,1)S(1)}, bf16[8,144,128]{2,1,0:T(8,128)(2,1)S(1)}, u32[]{:S(2)}, u32[]{:S(2)}) collective-permute-start(bf16[8,144,128]{2,1,0:T(8,128)(2,1)S(1)} %constant_dynamic-update-slice_fusion.6.refs_0_), channel_id=1, source_target_pairs={{0,1},{1,0},{2,3},{3,2},{4,5},{5,4},{6,7},{7,6},{8,9},{9,8},{10,11... | collective-permute-start | bytes 884744 | tf_op jit(solution)/shard_map/ppermute | solution.py:714
  79.0 1.9 %collective-permute-start.20 = (bf16[4,160,128]{2,1,0:T(8,128)(2,1)S(1)}, bf16[4,160,128]{2,1,0:T(8,128)(2,1)S(1)}, u32[]{:S(2)}, u32[]{:S(2)}) collective-permute-start(bf16[4,160,128]{2,1,0:T(8,128)(2,1)S(1)} %add_convert_fusion.3), channel_id=1, source_target_pairs={{0,2},{1,3},{2,0},{3,1},{4,6},{5,7},{6,4},{7,5},{8,10},{9,11},{10,... | collective-permute-start | bytes 491528 | tf_op jit(solution)/shard_map/ppermute | solution.py:714
  80.9 1.9 %collective-permute-done.21 = bf16[4,288,128]{2,1,0:T(8,128)(2,1)S(1)} collective-permute-done((bf16[4,288,128]{2,1,0:T(8,128)(2,1)S(1)}, bf16[4,288,128]{2,1,0:T(8,128)(2,1)S(1)}, u32[]{:S(2)}, u32[]{:S(2)}) %collective-permute-start.21) | collective-permute-done | bytes 294944 | tf_op jit(solution)/shard_map/ppermute | solution.py:714
  82.9 2.4 %collective-permute-start.23 = (bf16[8,288,128]{2,1,0:T(8,128)(2,1)S(1)}, bf16[8,288,128]{2,1,0:T(8,128)(2,1)S(1)}, u32[]{:S(2)}, u32[]{:S(2)}) collective-permute-start(bf16[8,288,128]{2,1,0:T(8,128)(2,1)S(1)} %constant_dynamic-update-slice_fusion.8.mine_low), channel_id=1, source_target_pairs={{0,1},{1,0},{2,3},{3,2},{4,5},{5,4},{6,7},{7,6},{8,9},{9,8},{10,11... | collective-permute-start | bytes 1769480 | tf_op jit(solution)/shard_map/ppermute | solution.py:714
  85.3 1.0 assemble.1
  86.4 0.1 collective-permute-start.25
  86.4 0.5 collective-permute-start.26
  86.9 0.1 collective-permute-start.27
  87.0 1.0 collective-permute-done.25.refs_2_
  88.0 0.4 collective-permute-done.26.refs_3_
  88.4 0.1 class_gradients.1
  88.5 4.6 %collective-permute-done.23.mine_high = bf16[8,288,128]{2,1,0:T(8,128)(2,1)S(1)} collective-permute-done((bf16[8,288,128]{2,1,0:T(8,128)(2,1)S(1)}, bf16[8,288,128]{2,1,0:T(8,128)(2,1)S(1)}, u32[]{:S(2)}, u32[]{:S(2)}) %collective-permute-start.23) | collective-permute-done | bytes 589856 | tf_op jit(solution)/shard_map/ppermute | solution.py:714
  93.2 1.2 %collective-permute-start.28 = (bf16[8,288,128]{2,1,0:T(8,128)(2,1)S(1)}, bf16[8,288,128]{2,1,0:T(8,128)(2,1)S(1)}, u32[]{:S(2)}, u32[]{:S(2)}) collective-permute-start(bf16[8,288,128]{2,1,0:T(8,128)(2,1)S(1)} %collective-permute-done.23.mine_high), channel_id=1, source_target_pairs={{0,16},{16,0},{1,17},{17,1},{2,18},{18,2},{3,19},{19,3},{4,20},{20... | collective-permute-start | bytes 1769480 | tf_op jit(solution)/shard_map/ppermute | solution.py:703
  94.4 2.4 %collective-permute-start.22 = (bf16[8,160,128]{2,1,0:T(8,128)(2,1)S(1)}, bf16[8,160,128]{2,1,0:T(8,128)(2,1)S(1)}, u32[]{:S(2)}, u32[]{:S(2)}) collective-permute-start(bf16[8,160,128]{2,1,0:T(8,128)(2,1)S(1)} %constant_dynamic-update-slice_fusion.10.mine_low), channel_id=1, source_target_pairs={{0,1},{1,0},{2,3},{3,2},{4,5},{5,4},{6,7},{7,6},{8,9},{9,8},{10,11... | collective-permute-start | bytes 983048 | tf_op jit(solution)/shard_map/ppermute | solution.py:714
  96.8 2.5 %fc_outputs.1 = (f32[384,1536]{1,0:T(8,128)}, f32[1536,384]{1,0:T(8,128)}) custom-call(bf16[8,288,128]{2,1,0:T(8,128)(2,1)S(1)} %constant_dynamic-update-slice_fusion.8.mine_low, bf16[8,288,128]{2,1,0:T(8,128)(2,1)S(1)} %collective-permute-done.23.mine_high, ...), custom_call_target="tpu_custom_call", output_to_operand_aliasing={{0}: (4, {}), {1}: (5, {})} | custom-call | bytes 1 | tf_op jit(solution)/shard_map/fc_outputs/pallas_call | solution.py:688
  99.3 2.5 %collective-permute-done.22.mine_high = bf16[8,160,128]{2,1,0:T(8,128)(2,1)S(1)} collective-permute-done((bf16[8,160,128]{2,1,0:T(8,128)(2,1)S(1)}, bf16[8,160,128]{2,1,0:T(8,128)(2,1)S(1)}, u32[]{:S(2)}, u32[]{:S(2)}) %collective-permute-start.22) | collective-permute-done | bytes 327712 | tf_op jit(solution)/shard_map/ppermute | solution.py:714
  101.9 1.6 %collective-permute-done.30.other_high = bf16[8,160,128]{2,1,0:T(8,128)(2,1)S(1)} collective-permute-done((bf16[8,160,128]{2,1,0:T(8,128)(2,1)S(1)}, bf16[8,160,128]{2,1,0:T(8,128)(2,1)S(1)}, u32[]{:S(2)}, u32[]{:S(2)}) %collective-permute-start.30) | collective-permute-done | bytes 327712 | tf_op jit(solution)/shard_map/ppermute | solution.py:703
  103.5 2.3 %qkv_outputs.1 = (f32[384,1152]{1,0:T(8,128)}, f32[384,384]{1,0:T(8,128)}, f32[1,384]{1,0:T(1,128)}, f32[1,384]{1,0:T(1,128)}, f32[1,768]{1,0:T(1,128)}, /*index...) custom-call(bf16[8,160,128]{2,1,0:T(8,128)(2,1)S(1)} %constant_dynam, ...), custom_call_target="tpu_custom_call", output_to_operand_aliasing={{0}: (4, {}), {1}: (5, {})} | custom-call | bytes 1 | tf_op jit(solution)/shard_map/qkv_outputs/pallas_call | solution.py:688
  (73 shorter events, 0.9 us)
Async XLA Ops:
  0.7 2.8 %collective-permute-start.1 = (bf16[384,1152]{1,0:T(8,128)(2,1)}, bf16[384,1152]{1,0:T(8,128)(2,1)S(1)}, u32[]{:S(2)}, u32[]{:S(2)}) collective-permute-start(bf16[384,1152]{1,0:T(8,128)(2,1)} %bitcast.14), channel_id=1, source_target_pairs={{0,16},{16,0},{1,17},{17,1},{2,18},{18,2},{3,19},{19,3},{4,20},{20... | collective-permute-start | bytes 2654216 | tf_op jit(solution)/shard_map/ppermute | solution.py:703
  3.4 9.8 %collective-permute-start.3 = (bf16[384,1536]{1,0:T(8,128)(2,1)}, bf16[384,1536]{1,0:T(8,128)(2,1)S(1)}, u32[]{:S(2)}, u32[]{:S(2)}) collective-permute-start(bf16[384,1536]{1,0:T(8,128)(2,1)} %bitcast.19), channel_id=1, source_target_pairs={{0,16},{16,0},{1,17},{17,1},{2,18},{18,2},{3,19},{19,3},{4,20},{20... | collective-permute-start | bytes 3538952 | tf_op jit(solution)/shard_map/ppermute | solution.py:703
  3.8 9.5 %collective-permute-start.4 = (bf16[1536,384]{1,0:T(8,128)(2,1)}, bf16[1536,384]{1,0:T(8,128)(2,1)S(1)}, u32[]{:S(2)}, u32[]{:S(2)}) collective-permute-start(bf16[1536,384]{1,0:T(8,128)(2,1)} %bitcast.22), channel_id=1, source_target_pairs={{0,16},{16,0},{1,17},{17,1},{2,18},{18,2},{3,19},{19,3},{4,20},{20... | collective-permute-start | bytes 3538952 | tf_op jit(solution)/shard_map/ppermute | solution.py:703
  4.0 9.3 %collective-permute-start.2 = (bf16[384,384]{1,0:T(8,128)(2,1)}, bf16[384,384]{1,0:T(8,128)(2,1)S(1)}, u32[]{:S(2)}, u32[]{:S(2)}) collective-permute-start(bf16[384,384]{1,0:T(8,128)(2,1)} %bitcast.25), channel_id=1, source_target_pairs={{0,16},{16,0},{1,17},{17,1},{2,18},{18,2},{3,19},{19,3},{4,20},{20... | collective-permute-start | bytes 884744 | tf_op jit(solution)/shard_map/ppermute | solution.py:703
  6.0 2.6 %collective-permute-start = (bf16[16,384]{1,0:T(8,128)(2,1)}, bf16[16,384]{1,0:T(8,128)(2,1)S(1)}, u32[]{:S(2)}, u32[]{:S(2)}) collective-permute-start(bf16[16,384]{1,0:T(8,128)(2,1)} %get-tuple-element.125.vec_own.refs_7_.refs_8_), channel_id=1, source_target_pairs={{0,16},{16,0},{1,17},{17,1},{2,18},{18,2},{3,19},{19,3},{4,20},{20... | collective-permute-start | bytes 36872 | tf_op jit(solution)/shard_map/ppermute | solution.py:703
  6.9 1.7 %copy-start = (bf16[1,384,1152]{2,1,0:T(8,128)(2,1)S(1)}, bf16[1,384,1152]{2,1,0:T(8,128)(2,1)}, u32[]{:S(2)}) copy-start(bf16[1,384,1152]{2,1,0:T(8,128)(2,1)} %param.27) | copy-start | bytes 2654212
  7.0 1.7 %copy-start.4 = (bf16[16,384]{1,0:T(8,128)(2,1)S(1)}, bf16[16,384]{1,0:T(8,128)(2,1)}, u32[]{:S(2)}) copy-start(bf16[16,384]{1,0:T(8,128)(2,1)} %get-tuple-element.125.vec_own.refs_7_.refs_8_) | copy-start | bytes 36868
  7.0 1.7 %copy-start.5 = (s32[4,196]{1,0:T(4,128)S(1)}, s32[4,196]{1,0:T(4,128)}, u32[]{:S(2)}) copy-start(s32[4,196]{1,0:T(4,128)} %refs_2_.5) | copy-start | bytes 9412
  7.0 1.7 %copy-start.8 = (f32[1,384]{1,0:T(1,128)S(1)}, f32[1,384]{1,0:T(1,128)}, u32[]{:S(2)}) copy-start(f32[1,384]{1,0:T(1,128)} %get-tuple-element.126.bias_ref.refs_11_) | copy-start | bytes 4612
  8.2 5.1 %copy-start.3 = (bf16[1,384,384]{2,1,0:T(8,128)(2,1)S(1)}, bf16[1,384,384]{2,1,0:T(8,128)(2,1)}, u32[]{:S(2)}) copy-start(bf16[1,384,384]{2,1,0:T(8,128)(2,1)} %param.32) | copy-start | bytes 884740
  8.6 4.7 %copy-start.1 = (bf16[1,384,1536]{2,1,0:T(8,128)(2,1)S(1)}, bf16[1,384,1536]{2,1,0:T(8,128)(2,1)}, u32[]{:S(2)}) copy-start(bf16[1,384,1536]{2,1,0:T(8,128)(2,1)} %param.37) | copy-start | bytes 3538948
  8.7 4.7 %copy-start.2 = (bf16[1,1536,384]{2,1,0:T(8,128)(2,1)S(1)}, bf16[1,1536,384]{2,1,0:T(8,128)(2,1)}, u32[]{:S(2)}) copy-start(bf16[1,1536,384]{2,1,0:T(8,128)(2,1)} %param.39) | copy-start | bytes 3538948
  8.7 4.7 %copy-start.9 = (bf16[4,384]{1,0:T(4,128)(2,1)S(1)}, bf16[4,384]{1,0:T(4,128)(2,1)}, u32[]{:S(2)}) copy-start(bf16[4,384]{1,0:T(4,128)(2,1)} %class_ref.1) | copy-start | bytes 9220
  8.7 4.7 %copy-start.10 = (bf16[4,384]{1,0:T(4,128)(2,1)S(1)}, bf16[4,384]{1,0:T(4,128)(2,1)}, u32[]{:S(2)}) copy-start(bf16[4,384]{1,0:T(4,128)(2,1)} %cot_ref.1) | copy-start | bytes 9220
  13.4 13.7 %copy-start.6 = (f32[8,384]{1,0:T(8,128)S(1)}, f32[8,384]{1,0:T(8,128)}, u32[]{:S(2)}) copy-start(f32[8,384]{1,0:T(8,128)} %get-tuple-element.138.refs_12_) | copy-start | bytes 36868
  13.4 13.6 %copy-start.7 = (f32[8,384]{1,0:T(8,128)S(1)}, f32[8,384]{1,0:T(8,128)}, u32[]{:S(2)}) copy-start(f32[8,384]{1,0:T(8,128)} %get-tuple-element.139.refs_13_) | copy-start | bytes 36868
  26.6 4.3 %collective-permute-start.5 = (bf16[16,288,128]{2,1,0:T(8,128)(2,1)S(1)}, bf16[16,288,128]{2,1,0:T(8,128)(2,1)S(1)}, u32[]{:S(2)}, u32[]{:S(2)}) collective-permute-start(bf16[16,288,128]{2,1,0:T(8,128)(2,1)S(1)} %get-tuple-element.133), channel_id=1, source_target_pairs={{0,16},{16,0},{1,17},{17,1},{2,18},{18,2},{3,19},{19,3},{4,20},{20... | collective-permute-start | bytes 3538952 | tf_op jit(solution)/shard_map/ppermute | solution.py:703
  31.0 10.7 %collective-permute-start.8 = (bf16[8,288,128]{2,1,0:T(8,128)(2,1)S(1)}, bf16[8,288,128]{2,1,0:T(8,128)(2,1)S(1)}, u32[]{:S(2)}, u32[]{:S(2)}) collective-permute-start(bf16[8,288,128]{2,1,0:T(8,128)(2,1)S(1)} %add_convert_fusion), channel_id=1, source_target_pairs={{0,1},{1,0},{2,3},{3,2},{4,5},{5,4},{6,7},{7,6},{8,9},{9,8},{10,11... | collective-permute-start | bytes 1769480 | tf_op jit(solution)/shard_map/ppermute | solution.py:714
  41.0 2.8 %collective-permute-start.7 = (bf16[16,160,128]{2,1,0:T(8,128)(2,1)S(1)}, bf16[16,160,128]{2,1,0:T(8,128)(2,1)S(1)}, u32[]{:S(2)}, u32[]{:S(2)}) collective-permute-start(bf16[16,160,128]{2,1,0:T(8,128)(2,1)S(1)} %get-tuple-element.159), channel_id=1, source_target_pairs={{0,16},{16,0},{1,17},{17,1},{2,18},{18,2},{3,19},{19,3},{4,20},{20... | collective-permute-start | bytes 1966088 | tf_op jit(solution)/shard_map/ppermute | solution.py:703
  41.3 4.3 %collective-permute-start.6 = (bf16[2,208,208]{2,1,0:T(8,128)(2,1)S(1)}, bf16[2,208,208]{2,1,0:T(8,128)(2,1)S(1)}, u32[]{:S(2)}, u32[]{:S(2)}) collective-permute-start(bf16[2,208,208]{2,1,0:T(8,128)(2,1)S(1)} %get-tuple-element.153), channel_id=1, source_target_pairs={{0,16},{16,0},{1,17},{17,1},{2,18},{18,2},{3,19},{19,3},{4,20},{20... | collective-permute-start | bytes 519176 | tf_op jit(solution)/shard_map/ppermute | solution.py:703
  41.9 9.5 %collective-permute-start.10 = (bf16[4,288,128]{2,1,0:T(8,128)(2,1)S(1)}, bf16[4,288,128]{2,1,0:T(8,128)(2,1)S(1)}, u32[]{:S(2)}, u32[]{:S(2)}) collective-permute-start(bf16[4,288,128]{2,1,0:T(8,128)(2,1)S(1)} %add_convert_fusion.2), channel_id=1, source_target_pairs={{0,2},{1,3},{2,0},{3,1},{4,6},{5,7},{6,4},{7,5},{8,10},{9,11},{10,... | collective-permute-start | bytes 884744 | tf_op jit(solution)/shard_map/ppermute | solution.py:714
  43.9 9.9 %collective-permute-start.9 = (bf16[8,160,128]{2,1,0:T(8,128)(2,1)S(1)}, bf16[8,160,128]{2,1,0:T(8,128)(2,1)S(1)}, u32[]{:S(2)}, u32[]{:S(2)}) collective-permute-start(bf16[8,160,128]{2,1,0:T(8,128)(2,1)S(1)} %add_convert_fusion.1), channel_id=1, source_target_pairs={{0,1},{1,0},{2,3},{3,2},{4,5},{5,4},{6,7},{7,6},{8,9},{9,8},{10,11... | collective-permute-start | bytes 983048 | tf_op jit(solution)/shard_map/ppermute | solution.py:714
  51.5 6.6 %collective-permute-start.12 = (bf16[2,288,128]{2,1,0:T(8,128)(2,1)S(1)}, bf16[2,288,128]{2,1,0:T(8,128)(2,1)S(1)}, u32[]{:S(2)}, u32[]{:S(2)}) collective-permute-start(bf16[2,288,128]{2,1,0:T(8,128)(2,1)S(1)} %add_convert_fusion.9), channel_id=1, source_target_pairs={{0,4},{1,5},{2,6},{3,7},{4,0},{5,1},{6,2},{7,3},{8,12},{9,13},{10,... | collective-permute-start | bytes 442376 | tf_op jit(solution)/shard_map/ppermute | solution.py:714
  53.9 6.6 %collective-permute-start.11 = (bf16[4,160,128]{2,1,0:T(8,128)(2,1)S(1)}, bf16[4,160,128]{2,1,0:T(8,128)(2,1)S(1)}, u32[]{:S(2)}, u32[]{:S(2)}) collective-permute-start(bf16[4,160,128]{2,1,0:T(8,128)(2,1)S(1)} %add_convert_fusion.6), channel_id=1, source_target_pairs={{0,2},{1,3},{2,0},{3,1},{4,6},{5,7},{6,4},{7,5},{8,10},{9,11},{10,... | collective-permute-start | bytes 491528 | tf_op jit(solution)/shard_map/ppermute | solution.py:714
  55.5 7.3 %collective-permute-start.15 = (bf16[1,144,128]{2,1,0:T(8,128)(2,1)S(1)}, bf16[1,144,128]{2,1,0:T(8,128)(2,1)S(1)}, u32[]{:S(2)}, u32[]{:S(2)}) collective-permute-start(bf16[1,144,128]{2,1,0:T(8,128)(2,1)S(1)} %bitcast.30), channel_id=1, source_target_pairs={{0,8},{1,9},{2,10},{3,11},{4,12},{5,13},{6,14},{7,15},{8,0},{9,1},... | collective-permute-start | bytes 110600 | tf_op jit(solution)/shard_map/ppermute | solution.py:714
  58.3 8.7 %collective-permute-start.14 = (bf16[2,288,128]{2,1,0:T(8,128)(2,1)S(1)}, bf16[2,288,128]{2,1,0:T(8,128)(2,1)S(1)}, u32[]{:S(2)}, u32[]{:S(2)}) collective-permute-start(bf16[2,288,128]{2,1,0:T(8,128)(2,1)S(1)} %pad_maximum_fusion.2), channel_id=1, source_target_pairs={{0,8},{1,9},{2,10},{3,11},{4,12},{5,13},{6,14},{7,15},{8,0},{9,1},... | collective-permute-start | bytes 442376 | tf_op jit(solution)/shard_map/ppermute | solution.py:714
  60.7 7.0 %collective-permute-start.13 = (bf16[4,160,128]{2,1,0:T(8,128)(2,1)S(1)}, bf16[4,160,128]{2,1,0:T(8,128)(2,1)S(1)}, u32[]{:S(2)}, u32[]{:S(2)}) collective-permute-start(bf16[4,160,128]{2,1,0:T(8,128)(2,1)S(1)} %pad_maximum_fusion), channel_id=1, source_target_pairs={{0,4},{1,5},{2,6},{3,7},{4,0},{5,1},{6,2},{7,3},{8,12},{9,13},{10,... | collective-permute-start | bytes 491528 | tf_op jit(solution)/shard_map/ppermute | solution.py:714
  62.8 7.0 %collective-permute-start.17 = (bf16[2,144,128]{2,1,0:T(8,128)(2,1)S(1)}, bf16[2,144,128]{2,1,0:T(8,128)(2,1)S(1)}, u32[]{:S(2)}, u32[]{:S(2)}) collective-permute-start(bf16[2,144,128]{2,1,0:T(8,128)(2,1)S(1)} %constant_dynamic-update-slice_fusion), channel_id=1, source_target_pairs={{0,4},{1,5},{2,6},{3,7},{4,0},{5,1},{6,2},{7,3},{8,12},{9,13},{10,... | collective-permute-start | bytes 221192 | tf_op jit(solution)/shard_map/ppermute | solution.py:714
  67.1 7.2 %collective-permute-start.19 = (bf16[2,288,128]{2,1,0:T(8,128)(2,1)S(1)}, bf16[2,288,128]{2,1,0:T(8,128)(2,1)S(1)}, u32[]{:S(2)}, u32[]{:S(2)}) collective-permute-start(bf16[2,288,128]{2,1,0:T(8,128)(2,1)S(1)} %add_convert_fusion.7), channel_id=1, source_target_pairs={{0,4},{1,5},{2,6},{3,7},{4,0},{5,1},{6,2},{7,3},{8,12},{9,13},{10,... | collective-permute-start | bytes 442376 | tf_op jit(solution)/shard_map/ppermute | solution.py:714
  67.7 11.2 %collective-permute-start.16 = (bf16[4,160,128]{2,1,0:T(8,128)(2,1)S(1)}, bf16[4,160,128]{2,1,0:T(8,128)(2,1)S(1)}, u32[]{:S(2)}, u32[]{:S(2)}) collective-permute-start(bf16[4,160,128]{2,1,0:T(8,128)(2,1)S(1)} %pad_maximum_fusion.1), channel_id=1, source_target_pairs={{0,8},{1,9},{2,10},{3,11},{4,12},{5,13},{6,14},{7,15},{8,0},{9,1},... | collective-permute-start | bytes 491528 | tf_op jit(solution)/shard_map/ppermute | solution.py:714
  69.8 6.6 %collective-permute-start.18 = (bf16[4,144,128]{2,1,0:T(8,128)(2,1)S(1)}, bf16[4,144,128]{2,1,0:T(8,128)(2,1)S(1)}, u32[]{:S(2)}, u32[]{:S(2)}) collective-permute-start(bf16[4,144,128]{2,1,0:T(8,128)(2,1)S(1)} %constant_dynamic-update-slice_fusion.2), channel_id=1, source_target_pairs={{0,2},{1,3},{2,0},{3,1},{4,6},{5,7},{6,4},{7,5},{8,10},{9,11},{10,... | collective-permute-start | bytes 442376 | tf_op jit(solution)/shard_map/ppermute | solution.py:714
  74.3 8.5 %collective-permute-start.21 = (bf16[4,288,128]{2,1,0:T(8,128)(2,1)S(1)}, bf16[4,288,128]{2,1,0:T(8,128)(2,1)S(1)}, u32[]{:S(2)}, u32[]{:S(2)}) collective-permute-start(bf16[4,288,128]{2,1,0:T(8,128)(2,1)S(1)} %constant_dynamic-update-slice_fusion.4), channel_id=1, source_target_pairs={{0,2},{1,3},{2,0},{3,1},{4,6},{5,7},{6,4},{7,5},{8,10},{9,11},{10,... | collective-permute-start | bytes 884744 | tf_op jit(solution)/shard_map/ppermute | solution.py:714
  76.5 9.8 %collective-permute-start.24 = (bf16[8,144,128]{2,1,0:T(8,128)(2,1)S(1)}, bf16[8,144,128]{2,1,0:T(8,128)(2,1)S(1)}, u32[]{:S(2)}, u32[]{:S(2)}) collective-permute-start(bf16[8,144,128]{2,1,0:T(8,128)(2,1)S(1)} %constant_dynamic-update-slice_fusion.6.refs_0_), channel_id=1, source_target_pairs={{0,1},{1,0},{2,3},{3,2},{4,5},{5,4},{6,7},{7,6},{8,9},{9,8},{10,11... | collective-permute-start | bytes 884744 | tf_op jit(solution)/shard_map/ppermute | solution.py:714
  79.0 7.3 %collective-permute-start.20 = (bf16[4,160,128]{2,1,0:T(8,128)(2,1)S(1)}, bf16[4,160,128]{2,1,0:T(8,128)(2,1)S(1)}, u32[]{:S(2)}, u32[]{:S(2)}) collective-permute-start(bf16[4,160,128]{2,1,0:T(8,128)(2,1)S(1)} %add_convert_fusion.3), channel_id=1, source_target_pairs={{0,2},{1,3},{2,0},{3,1},{4,6},{5,7},{6,4},{7,5},{8,10},{9,11},{10,... | collective-permute-start | bytes 491528 | tf_op jit(solution)/shard_map/ppermute | solution.py:714
  82.9 10.3 %collective-permute-start.23 = (bf16[8,288,128]{2,1,0:T(8,128)(2,1)S(1)}, bf16[8,288,128]{2,1,0:T(8,128)(2,1)S(1)}, u32[]{:S(2)}, u32[]{:S(2)}) collective-permute-start(bf16[8,288,128]{2,1,0:T(8,128)(2,1)S(1)} %constant_dynamic-update-slice_fusion.8.mine_low), channel_id=1, source_target_pairs={{0,1},{1,0},{2,3},{3,2},{4,5},{5,4},{6,7},{7,6},{8,9},{9,8},{10,11... | collective-permute-start | bytes 1769480 | tf_op jit(solution)/shard_map/ppermute | solution.py:714
  86.4 1.6 %collective-permute-start.25 = (bf16[8,144,128]{2,1,0:T(8,128)(2,1)S(1)}, bf16[8,144,128]{2,1,0:T(8,128)(2,1)S(1)}, u32[]{:S(2)}, u32[]{:S(2)}) collective-permute-start(bf16[8,144,128]{2,1,0:T(8,128)(2,1)S(1)} %constant_dynamic-update-slice_fusion.6.refs_0_), channel_id=1, source_target_pairs={{0,16},{16,0},{1,17},{17,1},{2,18},{18,2},{3,19},{19,3},{4,20},{20... | collective-permute-start | bytes 884744 | tf_op jit(solution)/shard_map/ppermute | solution.py:703
  86.4 2.0 %collective-permute-start.26 = (bf16[8,144,128]{2,1,0:T(8,128)(2,1)S(1)}, bf16[8,144,128]{2,1,0:T(8,128)(2,1)S(1)}, u32[]{:S(2)}, u32[]{:S(2)}) collective-permute-start(bf16[8,144,128]{2,1,0:T(8,128)(2,1)S(1)} %collective-permute-done.24.refs_1_), channel_id=1, source_target_pairs={{0,16},{16,0},{1,17},{17,1},{2,18},{18,2},{3,19},{19,3},{4,20},{20... | collective-permute-start | bytes 884744 | tf_op jit(solution)/shard_map/ppermute | solution.py:703
  86.9 9.9 %collective-permute-start.27 = (bf16[8,288,128]{2,1,0:T(8,128)(2,1)S(1)}, bf16[8,288,128]{2,1,0:T(8,128)(2,1)S(1)}, u32[]{:S(2)}, u32[]{:S(2)}) collective-permute-start(bf16[8,288,128]{2,1,0:T(8,128)(2,1)S(1)} %constant_dynamic-update-slice_fusion.8.mine_low), channel_id=1, source_target_pairs={{0,16},{16,0},{1,17},{17,1},{2,18},{18,2},{3,19},{19,3},{4,20},{20... | collective-permute-start | bytes 1769480 | tf_op jit(solution)/shard_map/ppermute | solution.py:703
  93.2 3.6 %collective-permute-start.28 = (bf16[8,288,128]{2,1,0:T(8,128)(2,1)S(1)}, bf16[8,288,128]{2,1,0:T(8,128)(2,1)S(1)}, u32[]{:S(2)}, u32[]{:S(2)}) collective-permute-start(bf16[8,288,128]{2,1,0:T(8,128)(2,1)S(1)} %collective-permute-done.23.mine_high), channel_id=1, source_target_pairs={{0,16},{16,0},{1,17},{17,1},{2,18},{18,2},{3,19},{19,3},{4,20},{20... | collective-permute-start | bytes 1769480 | tf_op jit(solution)/shard_map/ppermute | solution.py:703
  94.4 7.4 %collective-permute-start.22 = (bf16[8,160,128]{2,1,0:T(8,128)(2,1)S(1)}, bf16[8,160,128]{2,1,0:T(8,128)(2,1)S(1)}, u32[]{:S(2)}, u32[]{:S(2)}) collective-permute-start(bf16[8,160,128]{2,1,0:T(8,128)(2,1)S(1)} %constant_dynamic-update-slice_fusion.10.mine_low), channel_id=1, source_target_pairs={{0,1},{1,0},{2,3},{3,2},{4,5},{5,4},{6,7},{7,6},{8,9},{9,8},{10,11... | collective-permute-start | bytes 983048 | tf_op jit(solution)/shard_map/ppermute | solution.py:714
  96.8 5.1 %collective-permute-start.29 = (bf16[8,160,128]{2,1,0:T(8,128)(2,1)S(1)}, bf16[8,160,128]{2,1,0:T(8,128)(2,1)S(1)}, u32[]{:S(2)}, u32[]{:S(2)}) collective-permute-start(bf16[8,160,128]{2,1,0:T(8,128)(2,1)S(1)} %constant_dynamic-update-slice_fusion.10.mine_low), channel_id=1, source_target_pairs={{0,16},{16,0},{1,17},{17,1},{2,18},{18,2},{3,19},{19,3},{4,20},{20... | collective-permute-start | bytes 983048 | tf_op jit(solution)/shard_map/ppermute | solution.py:703
  101.9 1.6 %collective-permute-start.30 = (bf16[8,160,128]{2,1,0:T(8,128)(2,1)S(1)}, bf16[8,160,128]{2,1,0:T(8,128)(2,1)S(1)}, u32[]{:S(2)}, u32[]{:S(2)}) collective-permute-start(bf16[8,160,128]{2,1,0:T(8,128)(2,1)S(1)} %collective-permute-done.22.mine_high), channel_id=1, source_target_pairs={{0,16},{16,0},{1,17},{17,1},{2,18},{18,2},{3,19},{19,3},{4,20},{20... | collective-permute-start | bytes 983048 | tf_op jit(solution)/shard_map/ppermute | solution.py:703

commit v3 on v2

--- a/solution.py
+++ b/solution.py
@@ -54,6 +54,15 @@
 
 def chosen(is_first, first, other):
     return jnp.where(is_first, first, other)
+
+
+def scaled_rows(rows, factors):
+    size = rows.shape[0] // HEADS
+    parts = []
+    for head, factor in enumerate(factors):
+        part = rows[head * size : (head + 1) * size]
+        parts.append(part * jnp.full((1, rows.shape[1]), factor, F32).astype(BF16))
+    return jnp.concatenate(parts, axis=0)
 
 
 def transposed(rows):
@@ -146,23 +155,19 @@
         q_ref[b, length:] = pad_rows
         k_ref[b, length:] = pad_rows
         v_ref[b, length:] = pad_rows
-        q_t = transposed(q_ref[b].astype(F32))
-        v_t = transposed(v_ref[b].astype(F32))
+        q_t = transposed(q_ref[b])
+        v_t = transposed(v_ref[b])
         keep = keeps[:length, b : b + 1]
         allowed = (keep > 0.0) | same
         for h in range(HEADS):
-            scaled_q = jnp.concatenate(
-                [q_t[c * size : (c + 1) * size] * mixing[0, h, c] for c in range(HEADS)], axis=0
-            ).astype(BF16)
+            scaled_q = scaled_rows(q_t, [mixing[0, h, c] for c in range(HEADS)])
             scores = jnp.where(allowed, mm(low_k, scaled_q) * scale, -1e30)
             top = jnp.max(scores, axis=0, keepdims=True)
             weights = jnp.exp2(scores - top)
             weights = weights * (1.0 / jnp.sum(weights, axis=0, keepdims=True))
             pt_ref[b, h * lanes : h * lanes + length] = weights.astype(BF16)
             pt_ref[b, h * lanes + length : (h + 1) * lanes] = jnp.zeros((lanes - length, lanes), BF16)
-            vs_ref[:, h * lanes : (h + 1) * lanes] = jnp.concatenate(
-                [v_t[c * size : (c + 1) * size] * mixing[1, c, h] for c in range(HEADS)], axis=0
-            ).astype(BF16)
+            vs_ref[:, h * lanes : (h + 1) * lanes] = scaled_rows(v_t, [mixing[1, c, h] for c in range(HEADS)])
         mixed = transposed(mm(vs_ref[...], pt_ref[b]))[:length]
         low_f = low_v.astype(F32)
         extra = bias_ref[...] * (col_sum(low_f * keep) + (1.0 - keep) * low_f)
@@ -384,6 +389,8 @@
     )
     block_copy(blocks, kept_ref, 0, 16)
     block_copy(blocks, send_ref, 16, 16)
+    send_ref[16, 0:144] = factor_ref[...]
+    send_ref[16, 144:288] = jnp.zeros((144, 128), BF16)
 
 
 def attention_backward(
@@ -403,8 +410,8 @@
     da = mm_nt(bg, p_ref[...]).astype(BF16)
     da_ref[:length] = da
     da_ref[length:] = jnp.zeros((lanes - length, width), BF16)
-    da_t = transposed(da_ref[...].astype(F32))
-    k_t = transposed(k_ref[b].astype(F32))
+    da_t = transposed(da_ref[...])
+    k_t = transposed(k_ref[b])
     low_v = v_ref[b, :length]
     val_f = low_v.astype(F32)
     key_f = k_ref[b, :length].astype(F32)
@@ -414,9 +421,7 @@
     bias_sum = col_sum(da_f * (col_sum(val_f * keep) + (1.0 - keep) * val_f))
     post_parts = []
     for c in range(HEADS):
-        scaled = jnp.concatenate(
-            [da_t[h * size : (h + 1) * size] * mixing[1, h, c] for h in range(HEADS)], axis=0
-        ).astype(BF16)
+        scaled = scaled_rows(da_t, [mixing[1, h, c] for h in range(HEADS)])
         dp = mm(low_v, scaled)
         weights = pt_ref[b, c * lanes : c * lanes + length]
         w_f = weights.astype(F32)
@@ -426,9 +431,7 @@
         moved = mm(weights, da_ref[...])
         dv = dv + moved * post_rows[c : c + 1]
         post_parts.append(col_sum(moved * val_f))
-        ks_ref[:, c * lanes : (c + 1) * lanes] = jnp.concatenate(
-            [k_t[h * size : (h + 1) * size] * mixing[0, c, h] for h in range(HEADS)], axis=0
-        ).astype(BF16)
+        ks_ref[:, c * lanes : (c + 1) * lanes] = scaled_rows(k_t, [mixing[0, c, h] for h in range(HEADS)])
     dk = jnp.zeros((length, width), F32)
     pre_parts = []
     for h in range(HEADS):
@@ -517,15 +520,78 @@
         out[...] = rows.astype(BF16)
 
 
-def join_pieces(low, high, target):
-    target[0:8] = low[:, : target.shape[1]]
-    target[8:16] = high[:, : target.shape[1]]
-
-
-def unpack(mine, other, block, start):
-    source = mine if block < 16 else other
-    at = block_position(block) & 15
-    return [source[at, start + k * 48 : start + (k + 1) * 48].astype(F32) for k in range(3)]
+def place_blocks(start, pieces, outs, held, sems):
+    qkv_out, proj_out, fc1_out, fc2_out = outs
+    for half in range(2):
+        for n in range(8):
+            block = position_block(half * 16 + start + n)
+            slot = (half * 8 + n) * 3
+            for at in range(3):
+                source = pieces[0 if at < 2 else 1][half]
+                for k in range(3):
+                    rows = slice(k * 48 + (144 if at == 1 else 0), (k + 1) * 48 + (144 if at == 1 else 0))
+                    held[slot + at, :, k * 128 : (k + 1) * 128] = source[n, rows].astype(F32)
+            down = pl.ds(pl.multiple_of((block >> 2) * 48, 48), 48)
+            along = pl.ds(pl.multiple_of((block & 3) * 384, 384), 384)
+            rows = pl.ds(pl.multiple_of(block * 48, 48), 48)
+            pltpu.make_async_copy(held.at[slot], fc1_out.at[down, along], sems.at[slot]).start()
+            pltpu.make_async_copy(held.at[slot + 1], fc2_out.at[rows], sems.at[slot + 1]).start()
+            last = (block & 3) == 3
+
+            @pl.when(last)
+            def _():
+                pltpu.make_async_copy(held.at[slot + 2], proj_out.at[down], sems.at[slot + 2]).start()
+
+            @pl.when(jnp.logical_not(last))
+            def _():
+                pltpu.make_async_copy(held.at[slot + 2], qkv_out.at[down, along], sems.at[slot + 2]).start()
+
+
+def wait_blocks(outs, held, sems):
+    for slot in range(48):
+        pltpu.make_async_copy(held.at[slot], outs[3].at[pl.ds(0, 48)], sems.at[slot]).wait()
+
+
+def first_outputs(*refs):
+    pieces, outs, (held, sems) = refs[:4], refs[8:12], refs[12:]
+
+    @pl.when(lax.axis_index("pipe") == 0)
+    def _():
+        place_blocks(0, (pieces[0:2], pieces[2:4]), outs, held, sems)
+        wait_blocks(outs, held, sems)
+
+
+def last_outputs(*refs):
+    pieces, lows, outs, vec_outs = refs[:4], refs[4:6], refs[10:14], refs[14:24]
+    pre_out, post_out, bias_out, held, vec_held, tall_ref, sems = refs[24:]
+    first = lax.axis_index("pipe") == 0
+    width = outs[1].shape[0]
+
+    @pl.when(first)
+    def _():
+        place_blocks(8, (pieces[0:2], pieces[2:4]), outs, held, sems)
+
+    for half in range(2):
+        vec_held[half * 16 : half * 16 + 8] = lows[half][:, 144:160].astype(F32)
+        vec_held[half * 16 + 8 : half * 16 + 16] = pieces[2 + half][:, 144:160].astype(F32)
+    for block in range(32):
+        tall_ref[block * 4 : block * 4 + 4] = vec_held[block_position(block)][0:4]
+    rows = [
+        chosen(first, tall_ref[k * 16 : (k + 1) * 16], tall_ref[48 + k * 16 : 48 + (k + 1) * 16]) for k in range(3)
+    ]
+    rows = jnp.concatenate(rows, axis=1)
+    at = 0
+    for out in vec_outs:
+        for k in range(out.shape[1] // width):
+            out[:, k * width : (k + 1) * width] = rows[at : at + 1]
+            at += 1
+    pre_out[...] = tall_ref[96:104, 0:HEADS]
+    post_out[...] = tall_ref[104:112].T[0:HEADS]
+    bias_out[...] = tall_ref[112:113, 0:HEADS]
+
+    @pl.when(first)
+    def _():
+        wait_blocks(outs, held, sems)
 
 
 def class_gradients(*refs):
@@ -586,35 +652,11 @@
             copy.wait()
 
 
-def fc_outputs(mine_low, mine_high, other_low, other_high, fc1_in, fc2_in, fc1_out, fc2_out, mine, other, fc1, fc2, sems):
-    del fc1_in, fc2_in
-
-    @pl.when(lax.axis_index("pipe") == 0)
-    def _():
-        join_pieces(mine_low, mine_high, mine)
-        join_pieces(other_low, other_high, other)
-        copies = []
-        for rb in range(8):
-            for cb in range(4):
-                block = rb * 4 + cb
-                for k, piece in enumerate(unpack(mine, other, block, 0)):
-                    fc1[rb * 48 : (rb + 1) * 48, cb * 384 + k * 128 : cb * 384 + (k + 1) * 128] = piece
-                for k, piece in enumerate(unpack(mine, other, block, 144)):
-                    fc2[block * 48 : (block + 1) * 48, k * 128 : (k + 1) * 128] = piece
-            for n, (source, target, tall) in enumerate(((fc1, fc1_out, 48), (fc2, fc2_out, 192))):
-                rows = pl.ds(rb * tall, tall)
-                copies.append(pltpu.make_async_copy(source.at[rows], target.at[rows], sems.at[rb * 2 + n]))
-                copies[-1].start()
-        for copy in copies:
-            copy.wait()
-
-
 def join_factors(pieces, factors):
     at = 0
     for piece in pieces:
-        count, start = piece.shape[0], piece.shape[1] - 144
-        factors[at : at + count] = piece[:, start:]
-        at += count
+        factors[at : at + piece.shape[0]] = piece[...]
+        at += piece.shape[0]
 
 
 def factor_rows(factors, part, start, group):
@@ -628,55 +670,6 @@
     col = lax.broadcasted_iota(jnp.int32, (rows, cols), 1)
     wanted = (row >> 1) * 16 + kind * IMGS + (row & 1)
     return mm(jnp.where(col == wanted, 1.0, 0.0).astype(BF16), vectors).astype(BF16)
-
-
-def qkv_outputs(mine_low, mine_high, other_low, other_high, qkv_in, proj_in, *refs):
-    del qkv_in, proj_in
-    qkv_out, proj_out = refs[:2]
-    vec_outs, (pre_out, post_out, bias_out, mine, other, tall_ref, qkv, proj, sems) = refs[2:12], refs[12:]
-    first = lax.axis_index("pipe") == 0
-    width = proj_out.shape[0]
-    join_pieces(mine_low, mine_high, mine)
-    join_pieces(other_low, other_high, other)
-
-    @pl.when(first)
-    def _():
-        for rb in range(8):
-            rows = slice(rb * 48, (rb + 1) * 48)
-            for cb in range(4):
-                for k, piece in enumerate(unpack(mine, other, rb * 4 + cb, 0)):
-                    if cb < 3:
-                        qkv[rows, cb * 384 + k * 128 : cb * 384 + (k + 1) * 128] = piece
-                    else:
-                        proj[rows, k * 128 : (k + 1) * 128] = piece
-            rows = pl.ds(rb * 48, 48)
-            pltpu.make_async_copy(qkv.at[rows], qkv_out.at[rows], sems.at[rb]).start()
-            pltpu.make_async_copy(proj.at[rows], proj_out.at[rows], sems.at[8 + rb]).start()
-
-    for block in range(32):
-        at = block_position(block) & 15
-        here, there = mine[at, 144:160].astype(F32), other[at, 144:160].astype(F32)
-        low = chosen(first, here, there) if block < 16 else chosen(first, there, here)
-        tall_ref[block * 4 : block * 4 + 4] = low[0:4]
-    rows = [
-        chosen(first, tall_ref[k * 16 : (k + 1) * 16], tall_ref[48 + k * 16 : 48 + (k + 1) * 16]) for k in range(3)
-    ]
-    rows = jnp.concatenate(rows, axis=1)
-    at = 0
-    for out in vec_outs:
-        for k in range(out.shape[1] // width):
-            out[:, k * width : (k + 1) * width] = rows[at : at + 1]
-            at += 1
-    pre_out[...] = tall_ref[96:104, 0:HEADS]
-    post_out[...] = tall_ref[104:112].T[0:HEADS]
-    bias_out[...] = tall_ref[112:113, 0:HEADS]
-
-    @pl.when(first)
-    def _():
-        for rb in range(8):
-            rows = pl.ds(rb * 48, 48)
-            pltpu.make_async_copy(qkv.at[rows], qkv_out.at[rows], sems.at[rb]).wait()
-            pltpu.make_async_copy(proj.at[rows], proj_out.at[rows], sems.at[8 + rb]).wait()
 
 
 VM = pl.BlockSpec(memory_space=pltpu.VMEM)
@@ -703,15 +696,10 @@
     return lax.ppermute(array, "pipe", [(0, 1), (1, 0)])
 
 
-def core_pairs(dp, bits):
-    return [
-        (core * dp + i, core * dp + (i ^ bit)) for core, bit in enumerate(bits) for i in range(dp)
-    ]
-
-
-def exchanged(array, bits):
+def exchanged(array, bits, cores=(0, 1)):
     dp = lax.axis_size("dp")
-    return lax.ppermute(array, ("pipe", "dp"), core_pairs(dp, bits))
+    pairs = [(core * dp + i, core * dp + (i ^ bits[core])) for core in cores for i in range(dp)]
+    return lax.ppermute(array, ("pipe", "dp"), pairs)
 
 
 def total(pieces, start, stop):
@@ -726,7 +714,9 @@
 NEAR, FAR = (4, 4), (8, 8)
 LONG = (("halve", (1, 2)), ("halve", (2, 1)), ("halve", NEAR), ("swap", FAR), ("collect", NEAR), ("collect", (2, 1)), ("collect", (1, 2)))
 SHORT = (("halve", (1, 2)), ("halve", (2, 1)), ("swap", NEAR), ("swap", FAR), ("collect", (2, 1)), ("collect", (1, 2)))
-GATHER = (("collect", FAR), ("collect", NEAR), ("collect", (2, 1)), ("collect", (1, 2)))
+
+
+GATHER = (("gather", FAR), ("gather", NEAR), ("gather", (2, 1)), ("gather", (1, 2)))
 
 
 class Stream:
@@ -749,14 +739,15 @@
             self.pieces = [piece[: count // 2] for piece in self.pieces] + [exchanged(self.leaving, bits)]
         elif kind == "swap":
             run = 1 if bits == FAR else 2
-            starts = [at ^ run for at in range(0, count, run)]
-            self.leaving = jnp.concatenate([total(self.pieces, at, at + run) for at in starts], axis=0)
-            self.pieces = [total(self.pieces, 0, count), exchanged(self.leaving, bits)]
+            mid = total(self.pieces, 0, count)
+            self.leaving = jnp.concatenate([total(self.pieces, at ^ run, (at ^ run) + run) for at in range(0, count, run)])
+            got = exchanged(self.leaving, bits)
+            self.pieces = [mid, got]
             if self.steps[self.at][0] == "collect":
-                self.pieces = [total(self.pieces, 0, count)]
+                self.pieces = [total([mid, got[:count]], 0, count)]
         else:
             self.leaving = jnp.concatenate(self.pieces, axis=0) if len(self.pieces) > 1 else self.pieces[0]
-            self.pieces = [self.leaving, exchanged(self.leaving, bits)]
+            self.pieces = [self.leaving, exchanged(self.leaving, bits, (1,) if kind == "gather" else (0, 1))]
 
     def halves(self):
         if self.whole:
@@ -793,10 +784,10 @@
         sems=13,
     )
     vec_got = swapped(vec_own)
-    p_late, f1_late, f2_late = after((p_own, f1_own, f2_own), w_got)
-    p_got, f1_got, f2_got = swapped(p_late), swapped(f1_late), swapped(f2_late)
     mixing = jnp.stack([mix_pre, mix_post]).astype(F32)
     rows = jnp.pad(patches, ((0, 0), (0, length - count), (0, 0)))
+    p_late, f1_late, f2_late = after((p_own, f1_own, f2_own), w_got, vec_got, rows)
+    p_got, f1_got, f2_got = swapped(p_late), swapped(f1_late), swapped(f2_late)
 
     token_shape = (IMGS, length, width)
     wide_shape = (IMGS, lanes, width)
@@ -818,7 +809,7 @@
         [(VM, att), (VM, rows), (VM, keep_mask), (VM, class_token), (VM, class_cotangent), (VM, vec_own),
          (VM, vec_got), (HB, p_own), (HB, p_got), (HB, f1_own), (HB, f1_got), (HB, f2_own), (HB, f2_got), (HB, w_own),
          (HB, w_got)],
-        [((16, 288, 128), BF16), ((16, 288, 128), BF16), (token_shape, F32), (vec_shape, F32), (vec_shape, F32),
+        [((17, 288, 128), BF16), ((16, 288, 128), BF16), (token_shape, F32), (vec_shape, F32), (vec_shape, F32),
          ((16, half), BF16), ((16, half), BF16), ((144, 128), BF16)],
         [((width, width), BF16), ((width, hidden_width), BF16), ((hidden_width, width), BF16),
          ((width, width), BF16), ((width, hidden_width), BF16), ((hidden_width, width), BF16),
@@ -843,7 +834,8 @@
         )
 
     got1 = swapped(send1)
-    stream1, shared = Stream((kept1, got1), LONG), Stream((factors[None],), GATHER)
+    factors_got = got1[16, :144]
+    stream1, shared = Stream((kept1, got1), LONG), Stream((factors[None], factors_got[None]), GATHER)
     join0, sum0 = image_backward(0, mg)
     stream1.wait(join0)
     stream1.step()
@@ -860,6 +852,7 @@
         sems=1,
     )
     got2, half_got = swapped(send2), swapped(other_half)
+    stream2 = Stream((kept2, got2), SHORT)
     patch_out, class_result, class_grad = call(
         assemble,
         [(VM, own_half), (VM, half_got), (VM, class_own)],
@@ -874,20 +867,19 @@
             turn.last = stream.wait(*turn.last) or (stream.step(), stream.leaving)[1:]
 
     turn.last = (kept2,)
-    stream2 = Stream((kept2, got2), SHORT)
     turn(stream1, stream2)
-    stream1.wait(half_got)
-    turn(stream1, stream2, shared, stream1, stream2, shared, stream1, stream2, shared, stream1, shared, stream2, stream1)
-    stream2.wait(patch_out, class_result, class_grad)
+    turn.last += (half_got,)
+    turn(shared, stream1, stream2, shared, stream1, stream2, shared, shared, stream1, stream2, stream1)
+    turn.last += tuple(shared.pieces)
     turn(stream2)
+    turn.last += (patch_out, class_result, class_grad)
+    turn(stream1, stream2)
     if dp == 16:
         factor_parts = after(tuple(shared.pieces), stream2.leaving)
     else:
-        factor_parts = (lax.all_gather(factors, "dp"),)
-    factor_parts += tuple(swapped(part) for part in factor_parts)
-    low1, high1 = stream1.halves()
+        factor_parts = tuple(lax.all_gather(part, "dp") for part in (factors, factors_got))
     matrices = [((width, 3 * width), F32), ((width, width), F32), ((width, hidden_width), F32), ((hidden_width, width), F32)]
-    qkv1, proj1, fc11, fc21 = call(
+    outs = call(
         class_gradients,
         [(VM, part) for part in factor_parts]
         + [(HB, w_own), (HB, p_own), (HB, f1_own), (HB, f2_own), (VM, vec_own)],
@@ -898,35 +890,35 @@
         sems=10,
         far=4,
     )
-    low1_other, high1 = swapped(low1), after(high1, fc11)
-    high1_other = swapped(high1)
-    low2, high2 = stream2.halves()
-    low2_other = swapped(low2)
-    fc1_out, fc2_out = call(
-        fc_outputs,
-        [(VM, low1), (VM, high1), (VM, low1_other), (VM, high1_other), (HB, fc11), (HB, fc21)],
-        matrices[2:],
-        [((16, 288, 128), BF16), ((16, 288, 128), BF16)] + matrices[2:],
-        "fc_outputs",
+    (low1, high1), (low2, high2) = stream1.halves(), stream2.halves()
+    low1_other, low2_other = swapped(low1), swapped(low2)
+    held_blocks = ((48, 48, width), F32)
+    outs = call(
+        first_outputs,
+        [(VM, low1), (VM, low1_other), (VM, low2), (VM, low2_other)] + [(HB, out) for out in outs],
+        matrices,
+        [held_blocks],
+        "first_outputs",
         LIMIT_D,
-        sems=16,
-        far=2,
-        aliases={4: 0, 5: 1},
-    )
-    high2 = after(high2, fc1_out)
-    high2_other = swapped(high2)
-    qkv_out, proj_out, *small_outs = call(
-        qkv_outputs,
-        [(VM, low2), (VM, high2), (VM, low2_other), (VM, high2_other), (HB, qkv1), (HB, proj1)],
-        matrices[:2]
+        sems=48,
+        far=4,
+        aliases={4 + n: n for n in range(4)},
+    )
+    high1, high2 = after((high1, high2), outs[0])
+    high1_other, high2_other = swapped(high1), swapped(high2)
+    qkv_out, proj_out, fc1_out, fc2_out, *small_outs = call(
+        last_outputs,
+        [(VM, high1), (VM, high1_other), (VM, high2), (VM, high2_other), (VM, low2), (VM, low2_other)]
+        + [(HB, out) for out in outs],
+        matrices
         + [((1, size * width), F32) for size in (1, 1, 2, 1, 1, 1, 1, 4, 1, 1)]
         + [((HEADS, HEADS), F32), ((HEADS, HEADS), F32), ((1, HEADS), F32)],
-        [((16, 160, 128), BF16), ((16, 160, 128), BF16), ((128, 128), F32)] + matrices[:2],
-        "qkv_outputs",
+        [held_blocks, ((32, 16, 128), F32), ((128, 128), F32)],
+        "last_outputs",
         LIMIT_D,
-        sems=16,
-        far=2,
-        aliases={4: 0, 5: 1},
+        sems=48,
+        far=4,
+        aliases={6 + n: n for n in range(4)},
     )
     n1g, n1b, qvb, pb, sa, n2g, n2b, f1b, f2b, sm, pre, post, bias = small_outs
     return (

time: 107 us -> 97.9 us (0.915)
  starting transfers between devices: 35.1 us -> 25.7 us
  waiting for transfers between devices: 29.4 us -> 31.2 us
    ppermute x17, starting transfers between devices: 30.5 us -> 22.4 us  [exchanged(): return lax.ppermute(array, ('pipe', 'dp'), pairs)]
    ppermute x17, waiting for transfers between devices: 23.8 us -> 28.3 us  [exchanged(): return lax.ppermute(array, ('pipe', 'dp'), pairs)]
    ppermute x14 -> x12, waiting for transfers between devices: 5.66 us -> 2.94 us  [swapped(): return lax.ppermute(array, 'pipe', [(0, 1), (1, 0)])]
    ppermute x14 -> x12, starting transfers between devices: 4.56 us -> 3.34 us  [swapped(): return lax.ppermute(array, 'pipe', [(0, 1), (1, 0)])]
  transfers between devices with their start and end apart: 31 -> 29, of which waited for: 14 -> 10; matrix products, arithmetic and copies ran while one was open for 3% -> 3% of each run, Pallas kernels for 20% -> 21%
where the time goes in v3:
time: 97.9 us; the launch traced here: 97.6 us
  Pallas kernels  36.2 us (37%)
  waiting for transfers between devices  31.2 us (32%)
  starting transfers between devices  25.7 us (26%)
  local copies, waits for them, and re-layouts  1.93 us (2%)
  between operations  1.46 us (1%)
  other arithmetic  1.11 us (1%)
    pallas_call x10, Pallas kernels, call(): pl.pallas_call(body, out_shape=[jax.ShapeDtypeStruct(shape, kind) for sha...  36.2 us
    ppermute x17, waiting for transfers between devices, exchanged(): return lax.ppermute(array, ('pipe', 'dp'), pairs)  28.3 us
    ppermute x17, starting transfers between devices, exchanged(): return lax.ppermute(array, ('pipe', 'dp'), pairs)  22.4 us
    ppermute x12, starting transfers between devices, swapped(): return lax.ppermute(array, 'pipe', [(0, 1), (1, 0)])  3.34 us
    ppermute x12, waiting for transfers between devices, swapped(): return lax.ppermute(array, 'pipe', [(0, 1), (1, 0)])  2.94 us
  transfers between devices with their start and end apart: 29, of which 10 were waited for; matrix products, arithmetic and copies ran while one was open for 3% of the time, Pallas kernels for 21%

profile of v3, /device:TPU:0, one launch (start us, length us, event | category | flops | bytes accessed | tf_op | source)
XLA Modules:
  0.0 97.6 jit_solution(15556139595071888957)
XLA Ops:
  0.7 0.5 collective-permute-start.1
  1.2 1.7 %prepare.1 = (bf16[16,384]{1,0:T(8,128)(2,1)}, f32[8,384]{1,0:T(8,128)}, f32[8,384]{1,0:T(8,128)}, f32[1,384]{1,0:T(1,128)}) custom-call(bf16[1,384]{1,0:T(2,128)(2,1)} %refs_0_.1, bf16[1,384]{1,0:T(2,128)(2,1)} %refs_1_.1, bf16[1,768]{1,0:T(2,128)(2,1)} %refs_2_.3, bf16[1,384]{1,0:T(2,128)(2,1)} %refs_3_.1, bf16[1,384]{1,0:T(2,128)(2,1)} %refs_4_.1, ...), custom_call_target="tpu_custom_call" | custom-call | bytes 1 | tf_op jit(solution)/shard_map/prepare/pallas_call | solution.py:681
  2.9 0.0 copy-start
  2.9 0.0 copy-start.4
  3.0 0.2 collective-permute-start
  3.1 1.3 %copy.49 = bf16[4,196,384]{2,1,0:T(8,128)(2,1)S(1)} copy(bf16[4,196,384]{2,0,1:T(4,128)(2,1)} %param.21) | data formatting | bytes 1204224 | tf_op args[0]
  4.4 0.1 pad.4.rows_ref
  4.5 0.0 copy-start.2
  4.5 0.0 copy-start.10
  4.5 0.4 collective-permute-start.3
  4.9 0.2 collective-permute-start.4
  5.1 0.3 collective-permute-start.2
  5.5 4.3 %attention_forward.1 = (bf16[2,208,384]{2,1,0:T(8,128)(2,1)S(1)}, bf16[2,208,384]{2,1,0:T(8,128)(2,1)S(1)}, bf16[2,256,384]{2,1,0:T(8,128)(2,1)S(1)}, bf16[2,256...) custom-call(f32[2,8,8]{2,1,0:T(8,128)S(1)} %maximum_convert_fusion.mixing.refs_0_, ...), custom_call_target="tpu_custom_call" | custom-call | bytes 1 | tf_op jit(solution)/shard_map/attention_forward/pallas_call | solution.py:681
  9.8 13.2 %middle_kernel.1 = (bf16[17,288,128]{2,1,0:T(8,128)(2,1)S(1)}, bf16[16,288,128]{2,1,0:T(8,128)(2,1)S(1)}, f32[2,208,384]{2,1,0:T(8,128)S(1)}, f32[16,384]{1,0:T(...) custom-call(bf16[2,208,384]{2,1,0:T(8,128)(2,1)S(1)} %get-tuple-elem, ...), custom_call_target="tpu_custom_call" | custom-call | bytes 1 | tf_op jit(solution)/shard_map/middle_kernel/pallas_call | solution.py:681
  23.0 0.3 collective-permute-start.5
  23.4 3.6 %attention_backward_0.1 = (bf16[208,1152]{1,0:T(8,128)(2,1)S(1)}, f32[24,384]{1,0:T(8,128)S(1)}) custom-call(f32[2,8,8]{2,1,0:T(8,128)S(1)} %maximum_convert_fusion.mixing.refs_0_, f32[2,208,384]{2,1,0:T(8,128)S(1)} %get-tuple-element.144.refs_1_.mg_ref, s32[4,196]{1,0:T(4,128)S(1)} %copy-done.5, bf16[2,256,384]{2,1,0:T(8,128)(2,1)S(1)} %get-tuple-element.133.refs_3_, ...), custom_call_target="tpu_custom_call" | custom-call | bytes 1 | tf_op jit(solution)/shard_map/attention_backward_0/pallas_call | solution.py:681
  27.0 0.2 add_convert_fusion
  27.2 2.8 %collective-permute-start.7 = (bf16[8,288,128]{2,1,0:T(8,128)(2,1)S(1)}, bf16[8,288,128]{2,1,0:T(8,128)(2,1)S(1)}, u32[]{:S(2)}, u32[]{:S(2)}) collective-permute-start(bf16[8,288,128]{2,1,0:T(8,128)(2,1)S(1)} %add_convert_fusion), channel_id=1, source_target_pairs={{0,1},{1,0},{2,3},{3,2},{4,5},{5,4},{6,7},{7,6},{8,9},{9,8},{10,11... | collective-permute-start | bytes 1769480 | tf_op jit(solution)/shard_map/ppermute | solution.py:702
  30.0 3.9 %attention_backward_1.1 = (bf16[208,1152]{1,0:T(8,128)(2,1)S(1)}, f32[24,384]{1,0:T(8,128)S(1)}) custom-call(f32[2,8,8]{2,1,0:T(8,128)S(1)} %maximum_convert_fusion.mixing.refs_0_, f32[2,208,384]{2,1,0:T(8,128)S(1)} %get-tuple-element.144.refs_1_.mg_ref, s32[4,196]{1,0:T(4,128)S(1)} %copy-done.5, bf16[2,256,384]{2,1,0:T(8,128)(2,1)S(1)} %get-tuple-element.133.refs_3_, ...), custom_call_target="tpu_custom_call" | custom-call | bytes 1 | tf_op jit(solution)/shard_map/attention_backward_1/pallas_call | solution.py:681
  33.9 3.3 %input_gradients.1 = (bf16[16,160,128]{2,1,0:T(8,128)(2,1)S(1)}, bf16[16,160,128]{2,1,0:T(8,128)(2,1)S(1)}, f32[2,192,208]{2,1,0:T(8,128)S(1)}, bf16[2,208,208]{2,1,0:T(8,128)(2,1)S(1)}) custom-call(f32[2,208,384]{2,1,0:T(8,128)S(1)} %get-tuple-element.144.refs_1_.mg_ref, bf16[4,208,384]{2,1,0:T(8,128)(2,1)S(1)} %pad.4.rows_ref, ...), custom_call_target="tpu_custom_call" | custom-call | bytes 1 | tf_op jit(solution)/shard_map/input_gradients/pallas_call | solution.py:681
  37.1 0.1 collective-permute-start.9
  37.3 0.6 collective-permute-start.6
  38.0 0.1 add_convert_fusion.2
  38.1 2.1 %collective-permute-start.8 = (bf16[4,288,128]{2,1,0:T(8,128)(2,1)S(1)}, bf16[4,288,128]{2,1,0:T(8,128)(2,1)S(1)}, u32[]{:S(2)}, u32[]{:S(2)}) collective-permute-start(bf16[4,288,128]{2,1,0:T(8,128)(2,1)S(1)} %add_convert_fusion.2), channel_id=1, source_target_pairs={{0,2},{1,3},{2,0},{3,1},{4,6},{5,7},{6,4},{7,5},{8,10},{9,11},{10,... | collective-permute-start | bytes 884744 | tf_op jit(solution)/shard_map/ppermute | solution.py:702
  40.2 0.1 add_convert_fusion.1
  40.3 1.6 %collective-permute-start.12 = (bf16[8,160,128]{2,1,0:T(8,128)(2,1)S(1)}, bf16[8,160,128]{2,1,0:T(8,128)(2,1)S(1)}, u32[]{:S(2)}, u32[]{:S(2)}) collective-permute-start(bf16[8,160,128]{2,1,0:T(8,128)(2,1)S(1)} %add_convert_fusion.1), channel_id=1, source_target_pairs={{0,1},{1,0},{2,3},{3,2},{4,5},{5,4},{6,7},{7,6},{8,9},{9,8},{10,11... | collective-permute-start | bytes 983048 | tf_op jit(solution)/shard_map/ppermute | solution.py:702
  41.9 0.7 collective-permute-start.11
  42.6 5.0 %collective-permute-done.8 = bf16[4,288,128]{2,1,0:T(8,128)(2,1)S(1)} collective-permute-done((bf16[4,288,128]{2,1,0:T(8,128)(2,1)S(1)}, bf16[4,288,128]{2,1,0:T(8,128)(2,1)S(1)}, u32[]{:S(2)}, u32[]{:S(2)}) %collective-permute-start.8) | collective-permute-done | bytes 294944 | tf_op jit(solution)/shard_map/ppermute | solution.py:702
  47.6 0.1 add_convert_fusion.9
  47.7 2.6 %collective-permute-start.10 = (bf16[2,288,128]{2,1,0:T(8,128)(2,1)S(1)}, bf16[2,288,128]{2,1,0:T(8,128)(2,1)S(1)}, u32[]{:S(2)}, u32[]{:S(2)}) collective-permute-start(bf16[2,288,128]{2,1,0:T(8,128)(2,1)S(1)} %add_convert_fusion.9), channel_id=1, source_target_pairs={{0,4},{1,5},{2,6},{3,7},{4,0},{5,1},{6,2},{7,3},{8,12},{9,13},{10,... | collective-permute-start | bytes 442376 | tf_op jit(solution)/shard_map/ppermute | solution.py:702
  50.3 0.1 add_convert_fusion.6
  50.4 1.6 %collective-permute-start.15 = (bf16[4,160,128]{2,1,0:T(8,128)(2,1)S(1)}, bf16[4,160,128]{2,1,0:T(8,128)(2,1)S(1)}, u32[]{:S(2)}, u32[]{:S(2)}) collective-permute-start(bf16[4,160,128]{2,1,0:T(8,128)(2,1)S(1)} %add_convert_fusion.6), channel_id=1, source_target_pairs={{0,2},{1,3},{2,0},{3,1},{4,6},{5,7},{6,4},{7,5},{8,10},{9,11},{10,... | collective-permute-start | bytes 491528 | tf_op jit(solution)/shard_map/ppermute | solution.py:702
  52.0 0.7 collective-permute-start.14
  52.7 0.7 collective-permute-done.10
  53.4 0.1 add_convert_fusion.13
  53.5 3.1 %collective-permute-start.13 = (bf16[2,288,128]{2,1,0:T(8,128)(2,1)S(1)}, bf16[2,288,128]{2,1,0:T(8,128)(2,1)S(1)}, u32[]{:S(2)}, u32[]{:S(2)}) collective-permute-start(bf16[2,288,128]{2,1,0:T(8,128)(2,1)S(1)} %pad_maximum_fusion.2), channel_id=1, source_target_pairs={{0,8},{1,9},{2,10},{3,11},{4,12},{5,13},{6,14},{7,15},{8,0},{9,1},... | collective-permute-start | bytes 442376 | tf_op jit(solution)/shard_map/ppermute | solution.py:702
  56.6 0.1 add_convert_fusion.11
  56.8 0.7 collective-permute-start.16
  57.5 0.1 add_convert_fusion.5
  57.6 1.6 %collective-permute-start.18 = (bf16[4,160,128]{2,1,0:T(8,128)(2,1)S(1)}, bf16[4,160,128]{2,1,0:T(8,128)(2,1)S(1)}, u32[]{:S(2)}, u32[]{:S(2)}) collective-permute-start(bf16[4,160,128]{2,1,0:T(8,128)(2,1)S(1)} %pad_maximum_fusion), channel_id=1, source_target_pairs={{0,4},{1,5},{2,6},{3,7},{4,0},{5,1},{6,2},{7,3},{8,12},{9,13},{10,... | collective-permute-start | bytes 491528 | tf_op jit(solution)/shard_map/ppermute | solution.py:702
  59.2 4.2 %collective-permute-done.13 = bf16[2,288,128]{2,1,0:T(8,128)(2,1)S(1)} collective-permute-done((bf16[2,288,128]{2,1,0:T(8,128)(2,1)S(1)}, bf16[2,288,128]{2,1,0:T(8,128)(2,1)S(1)}, u32[]{:S(2)}, u32[]{:S(2)}) %collective-permute-start.13) | collective-permute-done | bytes 147488 | tf_op jit(solution)/shard_map/ppermute | solution.py:702
  63.4 0.1 add_convert_fusion.7
  63.6 0.7 collective-permute-start.21
  64.3 0.1 collective-permute-start.17
  64.4 1.9 %collective-permute-done.18 = bf16[4,160,128]{2,1,0:T(8,128)(2,1)S(1)} collective-permute-done((bf16[4,160,128]{2,1,0:T(8,128)(2,1)S(1)}, bf16[4,160,128]{2,1,0:T(8,128)(2,1)S(1)}, u32[]{:S(2)}, u32[]{:S(2)}) %collective-permute-start.18) | collective-permute-done | bytes 163872 | tf_op jit(solution)/shard_map/ppermute | solution.py:702
  66.4 1.2 %collective-permute-start.20 = (bf16[4,160,128]{2,1,0:T(8,128)(2,1)S(1)}, bf16[4,160,128]{2,1,0:T(8,128)(2,1)S(1)}, u32[]{:S(2)}, u32[]{:S(2)}) collective-permute-start(bf16[4,160,128]{2,1,0:T(8,128)(2,1)S(1)} %pad_maximum_fusion.1), channel_id=1, source_target_pairs={{0,8},{1,9},{2,10},{3,11},{4,12},{5,13},{6,14},{7,15},{8,0},{9,1},... | collective-permute-start | bytes 491528 | tf_op jit(solution)/shard_map/ppermute | solution.py:702
  67.6 2.2 %collective-permute-done.17 = bf16[2,288,128]{2,1,0:T(8,128)(2,1)S(1)} collective-permute-done((bf16[2,288,128]{2,1,0:T(8,128)(2,1)S(1)}, bf16[2,288,128]{2,1,0:T(8,128)(2,1)S(1)}, u32[]{:S(2)}, u32[]{:S(2)}) %collective-permute-start.17) | collective-permute-done | bytes 147488 | tf_op jit(solution)/shard_map/ppermute | solution.py:702
  69.9 0.2 collective-permute-start.19
  70.1 1.0 assemble.1
  71.0 6.3 %collective-permute-done.20 = bf16[4,160,128]{2,1,0:T(8,128)(2,1)S(1)} collective-permute-done((bf16[4,160,128]{2,1,0:T(8,128)(2,1)S(1)}, bf16[4,160,128]{2,1,0:T(8,128)(2,1)S(1)}, u32[]{:S(2)}, u32[]{:S(2)}) %collective-permute-start.20) | collective-permute-done | bytes 163872 | tf_op jit(solution)/shard_map/ppermute | solution.py:702
  77.3 0.1 add_convert_fusion.3
  77.4 0.8 collective-permute-start.23
  78.3 0.1 collective-permute-start.25
  78.4 1.3 %collective-permute-start.22 = (bf16[8,288,128]{2,1,0:T(8,128)(2,1)S(1)}, bf16[8,288,128]{2,1,0:T(8,128)(2,1)S(1)}, u32[]{:S(2)}, u32[]{:S(2)}) collective-permute-start(bf16[8,288,128]{2,1,0:T(8,128)(2,1)S(1)} %constant_dynamic-update-slice_fusion.10.refs_0_), channel_id=1, source_target_pairs={{0,1},{1,0},{2,3},{3,2},{4,5},{5,4},{6,7},{7,6},{8,9},{9,8},{10,11... | collective-permute-start | bytes 1769480 | tf_op jit(solution)/shard_map/ppermute | solution.py:702
  79.8 4.4 %collective-permute-done.23 = bf16[4,160,128]{2,1,0:T(8,128)(2,1)S(1)} collective-permute-done((bf16[4,160,128]{2,1,0:T(8,128)(2,1)S(1)}, bf16[4,160,128]{2,1,0:T(8,128)(2,1)S(1)}, u32[]{:S(2)}, u32[]{:S(2)}) %collective-permute-start.23) | collective-permute-done | bytes 163872 | tf_op jit(solution)/shard_map/ppermute | solution.py:702
  84.2 0.1 collective-permute-start.26
  84.3 0.7 collective-permute-start.24
  85.0 0.1 class_gradients.1
  85.1 0.8 collective-permute-done.26.refs_3_.refs_5_
  85.9 2.3 %first_outputs.1 = (f32[384,1152]{1,0:T(8,128)}, f32[384,384]{1,0:T(8,128)}, f32[384,1536]{1,0:T(8,128)}, f32[1536,384]{1,0:T(8,128)}) custom-call(bf16[8,288,128]{2,1,0:T(8,128)(2,1)S(1)} %constant_dynamic-update-slice_fusion.10.refs_0_, ...), custom_call_target="tpu_custom_call", output_to_operand_aliasing={{0}: (4, {}), {1}: (5, {}), {2}: (6, {}), {3}: (7, {})} | custom-call | bytes 1 | tf_op jit(solution)/shard_map/first_outputs/pallas_call | solution.py:681
  88.2 3.6 %collective-permute-done.24.refs_2_ = bf16[8,160,128]{2,1,0:T(8,128)(2,1)S(1)} collective-permute-done((bf16[8,160,128]{2,1,0:T(8,128)(2,1)S(1)}, bf16[8,160,128]{2,1,0:T(8,128)(2,1)S(1)}, u32[]{:S(2)}, u32[]{:S(2)}) %collective-permute-start.24) | collective-permute-done | bytes 327712 | tf_op jit(solution)/shard_map/ppermute | solution.py:702
  91.8 0.6 collective-permute-start.27
  92.4 2.1 %collective-permute-done.28.refs_3_ = bf16[8,160,128]{2,1,0:T(8,128)(2,1)S(1)} collective-permute-done((bf16[8,160,128]{2,1,0:T(8,128)(2,1)S(1)}, bf16[8,160,128]{2,1,0:T(8,128)(2,1)S(1)}, u32[]{:S(2)}, u32[]{:S(2)}) %collective-permute-start.28) | collective-permute-done | bytes 327712 | tf_op jit(solution)/shard_map/ppermute | solution.py:696
  94.5 2.9 %last_outputs.1 = (f32[384,1152]{1,0:T(8,128)}, f32[384,384]{1,0:T(8,128)}, f32[384,1536]{1,0:T(8,128)}, f32[1536,384]{1,0:T(8,128)}, f32[1,384]{1,0:T(1,128)}, ...) custom-call(bf16[8,288,128]{2,1,0:T(8,128)(2,1)S(1)} %collective-per, ...), custom_call_target="tpu_custom_call", output_to_operand_aliasing={{0}: (6, {}), {1}: (7, {}), {2}: (8, {}), {3}: (9, {})} | custom-call | bytes 1 | tf_op jit(solution)/shard_map/last_outputs/pallas_call | solution.py:681
  (76 shorter events, 0.8 us)
Async XLA Ops:
  0.7 3.9 %copy-start.1 = (bf16[1,384,1536]{2,1,0:T(8,128)(2,1)S(1)}, bf16[1,384,1536]{2,1,0:T(8,128)(2,1)}, u32[]{:S(2)}) copy-start(bf16[1,384,1536]{2,1,0:T(8,128)(2,1)} %param.37) | copy-start | bytes 3538948
  0.7 4.4 %copy-start.3 = (bf16[1,384,384]{2,1,0:T(8,128)(2,1)S(1)}, bf16[1,384,384]{2,1,0:T(8,128)(2,1)}, u32[]{:S(2)}) copy-start(bf16[1,384,384]{2,1,0:T(8,128)(2,1)} %param.32) | copy-start | bytes 884740
  0.7 3.8 %collective-permute-start.1 = (bf16[384,1152]{1,0:T(8,128)(2,1)}, bf16[384,1152]{1,0:T(8,128)(2,1)S(1)}, u32[]{:S(2)}, u32[]{:S(2)}) collective-permute-start(bf16[384,1152]{1,0:T(8,128)(2,1)} %bitcast.14), channel_id=1, source_target_pairs={{0,16},{16,0},{1,17},{17,1},{2,18},{18,2},{3,19},{19,3},{4,20},{20... | collective-permute-start | bytes 2654216 | tf_op jit(solution)/shard_map/ppermute | solution.py:696
  1.2 4.2 %copy-start.11 = (bf16[8,8]{1,0:T(8,128)(2,1)S(1)}, bf16[8,8]{1,0:T(8,128)(2,1)}, u32[]{:S(2)}) copy-start(bf16[8,8]{1,0:T(8,128)(2,1)} %refs_11_.1) | copy-start | bytes 388
  1.2 4.2 %copy-start.12 = (bf16[8,8]{1,0:T(8,128)(2,1)S(1)}, bf16[8,8]{1,0:T(8,128)(2,1)}, u32[]{:S(2)}) copy-start(bf16[8,8]{1,0:T(8,128)(2,1)} %refs_10_.1) | copy-start | bytes 388
  2.9 2.5 %copy-start = (bf16[1,384,1152]{2,1,0:T(8,128)(2,1)S(1)}, bf16[1,384,1152]{2,1,0:T(8,128)(2,1)}, u32[]{:S(2)}) copy-start(bf16[1,384,1152]{2,1,0:T(8,128)(2,1)} %param.27) | copy-start | bytes 2654212
  2.9 2.5 %copy-start.4 = (bf16[16,384]{1,0:T(8,128)(2,1)S(1)}, bf16[16,384]{1,0:T(8,128)(2,1)}, u32[]{:S(2)}) copy-start(bf16[16,384]{1,0:T(8,128)(2,1)} %get-tuple-element.124.vec_own.refs_7_.refs_6_) | copy-start | bytes 36868
  2.9 2.5 %copy-start.5 = (s32[4,196]{1,0:T(4,128)S(1)}, s32[4,196]{1,0:T(4,128)}, u32[]{:S(2)}) copy-start(s32[4,196]{1,0:T(4,128)} %refs_2_.5) | copy-start | bytes 9412
  3.0 2.5 %copy-start.8 = (f32[1,384]{1,0:T(1,128)S(1)}, f32[1,384]{1,0:T(1,128)}, u32[]{:S(2)}) copy-start(f32[1,384]{1,0:T(1,128)} %get-tuple-element.125.bias_ref.refs_11_) | copy-start | bytes 4612
  3.0 1.5 %collective-permute-start = (bf16[16,384]{1,0:T(8,128)(2,1)}, bf16[16,384]{1,0:T(8,128)(2,1)S(1)}, u32[]{:S(2)}, u32[]{:S(2)}) collective-permute-start(bf16[16,384]{1,0:T(8,128)(2,1)} %get-tuple-element.124.vec_own.refs_7_.refs_6_), channel_id=1, source_target_pairs={{0,16},{16,0},{1,17},{17,1},{2,18},{18,2},{3,19},{19,3},{4,20},{20... | collective-permute-start | bytes 36872 | tf_op jit(solution)/shard_map/ppermute | solution.py:696
  4.5 5.3 %copy-start.2 = (bf16[1,1536,384]{2,1,0:T(8,128)(2,1)S(1)}, bf16[1,1536,384]{2,1,0:T(8,128)(2,1)}, u32[]{:S(2)}) copy-start(bf16[1,1536,384]{2,1,0:T(8,128)(2,1)} %param.39) | copy-start | bytes 3538948
  4.5 5.3 %copy-start.9 = (bf16[4,384]{1,0:T(4,128)(2,1)S(1)}, bf16[4,384]{1,0:T(4,128)(2,1)}, u32[]{:S(2)}) copy-start(bf16[4,384]{1,0:T(4,128)(2,1)} %class_ref.1) | copy-start | bytes 9220
  4.5 5.3 %copy-start.10 = (bf16[4,384]{1,0:T(4,128)(2,1)S(1)}, bf16[4,384]{1,0:T(4,128)(2,1)}, u32[]{:S(2)}) copy-start(bf16[4,384]{1,0:T(4,128)(2,1)} %cot_ref.1) | copy-start | bytes 9220
  4.5 5.2 %collective-permute-start.3 = (bf16[384,1536]{1,0:T(8,128)(2,1)S(1)}, bf16[384,1536]{1,0:T(8,128)(2,1)S(1)}, u32[]{:S(2)}, u32[]{:S(2)}) collective-permute-start(bf16[384,1536]{1,0:T(8,128)(2,1)S(1)} %bitcast.19), channel_id=1, source_target_pairs={{0,16},{16,0},{1,17},{17,1},{2,18},{18,2},{3,19},{19,3},{4,20},{20... | collective-permute-start | bytes 3538952 | tf_op jit(solution)/shard_map/ppermute | solution.py:696
  4.9 4.9 %collective-permute-start.4 = (bf16[1536,384]{1,0:T(8,128)(2,1)}, bf16[1536,384]{1,0:T(8,128)(2,1)S(1)}, u32[]{:S(2)}, u32[]{:S(2)}) collective-permute-start(bf16[1536,384]{1,0:T(8,128)(2,1)} %bitcast.22), channel_id=1, source_target_pairs={{0,16},{16,0},{1,17},{17,1},{2,18},{18,2},{3,19},{19,3},{4,20},{20... | collective-permute-start | bytes 3538952 | tf_op jit(solution)/shard_map/ppermute | solution.py:696
  5.1 4.6 %collective-permute-start.2 = (bf16[384,384]{1,0:T(8,128)(2,1)S(1)}, bf16[384,384]{1,0:T(8,128)(2,1)S(1)}, u32[]{:S(2)}, u32[]{:S(2)}) collective-permute-start(bf16[384,384]{1,0:T(8,128)(2,1)S(1)} %bitcast.25), channel_id=1, source_target_pairs={{0,16},{16,0},{1,17},{17,1},{2,18},{18,2},{3,19},{19,3},{4,20},{20... | collective-permute-start | bytes 884744 | tf_op jit(solution)/shard_map/ppermute | solution.py:696
  9.8 13.6 %copy-start.6 = (f32[8,384]{1,0:T(8,128)S(1)}, f32[8,384]{1,0:T(8,128)}, u32[]{:S(2)}) copy-start(f32[8,384]{1,0:T(8,128)} %get-tuple-element.137.refs_12_) | copy-start | bytes 36868
  9.8 13.6 %copy-start.7 = (f32[8,384]{1,0:T(8,128)S(1)}, f32[8,384]{1,0:T(8,128)}, u32[]{:S(2)}) copy-start(f32[8,384]{1,0:T(8,128)} %get-tuple-element.138.refs_13_) | copy-start | bytes 36868
  23.0 4.0 %collective-permute-start.5 = (bf16[17,288,128]{2,1,0:T(8,128)(2,1)S(1)}, bf16[17,288,128]{2,1,0:T(8,128)(2,1)S(1)}, u32[]{:S(2)}, u32[]{:S(2)}) collective-permute-start(bf16[17,288,128]{2,1,0:T(8,128)(2,1)S(1)} %get-tuple-element.132), channel_id=1, source_target_pairs={{0,16},{16,0},{1,17},{17,1},{2,18},{18,2},{3,19},{19,3},{4,20},{20... | collective-permute-start | bytes 3760136 | tf_op jit(solution)/shard_map/ppermute | solution.py:696
  27.2 10.7 %collective-permute-start.7 = (bf16[8,288,128]{2,1,0:T(8,128)(2,1)S(1)}, bf16[8,288,128]{2,1,0:T(8,128)(2,1)S(1)}, u32[]{:S(2)}, u32[]{:S(2)}) collective-permute-start(bf16[8,288,128]{2,1,0:T(8,128)(2,1)S(1)} %add_convert_fusion), channel_id=1, source_target_pairs={{0,1},{1,0},{2,3},{3,2},{4,5},{5,4},{6,7},{7,6},{8,9},{9,8},{10,11... | collective-permute-start | bytes 1769480 | tf_op jit(solution)/shard_map/ppermute | solution.py:702
  37.1 3.0 %collective-permute-start.9 = (bf16[16,160,128]{2,1,0:T(8,128)(2,1)S(1)}, bf16[16,160,128]{2,1,0:T(8,128)(2,1)S(1)}, u32[]{:S(2)}, u32[]{:S(2)}) collective-permute-start(bf16[16,160,128]{2,1,0:T(8,128)(2,1)S(1)} %get-tuple-element.162), channel_id=1, source_target_pairs={{0,16},{16,0},{1,17},{17,1},{2,18},{18,2},{3,19},{19,3},{4,20},{20... | collective-permute-start | bytes 1966088 | tf_op jit(solution)/shard_map/ppermute | solution.py:696
  37.3 4.6 %collective-permute-start.6 = (bf16[2,208,208]{2,1,0:T(8,128)(2,1)S(1)}, bf16[2,208,208]{2,1,0:T(8,128)(2,1)S(1)}, u32[]{:S(2)}, u32[]{:S(2)}) collective-permute-start(bf16[2,208,208]{2,1,0:T(8,128)(2,1)S(1)} %get-tuple-element.152), channel_id=1, source_target_pairs={{0,16},{16,0},{1,17},{17,1},{2,18},{18,2},{3,19},{19,3},{4,20},{20... | collective-permute-start | bytes 519176 | tf_op jit(solution)/shard_map/ppermute | solution.py:696
  38.1 9.5 %collective-permute-start.8 = (bf16[4,288,128]{2,1,0:T(8,128)(2,1)S(1)}, bf16[4,288,128]{2,1,0:T(8,128)(2,1)S(1)}, u32[]{:S(2)}, u32[]{:S(2)}) collective-permute-start(bf16[4,288,128]{2,1,0:T(8,128)(2,1)S(1)} %add_convert_fusion.2), channel_id=1, source_target_pairs={{0,2},{1,3},{2,0},{3,1},{4,6},{5,7},{6,4},{7,5},{8,10},{9,11},{10,... | collective-permute-start | bytes 884744 | tf_op jit(solution)/shard_map/ppermute | solution.py:702
  40.3 10.0 %collective-permute-start.12 = (bf16[8,160,128]{2,1,0:T(8,128)(2,1)S(1)}, bf16[8,160,128]{2,1,0:T(8,128)(2,1)S(1)}, u32[]{:S(2)}, u32[]{:S(2)}) collective-permute-start(bf16[8,160,128]{2,1,0:T(8,128)(2,1)S(1)} %add_convert_fusion.1), channel_id=1, source_target_pairs={{0,1},{1,0},{2,3},{3,2},{4,5},{5,4},{6,7},{7,6},{8,9},{9,8},{10,11... | collective-permute-start | bytes 983048 | tf_op jit(solution)/shard_map/ppermute | solution.py:702
  41.9 10.0 %collective-permute-start.11 = (bf16[2,144,128]{2,1,0:T(8,128)(2,1)S(1)}, bf16[2,144,128]{2,1,0:T(8,128)(2,1)S(1)}, u32[]{:S(2)}, u32[]{:S(2)}) collective-permute-start(bf16[2,144,128]{2,1,0:T(8,128)(2,1)S(1)} %constant_dynamic-update-slice_fusion), channel_id=1, source_target_pairs={{16,24},{17,25},{18,26},{19,27},{20,28},{21,29},{22,30},{23,31},{2... | collective-permute-start | bytes 221192 | tf_op jit(solution)/shard_map/ppermute | solution.py:702
  47.7 5.7 %collective-permute-start.10 = (bf16[2,288,128]{2,1,0:T(8,128)(2,1)S(1)}, bf16[2,288,128]{2,1,0:T(8,128)(2,1)S(1)}, u32[]{:S(2)}, u32[]{:S(2)}) collective-permute-start(bf16[2,288,128]{2,1,0:T(8,128)(2,1)S(1)} %add_convert_fusion.9), channel_id=1, source_target_pairs={{0,4},{1,5},{2,6},{3,7},{4,0},{5,1},{6,2},{7,3},{8,12},{9,13},{10,... | collective-permute-start | bytes 442376 | tf_op jit(solution)/shard_map/ppermute | solution.py:702
  50.4 6.3 %collective-permute-start.15 = (bf16[4,160,128]{2,1,0:T(8,128)(2,1)S(1)}, bf16[4,160,128]{2,1,0:T(8,128)(2,1)S(1)}, u32[]{:S(2)}, u32[]{:S(2)}) collective-permute-start(bf16[4,160,128]{2,1,0:T(8,128)(2,1)S(1)} %add_convert_fusion.6), channel_id=1, source_target_pairs={{0,2},{1,3},{2,0},{3,1},{4,6},{5,7},{6,4},{7,5},{8,10},{9,11},{10,... | collective-permute-start | bytes 491528 | tf_op jit(solution)/shard_map/ppermute | solution.py:702
  52.0 4.7 %collective-permute-start.14 = (bf16[4,144,128]{2,1,0:T(8,128)(2,1)S(1)}, bf16[4,144,128]{2,1,0:T(8,128)(2,1)S(1)}, u32[]{:S(2)}, u32[]{:S(2)}) collective-permute-start(bf16[4,144,128]{2,1,0:T(8,128)(2,1)S(1)} %constant_dynamic-update-slice_fusion.2), channel_id=1, source_target_pairs={{16,20},{17,21},{18,22},{19,23},{20,16},{21,17},{22,18},{23,19},{2... | collective-permute-start | bytes 442376 | tf_op jit(solution)/shard_map/ppermute | solution.py:702
  53.5 9.9 %collective-permute-start.13 = (bf16[2,288,128]{2,1,0:T(8,128)(2,1)S(1)}, bf16[2,288,128]{2,1,0:T(8,128)(2,1)S(1)}, u32[]{:S(2)}, u32[]{:S(2)}) collective-permute-start(bf16[2,288,128]{2,1,0:T(8,128)(2,1)S(1)} %pad_maximum_fusion.2), channel_id=1, source_target_pairs={{0,8},{1,9},{2,10},{3,11},{4,12},{5,13},{6,14},{7,15},{8,0},{9,1},... | collective-permute-start | bytes 442376 | tf_op jit(solution)/shard_map/ppermute | solution.py:702
  56.8 6.7 %collective-permute-start.16 = (bf16[8,144,128]{2,1,0:T(8,128)(2,1)S(1)}, bf16[8,144,128]{2,1,0:T(8,128)(2,1)S(1)}, u32[]{:S(2)}, u32[]{:S(2)}) collective-permute-start(bf16[8,144,128]{2,1,0:T(8,128)(2,1)S(1)} %constant_dynamic-update-slice_fusion.4), channel_id=1, source_target_pairs={{16,17},{17,16},{18,19},{19,18},{20,21},{21,20},{22,23},{23,22},{2... | collective-permute-start | bytes 884744 | tf_op jit(solution)/shard_map/ppermute | solution.py:702
  57.6 8.7 %collective-permute-start.18 = (bf16[4,160,128]{2,1,0:T(8,128)(2,1)S(1)}, bf16[4,160,128]{2,1,0:T(8,128)(2,1)S(1)}, u32[]{:S(2)}, u32[]{:S(2)}) collective-permute-start(bf16[4,160,128]{2,1,0:T(8,128)(2,1)S(1)} %pad_maximum_fusion), channel_id=1, source_target_pairs={{0,4},{1,5},{2,6},{3,7},{4,0},{5,1},{6,2},{7,3},{8,12},{9,13},{10,... | collective-permute-start | bytes 491528 | tf_op jit(solution)/shard_map/ppermute | solution.py:702
  63.6 13.7 %collective-permute-start.21 = (bf16[16,144,128]{2,1,0:T(8,128)(2,1)S(1)}, bf16[16,144,128]{2,1,0:T(8,128)(2,1)S(1)}, u32[]{:S(2)}, u32[]{:S(2)}) collective-permute-start(bf16[16,144,128]{2,1,0:T(8,128)(2,1)S(1)} %constant_dynamic-update-slice_fusion.6.refs_0_), channel_id=1, source_target_pairs={{16,18},{17,19},{18,16},{19,17},{20,22},{21,23},{22,20},{23,21},{2... | collective-permute-start | bytes 1769480 | tf_op jit(solution)/shard_map/ppermute | solution.py:702
  64.3 5.5 %collective-permute-start.17 = (bf16[2,288,128]{2,1,0:T(8,128)(2,1)S(1)}, bf16[2,288,128]{2,1,0:T(8,128)(2,1)S(1)}, u32[]{:S(2)}, u32[]{:S(2)}) collective-permute-start(bf16[2,288,128]{2,1,0:T(8,128)(2,1)S(1)} %add_convert_fusion.7), channel_id=1, source_target_pairs={{0,4},{1,5},{2,6},{3,7},{4,0},{5,1},{6,2},{7,3},{8,12},{9,13},{10,... | collective-permute-start | bytes 442376 | tf_op jit(solution)/shard_map/ppermute | solution.py:702
  66.4 10.9 %collective-permute-start.20 = (bf16[4,160,128]{2,1,0:T(8,128)(2,1)S(1)}, bf16[4,160,128]{2,1,0:T(8,128)(2,1)S(1)}, u32[]{:S(2)}, u32[]{:S(2)}) collective-permute-start(bf16[4,160,128]{2,1,0:T(8,128)(2,1)S(1)} %pad_maximum_fusion.1), channel_id=1, source_target_pairs={{0,8},{1,9},{2,10},{3,11},{4,12},{5,13},{6,14},{7,15},{8,0},{9,1},... | collective-permute-start | bytes 491528 | tf_op jit(solution)/shard_map/ppermute | solution.py:702
  69.9 8.3 %collective-permute-start.19 = (bf16[4,288,128]{2,1,0:T(8,128)(2,1)S(1)}, bf16[4,288,128]{2,1,0:T(8,128)(2,1)S(1)}, u32[]{:S(2)}, u32[]{:S(2)}) collective-permute-start(bf16[4,288,128]{2,1,0:T(8,128)(2,1)S(1)} %constant_dynamic-update-slice_fusion.8), channel_id=1, source_target_pairs={{0,2},{1,3},{2,0},{3,1},{4,6},{5,7},{6,4},{7,5},{8,10},{9,11},{10,... | collective-permute-start | bytes 884744 | tf_op jit(solution)/shard_map/ppermute | solution.py:702
  77.4 6.8 %collective-permute-start.23 = (bf16[4,160,128]{2,1,0:T(8,128)(2,1)S(1)}, bf16[4,160,128]{2,1,0:T(8,128)(2,1)S(1)}, u32[]{:S(2)}, u32[]{:S(2)}) collective-permute-start(bf16[4,160,128]{2,1,0:T(8,128)(2,1)S(1)} %add_convert_fusion.3), channel_id=1, source_target_pairs={{0,2},{1,3},{2,0},{3,1},{4,6},{5,7},{6,4},{7,5},{8,10},{9,11},{10,... | collective-permute-start | bytes 491528 | tf_op jit(solution)/shard_map/ppermute | solution.py:702
  78.3 7.6 %collective-permute-start.25 = (bf16[8,288,128]{2,1,0:T(8,128)(2,1)S(1)}, bf16[8,288,128]{2,1,0:T(8,128)(2,1)S(1)}, u32[]{:S(2)}, u32[]{:S(2)}) collective-permute-start(bf16[8,288,128]{2,1,0:T(8,128)(2,1)S(1)} %constant_dynamic-update-slice_fusion.10.refs_0_), channel_id=1, source_target_pairs={{0,16},{16,0},{1,17},{17,1},{2,18},{18,2},{3,19},{19,3},{4,20},{20... | collective-permute-start | bytes 1769480 | tf_op jit(solution)/shard_map/ppermute | solution.py:696
  78.4 13.4 %collective-permute-start.22 = (bf16[8,288,128]{2,1,0:T(8,128)(2,1)S(1)}, bf16[8,288,128]{2,1,0:T(8,128)(2,1)S(1)}, u32[]{:S(2)}, u32[]{:S(2)}) collective-permute-start(bf16[8,288,128]{2,1,0:T(8,128)(2,1)S(1)} %constant_dynamic-update-slice_fusion.10.refs_0_), channel_id=1, source_target_pairs={{0,1},{1,0},{2,3},{3,2},{4,5},{5,4},{6,7},{7,6},{8,9},{9,8},{10,11... | collective-permute-start | bytes 1769480 | tf_op jit(solution)/shard_map/ppermute | solution.py:702
  84.2 1.7 %collective-permute-start.26 = (bf16[8,160,128]{2,1,0:T(8,128)(2,1)S(1)}, bf16[8,160,128]{2,1,0:T(8,128)(2,1)S(1)}, u32[]{:S(2)}, u32[]{:S(2)}) collective-permute-start(bf16[8,160,128]{2,1,0:T(8,128)(2,1)S(1)} %constant_dynamic-update-slice_fusion.12.refs_2_.refs_4_), channel_id=1, source_target_pairs={{0,16},{16,0},{1,17},{17,1},{2,18},{18,2},{3,19},{19,3},{4,20},{20... | collective-permute-start | bytes 983048 | tf_op jit(solution)/shard_map/ppermute | solution.py:696
  84.3 7.6 %collective-permute-start.24 = (bf16[8,160,128]{2,1,0:T(8,128)(2,1)S(1)}, bf16[8,160,128]{2,1,0:T(8,128)(2,1)S(1)}, u32[]{:S(2)}, u32[]{:S(2)}) collective-permute-start(bf16[8,160,128]{2,1,0:T(8,128)(2,1)S(1)} %constant_dynamic-update-slice_fusion.12.refs_2_.refs_4_), channel_id=1, source_target_pairs={{0,1},{1,0},{2,3},{3,2},{4,5},{5,4},{6,7},{7,6},{8,9},{9,8},{10,11... | collective-permute-start | bytes 983048 | tf_op jit(solution)/shard_map/ppermute | solution.py:702
  91.8 2.7 %collective-permute-start.27 = (bf16[8,288,128]{2,1,0:T(8,128)(2,1)S(1)}, bf16[8,288,128]{2,1,0:T(8,128)(2,1)S(1)}, u32[]{:S(2)}, u32[]{:S(2)}) collective-permute-start(bf16[8,288,128]{2,1,0:T(8,128)(2,1)S(1)} %collective-permute-done.22.refs_0_), channel_id=1, source_target_pairs={{0,16},{16,0},{1,17},{17,1},{2,18},{18,2},{3,19},{19,3},{4,20},{20... | collective-permute-start | bytes 1769480 | tf_op jit(solution)/shard_map/ppermute | solution.py:696
  92.4 2.1 %collective-permute-start.28 = (bf16[8,160,128]{2,1,0:T(8,128)(2,1)S(1)}, bf16[8,160,128]{2,1,0:T(8,128)(2,1)S(1)}, u32[]{:S(2)}, u32[]{:S(2)}) collective-permute-start(bf16[8,160,128]{2,1,0:T(8,128)(2,1)S(1)} %collective-permute-done.24.refs_2_), channel_id=1, source_target_pairs={{0,16},{16,0},{1,17},{17,1},{2,18},{18,2},{3,19},{19,3},{4,20},{20... | collective-permute-start | bytes 983048 | tf_op jit(solution)/shard_map/ppermute | solution.py:696

commit v4 on v3

--- a/solution.py
+++ b/solution.py
@@ -215,9 +215,9 @@
 ):
     first = lax.axis_index("pipe") == 0
     p0_copy = fetch(first, p_own, p_got, p0_ref, sems.at[0])
+    w1_copy = fetch(first, w_got, w_own, w1_ref, sems.at[3])
     f10_copy = fetch(first, f1_own, f1_got, f10, sems.at[1])
     f20_copy = fetch(first, f2_own, f2_got, f20, sems.at[2])
-    w1_copy = fetch(first, w_got, w_own, w1_ref, sems.at[3])
     p1_copy = fetch(first, p_got, p_own, p1_ref, sems.at[4])
     f11_copy = fetch(first, f1_got, f1_own, f11, sems.at[5])
     f21_copy = fetch(first, f2_got, f2_own, f21, sems.at[6])
@@ -237,15 +237,36 @@
     def wide_bias(v):
         return jnp.concatenate([v[8 + k : 9 + k] for k in range(4)], axis=1)
 
+    blank = jnp.zeros((8 - IMGS, width), F32)
+    class_rows = jnp.concatenate([own_images(first, class_ref[...].astype(F32)), blank], axis=0)
+    w1_copy.wait()
+    normal_c, _ = normed(class_rows)
+    hidden_c = (normal_c * vec1[0:1] + vec1[1:2]).astype(BF16)
+    query = (mm(hidden_c, w1_ref[:, :width]) + vec1[2:3]).astype(BF16).astype(F32)
+    mask = head_mask(IMGS * HEADS, width)
+
+    def spread(rows):
+        both = jnp.concatenate(
+            [jnp.broadcast_to(rows[b : b + 1], (HEADS, width)) for b in range(IMGS)], axis=0
+        )
+        return jnp.where(mask, both, 0.0)
+
+    def gathered(rows):
+        kept = jnp.where(mask, rows, 0.0)
+        parts = [col_sum(kept[b * HEADS : (b + 1) * HEADS]) for b in range(IMGS)]
+        return jnp.concatenate(parts + [jnp.zeros((8 - IMGS, width), F32)], axis=0)
+
+    query_rows = mm_nt(spread(query).astype(BF16), w1_ref[:, width : 2 * width]).astype(BF16)
+
     p0_copy.wait()
     branch = mm(att_ref[...].reshape(flat, width), p0_ref[...]) + vec[4:5]
     middle = token_rows(rows_ref).astype(F32) + vec[5:6] * branch
     normal, norm_scale = normed(middle)
     inner_low = (normal * vec[6:7] + vec[7:8]).astype(BF16)
+    f10_copy.wait()
     bias = wide_bias(vec)
-    step = 384
-    f10_copy.wait()
-    for k in range(4):
+    step = f10.shape[1] // 2
+    for k in range(2):
         cut = slice(k * step, (k + 1) * step)
         inner = mm(inner_low, f10[:, cut]) + bias[:, cut]
         active, slope = gelu_pair(inner)
@@ -255,26 +276,10 @@
     outer = mm(act_ref[...], f20[...]) + vec[12:13]
     sent = (middle + vec[13:14] * outer).astype(BF16).astype(F32)
 
-    blank = jnp.zeros((8 - IMGS, width), F32)
-    class_rows = jnp.concatenate([own_images(first, class_ref[...].astype(F32)), blank], axis=0)
-    w1_copy.wait()
-    normal_c, _ = normed(class_rows)
-    hidden_c = (normal_c * vec1[0:1] + vec1[1:2]).astype(BF16)
-    query = (mm(hidden_c, w1_ref[:, :width]) + vec1[2:3]).astype(BF16).astype(F32)
-    mask = head_mask(IMGS * HEADS, width)
-
-    def spread(rows):
-        both = jnp.concatenate(
-            [jnp.broadcast_to(rows[b : b + 1], (HEADS, width)) for b in range(IMGS)], axis=0
-        )
-        return jnp.where(mask, both, 0.0)
-
-    def gathered(rows):
-        kept = jnp.where(mask, rows, 0.0)
-        parts = [col_sum(kept[b * HEADS : (b + 1) * HEADS]) for b in range(IMGS)]
-        return jnp.concatenate(parts + [jnp.zeros((8 - IMGS, width), F32)], axis=0)
-
-    query_rows = mm_nt(spread(query).astype(BF16), w1_ref[:, width : 2 * width]).astype(BF16)
+    upper1 = jnp.concatenate([own_images(first, cot_ref[...].astype(F32)), blank], axis=0)
+    og1 = (upper1 * vec1[13:14]).astype(BF16)
+    f21_copy.wait()
+    dact1 = mm_nt(og1, f21[...])
     at_row = lax.broadcasted_iota(jnp.int32, (length, width), 0)
     hiddens, normals, scales, probs, low_probs, sums, whs = [], [], [], [], [], [], []
     for b in range(IMGS):
@@ -302,14 +307,11 @@
     normal2, scale2 = normed(middle1)
     inner1 = (normal2 * vec1[6:7] + vec1[7:8]).astype(BF16)
     f11_copy.wait()
-    f21_copy.wait()
     active1, slope1 = gelu_pair(mm(inner1, f11[...]) + wide_bias(vec1))
     outer1 = mm(active1.astype(BF16), f21[...]) + vec1[12:13]
     class_result = middle1 + vec1[13:14] * outer1
 
-    upper1 = jnp.concatenate([own_images(first, cot_ref[...].astype(F32)), blank], axis=0)
-    og1 = (upper1 * vec1[13:14]).astype(BF16)
-    ig1 = (mm_nt(og1, f21[...]) * slope1).astype(BF16)
+    ig1 = (dact1 * slope1).astype(BF16)
     dh2 = mm_nt(ig1, f11[...])
     mg1 = upper1 + norm_back(normal2, scale2, dh2 * vec1[6:7])
     bg1 = (mg1 * vec1[5:6]).astype(BF16)
@@ -326,19 +328,29 @@
     g_rows = jnp.concatenate(gs, axis=0).astype(BF16)
     dq1 = gathered(mm(g_rows, w1_ref[:, width : 2 * width])).astype(BF16)
     dclass = mm_nt(dq1, w1_ref[:, :width])
-    uppers, class_grads = [], []
+    uppers, grads = [], []
     n1g, n1b = jnp.zeros((1, width), F32), jnp.zeros((1, width), F32)
     for b in range(IMGS):
         part = slice(b * HEADS, (b + 1) * HEADS)
         left = jnp.concatenate([low_grads[b], low_probs[b]], axis=0)
         right = jnp.concatenate([query_rows[part], value_rows[part]], axis=0)
         dh1 = mm_tn(left, right)
-        dh1 = jnp.where(at_row == patches, dh1 + dclass[b : b + 1], dh1)
+        grads.append(dh1)
         n1g = n1g + col_sum(dh1 * normals[b])
         n1b = n1b + col_sum(dh1)
         dtokens = norm_back(normals[b], scales[b], dh1 * vec1[0:1])
-        class_grads.append(dtokens[patches : patches + 1] + mg1[b : b + 1])
         uppers.append(jnp.where(at_row < patches, dtokens, 0.0).astype(BF16).astype(F32))
+
+    def class_row(arrays):
+        return jnp.concatenate([array[patches : patches + 1] for array in arrays], axis=0)
+
+    dclass = dclass[0:IMGS]
+    class_normal = class_row(normals)
+    n1g = n1g + col_sum(dclass * class_normal)
+    n1b = n1b + col_sum(dclass)
+    class_grads = [
+        mg1[0:IMGS] + norm_back(class_normal, class_row(scales), (class_row(grads) + dclass) * vec1[0:1])
+    ]
     upper = jnp.concatenate(uppers, axis=0)
     class_rows = jnp.concatenate([class_result] + class_grads + [blank], axis=0)
     low_half, high_half = class_rows[:, : width // 2], class_rows[:, width // 2 :]
@@ -373,11 +385,13 @@
     put_blocks(blocks, mm_tn(act_ref[...], og), 144, (1, 0))
     dh = jnp.zeros((flat, width), F32)
     fc1_sums = []
-    for k in range(4):
+    step = f10.shape[1] // 1
+    for k in range(1):
         cut = slice(k * step, (k + 1) * step)
         ig = (mm_nt(og, f20[cut, :]) * gp_ref[:, cut].astype(F32)).astype(BF16)
-        fc1_sums.append(col_sum(ig.astype(F32)))
-        put_blocks(blocks, mm_tn(inner_low, ig), 0, (4, k))
+        ig_sum = col_sum(ig.astype(F32))
+        fc1_sums += [ig_sum[:, at : at + width] for at in range(0, step, width)]
+        put_blocks(blocks, mm_tn(inner_low, ig), 0, (4, k * step // width))
         dh = dh + mm_nt(ig, f10[:, cut])
     mg = upper + norm_back(normal, norm_scale, dh * vec[6:7])
     mg_ref[...] = mg.reshape(IMGS, length, width)
@@ -450,7 +464,7 @@
 def input_gradients(
     mg_ref, rows_ref, hid_ref, att_ref, join0, join1, sum0, sum1, vec_in, vec_in1, vec_own, vec_got, w_own, w_got,
     class_other,
-    send_ref, kept_ref, own_half, other_half, w_ref, join_ref, blocks, tall_ref, sems,
+    send_ref, kept_ref, vec_part, own_half, other_half, w_ref, join_ref, blocks, sems,
 ):
     first = lax.axis_index("pipe") == 0
     w_copy = fetch(first, w_own, w_got, w_ref, sems.at[0])
@@ -465,8 +479,7 @@
     join_ref[:length] = join0[...]
     join_ref[length:] = join1[...]
     hidden = hid_ref[...].reshape(flat, width)
-    for k in range(3):
-        put_blocks(blocks, mm_tn(hidden, join_ref[:, k * width : (k + 1) * width]), 0, (4, k))
+    put_blocks(blocks, mm_tn(hidden, join_ref[...]), 0, (4, 0))
     w_copy.wait()
     dh = mm_nt(join_ref[...], w_ref[...])
     normal, norm_scale = normed(token_rows(rows_ref).astype(F32))
@@ -493,15 +506,14 @@
         sum0[...] + sum1[...], groups, (((1,), (0,)), ((), ())),
         preferred_element_type=F32, precision=lax.Precision.HIGHEST,
     )
-    tall_ref[...] = jnp.concatenate(
+    tall = jnp.concatenate(
         [vec0[:, k * 128 : (k + 1) * 128] for k in range(3)]
         + [vec_in1[:, k * 128 : (k + 1) * 128] for k in range(3)]
-        + [small, jnp.zeros((8, 128), F32)],
+        + [small, jnp.zeros((24, 128), F32)],
         axis=0,
     )
-    filler = jnp.zeros((12, 128), F32)
-    for n in range(32):
-        blocks[n, 144:160] = jnp.concatenate([tall_ref[n * 4 : n * 4 + 4], filler], axis=0).astype(BF16)
+    vec_part[0] = tall.astype(BF16)
+    send_ref[16] = tall.astype(BF16)
     block_copy(blocks, kept_ref, 0, 16)
     block_copy(blocks, send_ref, 16, 16)
 
@@ -520,78 +532,59 @@
         out[...] = rows.astype(BF16)
 
 
-def place_blocks(start, pieces, outs, held, sems):
-    qkv_out, proj_out, fc1_out, fc2_out = outs
-    for half in range(2):
-        for n in range(8):
-            block = position_block(half * 16 + start + n)
-            slot = (half * 8 + n) * 3
-            for at in range(3):
-                source = pieces[0 if at < 2 else 1][half]
-                for k in range(3):
-                    rows = slice(k * 48 + (144 if at == 1 else 0), (k + 1) * 48 + (144 if at == 1 else 0))
-                    held[slot + at, :, k * 128 : (k + 1) * 128] = source[n, rows].astype(F32)
-            down = pl.ds(pl.multiple_of((block >> 2) * 48, 48), 48)
-            along = pl.ds(pl.multiple_of((block & 3) * 384, 384), 384)
-            rows = pl.ds(pl.multiple_of(block * 48, 48), 48)
-            pltpu.make_async_copy(held.at[slot], fc1_out.at[down, along], sems.at[slot]).start()
-            pltpu.make_async_copy(held.at[slot + 1], fc2_out.at[rows], sems.at[slot + 1]).start()
-            last = (block & 3) == 3
-
-            @pl.when(last)
-            def _():
-                pltpu.make_async_copy(held.at[slot + 2], proj_out.at[down], sems.at[slot + 2]).start()
-
-            @pl.when(jnp.logical_not(last))
-            def _():
-                pltpu.make_async_copy(held.at[slot + 2], qkv_out.at[down, along], sems.at[slot + 2]).start()
-
-
-def wait_blocks(outs, held, sems):
-    for slot in range(48):
-        pltpu.make_async_copy(held.at[slot], outs[3].at[pl.ds(0, 48)], sems.at[slot]).wait()
-
-
-def first_outputs(*refs):
-    pieces, outs, (held, sems) = refs[:4], refs[8:12], refs[12:]
+def place_blocks(plan, *refs):
+    count = 2 * len(plan)
+    pieces, (qkv_out, proj_out, fc1_out, fc2_out), (held, sems) = refs[:count], refs[count + 4 : count + 8], refs[count + 8 :]
+
+    def put(at, source, n, first, target):
+        for k in range(3):
+            held[at, :, k * 128 : (k + 1) * 128] = source[n, first + k * 48 : first + (k + 1) * 48].astype(F32)
+        pltpu.make_async_copy(held.at[at], target, sems.at[at]).start()
 
     @pl.when(lax.axis_index("pipe") == 0)
     def _():
-        place_blocks(0, (pieces[0:2], pieces[2:4]), outs, held, sems)
-        wait_blocks(outs, held, sems)
-
-
-def last_outputs(*refs):
-    pieces, lows, outs, vec_outs = refs[:4], refs[4:6], refs[10:14], refs[14:24]
-    pre_out, post_out, bias_out, held, vec_held, tall_ref, sems = refs[24:]
+        slot = 0
+        for which, source in enumerate(pieces):
+            stream, start = plan[which // 2]
+            for n in range(source.shape[0]):
+                block = position_block((which % 2) * 16 + start + n)
+                down = pl.ds(pl.multiple_of((block >> 2) * 48, 48), 48)
+                along = pl.ds(pl.multiple_of((block & 3) * 384, 384), 384)
+                if stream == 0:
+                    put(slot, source, n, 0, fc1_out.at[down, along])
+                    put(slot + 1, source, n, 144, fc2_out.at[pl.ds(pl.multiple_of(block * 48, 48), 48)])
+                    slot += 2
+                else:
+                    last = (block & 3) == 3
+
+                    @pl.when(last)
+                    def _():
+                        put(slot, source, n, 0, proj_out.at[down])
+
+                    @pl.when(jnp.logical_not(last))
+                    def _():
+                        put(slot, source, n, 0, qkv_out.at[down, along])
+
+                    slot += 1
+        for at in range(slot):
+            pltpu.make_async_copy(held.at[at], fc2_out.at[pl.ds(0, 48)], sems.at[at]).wait()
+
+
+def vector_outputs(part, *refs):
+    vec_outs, (pre_out, post_out, bias_out) = refs[:10], refs[10:]
     first = lax.axis_index("pipe") == 0
-    width = outs[1].shape[0]
-
-    @pl.when(first)
-    def _():
-        place_blocks(8, (pieces[0:2], pieces[2:4]), outs, held, sems)
-
-    for half in range(2):
-        vec_held[half * 16 : half * 16 + 8] = lows[half][:, 144:160].astype(F32)
-        vec_held[half * 16 + 8 : half * 16 + 16] = pieces[2 + half][:, 144:160].astype(F32)
-    for block in range(32):
-        tall_ref[block * 4 : block * 4 + 4] = vec_held[block_position(block)][0:4]
-    rows = [
-        chosen(first, tall_ref[k * 16 : (k + 1) * 16], tall_ref[48 + k * 16 : 48 + (k + 1) * 16]) for k in range(3)
-    ]
+    width = vec_outs[0].shape[1]
+    tall = part[0].astype(F32)
+    rows = [chosen(first, tall[k * 16 : (k + 1) * 16], tall[48 + k * 16 : 48 + (k + 1) * 16]) for k in range(3)]
     rows = jnp.concatenate(rows, axis=1)
     at = 0
     for out in vec_outs:
         for k in range(out.shape[1] // width):
             out[:, k * width : (k + 1) * width] = rows[at : at + 1]
             at += 1
-    pre_out[...] = tall_ref[96:104, 0:HEADS]
-    post_out[...] = tall_ref[104:112].T[0:HEADS]
-    bias_out[...] = tall_ref[112:113, 0:HEADS]
-
-    @pl.when(first)
-    def _():
-        wait_blocks(outs, held, sems)
+    pre_out[...] = tall[96:104, 0:HEADS]
+    post_out[...] = tall[104:112].T[0:HEADS]
+    bias_out[...] = tall[112:113, 0:HEADS]
 
 
 def class_gradients(*refs):
@@ -712,48 +705,65 @@
 
 
 NEAR, FAR = (4, 4), (8, 8)
-LONG = (("halve", (1, 2)), ("halve", (2, 1)), ("halve", NEAR), ("swap", FAR), ("collect", NEAR), ("collect", (2, 1)), ("collect", (1, 2)))
+LONG = (("halve", (1, 2)), ("halve", (2, 1)), ("halve", NEAR), ("swap", FAR), ("collect", NEAR), ("pair", (2, 1)), ("last", (1, 2)))
 SHORT = (("halve", (1, 2)), ("halve", (2, 1)), ("swap", NEAR), ("swap", FAR), ("collect", (2, 1)), ("collect", (1, 2)))
-
-
 GATHER = (("gather", FAR), ("gather", NEAR), ("gather", (2, 1)), ("gather", (1, 2)))
 
 
 class Stream:
-    def __init__(self, pieces, steps):
-        self.pieces, self.steps, self.at = list(pieces), steps, 0
+    def __init__(self, pieces, steps, rider=None):
+        self.pieces, self.steps, self.rider, self.at = list(pieces), steps, rider, 0
         self.whole = lax.axis_size("dp") == 16
-        self.leaving = self.pieces[0]
+        self.leaving, self.count = self.pieces[0], 16 if steps is not GATHER else 1
 
     def wait(self, *others):
         self.pieces = list(after(tuple(self.pieces), *others))
+
+    def swap(self, message, bits):
+        count = message.shape[0]
+        self.leaving = message if self.rider is None else jnp.concatenate([message, self.rider])
+        got = exchanged(self.leaving, bits)
+        if self.rider is not None:
+            self.rider = total([self.rider, got[count:]], 0, 1)
+        return got
 
     def step(self):
         if not self.whole:
             return
         kind, bits = self.steps[self.at]
         self.at += 1
-        count = min(piece.shape[0] for piece in self.pieces)
+        count = self.count
         if kind == "halve":
-            self.leaving = total(self.pieces, count // 2, count)
-            self.pieces = [piece[: count // 2] for piece in self.pieces] + [exchanged(self.leaving, bits)]
+            got = self.swap(total(self.pieces, count // 2, count), bits)
+            self.pieces, self.count = self.pieces + [got], count // 2
         elif kind == "swap":
             run = 1 if bits == FAR else 2
             mid = total(self.pieces, 0, count)
-            self.leaving = jnp.concatenate([total(self.pieces, at ^ run, (at ^ run) + run) for at in range(0, count, run)])
-            got = exchanged(self.leaving, bits)
-            self.pieces = [mid, got]
-            if self.steps[self.at][0] == "collect":
-                self.pieces = [total([mid, got[:count]], 0, count)]
+            turned = [total(self.pieces, at ^ run, (at ^ run) + run) for at in range(0, count, run)]
+            self.pieces = [mid, self.swap(jnp.concatenate(turned), bits)]
+            if self.steps[self.at][0] in ("collect", "pair"):
+                self.pieces = [total(self.pieces, 0, count)]
+        elif kind == "last":
+            self.leaving = self.pieces[1]
+            self.pieces = self.pieces + [exchanged(self.leaving, bits)]
         else:
             self.leaving = jnp.concatenate(self.pieces, axis=0) if len(self.pieces) > 1 else self.pieces[0]
+            if kind == "pair":
+                later = self.steps[self.at][1]
+                self.pieces = [self.leaving, exchanged(self.leaving, bits), exchanged(self.leaving, later)]
+                return
             self.pieces = [self.leaving, exchanged(self.leaving, bits, (1,) if kind == "gather" else (0, 1))]
 
-    def halves(self):
+    def parts(self):
         if self.whole:
             return self.pieces
         whole = lax.psum(total(self.pieces, 0, 16).astype(F32), "dp").astype(BF16)
-        return whole[:8], whole[8:]
+        return [whole[at : at + 4] for at in range(0, 16, 4)]
+
+    def ridden(self):
+        if self.whole:
+            return self.rider
+        return lax.psum(self.rider.astype(F32), "dp").astype(BF16)
 
 
 def local(
@@ -841,38 +851,46 @@
     stream1.step()
     join1, sum1 = image_backward(1, after(mg, stream1.leaving))
     mg = after(mg, join1)
-    send2, kept2, own_half, other_half = call(
+    send2, kept2, vec_part, own_half, other_half = call(
         input_gradients,
         [(VM, mg), (VM, rows), (VM, hid), (VM, att), (VM, join0), (VM, join1), (VM, sum0), (VM, sum1), (VM, vec0),
          (VM, vec1), (VM, vec_own), (VM, vec_got), (HB, w_own), (HB, w_got), (VM, class_other)],
-        [((16, 160, 128), BF16), ((16, 160, 128), BF16), ((IMGS, half, length), F32), ((IMGS, half + 16, length), BF16)],
-        [((width, 3 * width), BF16), ((flat, 3 * width), BF16), ((32, 160, 128), BF16), ((128, 128), F32)],
+        [((17, 144, 128), BF16), ((16, 144, 128), BF16), ((1, 144, 128), BF16), ((IMGS, half, length), F32), ((IMGS, half + 16, length), BF16)],
+        [((width, 3 * width), BF16), ((flat, 3 * width), BF16), ((32, 144, 128), BF16)],
         "input_gradients",
         LIMIT_C,
         sems=1,
     )
     got2, half_got = swapped(send2), swapped(other_half)
-    stream2 = Stream((kept2, got2), SHORT)
+    stream2 = Stream((kept2, got2), SHORT, total([vec_part, got2[16:]], 0, 1))
+    def turn(*streams):
+        for stream in streams:
+            turn.last = stream.wait(*turn.last) or (stream.step(), stream.leaving)[1:]
+
+    turn.last = (kept2,)
+    turn(stream1, stream2)
+    turn.last += (half_got,)
+    turn(shared, stream1, stream2, shared, stream1, stream2, shared, shared, stream1, stream2, stream1)
     patch_out, class_result, class_grad = call(
         assemble,
-        [(VM, own_half), (VM, half_got), (VM, class_own)],
+        [(VM, part) for part in after((own_half, half_got, class_own), stream1.leaving)],
         [((2 * IMGS, half, count), F32), ((2 * IMGS, half), BF16), ((2 * IMGS, half), BF16)],
         [],
         "assemble",
         LIMIT_C,
     )
-
-    def turn(*streams):
-        for stream in streams:
-            turn.last = stream.wait(*turn.last) or (stream.step(), stream.leaving)[1:]
-
-    turn.last = (kept2,)
-    turn(stream1, stream2)
-    turn.last += (half_got,)
-    turn(shared, stream1, stream2, shared, stream1, stream2, shared, shared, stream1, stream2, stream1)
     turn.last += tuple(shared.pieces)
     turn(stream2)
-    turn.last += (patch_out, class_result, class_grad)
+    small_outs = call(
+        vector_outputs,
+        [(VM, stream2.ridden())],
+        [((1, size * width), F32) for size in (1, 1, 2, 1, 1, 1, 1, 4, 1, 1)]
+        + [((HEADS, HEADS), F32), ((HEADS, HEADS), F32), ((1, HEADS), F32)],
+        [],
+        "vector_outputs",
+        LIMIT_C,
+    )
+    turn.last += (patch_out, class_result, class_grad, small_outs)
     turn(stream1, stream2)
     if dp == 16:
         factor_parts = after(tuple(shared.pieces), stream2.leaving)
@@ -890,36 +908,31 @@
         sems=10,
         far=4,
     )
-    (low1, high1), (low2, high2) = stream1.halves(), stream2.halves()
-    low1_other, low2_other = swapped(low1), swapped(low2)
-    held_blocks = ((48, 48, width), F32)
-    outs = call(
-        first_outputs,
-        [(VM, low1), (VM, low1_other), (VM, low2), (VM, low2_other)] + [(HB, out) for out in outs],
-        matrices,
-        [held_blocks],
-        "first_outputs",
-        LIMIT_D,
-        sems=48,
-        far=4,
-        aliases={4 + n: n for n in range(4)},
-    )
-    high1, high2 = after((high1, high2), outs[0])
-    high1_other, high2_other = swapped(high1), swapped(high2)
-    qkv_out, proj_out, fc1_out, fc2_out, *small_outs = call(
-        last_outputs,
-        [(VM, high1), (VM, high1_other), (VM, high2), (VM, high2_other), (VM, low2), (VM, low2_other)]
-        + [(HB, out) for out in outs],
-        matrices
-        + [((1, size * width), F32) for size in (1, 1, 2, 1, 1, 1, 1, 4, 1, 1)]
-        + [((HEADS, HEADS), F32), ((HEADS, HEADS), F32), ((1, HEADS), F32)],
-        [held_blocks, ((32, 16, 128), F32), ((128, 128), F32)],
-        "last_outputs",
-        LIMIT_D,
-        sems=48,
-        far=4,
-        aliases={6 + n: n for n in range(4)},
-    )
+    parts = [], []
+    for at, stream in enumerate((stream1, stream2)):
+        start = 0
+        for part in stream.parts():
+            parts[at].append((at, start, part))
+            start += part.shape[0]
+    for name in ("first_outputs", "last_outputs"):
+        chosen_parts = [part for group in parts for part in group if (part[1] < 8 or part[2].shape[0] == 4 and part[1] < 12) == (name == "first_outputs")]
+        if name == "last_outputs":
+            chosen_parts = [(at, start, after(part, outs[0])) for at, start, part in chosen_parts]
+        plan = [(at, start) for at, start, _ in chosen_parts]
+        slots = sum(2 * part.shape[0] * (2 - at) for at, _, part in chosen_parts)
+        arrays = [(VM, array) for _, _, part in chosen_parts for array in (part, swapped(part))]
+        outs = call(
+            lambda *refs: place_blocks(plan, *refs),
+            arrays + [(HB, out) for out in outs],
+            matrices,
+            [((slots, 48, width), F32)],
+            name,
+            LIMIT_D,
+            sems=slots,
+            far=4,
+            aliases={len(arrays) + n: n for n in range(4)},
+        )
+    qkv_out, proj_out, fc1_out, fc2_out = outs
     n1g, n1b, qvb, pb, sa, n2g, n2b, f1b, f2b, sm, pre, post, bias = small_outs
     return (
         class_result, patch_out.transpose(0, 2, 1), class_grad, n1g, n1b, qkv_out[None], qvb, proj_out[None], pb, sa, n2g, n2b,

time: 97.9 us -> 96.4 us (0.985)
  starting transfers between devices: 25.7 us -> 29.9 us
  waiting for transfers between devices: 31.2 us -> 27.2 us
  Pallas kernels: 36.2 us -> 34.8 us
    ppermute x17 -> x18, waiting for transfers between devices: 28.3 us -> 25.5 us  [exchanged(): return lax.ppermute(array, ('pipe', 'dp'), pairs)]
    ppermute x17 -> x18, starting transfers between devices: 22.4 us -> 24.5 us  [exchanged(): return lax.ppermute(array, ('pipe', 'dp'), pairs)]
    ppermute x12 -> x14, starting transfers between devices: 3.34 us -> 5.39 us  [swapped(): return lax.ppermute(array, 'pipe', [(0, 1), (1, 0)])]
    pallas_call x10 -> x11, Pallas kernels: 36.2 us -> 34.8 us  [call(): pl.pallas_call(body, out_shape=[jax.ShapeDtypeStruct(shape, kind) for sha...]
    ppermute x12 -> x14, waiting for transfers between devices: 2.94 us -> 1.61 us  [swapped(): return lax.ppermute(array, 'pipe', [(0, 1), (1, 0)])]
  transfers between devices with their start and end apart: 29 -> 32, of which waited for: 10 -> 11; matrix products, arithmetic and copies ran while one was open for 3% -> 3% of each run, Pallas kernels for 21% -> 22%
where the time goes in v4:
time: 96.4 us; the launch traced here: 96.1 us
  Pallas kernels  34.8 us (36%)
  starting transfers between devices  29.9 us (31%)
  waiting for transfers between devices  27.2 us (28%)
  local copies, waits for them, and re-layouts  1.6 us (2%)
  between operations  1.42 us (1%)
  other arithmetic  1.24 us (1%)
    pallas_call x11, Pallas kernels, call(): pl.pallas_call(body, out_shape=[jax.ShapeDtypeStruct(shape, kind) for sha...  34.8 us
    ppermute x18, waiting for transfers between devices, exchanged(): return lax.ppermute(array, ('pipe', 'dp'), pairs)  25.5 us
    ppermute x18, starting transfers between devices, exchanged(): return lax.ppermute(array, ('pipe', 'dp'), pairs)  24.5 us
    ppermute x14, starting transfers between devices, swapped(): return lax.ppermute(array, 'pipe', [(0, 1), (1, 0)])  5.39 us
  transfers between devices with their start and end apart: 32, of which 11 were waited for; matrix products, arithmetic and copies ran while one was open for 3% of the time, Pallas kernels for 22%

profile of v4, /device:TPU:0, one launch (start us, length us, event | category | flops | bytes accessed | tf_op | source)
XLA Modules:
  0.0 96.1 jit_solution(1004277032719404178)
XLA Ops:
  0.7 0.5 collective-permute-start.1
  1.2 1.7 %prepare.1 = (bf16[16,384]{1,0:T(8,128)(2,1)}, f32[8,384]{1,0:T(8,128)}, f32[8,384]{1,0:T(8,128)}, f32[1,384]{1,0:T(1,128)}) custom-call(bf16[1,384]{1,0:T(2,128)(2,1)} %refs_0_.1, bf16[1,384]{1,0:T(2,128)(2,1)} %refs_1_.1, bf16[1,768]{1,0:T(2,128)(2,1)} %refs_2_.3, bf16[1,384]{1,0:T(2,128)(2,1)} %refs_3_.1, bf16[1,384]{1,0:T(2,128)(2,1)} %refs_4_.1, ...), custom_call_target="tpu_custom_call" | custom-call | bytes 1 | tf_op jit(solution)/shard_map/prepare/pallas_call | solution.py:674
  3.0 0.2 collective-permute-start
  3.1 1.3 %copy.49 = bf16[4,196,384]{2,1,0:T(8,128)(2,1)S(1)} copy(bf16[4,196,384]{2,0,1:T(4,128)(2,1)} %param.21) | data formatting | bytes 1204224 | tf_op args[0]
  4.4 0.1 pad.4.rows_ref
  4.5 0.4 collective-permute-start.3
  4.9 0.2 collective-permute-start.4
  5.1 0.3 collective-permute-start.2
  5.5 4.3 %attention_forward.1 = (bf16[2,208,384]{2,1,0:T(8,128)(2,1)S(1)}, bf16[2,208,384]{2,1,0:T(8,128)(2,1)S(1)}, bf16[2,256,384]{2,1,0:T(8,128)(2,1)S(1)}, bf16[2,256...) custom-call(f32[2,8,8]{2,1,0:T(8,128)S(1)} %maximum_convert_fusion.mixing.refs_0_, ...), custom_call_target="tpu_custom_call" | custom-call | bytes 1 | tf_op jit(solution)/shard_map/attention_forward/pallas_call | solution.py:674
  9.8 12.2 %middle_kernel.1 = (bf16[17,288,128]{2,1,0:T(8,128)(2,1)S(1)}, bf16[16,288,128]{2,1,0:T(8,128)(2,1)S(1)}, f32[2,208,384]{2,1,0:T(8,128)S(1)}, f32[16,384]{1,0:T(...) custom-call(bf16[2,208,384]{2,1,0:T(8,128)(2,1)S(1)} %get-tuple-elem, ...), custom_call_target="tpu_custom_call" | custom-call | bytes 1 | tf_op jit(solution)/shard_map/middle_kernel/pallas_call | solution.py:674
  22.0 0.4 collective-permute-start.5
  22.4 3.8 %attention_backward_0.1 = (bf16[208,1152]{1,0:T(8,128)(2,1)S(1)}, f32[24,384]{1,0:T(8,128)S(1)}) custom-call(f32[2,8,8]{2,1,0:T(8,128)S(1)} %maximum_convert_fusion.mixing.refs_0_, f32[2,208,384]{2,1,0:T(8,128)S(1)} %get-tuple-element.149.refs_1_.mg_ref, s32[4,196]{1,0:T(4,128)S(1)} %copy-done.5, bf16[2,256,384]{2,1,0:T(8,128)(2,1)S(1)} %get-tuple-element.138.refs_3_, ...), custom_call_target="tpu_custom_call" | custom-call | bytes 1 | tf_op jit(solution)/shard_map/attention_backward_0/pallas_call | solution.py:674
  26.2 0.2 add_convert_fusion
  26.4 2.8 %collective-permute-start.7 = (bf16[8,288,128]{2,1,0:T(8,128)(2,1)S(1)}, bf16[8,288,128]{2,1,0:T(8,128)(2,1)S(1)}, u32[]{:S(2)}, u32[]{:S(2)}) collective-permute-start(bf16[8,288,128]{2,1,0:T(8,128)(2,1)S(1)} %add_convert_fusion), channel_id=1, source_target_pairs={{0,1},{1,0},{2,3},{3,2},{4,5},{5,4},{6,7},{7,6},{8,9},{9,8},{10,11... | collective-permute-start | bytes 1769480 | tf_op jit(solution)/shard_map/ppermute | solution.py:695
  29.2 3.7 %attention_backward_1.1 = (bf16[208,1152]{1,0:T(8,128)(2,1)S(1)}, f32[24,384]{1,0:T(8,128)S(1)}) custom-call(f32[2,8,8]{2,1,0:T(8,128)S(1)} %maximum_convert_fusion.mixing.refs_0_, f32[2,208,384]{2,1,0:T(8,128)S(1)} %get-tuple-element.149.refs_1_.mg_ref, s32[4,196]{1,0:T(4,128)S(1)} %copy-done.5, bf16[2,256,384]{2,1,0:T(8,128)(2,1)S(1)} %get-tuple-element.138.refs_3_, ...), custom_call_target="tpu_custom_call" | custom-call | bytes 1 | tf_op jit(solution)/shard_map/attention_backward_1/pallas_call | solution.py:674
  32.8 2.9 %input_gradients.1 = (bf16[17,144,128]{2,1,0:T(8,128)(2,1)S(1)}, bf16[16,144,128]{2,1,0:T(8,128)(2,1)S(1)}, bf16[1,144,128]{2,1,0:T(8,128)(2,1)S(1)}, f32[2,192,208]{2,1,0:T(8,128)S(1)}, bf16[2,208,208]{2,1,0:T(8,128)(2,1)S(1)}) custom-call(f32[2,208,384]{2,1,0:T(8,128)S(1)} %get-tuple-element.149.refs_1_.mg_ref, bf16[4,208,384]{2,1,0:T(8,128)(2,1)S(1)} %pad.4.rows_ref, ...), custom_call_target="tpu_custom_call" | custom-call | bytes 1 | tf_op jit(solution)/shard_map/input_gradients/pallas_call | solution.py:674
  35.8 0.1 collective-permute-start.9
  35.9 0.5 collective-permute-start.6
  36.4 0.7 collective-permute-done.7
  37.0 0.1 add_convert_fusion.2
  37.2 2.1 %collective-permute-start.8 = (bf16[4,288,128]{2,1,0:T(8,128)(2,1)S(1)}, bf16[4,288,128]{2,1,0:T(8,128)(2,1)S(1)}, u32[]{:S(2)}, u32[]{:S(2)}) collective-permute-start(bf16[4,288,128]{2,1,0:T(8,128)(2,1)S(1)} %add_convert_fusion.2), channel_id=1, source_target_pairs={{0,2},{1,3},{2,0},{3,1},{4,6},{5,7},{6,4},{7,5},{8,10},{9,11},{10,... | collective-permute-start | bytes 884744 | tf_op jit(solution)/shard_map/ppermute | solution.py:695
  39.3 0.1 add_convert_fusion.1
  39.4 1.6 %collective-permute-start.12 = (bf16[9,144,128]{2,1,0:T(8,128)(2,1)S(1)}, bf16[9,144,128]{2,1,0:T(8,128)(2,1)S(1)}, u32[]{:S(2)}, u32[]{:S(2)}) collective-permute-start(bf16[9,144,128]{2,1,0:T(8,128)(2,1)S(1)} %pad_maximum_fusion), channel_id=1, source_target_pairs={{0,1},{1,0},{2,3},{3,2},{4,5},{5,4},{6,7},{7,6},{8,9},{9,8},{10,11... | collective-permute-start | bytes 995336 | tf_op jit(solution)/shard_map/ppermute | solution.py:695
  41.0 0.7 collective-permute-start.11
  41.7 5.2 %collective-permute-done.8 = bf16[4,288,128]{2,1,0:T(8,128)(2,1)S(1)} collective-permute-done((bf16[4,288,128]{2,1,0:T(8,128)(2,1)S(1)}, bf16[4,288,128]{2,1,0:T(8,128)(2,1)S(1)}, u32[]{:S(2)}, u32[]{:S(2)}) %collective-permute-start.8) | collective-permute-done | bytes 294944 | tf_op jit(solution)/shard_map/ppermute | solution.py:695
  46.8 0.1 add_convert_fusion.9
  46.9 2.4 %collective-permute-start.10 = (bf16[2,288,128]{2,1,0:T(8,128)(2,1)S(1)}, bf16[2,288,128]{2,1,0:T(8,128)(2,1)S(1)}, u32[]{:S(2)}, u32[]{:S(2)}) collective-permute-start(bf16[2,288,128]{2,1,0:T(8,128)(2,1)S(1)} %add_convert_fusion.9), channel_id=1, source_target_pairs={{0,4},{1,5},{2,6},{3,7},{4,0},{5,1},{6,2},{7,3},{8,12},{9,13},{10,... | collective-permute-start | bytes 442376 | tf_op jit(solution)/shard_map/ppermute | solution.py:695
  49.4 0.1 add_convert_fusion.8
  49.5 1.6 %collective-permute-start.15 = (bf16[5,144,128]{2,1,0:T(8,128)(2,1)S(1)}, bf16[5,144,128]{2,1,0:T(8,128)(2,1)S(1)}, u32[]{:S(2)}, u32[]{:S(2)}) collective-permute-start(bf16[5,144,128]{2,1,0:T(8,128)(2,1)S(1)} %pad_maximum_fusion.1), channel_id=1, source_target_pairs={{0,2},{1,3},{2,0},{3,1},{4,6},{5,7},{6,4},{7,5},{8,10},{9,11},{10,... | collective-permute-start | bytes 552968 | tf_op jit(solution)/shard_map/ppermute | solution.py:695
  51.1 0.7 collective-permute-start.14
  51.8 0.7 collective-permute-done.10
  52.5 0.1 add_convert_fusion.13
  52.6 3.1 %collective-permute-start.13 = (bf16[2,288,128]{2,1,0:T(8,128)(2,1)S(1)}, bf16[2,288,128]{2,1,0:T(8,128)(2,1)S(1)}, u32[]{:S(2)}, u32[]{:S(2)}) collective-permute-start(bf16[2,288,128]{2,1,0:T(8,128)(2,1)S(1)} %pad_maximum_fusion.3), channel_id=1, source_target_pairs={{0,8},{1,9},{2,10},{3,11},{4,12},{5,13},{6,14},{7,15},{8,0},{9,1},... | collective-permute-start | bytes 442376 | tf_op jit(solution)/shard_map/ppermute | solution.py:695
  55.7 0.1 add_convert_fusion.11
  55.9 0.7 collective-permute-start.16
  56.6 0.1 add_convert_fusion.5
  56.7 1.6 %collective-permute-start.18 = (bf16[5,144,128]{2,1,0:T(8,128)(2,1)S(1)}, bf16[5,144,128]{2,1,0:T(8,128)(2,1)S(1)}, u32[]{:S(2)}, u32[]{:S(2)}) collective-permute-start(bf16[5,144,128]{2,1,0:T(8,128)(2,1)S(1)} %pad_maximum_fusion.2), channel_id=1, source_target_pairs={{0,4},{1,5},{2,6},{3,7},{4,0},{5,1},{6,2},{7,3},{8,12},{9,13},{10,... | collective-permute-start | bytes 552968 | tf_op jit(solution)/shard_map/ppermute | solution.py:695
  58.3 3.8 %collective-permute-done.13 = bf16[2,288,128]{2,1,0:T(8,128)(2,1)S(1)} collective-permute-done((bf16[2,288,128]{2,1,0:T(8,128)(2,1)S(1)}, bf16[2,288,128]{2,1,0:T(8,128)(2,1)S(1)}, u32[]{:S(2)}, u32[]{:S(2)}) %collective-permute-start.13) | collective-permute-done | bytes 147488 | tf_op jit(solution)/shard_map/ppermute | solution.py:695
  62.2 0.1 add_convert_fusion.6
  62.4 0.7 collective-permute-start.22
  63.1 0.1 collective-permute-start.17
  63.2 2.8 %collective-permute-done.18 = bf16[5,144,128]{2,1,0:T(8,128)(2,1)S(1)} collective-permute-done((bf16[5,144,128]{2,1,0:T(8,128)(2,1)S(1)}, bf16[5,144,128]{2,1,0:T(8,128)(2,1)S(1)}, u32[]{:S(2)}, u32[]{:S(2)}) %collective-permute-start.18) | collective-permute-done | bytes 184352 | tf_op jit(solution)/shard_map/ppermute | solution.py:695
  66.1 0.3 collective-permute-start.19
  66.4 1.9 %collective-permute-done.17 = bf16[2,288,128]{2,1,0:T(8,128)(2,1)S(1)} collective-permute-done((bf16[2,288,128]{2,1,0:T(8,128)(2,1)S(1)}, bf16[2,288,128]{2,1,0:T(8,128)(2,1)S(1)}, u32[]{:S(2)}, u32[]{:S(2)}) %collective-permute-start.17) | collective-permute-done | bytes 147488 | tf_op jit(solution)/shard_map/ppermute | solution.py:695
  68.3 0.8 collective-permute-start.20
  69.1 2.2 %collective-permute-start.21 = (bf16[4,288,128]{2,1,0:T(8,128)(2,1)S(1)}, bf16[4,288,128]{2,1,0:T(8,128)(2,1)S(1)}, u32[]{:S(2)}, u32[]{:S(2)}) collective-permute-start(bf16[4,288,128]{2,1,0:T(8,128)(2,1)S(1)} %constant_dynamic-update-slice_fusion.9.refs_0_), channel_id=1, source_target_pairs={{0,1},{1,0},{2,3},{3,2},{4,5},{5,4},{6,7},{7,6},{8,9},{9,8},{10,11... | collective-permute-start | bytes 884744 | tf_op jit(solution)/shard_map/ppermute | solution.py:695
  71.3 1.0 assemble.1
  72.3 5.0 %collective-permute-done.19 = bf16[5,144,128]{2,1,0:T(8,128)(2,1)S(1)} collective-permute-done((bf16[5,144,128]{2,1,0:T(8,128)(2,1)S(1)}, bf16[5,144,128]{2,1,0:T(8,128)(2,1)S(1)}, u32[]{:S(2)}, u32[]{:S(2)}) %collective-permute-start.19) | collective-permute-done | bytes 184352 | tf_op jit(solution)/shard_map/ppermute | solution.py:695
  77.3 0.1 add_convert_fusion.3
  77.4 1.2 %collective-permute-start.27 = (bf16[4,144,128]{2,1,0:T(8,128)(2,1)S(1)}, bf16[4,144,128]{2,1,0:T(8,128)(2,1)S(1)}, u32[]{:S(2)}, u32[]{:S(2)}) collective-permute-start(bf16[4,144,128]{2,1,0:T(8,128)(2,1)S(1)} %add_convert_fusion.3), channel_id=1, source_target_pairs={{0,2},{1,3},{2,0},{3,1},{4,6},{5,7},{6,4},{7,5},{8,10},{9,11},{10,... | collective-permute-start | bytes 442376 | tf_op jit(solution)/shard_map/ppermute | solution.py:695
  78.6 0.7 vector_outputs.1
  79.3 0.7 collective-permute-start.24
  80.0 0.5 collective-permute-start.26
  80.5 2.2 %collective-permute-done.27 = bf16[4,144,128]{2,1,0:T(8,128)(2,1)S(1)} collective-permute-done((bf16[4,144,128]{2,1,0:T(8,128)(2,1)S(1)}, bf16[4,144,128]{2,1,0:T(8,128)(2,1)S(1)}, u32[]{:S(2)}, u32[]{:S(2)}) %collective-permute-start.27) | collective-permute-done | bytes 147488 | tf_op jit(solution)/shard_map/ppermute | solution.py:695
  82.7 0.1 collective-permute-start.28
  82.8 1.2 %collective-permute-start.30 = (bf16[8,144,128]{2,1,0:T(8,128)(2,1)S(1)}, bf16[8,144,128]{2,1,0:T(8,128)(2,1)S(1)}, u32[]{:S(2)}, u32[]{:S(2)}) collective-permute-start(bf16[8,144,128]{2,1,0:T(8,128)(2,1)S(1)} %constant_dynamic-update-slice_fusion.11.refs_6_), channel_id=1, source_target_pairs={{0,1},{1,0},{2,3},{3,2},{4,5},{5,4},{6,7},{7,6},{8,9},{9,8},{10,11... | collective-permute-start | bytes 884744 | tf_op jit(solution)/shard_map/ppermute | solution.py:695
  84.0 0.9 collective-permute-start.23
  84.8 0.1 class_gradients.1
  85.0 2.8 %first_outputs.1 = (f32[384,1152]{1,0:T(8,128)}, f32[384,384]{1,0:T(8,128)}, f32[384,1536]{1,0:T(8,128)}, f32[1536,384]{1,0:T(8,128)}) custom-call(bf16[4,288,128]{2,1,0:T(8,128)(2,1)S(1)} %constant_dynamic-update-slice_fusion.9.refs_0_, ...), custom_call_target="tpu_custom_call", output_to_operand_aliasing={{0}: (8, {}), {1}: (9, {}), {2}: (10, {}), {3}: (11, {})} | custom-call | bytes 1 | tf_op jit(solution)/shard_map/first_outputs/pallas_call | solution.py:674
  87.8 1.7 %collective-permute-done.30.refs_2_ = bf16[8,144,128]{2,1,0:T(8,128)(2,1)S(1)} collective-permute-done((bf16[8,144,128]{2,1,0:T(8,128)(2,1)S(1)}, bf16[8,144,128]{2,1,0:T(8,128)(2,1)S(1)}, u32[]{:S(2)}, u32[]{:S(2)}) %collective-permute-start.30) | collective-permute-done | bytes 294944 | tf_op jit(solution)/shard_map/ppermute | solution.py:695
  89.5 1.6 %collective-permute-start.31 = (bf16[8,144,128]{2,1,0:T(8,128)(2,1)S(1)}, bf16[8,144,128]{2,1,0:T(8,128)(2,1)S(1)}, u32[]{:S(2)}, u32[]{:S(2)}) collective-permute-start(bf16[8,144,128]{2,1,0:T(8,128)(2,1)S(1)} %collective-permute-done.30.refs_2_), channel_id=1, source_target_pairs={{0,16},{16,0},{1,17},{17,1},{2,18},{18,2},{3,19},{19,3},{4,20},{20... | collective-permute-start | bytes 884744 | tf_op jit(solution)/shard_map/ppermute | solution.py:689
  91.2 1.5 %collective-permute-done.23.refs_0_ = bf16[4,288,128]{2,1,0:T(8,128)(2,1)S(1)} collective-permute-done((bf16[4,288,128]{2,1,0:T(8,128)(2,1)S(1)}, bf16[4,288,128]{2,1,0:T(8,128)(2,1)S(1)}, u32[]{:S(2)}, u32[]{:S(2)}) %collective-permute-start.23) | collective-permute-done | bytes 294944 | tf_op jit(solution)/shard_map/ppermute | solution.py:695
  92.7 1.6 %collective-permute-done.29.refs_1_ = bf16[4,288,128]{2,1,0:T(8,128)(2,1)S(1)} collective-permute-done((bf16[4,288,128]{2,1,0:T(8,128)(2,1)S(1)}, bf16[4,288,128]{2,1,0:T(8,128)(2,1)S(1)}, u32[]{:S(2)}, u32[]{:S(2)}) %collective-permute-start.29) | collective-permute-done | bytes 294944 | tf_op jit(solution)/shard_map/ppermute | solution.py:689
  94.3 1.7 %last_outputs.1 = (f32[384,1152]{1,0:T(8,128)}, f32[384,384]{1,0:T(8,128)}, f32[384,1536]{1,0:T(8,128)}, f32[1536,384]{1,0:T(8,128)}) custom-call(bf16[4,288,128]{2,1,0:T(8,128)(2,1)S(1)} %collective-permute-done.23.refs_0_, ...), custom_call_target="tpu_custom_call", output_to_operand_aliasing={{0}: (4, {}), {1}: (5, {}), {2}: (6, {}), {3}: (7, {})} | custom-call | bytes 1 | tf_op jit(solution)/shard_map/last_outputs/pallas_call | solution.py:674
  (76 shorter events, 0.6 us)
Async XLA Ops:
  0.7 3.9 %copy-start.1 = (bf16[1,384,1536]{2,1,0:T(8,128)(2,1)S(1)}, bf16[1,384,1536]{2,1,0:T(8,128)(2,1)}, u32[]{:S(2)}) copy-start(bf16[1,384,1536]{2,1,0:T(8,128)(2,1)} %param.37) | copy-start | bytes 3538948
  0.7 4.4 %copy-start.3 = (bf16[1,384,384]{2,1,0:T(8,128)(2,1)S(1)}, bf16[1,384,384]{2,1,0:T(8,128)(2,1)}, u32[]{:S(2)}) copy-start(bf16[1,384,384]{2,1,0:T(8,128)(2,1)} %param.32) | copy-start | bytes 884740
  0.7 3.8 %collective-permute-start.1 = (bf16[384,1152]{1,0:T(8,128)(2,1)}, bf16[384,1152]{1,0:T(8,128)(2,1)S(1)}, u32[]{:S(2)}, u32[]{:S(2)}) collective-permute-start(bf16[384,1152]{1,0:T(8,128)(2,1)} %bitcast.14), channel_id=1, source_target_pairs={{0,16},{16,0},{1,17},{17,1},{2,18},{18,2},{3,19},{19,3},{4,20},{20... | collective-permute-start | bytes 2654216 | tf_op jit(solution)/shard_map/ppermute | solution.py:689
  1.2 4.2 %copy-start.11 = (bf16[8,8]{1,0:T(8,128)(2,1)S(1)}, bf16[8,8]{1,0:T(8,128)(2,1)}, u32[]{:S(2)}) copy-start(bf16[8,8]{1,0:T(8,128)(2,1)} %refs_11_.1) | copy-start | bytes 388
  1.2 4.2 %copy-start.12 = (bf16[8,8]{1,0:T(8,128)(2,1)S(1)}, bf16[8,8]{1,0:T(8,128)(2,1)}, u32[]{:S(2)}) copy-start(bf16[8,8]{1,0:T(8,128)(2,1)} %refs_10_.1) | copy-start | bytes 388
  2.9 2.5 %copy-start = (bf16[1,384,1152]{2,1,0:T(8,128)(2,1)S(1)}, bf16[1,384,1152]{2,1,0:T(8,128)(2,1)}, u32[]{:S(2)}) copy-start(bf16[1,384,1152]{2,1,0:T(8,128)(2,1)} %param.27) | copy-start | bytes 2654212
  2.9 2.5 %copy-start.4 = (bf16[16,384]{1,0:T(8,128)(2,1)S(1)}, bf16[16,384]{1,0:T(8,128)(2,1)}, u32[]{:S(2)}) copy-start(bf16[16,384]{1,0:T(8,128)(2,1)} %get-tuple-element.129.vec_own.refs_7_.refs_6_) | copy-start | bytes 36868
  2.9 2.5 %copy-start.5 = (s32[4,196]{1,0:T(4,128)S(1)}, s32[4,196]{1,0:T(4,128)}, u32[]{:S(2)}) copy-start(s32[4,196]{1,0:T(4,128)} %refs_2_.5) | copy-start | bytes 9412
  3.0 2.5 %copy-start.8 = (f32[1,384]{1,0:T(1,128)S(1)}, f32[1,384]{1,0:T(1,128)}, u32[]{:S(2)}) copy-start(f32[1,384]{1,0:T(1,128)} %get-tuple-element.130.bias_ref.refs_11_) | copy-start | bytes 4612
  3.0 1.5 %collective-permute-start = (bf16[16,384]{1,0:T(8,128)(2,1)}, bf16[16,384]{1,0:T(8,128)(2,1)S(1)}, u32[]{:S(2)}, u32[]{:S(2)}) collective-permute-start(bf16[16,384]{1,0:T(8,128)(2,1)} %get-tuple-element.129.vec_own.refs_7_.refs_6_), channel_id=1, source_target_pairs={{0,16},{16,0},{1,17},{17,1},{2,18},{18,2},{3,19},{19,3},{4,20},{20... | collective-permute-start | bytes 36872 | tf_op jit(solution)/shard_map/ppermute | solution.py:689
  4.5 5.3 %copy-start.2 = (bf16[1,1536,384]{2,1,0:T(8,128)(2,1)S(1)}, bf16[1,1536,384]{2,1,0:T(8,128)(2,1)}, u32[]{:S(2)}) copy-start(bf16[1,1536,384]{2,1,0:T(8,128)(2,1)} %param.39) | copy-start | bytes 3538948
  4.5 5.3 %copy-start.9 = (bf16[4,384]{1,0:T(4,128)(2,1)S(1)}, bf16[4,384]{1,0:T(4,128)(2,1)}, u32[]{:S(2)}) copy-start(bf16[4,384]{1,0:T(4,128)(2,1)} %class_ref.1) | copy-start | bytes 9220
  4.5 5.3 %copy-start.10 = (bf16[4,384]{1,0:T(4,128)(2,1)S(1)}, bf16[4,384]{1,0:T(4,128)(2,1)}, u32[]{:S(2)}) copy-start(bf16[4,384]{1,0:T(4,128)(2,1)} %cot_ref.1) | copy-start | bytes 9220
  4.5 5.2 %collective-permute-start.3 = (bf16[384,1536]{1,0:T(8,128)(2,1)S(1)}, bf16[384,1536]{1,0:T(8,128)(2,1)S(1)}, u32[]{:S(2)}, u32[]{:S(2)}) collective-permute-start(bf16[384,1536]{1,0:T(8,128)(2,1)S(1)} %bitcast.19), channel_id=1, source_target_pairs={{0,16},{16,0},{1,17},{17,1},{2,18},{18,2},{3,19},{19,3},{4,20},{20... | collective-permute-start | bytes 3538952 | tf_op jit(solution)/shard_map/ppermute | solution.py:689
  4.9 4.9 %collective-permute-start.4 = (bf16[1536,384]{1,0:T(8,128)(2,1)}, bf16[1536,384]{1,0:T(8,128)(2,1)S(1)}, u32[]{:S(2)}, u32[]{:S(2)}) collective-permute-start(bf16[1536,384]{1,0:T(8,128)(2,1)} %bitcast.22), channel_id=1, source_target_pairs={{0,16},{16,0},{1,17},{17,1},{2,18},{18,2},{3,19},{19,3},{4,20},{20... | collective-permute-start | bytes 3538952 | tf_op jit(solution)/shard_map/ppermute | solution.py:689
  5.1 4.6 %collective-permute-start.2 = (bf16[384,384]{1,0:T(8,128)(2,1)S(1)}, bf16[384,384]{1,0:T(8,128)(2,1)S(1)}, u32[]{:S(2)}, u32[]{:S(2)}) collective-permute-start(bf16[384,384]{1,0:T(8,128)(2,1)S(1)} %bitcast.25), channel_id=1, source_target_pairs={{0,16},{16,0},{1,17},{17,1},{2,18},{18,2},{3,19},{19,3},{4,20},{20... | collective-permute-start | bytes 884744 | tf_op jit(solution)/shard_map/ppermute | solution.py:689
  9.8 12.6 %copy-start.6 = (f32[8,384]{1,0:T(8,128)S(1)}, f32[8,384]{1,0:T(8,128)}, u32[]{:S(2)}) copy-start(f32[8,384]{1,0:T(8,128)} %get-tuple-element.142.refs_12_) | copy-start | bytes 36868
  9.8 12.6 %copy-start.7 = (f32[8,384]{1,0:T(8,128)S(1)}, f32[8,384]{1,0:T(8,128)}, u32[]{:S(2)}) copy-start(f32[8,384]{1,0:T(8,128)} %get-tuple-element.143.refs_13_) | copy-start | bytes 36868
  22.0 4.2 %collective-permute-start.5 = (bf16[17,288,128]{2,1,0:T(8,128)(2,1)S(1)}, bf16[17,288,128]{2,1,0:T(8,128)(2,1)S(1)}, u32[]{:S(2)}, u32[]{:S(2)}) collective-permute-start(bf16[17,288,128]{2,1,0:T(8,128)(2,1)S(1)} %get-tuple-element.137), channel_id=1, source_target_pairs={{0,16},{16,0},{1,17},{17,1},{2,18},{18,2},{3,19},{19,3},{4,20},{20... | collective-permute-start | bytes 3760136 | tf_op jit(solution)/shard_map/ppermute | solution.py:689
  26.4 10.6 %collective-permute-start.7 = (bf16[8,288,128]{2,1,0:T(8,128)(2,1)S(1)}, bf16[8,288,128]{2,1,0:T(8,128)(2,1)S(1)}, u32[]{:S(2)}, u32[]{:S(2)}) collective-permute-start(bf16[8,288,128]{2,1,0:T(8,128)(2,1)S(1)} %add_convert_fusion), channel_id=1, source_target_pairs={{0,1},{1,0},{2,3},{3,2},{4,5},{5,4},{6,7},{7,6},{8,9},{9,8},{10,11... | collective-permute-start | bytes 1769480 | tf_op jit(solution)/shard_map/ppermute | solution.py:695
  35.8 3.5 %collective-permute-start.9 = (bf16[17,144,128]{2,1,0:T(8,128)(2,1)S(1)}, bf16[17,144,128]{2,1,0:T(8,128)(2,1)S(1)}, u32[]{:S(2)}, u32[]{:S(2)}) collective-permute-start(bf16[17,144,128]{2,1,0:T(8,128)(2,1)S(1)} %get-tuple-element.164), channel_id=1, source_target_pairs={{0,16},{16,0},{1,17},{17,1},{2,18},{18,2},{3,19},{19,3},{4,20},{20... | collective-permute-start | bytes 1880072 | tf_op jit(solution)/shard_map/ppermute | solution.py:689
  35.9 5.1 %collective-permute-start.6 = (bf16[2,208,208]{2,1,0:T(8,128)(2,1)S(1)}, bf16[2,208,208]{2,1,0:T(8,128)(2,1)S(1)}, u32[]{:S(2)}, u32[]{:S(2)}) collective-permute-start(bf16[2,208,208]{2,1,0:T(8,128)(2,1)S(1)} %get-tuple-element.157), channel_id=1, source_target_pairs={{0,16},{16,0},{1,17},{17,1},{2,18},{18,2},{3,19},{19,3},{4,20},{20... | collective-permute-start | bytes 519176 | tf_op jit(solution)/shard_map/ppermute | solution.py:689
  37.2 9.7 %collective-permute-start.8 = (bf16[4,288,128]{2,1,0:T(8,128)(2,1)S(1)}, bf16[4,288,128]{2,1,0:T(8,128)(2,1)S(1)}, u32[]{:S(2)}, u32[]{:S(2)}) collective-permute-start(bf16[4,288,128]{2,1,0:T(8,128)(2,1)S(1)} %add_convert_fusion.2), channel_id=1, source_target_pairs={{0,2},{1,3},{2,0},{3,1},{4,6},{5,7},{6,4},{7,5},{8,10},{9,11},{10,... | collective-permute-start | bytes 884744 | tf_op jit(solution)/shard_map/ppermute | solution.py:695
  39.4 9.9 %collective-permute-start.12 = (bf16[9,144,128]{2,1,0:T(8,128)(2,1)S(1)}, bf16[9,144,128]{2,1,0:T(8,128)(2,1)S(1)}, u32[]{:S(2)}, u32[]{:S(2)}) collective-permute-start(bf16[9,144,128]{2,1,0:T(8,128)(2,1)S(1)} %pad_maximum_fusion), channel_id=1, source_target_pairs={{0,1},{1,0},{2,3},{3,2},{4,5},{5,4},{6,7},{7,6},{8,9},{9,8},{10,11... | collective-permute-start | bytes 995336 | tf_op jit(solution)/shard_map/ppermute | solution.py:695
  41.0 10.1 %collective-permute-start.11 = (bf16[2,144,128]{2,1,0:T(8,128)(2,1)S(1)}, bf16[2,144,128]{2,1,0:T(8,128)(2,1)S(1)}, u32[]{:S(2)}, u32[]{:S(2)}) collective-permute-start(bf16[2,144,128]{2,1,0:T(8,128)(2,1)S(1)} %constant_dynamic-update-slice_fusion), channel_id=1, source_target_pairs={{16,24},{17,25},{18,26},{19,27},{20,28},{21,29},{22,30},{23,31},{2... | collective-permute-start | bytes 221192 | tf_op jit(solution)/shard_map/ppermute | solution.py:695
  46.9 5.6 %collective-permute-start.10 = (bf16[2,288,128]{2,1,0:T(8,128)(2,1)S(1)}, bf16[2,288,128]{2,1,0:T(8,128)(2,1)S(1)}, u32[]{:S(2)}, u32[]{:S(2)}) collective-permute-start(bf16[2,288,128]{2,1,0:T(8,128)(2,1)S(1)} %add_convert_fusion.9), channel_id=1, source_target_pairs={{0,4},{1,5},{2,6},{3,7},{4,0},{5,1},{6,2},{7,3},{8,12},{9,13},{10,... | collective-permute-start | bytes 442376 | tf_op jit(solution)/shard_map/ppermute | solution.py:695
  49.5 6.2 %collective-permute-start.15 = (bf16[5,144,128]{2,1,0:T(8,128)(2,1)S(1)}, bf16[5,144,128]{2,1,0:T(8,128)(2,1)S(1)}, u32[]{:S(2)}, u32[]{:S(2)}) collective-permute-start(bf16[5,144,128]{2,1,0:T(8,128)(2,1)S(1)} %pad_maximum_fusion.1), channel_id=1, source_target_pairs={{0,2},{1,3},{2,0},{3,1},{4,6},{5,7},{6,4},{7,5},{8,10},{9,11},{10,... | collective-permute-start | bytes 552968 | tf_op jit(solution)/shard_map/ppermute | solution.py:695
  51.1 4.8 %collective-permute-start.14 = (bf16[4,144,128]{2,1,0:T(8,128)(2,1)S(1)}, bf16[4,144,128]{2,1,0:T(8,128)(2,1)S(1)}, u32[]{:S(2)}, u32[]{:S(2)}) collective-permute-start(bf16[4,144,128]{2,1,0:T(8,128)(2,1)S(1)} %constant_dynamic-update-slice_fusion.2), channel_id=1, source_target_pairs={{16,20},{17,21},{18,22},{19,23},{20,16},{21,17},{22,18},{23,19},{2... | collective-permute-start | bytes 442376 | tf_op jit(solution)/shard_map/ppermute | solution.py:695
  52.6 9.6 %collective-permute-start.13 = (bf16[2,288,128]{2,1,0:T(8,128)(2,1)S(1)}, bf16[2,288,128]{2,1,0:T(8,128)(2,1)S(1)}, u32[]{:S(2)}, u32[]{:S(2)}) collective-permute-start(bf16[2,288,128]{2,1,0:T(8,128)(2,1)S(1)} %pad_maximum_fusion.3), channel_id=1, source_target_pairs={{0,8},{1,9},{2,10},{3,11},{4,12},{5,13},{6,14},{7,15},{8,0},{9,1},... | collective-permute-start | bytes 442376 | tf_op jit(solution)/shard_map/ppermute | solution.py:695
  55.9 6.4 %collective-permute-start.16 = (bf16[8,144,128]{2,1,0:T(8,128)(2,1)S(1)}, bf16[8,144,128]{2,1,0:T(8,128)(2,1)S(1)}, u32[]{:S(2)}, u32[]{:S(2)}) collective-permute-start(bf16[8,144,128]{2,1,0:T(8,128)(2,1)S(1)} %constant_dynamic-update-slice_fusion.4), channel_id=1, source_target_pairs={{16,17},{17,16},{18,19},{19,18},{20,21},{21,20},{22,23},{23,22},{2... | collective-permute-start | bytes 884744 | tf_op jit(solution)/shard_map/ppermute | solution.py:695
  56.7 9.3 %collective-permute-start.18 = (bf16[5,144,128]{2,1,0:T(8,128)(2,1)S(1)}, bf16[5,144,128]{2,1,0:T(8,128)(2,1)S(1)}, u32[]{:S(2)}, u32[]{:S(2)}) collective-permute-start(bf16[5,144,128]{2,1,0:T(8,128)(2,1)S(1)} %pad_maximum_fusion.2), channel_id=1, source_target_pairs={{0,4},{1,5},{2,6},{3,7},{4,0},{5,1},{6,2},{7,3},{8,12},{9,13},{10,... | collective-permute-start | bytes 552968 | tf_op jit(solution)/shard_map/ppermute | solution.py:695
  62.4 15.0 %collective-permute-start.22 = (bf16[16,144,128]{2,1,0:T(8,128)(2,1)S(1)}, bf16[16,144,128]{2,1,0:T(8,128)(2,1)S(1)}, u32[]{:S(2)}, u32[]{:S(2)}) collective-permute-start(bf16[16,144,128]{2,1,0:T(8,128)(2,1)S(1)} %constant_dynamic-update-slice_fusion.6.refs_0_), channel_id=1, source_target_pairs={{16,18},{17,19},{18,16},{19,17},{20,22},{21,23},{22,20},{23,21},{2... | collective-permute-start | bytes 1769480 | tf_op jit(solution)/shard_map/ppermute | solution.py:695
  63.1 5.2 %collective-permute-start.17 = (bf16[2,288,128]{2,1,0:T(8,128)(2,1)S(1)}, bf16[2,288,128]{2,1,0:T(8,128)(2,1)S(1)}, u32[]{:S(2)}, u32[]{:S(2)}) collective-permute-start(bf16[2,288,128]{2,1,0:T(8,128)(2,1)S(1)} %add_convert_fusion.6), channel_id=1, source_target_pairs={{0,4},{1,5},{2,6},{3,7},{4,0},{5,1},{6,2},{7,3},{8,12},{9,13},{10,... | collective-permute-start | bytes 442376 | tf_op jit(solution)/shard_map/ppermute | solution.py:695
  66.1 11.2 %collective-permute-start.19 = (bf16[5,144,128]{2,1,0:T(8,128)(2,1)S(1)}, bf16[5,144,128]{2,1,0:T(8,128)(2,1)S(1)}, u32[]{:S(2)}, u32[]{:S(2)}) collective-permute-start(bf16[5,144,128]{2,1,0:T(8,128)(2,1)S(1)} %constant_dynamic-update-slice_fusion.8), channel_id=1, source_target_pairs={{0,8},{1,9},{2,10},{3,11},{4,12},{5,13},{6,14},{7,15},{8,0},{9,1},... | collective-permute-start | bytes 552968 | tf_op jit(solution)/shard_map/ppermute | solution.py:695
  68.3 10.9 %collective-permute-start.20 = (bf16[4,288,128]{2,1,0:T(8,128)(2,1)S(1)}, bf16[4,288,128]{2,1,0:T(8,128)(2,1)S(1)}, u32[]{:S(2)}, u32[]{:S(2)}) collective-permute-start(bf16[4,288,128]{2,1,0:T(8,128)(2,1)S(1)} %constant_dynamic-update-slice_fusion.9.refs_0_), channel_id=1, source_target_pairs={{0,2},{1,3},{2,0},{3,1},{4,6},{5,7},{6,4},{7,5},{8,10},{9,11},{10,... | collective-permute-start | bytes 884744 | tf_op jit(solution)/shard_map/ppermute | solution.py:695
  69.1 10.1 %collective-permute-start.21 = (bf16[4,288,128]{2,1,0:T(8,128)(2,1)S(1)}, bf16[4,288,128]{2,1,0:T(8,128)(2,1)S(1)}, u32[]{:S(2)}, u32[]{:S(2)}) collective-permute-start(bf16[4,288,128]{2,1,0:T(8,128)(2,1)S(1)} %constant_dynamic-update-slice_fusion.9.refs_0_), channel_id=1, source_target_pairs={{0,1},{1,0},{2,3},{3,2},{4,5},{5,4},{6,7},{7,6},{8,9},{9,8},{10,11... | collective-permute-start | bytes 884744 | tf_op jit(solution)/shard_map/ppermute | solution.py:695
  77.4 5.2 %collective-permute-start.27 = (bf16[4,144,128]{2,1,0:T(8,128)(2,1)S(1)}, bf16[4,144,128]{2,1,0:T(8,128)(2,1)S(1)}, u32[]{:S(2)}, u32[]{:S(2)}) collective-permute-start(bf16[4,144,128]{2,1,0:T(8,128)(2,1)S(1)} %add_convert_fusion.3), channel_id=1, source_target_pairs={{0,2},{1,3},{2,0},{3,1},{4,6},{5,7},{6,4},{7,5},{8,10},{9,11},{10,... | collective-permute-start | bytes 442376 | tf_op jit(solution)/shard_map/ppermute | solution.py:695
  79.3 4.7 %collective-permute-start.24 = (bf16[4,288,128]{2,1,0:T(8,128)(2,1)S(1)}, bf16[4,288,128]{2,1,0:T(8,128)(2,1)S(1)}, u32[]{:S(2)}, u32[]{:S(2)}) collective-permute-start(bf16[4,288,128]{2,1,0:T(8,128)(2,1)S(1)} %constant_dynamic-update-slice_fusion.9.refs_0_), channel_id=1, source_target_pairs={{0,16},{16,0},{1,17},{17,1},{2,18},{18,2},{3,19},{19,3},{4,20},{20... | collective-permute-start | bytes 884744 | tf_op jit(solution)/shard_map/ppermute | solution.py:689
  80.0 5.0 %collective-permute-start.25 = (bf16[4,288,128]{2,1,0:T(8,128)(2,1)S(1)}, bf16[4,288,128]{2,1,0:T(8,128)(2,1)S(1)}, u32[]{:S(2)}, u32[]{:S(2)}) collective-permute-start(bf16[4,288,128]{2,1,0:T(8,128)(2,1)S(1)} %collective-permute-done.20.refs_2_), channel_id=1, source_target_pairs={{0,16},{16,0},{1,17},{17,1},{2,18},{18,2},{3,19},{19,3},{4,20},{20... | collective-permute-start | bytes 884744 | tf_op jit(solution)/shard_map/ppermute | solution.py:689
  80.0 5.0 %collective-permute-start.26 = (bf16[4,288,128]{2,1,0:T(8,128)(2,1)S(1)}, bf16[4,288,128]{2,1,0:T(8,128)(2,1)S(1)}, u32[]{:S(2)}, u32[]{:S(2)}) collective-permute-start(bf16[4,288,128]{2,1,0:T(8,128)(2,1)S(1)} %collective-permute-done.21.refs_4_), channel_id=1, source_target_pairs={{0,16},{16,0},{1,17},{17,1},{2,18},{18,2},{3,19},{19,3},{4,20},{20... | collective-permute-start | bytes 884744 | tf_op jit(solution)/shard_map/ppermute | solution.py:689
  82.7 2.3 %collective-permute-start.28 = (bf16[8,144,128]{2,1,0:T(8,128)(2,1)S(1)}, bf16[8,144,128]{2,1,0:T(8,128)(2,1)S(1)}, u32[]{:S(2)}, u32[]{:S(2)}) collective-permute-start(bf16[8,144,128]{2,1,0:T(8,128)(2,1)S(1)} %constant_dynamic-update-slice_fusion.11.refs_6_), channel_id=1, source_target_pairs={{0,16},{16,0},{1,17},{17,1},{2,18},{18,2},{3,19},{19,3},{4,20},{20... | collective-permute-start | bytes 884744 | tf_op jit(solution)/shard_map/ppermute | solution.py:689
  82.8 6.8 %collective-permute-start.30 = (bf16[8,144,128]{2,1,0:T(8,128)(2,1)S(1)}, bf16[8,144,128]{2,1,0:T(8,128)(2,1)S(1)}, u32[]{:S(2)}, u32[]{:S(2)}) collective-permute-start(bf16[8,144,128]{2,1,0:T(8,128)(2,1)S(1)} %constant_dynamic-update-slice_fusion.11.refs_6_), channel_id=1, source_target_pairs={{0,1},{1,0},{2,3},{3,2},{4,5},{5,4},{6,7},{7,6},{8,9},{9,8},{10,11... | collective-permute-start | bytes 884744 | tf_op jit(solution)/shard_map/ppermute | solution.py:695
  84.0 8.7 %collective-permute-start.23 = (bf16[4,288,128]{2,1,0:T(8,128)(2,1)S(1)}, bf16[4,288,128]{2,1,0:T(8,128)(2,1)S(1)}, u32[]{:S(2)}, u32[]{:S(2)}) collective-permute-start(bf16[4,288,128]{2,1,0:T(8,128)(2,1)S(1)} %collective-permute-done.20.refs_2_), channel_id=1, source_target_pairs={{0,1},{1,0},{2,3},{3,2},{4,5},{5,4},{6,7},{7,6},{8,9},{9,8},{10,11... | collective-permute-start | bytes 884744 | tf_op jit(solution)/shard_map/ppermute | solution.py:695
  89.5 3.2 %collective-permute-start.31 = (bf16[8,144,128]{2,1,0:T(8,128)(2,1)S(1)}, bf16[8,144,128]{2,1,0:T(8,128)(2,1)S(1)}, u32[]{:S(2)}, u32[]{:S(2)}) collective-permute-start(bf16[8,144,128]{2,1,0:T(8,128)(2,1)S(1)} %collective-permute-done.30.refs_2_), channel_id=1, source_target_pairs={{0,16},{16,0},{1,17},{17,1},{2,18},{18,2},{3,19},{19,3},{4,20},{20... | collective-permute-start | bytes 884744 | tf_op jit(solution)/shard_map/ppermute | solution.py:689
  92.7 1.6 %collective-permute-start.29 = (bf16[4,288,128]{2,1,0:T(8,128)(2,1)S(1)}, bf16[4,288,128]{2,1,0:T(8,128)(2,1)S(1)}, u32[]{:S(2)}, u32[]{:S(2)}) collective-permute-start(bf16[4,288,128]{2,1,0:T(8,128)(2,1)S(1)} %collective-permute-done.23.refs_0_), channel_id=1, source_target_pairs={{0,16},{16,0},{1,17},{17,1},{2,18},{18,2},{3,19},{19,3},{4,20},{20... | collective-permute-start | bytes 884744 | tf_op jit(solution)/shard_map/ppermute | solution.py:689

commit v5 on v4

--- a/solution.py
+++ b/solution.py
@@ -507,13 +507,15 @@
         preferred_element_type=F32, precision=lax.Precision.HIGHEST,
     )
     tall = jnp.concatenate(
-        [vec0[:, k * 128 : (k + 1) * 128] for k in range(3)]
+        [vec0[:14, :128], small[16:17], vec0[15:, :128]]
+        + [vec0[:, k * 128 : (k + 1) * 128] for k in (1, 2)]
         + [vec_in1[:, k * 128 : (k + 1) * 128] for k in range(3)]
-        + [small, jnp.zeros((24, 128), F32)],
+        + [small[:16]],
         axis=0,
     )
-    vec_part[0] = tall.astype(BF16)
-    send_ref[16] = tall.astype(BF16)
+    vec_part[...] = tall.astype(BF16)
+    send_ref[16, :112] = tall.astype(BF16)
+    send_ref[16, 112:] = jnp.zeros((32, 128), BF16)
     block_copy(blocks, kept_ref, 0, 16)
     block_copy(blocks, send_ref, 16, 16)
 
@@ -533,7 +535,7 @@
 
 
 def place_blocks(plan, *refs):
-    count = 2 * len(plan)
+    count = len(plan)
     pieces, (qkv_out, proj_out, fc1_out, fc2_out), (held, sems) = refs[:count], refs[count + 4 : count + 8], refs[count + 8 :]
 
     def put(at, source, n, first, target):
@@ -545,9 +547,9 @@
     def _():
         slot = 0
         for which, source in enumerate(pieces):
-            stream, start = plan[which // 2]
+            stream, start = plan[which]
             for n in range(source.shape[0]):
-                block = position_block((which % 2) * 16 + start + n)
+                block = position_block(start + n)
                 down = pl.ds(pl.multiple_of((block >> 2) * 48, 48), 48)
                 along = pl.ds(pl.multiple_of((block & 3) * 384, 384), 384)
                 if stream == 0:
@@ -574,7 +576,7 @@
     vec_outs, (pre_out, post_out, bias_out) = refs[:10], refs[10:]
     first = lax.axis_index("pipe") == 0
     width = vec_outs[0].shape[1]
-    tall = part[0].astype(F32)
+    tall = part[...].astype(F32)
     rows = [chosen(first, tall[k * 16 : (k + 1) * 16], tall[48 + k * 16 : 48 + (k + 1) * 16]) for k in range(3)]
     rows = jnp.concatenate(rows, axis=1)
     at = 0
@@ -584,7 +586,7 @@
             at += 1
     pre_out[...] = tall[96:104, 0:HEADS]
     post_out[...] = tall[104:112].T[0:HEADS]
-    bias_out[...] = tall[112:113, 0:HEADS]
+    bias_out[...] = tall[14:15, 0:HEADS]
 
 
 def class_gradients(*refs):
@@ -720,12 +722,14 @@
         self.pieces = list(after(tuple(self.pieces), *others))
 
     def swap(self, message, bits):
-        count = message.shape[0]
-        self.leaving = message if self.rider is None else jnp.concatenate([message, self.rider])
+        self.leaving = message
+        if self.rider is None:
+            return exchanged(self.leaving, bits)
+        self.leaving = jnp.concatenate([message.reshape(-1, 128), self.rider])
         got = exchanged(self.leaving, bits)
-        if self.rider is not None:
-            self.rider = total([self.rider, got[count:]], 0, 1)
-        return got
+        rows = got.shape[0] - self.rider.shape[0]
+        self.rider = total([self.rider, got[rows:]], 0, self.rider.shape[0])
+        return got[:rows].reshape(message.shape)
 
     def step(self):
         if not self.whole:
@@ -855,14 +859,14 @@
         input_gradients,
         [(VM, mg), (VM, rows), (VM, hid), (VM, att), (VM, join0), (VM, join1), (VM, sum0), (VM, sum1), (VM, vec0),
          (VM, vec1), (VM, vec_own), (VM, vec_got), (HB, w_own), (HB, w_got), (VM, class_other)],
-        [((17, 144, 128), BF16), ((16, 144, 128), BF16), ((1, 144, 128), BF16), ((IMGS, half, length), F32), ((IMGS, half + 16, length), BF16)],
+        [((17, 144, 128), BF16), ((16, 144, 128), BF16), ((112, 128), BF16), ((IMGS, half, length), F32), ((IMGS, half + 16, length), BF16)],
         [((width, 3 * width), BF16), ((flat, 3 * width), BF16), ((32, 144, 128), BF16)],
         "input_gradients",
         LIMIT_C,
         sems=1,
     )
     got2, half_got = swapped(send2), swapped(other_half)
-    stream2 = Stream((kept2, got2), SHORT, total([vec_part, got2[16:]], 0, 1))
+    stream2 = Stream((kept2, got2), SHORT, total([vec_part, got2[16, :112]], 0, 112))
     def turn(*streams):
         for stream in streams:
             turn.last = stream.wait(*turn.last) or (stream.step(), stream.leaving)[1:]
@@ -914,23 +918,29 @@
         for part in stream.parts():
             parts[at].append((at, start, part))
             start += part.shape[0]
+    early = [part for group in parts for part in group if part[1] < (12 if part[0] == 0 else 8)]
+    late = [part for group in parts for part in group if part[1] >= (12 if part[0] == 0 else 8)]
+    early = [placed for part in early for placed in (part, (part[0], part[1] + 16, swapped(part[2])))]
+    early += [part for part in late if part[0] == 0]
     for name in ("first_outputs", "last_outputs"):
-        chosen_parts = [part for group in parts for part in group if (part[1] < 8 or part[2].shape[0] == 4 and part[1] < 12) == (name == "first_outputs")]
         if name == "last_outputs":
-            chosen_parts = [(at, start, after(part, outs[0])) for at, start, part in chosen_parts]
+            late = [(at, start, after(part, outs[0])) for at, start, part in late]
+            own = [part for part in late if part[0] == 1]
+            chosen_parts = own + [(at, start + 16, swapped(part)) for at, start, part in late]
+        else:
+            chosen_parts = early
         plan = [(at, start) for at, start, _ in chosen_parts]
-        slots = sum(2 * part.shape[0] * (2 - at) for at, _, part in chosen_parts)
-        arrays = [(VM, array) for _, _, part in chosen_parts for array in (part, swapped(part))]
+        slots = sum(part.shape[0] * (2 - at) for at, _, part in chosen_parts)
         outs = call(
             lambda *refs: place_blocks(plan, *refs),
-            arrays + [(HB, out) for out in outs],
+            [(VM, part) for _, _, part in chosen_parts] + [(HB, out) for out in outs],
             matrices,
             [((slots, 48, width), F32)],
             name,
             LIMIT_D,
             sems=slots,
             far=4,
-            aliases={len(arrays) + n: n for n in range(4)},
+            aliases={len(plan) + n: n for n in range(4)},
         )
     qkv_out, proj_out, fc1_out, fc2_out = outs
     n1g, n1b, qvb, pb, sa, n2g, n2b, f1b, f2b, sm, pre, post, bias = small_outs

time: 96.4 us -> 94.5 us (0.980)
  waiting for transfers between devices: 27.2 us -> 23.5 us
  starting transfers between devices: 29.9 us -> 31.6 us
    ppermute x18, waiting for transfers between devices: 25.5 us -> 21.9 us  [exchanged(): return lax.ppermute(array, ('pipe', 'dp'), pairs)]
    ppermute x18, starting transfers between devices: 24.5 us -> 27.7 us  [exchanged(): return lax.ppermute(array, ('pipe', 'dp'), pairs)]
    ppermute x14, starting transfers between devices: 5.39 us -> 3.97 us  [swapped(): return lax.ppermute(array, 'pipe', [(0, 1), (1, 0)])]
  transfers between devices with their start and end apart: 32 -> 32, of which waited for: 11 -> 13; matrix products, arithmetic and copies ran while one was open for 3% -> 3% of each run, Pallas kernels for 22% -> 22%
where the time goes in v5:
time: 94.5 us; the launch traced here: 94.3 us
  Pallas kernels  34.8 us (37%)
  starting transfers between devices  31.6 us (33%)
  waiting for transfers between devices  23.5 us (25%)
  local copies, waits for them, and re-layouts  1.65 us (2%)
  between operations  1.44 us (2%)
  other arithmetic  1.2 us (1%)
    pallas_call x11, Pallas kernels, call(): pl.pallas_call(body, out_shape=[jax.ShapeDtypeStruct(shape, kind) for sha...  34.8 us
    ppermute x18, starting transfers between devices, exchanged(): return lax.ppermute(array, ('pipe', 'dp'), pairs)  27.7 us
    ppermute x18, waiting for transfers between devices, exchanged(): return lax.ppermute(array, ('pipe', 'dp'), pairs)  21.9 us
    ppermute x14, starting transfers between devices, swapped(): return lax.ppermute(array, 'pipe', [(0, 1), (1, 0)])  3.97 us
  transfers between devices with their start and end apart: 32, of which 13 were waited for; matrix products, arithmetic and copies ran while one was open for 3% of the time, Pallas kernels for 22%

profile of v5, /device:TPU:0, one launch (start us, length us, event | category | flops | bytes accessed | tf_op | source)
XLA Modules:
  0.0 94.3 jit_solution(12743078507351781769)
XLA Ops:
  0.7 0.5 collective-permute-start.1
  1.2 1.7 %prepare.1 = (bf16[16,384]{1,0:T(8,128)(2,1)}, f32[8,384]{1,0:T(8,128)}, f32[8,384]{1,0:T(8,128)}, f32[1,384]{1,0:T(1,128)}) custom-call(bf16[1,384]{1,0:T(2,128)(2,1)} %refs_0_.1, bf16[1,384]{1,0:T(2,128)(2,1)} %refs_1_.1, bf16[1,768]{1,0:T(2,128)(2,1)} %refs_2_.3, bf16[1,384]{1,0:T(2,128)(2,1)} %refs_3_.1, bf16[1,384]{1,0:T(2,128)(2,1)} %refs_4_.1, ...), custom_call_target="tpu_custom_call" | custom-call | bytes 1 | tf_op jit(solution)/shard_map/prepare/pallas_call | solution.py:676
  3.0 0.2 collective-permute-start
  3.1 1.3 %copy.49 = bf16[4,196,384]{2,1,0:T(8,128)(2,1)S(1)} copy(bf16[4,196,384]{2,0,1:T(4,128)(2,1)} %param.21) | data formatting | bytes 1204224 | tf_op args[0]
  4.5 0.4 collective-permute-start.3
  4.9 0.2 collective-permute-start.4
  5.1 0.3 collective-permute-start.2
  5.5 4.3 %attention_forward.1 = (bf16[2,208,384]{2,1,0:T(8,128)(2,1)S(1)}, bf16[2,208,384]{2,1,0:T(8,128)(2,1)S(1)}, bf16[2,256,384]{2,1,0:T(8,128)(2,1)S(1)}, bf16[2,256...) custom-call(f32[2,8,8]{2,1,0:T(8,128)S(1)} %maximum_convert_fusion.mixing.refs_0_, ...), custom_call_target="tpu_custom_call" | custom-call | bytes 1 | tf_op jit(solution)/shard_map/attention_forward/pallas_call | solution.py:676
  9.8 12.2 %middle_kernel.1 = (bf16[17,288,128]{2,1,0:T(8,128)(2,1)S(1)}, bf16[16,288,128]{2,1,0:T(8,128)(2,1)S(1)}, f32[2,208,384]{2,1,0:T(8,128)S(1)}, f32[16,384]{1,0:T(...) custom-call(bf16[2,208,384]{2,1,0:T(8,128)(2,1)S(1)} %get-tuple-elem, ...), custom_call_target="tpu_custom_call" | custom-call | bytes 1 | tf_op jit(solution)/shard_map/middle_kernel/pallas_call | solution.py:676
  22.0 0.4 collective-permute-start.5
  22.4 3.8 %attention_backward_0.1 = (bf16[208,1152]{1,0:T(8,128)(2,1)S(1)}, f32[24,384]{1,0:T(8,128)S(1)}) custom-call(f32[2,8,8]{2,1,0:T(8,128)S(1)} %maximum_convert_fusion.mixing.refs_0_, f32[2,208,384]{2,1,0:T(8,128)S(1)} %get-tuple-element.149.refs_1_.mg_ref, s32[4,196]{1,0:T(4,128)S(1)} %copy-done.5, bf16[2,256,384]{2,1,0:T(8,128)(2,1)S(1)} %get-tuple-element.138.refs_3_, ...), custom_call_target="tpu_custom_call" | custom-call | bytes 1 | tf_op jit(solution)/shard_map/attention_backward_0/pallas_call | solution.py:676
  26.2 0.2 add_convert_fusion
  26.4 2.8 %collective-permute-start.7 = (bf16[8,288,128]{2,1,0:T(8,128)(2,1)S(1)}, bf16[8,288,128]{2,1,0:T(8,128)(2,1)S(1)}, u32[]{:S(2)}, u32[]{:S(2)}) collective-permute-start(bf16[8,288,128]{2,1,0:T(8,128)(2,1)S(1)} %add_convert_fusion), channel_id=1, source_target_pairs={{0,1},{1,0},{2,3},{3,2},{4,5},{5,4},{6,7},{7,6},{8,9},{9,8},{10,11... | collective-permute-start | bytes 1769480 | tf_op jit(solution)/shard_map/ppermute | solution.py:697
  29.2 3.7 %attention_backward_1.1 = (bf16[208,1152]{1,0:T(8,128)(2,1)S(1)}, f32[24,384]{1,0:T(8,128)S(1)}) custom-call(f32[2,8,8]{2,1,0:T(8,128)S(1)} %maximum_convert_fusion.mixing.refs_0_, f32[2,208,384]{2,1,0:T(8,128)S(1)} %get-tuple-element.149.refs_1_.mg_ref, s32[4,196]{1,0:T(4,128)S(1)} %copy-done.5, bf16[2,256,384]{2,1,0:T(8,128)(2,1)S(1)} %get-tuple-element.138.refs_3_, ...), custom_call_target="tpu_custom_call" | custom-call | bytes 1 | tf_op jit(solution)/shard_map/attention_backward_1/pallas_call | solution.py:676
  32.8 3.0 %input_gradients.1 = (bf16[17,144,128]{2,1,0:T(8,128)(2,1)S(1)}, bf16[16,144,128]{2,1,0:T(8,128)(2,1)S(1)}, bf16[112,128]{1,0:T(8,128)(2,1)S(1)}, f32[2,192,208]{2,1,0:T(8,128)S(1)}, bf16[2,208,208]{2,1,0:T(8,128)(2,1)S(1)}) custom-call(f32[2,208,384]{2,1,0:T(8,128)S(1)} %get-tuple-element.149.refs_1_.mg_ref, bf16[4,208,384]{2,1,0:T(8,128)(2,1)S(1)} %pad.4.rows_ref, ...), custom_call_target="tpu_custom_call" | custom-call | bytes 1 | tf_op jit(solution)/shard_map/input_gradients/pallas_call | solution.py:676
  35.8 0.1 collective-permute-start.9
  35.9 0.5 collective-permute-start.6
  36.4 0.6 collective-permute-done.7
  37.0 0.1 add_convert_fusion.2
  37.2 2.1 %collective-permute-start.8 = (bf16[4,288,128]{2,1,0:T(8,128)(2,1)S(1)}, bf16[4,288,128]{2,1,0:T(8,128)(2,1)S(1)}, u32[]{:S(2)}, u32[]{:S(2)}) collective-permute-start(bf16[4,288,128]{2,1,0:T(8,128)(2,1)S(1)} %add_convert_fusion.2), channel_id=1, source_target_pairs={{0,2},{1,3},{2,0},{3,1},{4,6},{5,7},{6,4},{7,5},{8,10},{9,11},{10,... | collective-permute-start | bytes 884744 | tf_op jit(solution)/shard_map/ppermute | solution.py:697
  39.3 0.1 add_convert_fusion.1
  39.4 1.6 %collective-permute-start.12 = (bf16[1264,128]{1,0:T(8,128)(2,1)S(1)}, bf16[1264,128]{1,0:T(8,128)(2,1)S(1)}, u32[]{:S(2)}, u32[]{:S(2)}) collective-permute-start(bf16[1264,128]{1,0:T(8,128)(2,1)S(1)} %pad_maximum_fusion), channel_id=1, source_target_pairs={{0,1},{1,0},{2,3},{3,2},{4,5},{5,4},{6,7},{7,6},{8,9},{9,8},{10,11... | collective-permute-start | bytes 970760 | tf_op jit(solution)/shard_map/ppermute | solution.py:697
  41.0 0.7 collective-permute-start.11
  41.7 5.2 %collective-permute-done.8 = bf16[4,288,128]{2,1,0:T(8,128)(2,1)S(1)} collective-permute-done((bf16[4,288,128]{2,1,0:T(8,128)(2,1)S(1)}, bf16[4,288,128]{2,1,0:T(8,128)(2,1)S(1)}, u32[]{:S(2)}, u32[]{:S(2)}) %collective-permute-start.8) | collective-permute-done | bytes 294944 | tf_op jit(solution)/shard_map/ppermute | solution.py:697
  46.8 0.1 add_convert_fusion.8
  46.9 2.4 %collective-permute-start.10 = (bf16[2,288,128]{2,1,0:T(8,128)(2,1)S(1)}, bf16[2,288,128]{2,1,0:T(8,128)(2,1)S(1)}, u32[]{:S(2)}, u32[]{:S(2)}) collective-permute-start(bf16[2,288,128]{2,1,0:T(8,128)(2,1)S(1)} %add_convert_fusion.8), channel_id=1, source_target_pairs={{0,4},{1,5},{2,6},{3,7},{4,0},{5,1},{6,2},{7,3},{8,12},{9,13},{10,... | collective-permute-start | bytes 442376 | tf_op jit(solution)/shard_map/ppermute | solution.py:697
  49.5 1.6 %collective-permute-start.15 = (bf16[688,128]{1,0:T(8,128)(2,1)S(1)}, bf16[688,128]{1,0:T(8,128)(2,1)S(1)}, u32[]{:S(2)}, u32[]{:S(2)}) collective-permute-start(bf16[688,128]{1,0:T(8,128)(2,1)S(1)} %pad_maximum_fusion.1), channel_id=1, source_target_pairs={{0,2},{1,3},{2,0},{3,1},{4,6},{5,7},{6,4},{7,5},{8,10},{9,11},{10,... | collective-permute-start | bytes 528392 | tf_op jit(solution)/shard_map/ppermute | solution.py:697
  51.1 0.7 collective-permute-start.14
  51.8 0.7 collective-permute-done.10
  52.5 0.1 add_convert_fusion.12
  52.6 3.1 %collective-permute-start.13 = (bf16[2,288,128]{2,1,0:T(8,128)(2,1)S(1)}, bf16[2,288,128]{2,1,0:T(8,128)(2,1)S(1)}, u32[]{:S(2)}, u32[]{:S(2)}) collective-permute-start(bf16[2,288,128]{2,1,0:T(8,128)(2,1)S(1)} %pad_maximum_fusion.4), channel_id=1, source_target_pairs={{0,8},{1,9},{2,10},{3,11},{4,12},{5,13},{6,14},{7,15},{8,0},{9,1},... | collective-permute-start | bytes 442376 | tf_op jit(solution)/shard_map/ppermute | solution.py:697
  55.7 0.1 add_convert_fusion.10
  55.9 1.6 %collective-permute-start.18 = (bf16[688,128]{1,0:T(8,128)(2,1)S(1)}, bf16[688,128]{1,0:T(8,128)(2,1)S(1)}, u32[]{:S(2)}, u32[]{:S(2)}) collective-permute-start(bf16[688,128]{1,0:T(8,128)(2,1)S(1)} %pad_maximum_fusion.2), channel_id=1, source_target_pairs={{0,4},{1,5},{2,6},{3,7},{4,0},{5,1},{6,2},{7,3},{8,12},{9,13},{10,... | collective-permute-start | bytes 528392 | tf_op jit(solution)/shard_map/ppermute | solution.py:697
  57.6 0.7 collective-permute-start.16
  58.3 0.1 add_convert_fusion.4
  58.4 3.7 %collective-permute-done.13 = bf16[2,288,128]{2,1,0:T(8,128)(2,1)S(1)} collective-permute-done((bf16[2,288,128]{2,1,0:T(8,128)(2,1)S(1)}, bf16[2,288,128]{2,1,0:T(8,128)(2,1)S(1)}, u32[]{:S(2)}, u32[]{:S(2)}) %collective-permute-start.13) | collective-permute-done | bytes 147488 | tf_op jit(solution)/shard_map/ppermute | solution.py:697
  62.1 0.1 add_convert_fusion.5
  62.2 0.8 collective-permute-done.18
  63.2 0.7 collective-permute-start.20
  63.9 1.4 %collective-permute-start.17 = (bf16[2,288,128]{2,1,0:T(8,128)(2,1)S(1)}, bf16[2,288,128]{2,1,0:T(8,128)(2,1)S(1)}, u32[]{:S(2)}, u32[]{:S(2)}) collective-permute-start(bf16[2,288,128]{2,1,0:T(8,128)(2,1)S(1)} %add_convert_fusion.5), channel_id=1, source_target_pairs={{0,4},{1,5},{2,6},{3,7},{4,0},{5,1},{6,2},{7,3},{8,12},{9,13},{10,... | collective-permute-start | bytes 442376 | tf_op jit(solution)/shard_map/ppermute | solution.py:697
  65.4 1.6 %collective-permute-start.19 = (bf16[688,128]{1,0:T(8,128)(2,1)S(1)}, bf16[688,128]{1,0:T(8,128)(2,1)S(1)}, u32[]{:S(2)}, u32[]{:S(2)}) collective-permute-start(bf16[688,128]{1,0:T(8,128)(2,1)S(1)} %pad_maximum_fusion.3), channel_id=1, source_target_pairs={{0,8},{1,9},{2,10},{3,11},{4,12},{5,13},{6,14},{7,15},{8,0},{9,1},... | collective-permute-start | bytes 528392 | tf_op jit(solution)/shard_map/ppermute | solution.py:697
  67.0 3.4 %collective-permute-done.17 = bf16[2,288,128]{2,1,0:T(8,128)(2,1)S(1)} collective-permute-done((bf16[2,288,128]{2,1,0:T(8,128)(2,1)S(1)}, bf16[2,288,128]{2,1,0:T(8,128)(2,1)S(1)}, u32[]{:S(2)}, u32[]{:S(2)}) %collective-permute-start.17) | collective-permute-done | bytes 147488 | tf_op jit(solution)/shard_map/ppermute | solution.py:697
  70.4 0.1 collective-permute-start.22
  70.5 3.2 %collective-permute-start.23 = (bf16[4,288,128]{2,1,0:T(8,128)(2,1)S(1)}, bf16[4,288,128]{2,1,0:T(8,128)(2,1)S(1)}, u32[]{:S(2)}, u32[]{:S(2)}) collective-permute-start(bf16[4,288,128]{2,1,0:T(8,128)(2,1)S(1)} %constant_dynamic-update-slice_fusion.8.refs_0_), channel_id=1, source_target_pairs={{0,1},{1,0},{2,3},{3,2},{4,5},{5,4},{6,7},{7,6},{8,9},{9,8},{10,11... | collective-permute-start | bytes 884744 | tf_op jit(solution)/shard_map/ppermute | solution.py:697
  73.7 1.0 %assemble.1 = (f32[4,192,196]{2,1,0:T(8,128)}, bf16[4,192]{1,0:T(4,128)(2,1)}, bf16[4,192]{1,0:T(4,128)(2,1)}) custom-call(f32[2,192,208]{2,1,0:T(8,128)S(1)} %get-tuple-element.197.own_half, bf16[2,208,208]{2,1,0:T(8,128)(2,1)S(1)} %collective-permute-done.6.half_got, bf16[16,192]{1,0:T(8,128)(2,1)S(1)} %get-tuple-element.199.class_own), custom_call_target="tpu_custom_call" | custom-call | bytes 1 | tf_op jit(solution)/shard_map/assemble/pallas_call | solution.py:676
  74.7 2.4 %collective-permute-done.19 = bf16[688,128]{1,0:T(8,128)(2,1)S(1)} collective-permute-done((bf16[688,128]{1,0:T(8,128)(2,1)S(1)}, bf16[688,128]{1,0:T(8,128)(2,1)S(1)}, u32[]{:S(2)}, u32[]{:S(2)}) %collective-permute-start.19) | collective-permute-done | bytes 176160 | tf_op jit(solution)/shard_map/ppermute | solution.py:697
  77.2 0.7 collective-permute-start.21
  77.8 0.7 vector_outputs.1
  78.5 1.3 %collective-permute-done.22.refs_2_ = bf16[4,288,128]{2,1,0:T(8,128)(2,1)S(1)} collective-permute-done((bf16[4,288,128]{2,1,0:T(8,128)(2,1)S(1)}, bf16[4,288,128]{2,1,0:T(8,128)(2,1)S(1)}, u32[]{:S(2)}, u32[]{:S(2)}) %collective-permute-start.22) | collective-permute-done | bytes 294944 | tf_op jit(solution)/shard_map/ppermute | solution.py:697
  79.8 0.3 collective-permute-done.23.refs_4_
  80.0 0.2 collective-permute-start.25
  80.2 0.4 collective-permute-start.26
  80.5 1.3 %collective-permute-start.29 = (bf16[4,288,128]{2,1,0:T(8,128)(2,1)S(1)}, bf16[4,288,128]{2,1,0:T(8,128)(2,1)S(1)}, u32[]{:S(2)}, u32[]{:S(2)}) collective-permute-start(bf16[4,288,128]{2,1,0:T(8,128)(2,1)S(1)} %collective-permute-done.22.refs_2_), channel_id=1, source_target_pairs={{0,1},{1,0},{2,3},{3,2},{4,5},{5,4},{6,7},{7,6},{8,9},{9,8},{10,11... | collective-permute-start | bytes 884744 | tf_op jit(solution)/shard_map/ppermute | solution.py:697
  81.9 0.1 collective-permute-start.27
  82.0 0.4 collective-permute-done.21
  82.5 1.5 %collective-permute-start.24 = (bf16[8,144,128]{2,1,0:T(8,128)(2,1)S(1)}, bf16[8,144,128]{2,1,0:T(8,128)(2,1)S(1)}, u32[]{:S(2)}, u32[]{:S(2)}) collective-permute-start(bf16[8,144,128]{2,1,0:T(8,128)(2,1)S(1)} %constant_dynamic-update-slice_fusion.10.refs_6_), channel_id=1, source_target_pairs={{0,1},{1,0},{2,3},{3,2},{4,5},{5,4},{6,7},{7,6},{8,9},{9,8},{10,11... | collective-permute-start | bytes 884744 | tf_op jit(solution)/shard_map/ppermute | solution.py:697
  84.0 0.1 class_gradients.1
  84.1 3.2 %collective-permute-done.29.refs_8_ = bf16[4,288,128]{2,1,0:T(8,128)(2,1)S(1)} collective-permute-done((bf16[4,288,128]{2,1,0:T(8,128)(2,1)S(1)}, bf16[4,288,128]{2,1,0:T(8,128)(2,1)S(1)}, u32[]{:S(2)}, u32[]{:S(2)}) %collective-permute-start.29) | collective-permute-done | bytes 294944 | tf_op jit(solution)/shard_map/ppermute | solution.py:697
  87.3 3.1 %first_outputs.1 = (f32[384,1152]{1,0:T(8,128)}, f32[384,384]{1,0:T(8,128)}, f32[384,1536]{1,0:T(8,128)}, f32[1536,384]{1,0:T(8,128)}) custom-call(bf16[4,288,128]{2,1,0:T(8,128)(2,1)S(1)} %constant_dynamic-update-slice_fusion.8.refs_0_, ...), custom_call_target="tpu_custom_call", output_to_operand_aliasing={{0}: (9, {}), {1}: (10, {}), {2}: (11, {}), {3}: (12, {})} | custom-call | bytes 1 | tf_op jit(solution)/shard_map/first_outputs/pallas_call | solution.py:676
  90.3 0.7 collective-permute-start.30
  91.0 0.1 collective-permute-start.31
  91.1 1.1 %collective-permute-done.30.refs_1_ = bf16[4,288,128]{2,1,0:T(8,128)(2,1)S(1)} collective-permute-done((bf16[4,288,128]{2,1,0:T(8,128)(2,1)S(1)}, bf16[4,288,128]{2,1,0:T(8,128)(2,1)S(1)}, u32[]{:S(2)}, u32[]{:S(2)}) %collective-permute-start.30) | collective-permute-done | bytes 294944 | tf_op jit(solution)/shard_map/ppermute | solution.py:691
  92.2 0.4 collective-permute-done.31.refs_2_
  92.7 1.4 %last_outputs.1 = (f32[384,1152]{1,0:T(8,128)}, f32[384,384]{1,0:T(8,128)}, f32[384,1536]{1,0:T(8,128)}, f32[1536,384]{1,0:T(8,128)}) custom-call(bf16[8,144,128]{2,1,0:T(8,128)(2,1)S(1)} %collective-permute-done.24.refs_0_, ...), custom_call_target="tpu_custom_call", output_to_operand_aliasing={{0}: (3, {}), {1}: (4, {}), {2}: (5, {}), {3}: (6, {})} | custom-call | bytes 1 | tf_op jit(solution)/shard_map/last_outputs/pallas_call | solution.py:676
  (80 shorter events, 0.9 us)
Async XLA Ops:
  0.7 3.9 %copy-start.1 = (bf16[1,384,1536]{2,1,0:T(8,128)(2,1)S(1)}, bf16[1,384,1536]{2,1,0:T(8,128)(2,1)}, u32[]{:S(2)}) copy-start(bf16[1,384,1536]{2,1,0:T(8,128)(2,1)} %param.37) | copy-start | bytes 3538948
  0.7 4.4 %copy-start.3 = (bf16[1,384,384]{2,1,0:T(8,128)(2,1)S(1)}, bf16[1,384,384]{2,1,0:T(8,128)(2,1)}, u32[]{:S(2)}) copy-start(bf16[1,384,384]{2,1,0:T(8,128)(2,1)} %param.32) | copy-start | bytes 884740
  0.7 3.8 %collective-permute-start.1 = (bf16[384,1152]{1,0:T(8,128)(2,1)}, bf16[384,1152]{1,0:T(8,128)(2,1)S(1)}, u32[]{:S(2)}, u32[]{:S(2)}) collective-permute-start(bf16[384,1152]{1,0:T(8,128)(2,1)} %bitcast.28), channel_id=1, source_target_pairs={{0,16},{16,0},{1,17},{17,1},{2,18},{18,2},{3,19},{19,3},{4,20},{20... | collective-permute-start | bytes 2654216 | tf_op jit(solution)/shard_map/ppermute | solution.py:691
  1.2 4.2 %copy-start.11 = (bf16[8,8]{1,0:T(8,128)(2,1)S(1)}, bf16[8,8]{1,0:T(8,128)(2,1)}, u32[]{:S(2)}) copy-start(bf16[8,8]{1,0:T(8,128)(2,1)} %refs_11_.1) | copy-start | bytes 388
  1.2 4.2 %copy-start.12 = (bf16[8,8]{1,0:T(8,128)(2,1)S(1)}, bf16[8,8]{1,0:T(8,128)(2,1)}, u32[]{:S(2)}) copy-start(bf16[8,8]{1,0:T(8,128)(2,1)} %refs_10_.1) | copy-start | bytes 388
  2.9 2.5 %copy-start = (bf16[1,384,1152]{2,1,0:T(8,128)(2,1)S(1)}, bf16[1,384,1152]{2,1,0:T(8,128)(2,1)}, u32[]{:S(2)}) copy-start(bf16[1,384,1152]{2,1,0:T(8,128)(2,1)} %param.27) | copy-start | bytes 2654212
  2.9 2.5 %copy-start.4 = (bf16[16,384]{1,0:T(8,128)(2,1)S(1)}, bf16[16,384]{1,0:T(8,128)(2,1)}, u32[]{:S(2)}) copy-start(bf16[16,384]{1,0:T(8,128)(2,1)} %get-tuple-element.129.vec_own.refs_7_.refs_6_) | copy-start | bytes 36868
  2.9 2.5 %copy-start.5 = (s32[4,196]{1,0:T(4,128)S(1)}, s32[4,196]{1,0:T(4,128)}, u32[]{:S(2)}) copy-start(s32[4,196]{1,0:T(4,128)} %refs_2_.5) | copy-start | bytes 9412
  3.0 2.5 %copy-start.8 = (f32[1,384]{1,0:T(1,128)S(1)}, f32[1,384]{1,0:T(1,128)}, u32[]{:S(2)}) copy-start(f32[1,384]{1,0:T(1,128)} %get-tuple-element.130.bias_ref.refs_11_) | copy-start | bytes 4612
  3.0 1.5 %collective-permute-start = (bf16[16,384]{1,0:T(8,128)(2,1)}, bf16[16,384]{1,0:T(8,128)(2,1)S(1)}, u32[]{:S(2)}, u32[]{:S(2)}) collective-permute-start(bf16[16,384]{1,0:T(8,128)(2,1)} %get-tuple-element.129.vec_own.refs_7_.refs_6_), channel_id=1, source_target_pairs={{0,16},{16,0},{1,17},{17,1},{2,18},{18,2},{3,19},{19,3},{4,20},{20... | collective-permute-start | bytes 36872 | tf_op jit(solution)/shard_map/ppermute | solution.py:691
  4.5 5.3 %copy-start.2 = (bf16[1,1536,384]{2,1,0:T(8,128)(2,1)S(1)}, bf16[1,1536,384]{2,1,0:T(8,128)(2,1)}, u32[]{:S(2)}) copy-start(bf16[1,1536,384]{2,1,0:T(8,128)(2,1)} %param.39) | copy-start | bytes 3538948
  4.5 5.3 %copy-start.9 = (bf16[4,384]{1,0:T(4,128)(2,1)S(1)}, bf16[4,384]{1,0:T(4,128)(2,1)}, u32[]{:S(2)}) copy-start(bf16[4,384]{1,0:T(4,128)(2,1)} %class_ref.1) | copy-start | bytes 9220
  4.5 5.3 %copy-start.10 = (bf16[4,384]{1,0:T(4,128)(2,1)S(1)}, bf16[4,384]{1,0:T(4,128)(2,1)}, u32[]{:S(2)}) copy-start(bf16[4,384]{1,0:T(4,128)(2,1)} %cot_ref.1) | copy-start | bytes 9220
  4.5 5.2 %collective-permute-start.3 = (bf16[384,1536]{1,0:T(8,128)(2,1)S(1)}, bf16[384,1536]{1,0:T(8,128)(2,1)S(1)}, u32[]{:S(2)}, u32[]{:S(2)}) collective-permute-start(bf16[384,1536]{1,0:T(8,128)(2,1)S(1)} %bitcast.33), channel_id=1, source_target_pairs={{0,16},{16,0},{1,17},{17,1},{2,18},{18,2},{3,19},{19,3},{4,20},{20... | collective-permute-start | bytes 3538952 | tf_op jit(solution)/shard_map/ppermute | solution.py:691
  4.9 4.9 %collective-permute-start.4 = (bf16[1536,384]{1,0:T(8,128)(2,1)}, bf16[1536,384]{1,0:T(8,128)(2,1)S(1)}, u32[]{:S(2)}, u32[]{:S(2)}) collective-permute-start(bf16[1536,384]{1,0:T(8,128)(2,1)} %bitcast.36), channel_id=1, source_target_pairs={{0,16},{16,0},{1,17},{17,1},{2,18},{18,2},{3,19},{19,3},{4,20},{20... | collective-permute-start | bytes 3538952 | tf_op jit(solution)/shard_map/ppermute | solution.py:691
  5.1 4.6 %collective-permute-start.2 = (bf16[384,384]{1,0:T(8,128)(2,1)S(1)}, bf16[384,384]{1,0:T(8,128)(2,1)S(1)}, u32[]{:S(2)}, u32[]{:S(2)}) collective-permute-start(bf16[384,384]{1,0:T(8,128)(2,1)S(1)} %bitcast.39), channel_id=1, source_target_pairs={{0,16},{16,0},{1,17},{17,1},{2,18},{18,2},{3,19},{19,3},{4,20},{20... | collective-permute-start | bytes 884744 | tf_op jit(solution)/shard_map/ppermute | solution.py:691
  9.8 12.6 %copy-start.6 = (f32[8,384]{1,0:T(8,128)S(1)}, f32[8,384]{1,0:T(8,128)}, u32[]{:S(2)}) copy-start(f32[8,384]{1,0:T(8,128)} %get-tuple-element.142.refs_12_) | copy-start | bytes 36868
  9.8 12.6 %copy-start.7 = (f32[8,384]{1,0:T(8,128)S(1)}, f32[8,384]{1,0:T(8,128)}, u32[]{:S(2)}) copy-start(f32[8,384]{1,0:T(8,128)} %get-tuple-element.143.refs_13_) | copy-start | bytes 36868
  22.0 4.2 %collective-permute-start.5 = (bf16[17,288,128]{2,1,0:T(8,128)(2,1)S(1)}, bf16[17,288,128]{2,1,0:T(8,128)(2,1)S(1)}, u32[]{:S(2)}, u32[]{:S(2)}) collective-permute-start(bf16[17,288,128]{2,1,0:T(8,128)(2,1)S(1)} %get-tuple-element.137), channel_id=1, source_target_pairs={{0,16},{16,0},{1,17},{17,1},{2,18},{18,2},{3,19},{19,3},{4,20},{20... | collective-permute-start | bytes 3760136 | tf_op jit(solution)/shard_map/ppermute | solution.py:691
  26.4 10.6 %collective-permute-start.7 = (bf16[8,288,128]{2,1,0:T(8,128)(2,1)S(1)}, bf16[8,288,128]{2,1,0:T(8,128)(2,1)S(1)}, u32[]{:S(2)}, u32[]{:S(2)}) collective-permute-start(bf16[8,288,128]{2,1,0:T(8,128)(2,1)S(1)} %add_convert_fusion), channel_id=1, source_target_pairs={{0,1},{1,0},{2,3},{3,2},{4,5},{5,4},{6,7},{7,6},{8,9},{9,8},{10,11... | collective-permute-start | bytes 1769480 | tf_op jit(solution)/shard_map/ppermute | solution.py:697
  35.8 3.5 %collective-permute-start.9 = (bf16[17,144,128]{2,1,0:T(8,128)(2,1)S(1)}, bf16[17,144,128]{2,1,0:T(8,128)(2,1)S(1)}, u32[]{:S(2)}, u32[]{:S(2)}) collective-permute-start(bf16[17,144,128]{2,1,0:T(8,128)(2,1)S(1)} %get-tuple-element.164), channel_id=1, source_target_pairs={{0,16},{16,0},{1,17},{17,1},{2,18},{18,2},{3,19},{19,3},{4,20},{20... | collective-permute-start | bytes 1880072 | tf_op jit(solution)/shard_map/ppermute | solution.py:691
  35.9 5.1 %collective-permute-start.6 = (bf16[2,208,208]{2,1,0:T(8,128)(2,1)S(1)}, bf16[2,208,208]{2,1,0:T(8,128)(2,1)S(1)}, u32[]{:S(2)}, u32[]{:S(2)}) collective-permute-start(bf16[2,208,208]{2,1,0:T(8,128)(2,1)S(1)} %get-tuple-element.157), channel_id=1, source_target_pairs={{0,16},{16,0},{1,17},{17,1},{2,18},{18,2},{3,19},{19,3},{4,20},{20... | collective-permute-start | bytes 519176 | tf_op jit(solution)/shard_map/ppermute | solution.py:691
  37.2 9.7 %collective-permute-start.8 = (bf16[4,288,128]{2,1,0:T(8,128)(2,1)S(1)}, bf16[4,288,128]{2,1,0:T(8,128)(2,1)S(1)}, u32[]{:S(2)}, u32[]{:S(2)}) collective-permute-start(bf16[4,288,128]{2,1,0:T(8,128)(2,1)S(1)} %add_convert_fusion.2), channel_id=1, source_target_pairs={{0,2},{1,3},{2,0},{3,1},{4,6},{5,7},{6,4},{7,5},{8,10},{9,11},{10,... | collective-permute-start | bytes 884744 | tf_op jit(solution)/shard_map/ppermute | solution.py:697
  39.4 10.0 %collective-permute-start.12 = (bf16[1264,128]{1,0:T(8,128)(2,1)S(1)}, bf16[1264,128]{1,0:T(8,128)(2,1)S(1)}, u32[]{:S(2)}, u32[]{:S(2)}) collective-permute-start(bf16[1264,128]{1,0:T(8,128)(2,1)S(1)} %pad_maximum_fusion), channel_id=1, source_target_pairs={{0,1},{1,0},{2,3},{3,2},{4,5},{5,4},{6,7},{7,6},{8,9},{9,8},{10,11... | collective-permute-start | bytes 970760 | tf_op jit(solution)/shard_map/ppermute | solution.py:697
  41.0 10.1 %collective-permute-start.11 = (bf16[2,144,128]{2,1,0:T(8,128)(2,1)S(1)}, bf16[2,144,128]{2,1,0:T(8,128)(2,1)S(1)}, u32[]{:S(2)}, u32[]{:S(2)}) collective-permute-start(bf16[2,144,128]{2,1,0:T(8,128)(2,1)S(1)} %constant_dynamic-update-slice_fusion), channel_id=1, source_target_pairs={{16,24},{17,25},{18,26},{19,27},{20,28},{21,29},{22,30},{23,31},{2... | collective-permute-start | bytes 221192 | tf_op jit(solution)/shard_map/ppermute | solution.py:697
  46.9 5.6 %collective-permute-start.10 = (bf16[2,288,128]{2,1,0:T(8,128)(2,1)S(1)}, bf16[2,288,128]{2,1,0:T(8,128)(2,1)S(1)}, u32[]{:S(2)}, u32[]{:S(2)}) collective-permute-start(bf16[2,288,128]{2,1,0:T(8,128)(2,1)S(1)} %add_convert_fusion.8), channel_id=1, source_target_pairs={{0,4},{1,5},{2,6},{3,7},{4,0},{5,1},{6,2},{7,3},{8,12},{9,13},{10,... | collective-permute-start | bytes 442376 | tf_op jit(solution)/shard_map/ppermute | solution.py:697
  49.5 6.2 %collective-permute-start.15 = (bf16[688,128]{1,0:T(8,128)(2,1)S(1)}, bf16[688,128]{1,0:T(8,128)(2,1)S(1)}, u32[]{:S(2)}, u32[]{:S(2)}) collective-permute-start(bf16[688,128]{1,0:T(8,128)(2,1)S(1)} %pad_maximum_fusion.1), channel_id=1, source_target_pairs={{0,2},{1,3},{2,0},{3,1},{4,6},{5,7},{6,4},{7,5},{8,10},{9,11},{10,... | collective-permute-start | bytes 528392 | tf_op jit(solution)/shard_map/ppermute | solution.py:697
  51.1 6.4 %collective-permute-start.14 = (bf16[4,144,128]{2,1,0:T(8,128)(2,1)S(1)}, bf16[4,144,128]{2,1,0:T(8,128)(2,1)S(1)}, u32[]{:S(2)}, u32[]{:S(2)}) collective-permute-start(bf16[4,144,128]{2,1,0:T(8,128)(2,1)S(1)} %constant_dynamic-update-slice_fusion.2), channel_id=1, source_target_pairs={{16,20},{17,21},{18,22},{19,23},{20,16},{21,17},{22,18},{23,19},{2... | collective-permute-start | bytes 442376 | tf_op jit(solution)/shard_map/ppermute | solution.py:697
  52.6 9.4 %collective-permute-start.13 = (bf16[2,288,128]{2,1,0:T(8,128)(2,1)S(1)}, bf16[2,288,128]{2,1,0:T(8,128)(2,1)S(1)}, u32[]{:S(2)}, u32[]{:S(2)}) collective-permute-start(bf16[2,288,128]{2,1,0:T(8,128)(2,1)S(1)} %pad_maximum_fusion.4), channel_id=1, source_target_pairs={{0,8},{1,9},{2,10},{3,11},{4,12},{5,13},{6,14},{7,15},{8,0},{9,1},... | collective-permute-start | bytes 442376 | tf_op jit(solution)/shard_map/ppermute | solution.py:697
  55.9 7.1 %collective-permute-start.18 = (bf16[688,128]{1,0:T(8,128)(2,1)S(1)}, bf16[688,128]{1,0:T(8,128)(2,1)S(1)}, u32[]{:S(2)}, u32[]{:S(2)}) collective-permute-start(bf16[688,128]{1,0:T(8,128)(2,1)S(1)} %pad_maximum_fusion.2), channel_id=1, source_target_pairs={{0,4},{1,5},{2,6},{3,7},{4,0},{5,1},{6,2},{7,3},{8,12},{9,13},{10,... | collective-permute-start | bytes 528392 | tf_op jit(solution)/shard_map/ppermute | solution.py:697
  57.6 5.5 %collective-permute-start.16 = (bf16[8,144,128]{2,1,0:T(8,128)(2,1)S(1)}, bf16[8,144,128]{2,1,0:T(8,128)(2,1)S(1)}, u32[]{:S(2)}, u32[]{:S(2)}) collective-permute-start(bf16[8,144,128]{2,1,0:T(8,128)(2,1)S(1)} %constant_dynamic-update-slice_fusion.4), channel_id=1, source_target_pairs={{16,17},{17,16},{18,19},{19,18},{20,21},{21,20},{22,23},{23,22},{2... | collective-permute-start | bytes 884744 | tf_op jit(solution)/shard_map/ppermute | solution.py:697
  63.2 14.0 %collective-permute-start.20 = (bf16[16,144,128]{2,1,0:T(8,128)(2,1)S(1)}, bf16[16,144,128]{2,1,0:T(8,128)(2,1)S(1)}, u32[]{:S(2)}, u32[]{:S(2)}) collective-permute-start(bf16[16,144,128]{2,1,0:T(8,128)(2,1)S(1)} %constant_dynamic-update-slice_fusion.6.refs_0_), channel_id=1, source_target_pairs={{16,18},{17,19},{18,16},{19,17},{20,22},{21,23},{22,20},{23,21},{2... | collective-permute-start | bytes 1769480 | tf_op jit(solution)/shard_map/ppermute | solution.py:697
  63.9 6.5 %collective-permute-start.17 = (bf16[2,288,128]{2,1,0:T(8,128)(2,1)S(1)}, bf16[2,288,128]{2,1,0:T(8,128)(2,1)S(1)}, u32[]{:S(2)}, u32[]{:S(2)}) collective-permute-start(bf16[2,288,128]{2,1,0:T(8,128)(2,1)S(1)} %add_convert_fusion.5), channel_id=1, source_target_pairs={{0,4},{1,5},{2,6},{3,7},{4,0},{5,1},{6,2},{7,3},{8,12},{9,13},{10,... | collective-permute-start | bytes 442376 | tf_op jit(solution)/shard_map/ppermute | solution.py:697
  65.4 11.7 %collective-permute-start.19 = (bf16[688,128]{1,0:T(8,128)(2,1)S(1)}, bf16[688,128]{1,0:T(8,128)(2,1)S(1)}, u32[]{:S(2)}, u32[]{:S(2)}) collective-permute-start(bf16[688,128]{1,0:T(8,128)(2,1)S(1)} %pad_maximum_fusion.3), channel_id=1, source_target_pairs={{0,8},{1,9},{2,10},{3,11},{4,12},{5,13},{6,14},{7,15},{8,0},{9,1},... | collective-permute-start | bytes 528392 | tf_op jit(solution)/shard_map/ppermute | solution.py:697
  70.4 9.4 %collective-permute-start.22 = (bf16[4,288,128]{2,1,0:T(8,128)(2,1)S(1)}, bf16[4,288,128]{2,1,0:T(8,128)(2,1)S(1)}, u32[]{:S(2)}, u32[]{:S(2)}) collective-permute-start(bf16[4,288,128]{2,1,0:T(8,128)(2,1)S(1)} %constant_dynamic-update-slice_fusion.8.refs_0_), channel_id=1, source_target_pairs={{0,2},{1,3},{2,0},{3,1},{4,6},{5,7},{6,4},{7,5},{8,10},{9,11},{10,... | collective-permute-start | bytes 884744 | tf_op jit(solution)/shard_map/ppermute | solution.py:697
  70.5 9.5 %collective-permute-start.23 = (bf16[4,288,128]{2,1,0:T(8,128)(2,1)S(1)}, bf16[4,288,128]{2,1,0:T(8,128)(2,1)S(1)}, u32[]{:S(2)}, u32[]{:S(2)}) collective-permute-start(bf16[4,288,128]{2,1,0:T(8,128)(2,1)S(1)} %constant_dynamic-update-slice_fusion.8.refs_0_), channel_id=1, source_target_pairs={{0,1},{1,0},{2,3},{3,2},{4,5},{5,4},{6,7},{7,6},{8,9},{9,8},{10,11... | collective-permute-start | bytes 884744 | tf_op jit(solution)/shard_map/ppermute | solution.py:697
  77.2 5.2 %collective-permute-start.21 = (bf16[4,144,128]{2,1,0:T(8,128)(2,1)S(1)}, bf16[4,144,128]{2,1,0:T(8,128)(2,1)S(1)}, u32[]{:S(2)}, u32[]{:S(2)}) collective-permute-start(bf16[4,144,128]{2,1,0:T(8,128)(2,1)S(1)} %fusion), channel_id=1, source_target_pairs={{0,2},{1,3},{2,0},{3,1},{4,6},{5,7},{6,4},{7,5},{8,10},{9,11},{10,... | collective-permute-start | bytes 442376 | tf_op jit(solution)/shard_map/ppermute | solution.py:697
  80.0 2.5 %collective-permute-start.25 = (bf16[4,288,128]{2,1,0:T(8,128)(2,1)S(1)}, bf16[4,288,128]{2,1,0:T(8,128)(2,1)S(1)}, u32[]{:S(2)}, u32[]{:S(2)}) collective-permute-start(bf16[4,288,128]{2,1,0:T(8,128)(2,1)S(1)} %constant_dynamic-update-slice_fusion.8.refs_0_), channel_id=1, source_target_pairs={{0,16},{16,0},{1,17},{17,1},{2,18},{18,2},{3,19},{19,3},{4,20},{20... | collective-permute-start | bytes 884744 | tf_op jit(solution)/shard_map/ppermute | solution.py:691
  80.2 3.9 %collective-permute-start.26 = (bf16[4,288,128]{2,1,0:T(8,128)(2,1)S(1)}, bf16[4,288,128]{2,1,0:T(8,128)(2,1)S(1)}, u32[]{:S(2)}, u32[]{:S(2)}) collective-permute-start(bf16[4,288,128]{2,1,0:T(8,128)(2,1)S(1)} %collective-permute-done.22.refs_2_), channel_id=1, source_target_pairs={{0,16},{16,0},{1,17},{17,1},{2,18},{18,2},{3,19},{19,3},{4,20},{20... | collective-permute-start | bytes 884744 | tf_op jit(solution)/shard_map/ppermute | solution.py:691
  80.5 6.7 %collective-permute-start.29 = (bf16[4,288,128]{2,1,0:T(8,128)(2,1)S(1)}, bf16[4,288,128]{2,1,0:T(8,128)(2,1)S(1)}, u32[]{:S(2)}, u32[]{:S(2)}) collective-permute-start(bf16[4,288,128]{2,1,0:T(8,128)(2,1)S(1)} %collective-permute-done.22.refs_2_), channel_id=1, source_target_pairs={{0,1},{1,0},{2,3},{3,2},{4,5},{5,4},{6,7},{7,6},{8,9},{9,8},{10,11... | collective-permute-start | bytes 884744 | tf_op jit(solution)/shard_map/ppermute | solution.py:697
  81.9 2.2 %collective-permute-start.27 = (bf16[4,288,128]{2,1,0:T(8,128)(2,1)S(1)}, bf16[4,288,128]{2,1,0:T(8,128)(2,1)S(1)}, u32[]{:S(2)}, u32[]{:S(2)}) collective-permute-start(bf16[4,288,128]{2,1,0:T(8,128)(2,1)S(1)} %collective-permute-done.23.refs_4_), channel_id=1, source_target_pairs={{0,16},{16,0},{1,17},{17,1},{2,18},{18,2},{3,19},{19,3},{4,20},{20... | collective-permute-start | bytes 884744 | tf_op jit(solution)/shard_map/ppermute | solution.py:691
  82.4 4.9 %collective-permute-start.28 = (bf16[8,144,128]{2,1,0:T(8,128)(2,1)S(1)}, bf16[8,144,128]{2,1,0:T(8,128)(2,1)S(1)}, u32[]{:S(2)}, u32[]{:S(2)}) collective-permute-start(bf16[8,144,128]{2,1,0:T(8,128)(2,1)S(1)} %constant_dynamic-update-slice_fusion.10.refs_6_), channel_id=1, source_target_pairs={{0,16},{16,0},{1,17},{17,1},{2,18},{18,2},{3,19},{19,3},{4,20},{20... | collective-permute-start | bytes 884744 | tf_op jit(solution)/shard_map/ppermute | solution.py:691
  82.5 8.5 %collective-permute-start.24 = (bf16[8,144,128]{2,1,0:T(8,128)(2,1)S(1)}, bf16[8,144,128]{2,1,0:T(8,128)(2,1)S(1)}, u32[]{:S(2)}, u32[]{:S(2)}) collective-permute-start(bf16[8,144,128]{2,1,0:T(8,128)(2,1)S(1)} %constant_dynamic-update-slice_fusion.10.refs_6_), channel_id=1, source_target_pairs={{0,1},{1,0},{2,3},{3,2},{4,5},{5,4},{6,7},{7,6},{8,9},{9,8},{10,11... | collective-permute-start | bytes 884744 | tf_op jit(solution)/shard_map/ppermute | solution.py:697
  90.3 1.9 %collective-permute-start.30 = (bf16[4,288,128]{2,1,0:T(8,128)(2,1)S(1)}, bf16[4,288,128]{2,1,0:T(8,128)(2,1)S(1)}, u32[]{:S(2)}, u32[]{:S(2)}) collective-permute-start(bf16[4,288,128]{2,1,0:T(8,128)(2,1)S(1)} %collective-permute-done.29.refs_8_), channel_id=1, source_target_pairs={{0,16},{16,0},{1,17},{17,1},{2,18},{18,2},{3,19},{19,3},{4,20},{20... | collective-permute-start | bytes 884744 | tf_op jit(solution)/shard_map/ppermute | solution.py:691
  91.0 1.6 %collective-permute-start.31 = (bf16[8,144,128]{2,1,0:T(8,128)(2,1)S(1)}, bf16[8,144,128]{2,1,0:T(8,128)(2,1)S(1)}, u32[]{:S(2)}, u32[]{:S(2)}) collective-permute-start(bf16[8,144,128]{2,1,0:T(8,128)(2,1)S(1)} %collective-permute-done.24.refs_0_), channel_id=1, source_target_pairs={{0,16},{16,0},{1,17},{17,1},{2,18},{18,2},{3,19},{19,3},{4,20},{20... | collective-permute-start | bytes 884744 | tf_op jit(solution)/shard_map/ppermute | solution.py:691

commit v6 on v5

--- a/solution.py
+++ b/solution.py
@@ -502,20 +502,26 @@
     lane = lax.broadcasted_iota(jnp.int32, (width, 128), 1)
     feature = lax.broadcasted_iota(jnp.int32, (width, 128), 0)
     groups = jnp.where((feature >= lane * size) & (feature < lane * size + size), 1.0, 0.0)
-    small = lax.dot_general(
-        sum0[...] + sum1[...], groups, (((1,), (0,)), ((), ())),
-        preferred_element_type=F32, precision=lax.Precision.HIGHEST,
-    )
+    later = jnp.where((feature >= (lane - HEADS) * size) & (feature < (lane - HEADS) * size + size), 1.0, 0.0)
+
+    def head_sums(rows, heads):
+        return lax.dot_general(
+            rows, heads, (((1,), (0,)), ((), ())), preferred_element_type=F32, precision=lax.Precision.HIGHEST
+        )
+
+    sums = sum0[...] + sum1[...]
+    at_row = lax.broadcasted_iota(jnp.int32, (16, 128), 0)
+    small = head_sums(sums[:16], groups) + jnp.where(at_row == 0, head_sums(sums[16:24], later)[0:1], 0.0)
+    high = small.astype(BF16).astype(F32)
     tall = jnp.concatenate(
-        [vec0[:14, :128], small[16:17], vec0[15:, :128]]
-        + [vec0[:, k * 128 : (k + 1) * 128] for k in (1, 2)]
+        [vec0[:, k * 128 : (k + 1) * 128] for k in range(3)]
         + [vec_in1[:, k * 128 : (k + 1) * 128] for k in range(3)]
-        + [small[:16]],
+        + [high, small - high],
         axis=0,
     )
     vec_part[...] = tall.astype(BF16)
-    send_ref[16, :112] = tall.astype(BF16)
-    send_ref[16, 112:] = jnp.zeros((32, 128), BF16)
+    send_ref[16, :128] = tall.astype(BF16)
+    send_ref[16, 128:] = jnp.zeros((16, 128), BF16)
     block_copy(blocks, kept_ref, 0, 16)
     block_copy(blocks, send_ref, 16, 16)
 
@@ -584,9 +590,10 @@
         for k in range(out.shape[1] // width):
             out[:, k * width : (k + 1) * width] = rows[at : at + 1]
             at += 1
-    pre_out[...] = tall[96:104, 0:HEADS]
-    post_out[...] = tall[104:112].T[0:HEADS]
-    bias_out[...] = tall[14:15, 0:HEADS]
+    small = tall[96:112] + tall[112:128]
+    pre_out[...] = small[0:8, 0:HEADS]
+    post_out[...] = small[8:16].T[0:HEADS]
+    bias_out[...] = small[0:1, HEADS : 2 * HEADS]
 
 
 def class_gradients(*refs):
@@ -702,6 +709,13 @@
     return sum(parts[1:], parts[0]).astype(BF16)
 
 
+def ridden_sum(left, right):
+    both = left.astype(F32) + right.astype(F32)
+    small = both[96:112] + both[112:]
+    high = lax.reduce_precision(small, 8, 7)
+    return jnp.concatenate([both[:96], high, small - high], axis=0).astype(BF16)
+
+
 def after(arrays, *others):
     return lax.optimization_barrier((arrays, others))[0]
 
@@ -728,7 +742,7 @@
         self.leaving = jnp.concatenate([message.reshape(-1, 128), self.rider])
         got = exchanged(self.leaving, bits)
         rows = got.shape[0] - self.rider.shape[0]
-        self.rider = total([self.rider, got[rows:]], 0, self.rider.shape[0])
+        self.rider = ridden_sum(self.rider, got[rows:])
         return got[:rows].reshape(message.shape)
 
     def step(self):
@@ -859,14 +873,14 @@
         input_gradients,
         [(VM, mg), (VM, rows), (VM, hid), (VM, att), (VM, join0), (VM, join1), (VM, sum0), (VM, sum1), (VM, vec0),
          (VM, vec1), (VM, vec_own), (VM, vec_got), (HB, w_own), (HB, w_got), (VM, class_other)],
-        [((17, 144, 128), BF16), ((16, 144, 128), BF16), ((112, 128), BF16), ((IMGS, half, length), F32), ((IMGS, half + 16, length), BF16)],
+        [((17, 144, 128), BF16), ((16, 144, 128), BF16), ((128, 128), BF16), ((IMGS, half, length), F32), ((IMGS, half + 16, length), BF16)],
         [((width, 3 * width), BF16), ((flat, 3 * width), BF16), ((32, 144, 128), BF16)],
         "input_gradients",
         LIMIT_C,
         sems=1,
     )
     got2, half_got = swapped(send2), swapped(other_half)
-    stream2 = Stream((kept2, got2), SHORT, total([vec_part, got2[16, :112]], 0, 112))
+    stream2 = Stream((kept2, got2), SHORT, ridden_sum(vec_part, got2[16, :128]))
     def turn(*streams):
         for stream in streams:
             turn.last = stream.wait(*turn.last) or (stream.step(), stream.leaving)[1:]

time: 94.5 us -> 95.2 us (level)
  waiting for transfers between devices: 23.5 us -> 26 us
  starting transfers between devices: 31.6 us -> 29.5 us
    ppermute x18, waiting for transfers between devices: 21.9 us -> 24.5 us  [exchanged(): return lax.ppermute(array, ('pipe', 'dp'), pairs)]
    ppermute x18, starting transfers between devices: 27.7 us -> 25.7 us  [exchanged(): return lax.ppermute(array, ('pipe', 'dp'), pairs)]
  transfers between devices with their start and end apart: 32 -> 32, of which waited for: 13 -> 12; matrix products, arithmetic and copies ran while one was open for 3% -> 3% of each run, Pallas kernels for 22% -> 22%
where the time goes in v6:
time: 95.2 us; the launch traced here: 94.9 us
  Pallas kernels  34.9 us (37%)
  starting transfers between devices  29.5 us (31%)
  waiting for transfers between devices  26 us (27%)
  local copies, waits for them, and re-layouts  1.68 us (2%)
  between operations  1.53 us (2%)
  other arithmetic  1.29 us (1%)
    pallas_call x11, Pallas kernels, call(): pl.pallas_call(body, out_shape=[jax.ShapeDtypeStruct(shape, kind) for sha...  34.9 us
    ppermute x18, starting transfers between devices, exchanged(): return lax.ppermute(array, ('pipe', 'dp'), pairs)  25.7 us
    ppermute x18, waiting for transfers between devices, exchanged(): return lax.ppermute(array, ('pipe', 'dp'), pairs)  24.5 us
    ppermute x14, starting transfers between devices, swapped(): return lax.ppermute(array, 'pipe', [(0, 1), (1, 0)])  3.81 us
  transfers between devices with their start and end apart: 32, of which 12 were waited for; matrix products, arithmetic and copies ran while one was open for 3% of the time, Pallas kernels for 22%

profile of v6, /device:TPU:0, one launch (start us, length us, event | category | flops | bytes accessed | tf_op | source)
XLA Modules:
  0.0 94.9 jit_solution(7739943518081401298)
XLA Ops:
  0.7 0.5 collective-permute-start.1
  1.2 1.7 %prepare.1 = (bf16[16,384]{1,0:T(8,128)(2,1)}, f32[8,384]{1,0:T(8,128)}, f32[8,384]{1,0:T(8,128)}, f32[1,384]{1,0:T(1,128)}) custom-call(bf16[1,384]{1,0:T(2,128)(2,1)} %refs_0_.1, bf16[1,384]{1,0:T(2,128)(2,1)} %refs_1_.1, bf16[1,768]{1,0:T(2,128)(2,1)} %refs_2_.3, bf16[1,384]{1,0:T(2,128)(2,1)} %refs_3_.1, bf16[1,384]{1,0:T(2,128)(2,1)} %refs_4_.1, ...), custom_call_target="tpu_custom_call" | custom-call | bytes 1 | tf_op jit(solution)/shard_map/prepare/pallas_call | solution.py:683
  3.0 0.2 collective-permute-start
  3.1 1.3 %copy.49 = bf16[4,196,384]{2,1,0:T(8,128)(2,1)S(1)} copy(bf16[4,196,384]{2,0,1:T(4,128)(2,1)} %param.21) | data formatting | bytes 1204224 | tf_op args[0]
  4.5 0.4 collective-permute-start.3
  4.9 0.2 collective-permute-start.4
  5.1 0.3 collective-permute-start.2
  5.5 4.3 %attention_forward.1 = (bf16[2,208,384]{2,1,0:T(8,128)(2,1)S(1)}, bf16[2,208,384]{2,1,0:T(8,128)(2,1)S(1)}, bf16[2,256,384]{2,1,0:T(8,128)(2,1)S(1)}, bf16[2,256...) custom-call(f32[2,8,8]{2,1,0:T(8,128)S(1)} %maximum_convert_fusion.mixing.refs_0_, ...), custom_call_target="tpu_custom_call" | custom-call | bytes 1 | tf_op jit(solution)/shard_map/attention_forward/pallas_call | solution.py:683
  9.8 12.2 %middle_kernel.1 = (bf16[17,288,128]{2,1,0:T(8,128)(2,1)S(1)}, bf16[16,288,128]{2,1,0:T(8,128)(2,1)S(1)}, f32[2,208,384]{2,1,0:T(8,128)S(1)}, f32[16,384]{1,0:T(...) custom-call(bf16[2,208,384]{2,1,0:T(8,128)(2,1)S(1)} %get-tuple-elem, ...), custom_call_target="tpu_custom_call" | custom-call | bytes 1 | tf_op jit(solution)/shard_map/middle_kernel/pallas_call | solution.py:683
  22.0 0.4 collective-permute-start.5
  22.4 3.8 %attention_backward_0.1 = (bf16[208,1152]{1,0:T(8,128)(2,1)S(1)}, f32[24,384]{1,0:T(8,128)S(1)}) custom-call(f32[2,8,8]{2,1,0:T(8,128)S(1)} %maximum_convert_fusion.mixing.refs_0_, f32[2,208,384]{2,1,0:T(8,128)S(1)} %get-tuple-element.149.refs_1_.mg_ref, s32[4,196]{1,0:T(4,128)S(1)} %copy-done.5, bf16[2,256,384]{2,1,0:T(8,128)(2,1)S(1)} %get-tuple-element.138.refs_3_, ...), custom_call_target="tpu_custom_call" | custom-call | bytes 1 | tf_op jit(solution)/shard_map/attention_backward_0/pallas_call | solution.py:683
  26.2 0.2 add_convert_fusion
  26.4 2.8 %collective-permute-start.7 = (bf16[8,288,128]{2,1,0:T(8,128)(2,1)S(1)}, bf16[8,288,128]{2,1,0:T(8,128)(2,1)S(1)}, u32[]{:S(2)}, u32[]{:S(2)}) collective-permute-start(bf16[8,288,128]{2,1,0:T(8,128)(2,1)S(1)} %add_convert_fusion), channel_id=1, source_target_pairs={{0,1},{1,0},{2,3},{3,2},{4,5},{5,4},{6,7},{7,6},{8,9},{9,8},{10,11... | collective-permute-start | bytes 1769480 | tf_op jit(solution)/shard_map/ppermute | solution.py:704
  29.2 3.7 %attention_backward_1.1 = (bf16[208,1152]{1,0:T(8,128)(2,1)S(1)}, f32[24,384]{1,0:T(8,128)S(1)}) custom-call(f32[2,8,8]{2,1,0:T(8,128)S(1)} %maximum_convert_fusion.mixing.refs_0_, f32[2,208,384]{2,1,0:T(8,128)S(1)} %get-tuple-element.149.refs_1_.mg_ref, s32[4,196]{1,0:T(4,128)S(1)} %copy-done.5, bf16[2,256,384]{2,1,0:T(8,128)(2,1)S(1)} %get-tuple-element.138.refs_3_, ...), custom_call_target="tpu_custom_call" | custom-call | bytes 1 | tf_op jit(solution)/shard_map/attention_backward_1/pallas_call | solution.py:683
  32.8 3.0 %input_gradients.1 = (bf16[17,144,128]{2,1,0:T(8,128)(2,1)S(1)}, bf16[16,144,128]{2,1,0:T(8,128)(2,1)S(1)}, bf16[128,128]{1,0:T(8,128)(2,1)S(1)}, f32[2,192,208]{2,1,0:T(8,128)S(1)}, bf16[2,208,208]{2,1,0:T(8,128)(2,1)S(1)}) custom-call(f32[2,208,384]{2,1,0:T(8,128)S(1)} %get-tuple-element.149.refs_1_.mg_ref, bf16[4,208,384]{2,1,0:T(8,128)(2,1)S(1)} %pad.4.rows_ref, ...), custom_call_target="tpu_custom_call" | custom-call | bytes 1 | tf_op jit(solution)/shard_map/input_gradients/pallas_call | solution.py:683
  35.9 0.1 collective-permute-start.9
  36.0 0.5 collective-permute-start.6
  36.5 0.6 collective-permute-done.7
  37.0 0.1 add_convert_fusion.2
  37.2 2.1 %collective-permute-start.8 = (bf16[4,288,128]{2,1,0:T(8,128)(2,1)S(1)}, bf16[4,288,128]{2,1,0:T(8,128)(2,1)S(1)}, u32[]{:S(2)}, u32[]{:S(2)}) collective-permute-start(bf16[4,288,128]{2,1,0:T(8,128)(2,1)S(1)} %add_convert_fusion.2), channel_id=1, source_target_pairs={{0,2},{1,3},{2,0},{3,1},{4,6},{5,7},{6,4},{7,5},{8,10},{9,11},{10,... | collective-permute-start | bytes 884744 | tf_op jit(solution)/shard_map/ppermute | solution.py:704
  39.3 0.1 add_convert_fusion.1
  39.5 1.6 %collective-permute-start.12 = (bf16[1280,128]{1,0:T(8,128)(2,1)S(1)}, bf16[1280,128]{1,0:T(8,128)(2,1)S(1)}, u32[]{:S(2)}, u32[]{:S(2)}) collective-permute-start(bf16[1280,128]{1,0:T(8,128)(2,1)S(1)} %pad_maximum_fusion), channel_id=1, source_target_pairs={{0,1},{1,0},{2,3},{3,2},{4,5},{5,4},{6,7},{7,6},{8,9},{9,8},{10,11... | collective-permute-start | bytes 983048 | tf_op jit(solution)/shard_map/ppermute | solution.py:704
  41.0 0.7 collective-permute-start.11
  41.7 5.1 %collective-permute-done.8 = bf16[4,288,128]{2,1,0:T(8,128)(2,1)S(1)} collective-permute-done((bf16[4,288,128]{2,1,0:T(8,128)(2,1)S(1)}, bf16[4,288,128]{2,1,0:T(8,128)(2,1)S(1)}, u32[]{:S(2)}, u32[]{:S(2)}) %collective-permute-start.8) | collective-permute-done | bytes 294944 | tf_op jit(solution)/shard_map/ppermute | solution.py:704
  46.8 0.1 add_convert_fusion.8
  46.9 2.5 %collective-permute-start.10 = (bf16[2,288,128]{2,1,0:T(8,128)(2,1)S(1)}, bf16[2,288,128]{2,1,0:T(8,128)(2,1)S(1)}, u32[]{:S(2)}, u32[]{:S(2)}) collective-permute-start(bf16[2,288,128]{2,1,0:T(8,128)(2,1)S(1)} %add_convert_fusion.8), channel_id=1, source_target_pairs={{0,4},{1,5},{2,6},{3,7},{4,0},{5,1},{6,2},{7,3},{8,12},{9,13},{10,... | collective-permute-start | bytes 442376 | tf_op jit(solution)/shard_map/ppermute | solution.py:704
  49.6 1.6 %collective-permute-start.15 = (bf16[704,128]{1,0:T(8,128)(2,1)S(1)}, bf16[704,128]{1,0:T(8,128)(2,1)S(1)}, u32[]{:S(2)}, u32[]{:S(2)}) collective-permute-start(bf16[704,128]{1,0:T(8,128)(2,1)S(1)} %pad_maximum_fusion.1), channel_id=1, source_target_pairs={{0,2},{1,3},{2,0},{3,1},{4,6},{5,7},{6,4},{7,5},{8,10},{9,11},{10,... | collective-permute-start | bytes 540680 | tf_op jit(solution)/shard_map/ppermute | solution.py:704
  51.2 0.7 collective-permute-start.14
  51.9 0.7 collective-permute-done.10
  52.5 0.1 add_convert_fusion.12
  52.7 3.1 %collective-permute-start.13 = (bf16[2,288,128]{2,1,0:T(8,128)(2,1)S(1)}, bf16[2,288,128]{2,1,0:T(8,128)(2,1)S(1)}, u32[]{:S(2)}, u32[]{:S(2)}) collective-permute-start(bf16[2,288,128]{2,1,0:T(8,128)(2,1)S(1)} %pad_maximum_fusion.4), channel_id=1, source_target_pairs={{0,8},{1,9},{2,10},{3,11},{4,12},{5,13},{6,14},{7,15},{8,0},{9,1},... | collective-permute-start | bytes 442376 | tf_op jit(solution)/shard_map/ppermute | solution.py:704
  55.8 0.1 add_convert_fusion.10
  56.0 1.6 %collective-permute-start.18 = (bf16[704,128]{1,0:T(8,128)(2,1)S(1)}, bf16[704,128]{1,0:T(8,128)(2,1)S(1)}, u32[]{:S(2)}, u32[]{:S(2)}) collective-permute-start(bf16[704,128]{1,0:T(8,128)(2,1)S(1)} %pad_maximum_fusion.2), channel_id=1, source_target_pairs={{0,4},{1,5},{2,6},{3,7},{4,0},{5,1},{6,2},{7,3},{8,12},{9,13},{10,... | collective-permute-start | bytes 540680 | tf_op jit(solution)/shard_map/ppermute | solution.py:704
  57.6 0.7 collective-permute-start.16
  58.3 0.1 add_convert_fusion.4
  58.4 4.0 %collective-permute-done.13 = bf16[2,288,128]{2,1,0:T(8,128)(2,1)S(1)} collective-permute-done((bf16[2,288,128]{2,1,0:T(8,128)(2,1)S(1)}, bf16[2,288,128]{2,1,0:T(8,128)(2,1)S(1)}, u32[]{:S(2)}, u32[]{:S(2)}) %collective-permute-start.13) | collective-permute-done | bytes 147488 | tf_op jit(solution)/shard_map/ppermute | solution.py:704
  62.4 0.1 add_convert_fusion.5
  62.5 0.9 collective-permute-done.18
  63.5 0.7 collective-permute-start.20
  64.2 1.4 %collective-permute-start.17 = (bf16[2,288,128]{2,1,0:T(8,128)(2,1)S(1)}, bf16[2,288,128]{2,1,0:T(8,128)(2,1)S(1)}, u32[]{:S(2)}, u32[]{:S(2)}) collective-permute-start(bf16[2,288,128]{2,1,0:T(8,128)(2,1)S(1)} %add_convert_fusion.5), channel_id=1, source_target_pairs={{0,4},{1,5},{2,6},{3,7},{4,0},{5,1},{6,2},{7,3},{8,12},{9,13},{10,... | collective-permute-start | bytes 442376 | tf_op jit(solution)/shard_map/ppermute | solution.py:704
  65.7 1.6 %collective-permute-start.19 = (bf16[704,128]{1,0:T(8,128)(2,1)S(1)}, bf16[704,128]{1,0:T(8,128)(2,1)S(1)}, u32[]{:S(2)}, u32[]{:S(2)}) collective-permute-start(bf16[704,128]{1,0:T(8,128)(2,1)S(1)} %pad_maximum_fusion.3), channel_id=1, source_target_pairs={{0,8},{1,9},{2,10},{3,11},{4,12},{5,13},{6,14},{7,15},{8,0},{9,1},... | collective-permute-start | bytes 540680 | tf_op jit(solution)/shard_map/ppermute | solution.py:704
  67.4 3.8 %collective-permute-done.17 = bf16[2,288,128]{2,1,0:T(8,128)(2,1)S(1)} collective-permute-done((bf16[2,288,128]{2,1,0:T(8,128)(2,1)S(1)}, bf16[2,288,128]{2,1,0:T(8,128)(2,1)S(1)}, u32[]{:S(2)}, u32[]{:S(2)}) %collective-permute-start.17) | collective-permute-done | bytes 147488 | tf_op jit(solution)/shard_map/ppermute | solution.py:704
  71.2 0.1 collective-permute-start.22
  71.2 2.8 %collective-permute-start.23 = (bf16[4,288,128]{2,1,0:T(8,128)(2,1)S(1)}, bf16[4,288,128]{2,1,0:T(8,128)(2,1)S(1)}, u32[]{:S(2)}, u32[]{:S(2)}) collective-permute-start(bf16[4,288,128]{2,1,0:T(8,128)(2,1)S(1)} %constant_dynamic-update-slice_fusion.8.refs_0_), channel_id=1, source_target_pairs={{0,1},{1,0},{2,3},{3,2},{4,5},{5,4},{6,7},{7,6},{8,9},{9,8},{10,11... | collective-permute-start | bytes 884744 | tf_op jit(solution)/shard_map/ppermute | solution.py:704
  74.1 1.0 %assemble.1 = (f32[4,192,196]{2,1,0:T(8,128)}, bf16[4,192]{1,0:T(4,128)(2,1)}, bf16[4,192]{1,0:T(4,128)(2,1)}) custom-call(f32[2,192,208]{2,1,0:T(8,128)S(1)} %get-tuple-element.197.own_half, bf16[2,208,208]{2,1,0:T(8,128)(2,1)S(1)} %collective-permute-done.6.half_got, bf16[16,192]{1,0:T(8,128)(2,1)S(1)} %get-tuple-element.199.class_own), custom_call_target="tpu_custom_call" | custom-call | bytes 1 | tf_op jit(solution)/shard_map/assemble/pallas_call | solution.py:683
  75.0 2.6 %collective-permute-done.19 = bf16[704,128]{1,0:T(8,128)(2,1)S(1)} collective-permute-done((bf16[704,128]{1,0:T(8,128)(2,1)S(1)}, bf16[704,128]{1,0:T(8,128)(2,1)S(1)}, u32[]{:S(2)}, u32[]{:S(2)}) %collective-permute-start.19) | collective-permute-done | bytes 180256 | tf_op jit(solution)/shard_map/ppermute | solution.py:704
  77.8 0.4 collective-permute-start.21
  78.2 0.7 vector_outputs.1
  78.9 2.1 %collective-permute-done.22.refs_2_ = bf16[4,288,128]{2,1,0:T(8,128)(2,1)S(1)} collective-permute-done((bf16[4,288,128]{2,1,0:T(8,128)(2,1)S(1)}, bf16[4,288,128]{2,1,0:T(8,128)(2,1)S(1)}, u32[]{:S(2)}, u32[]{:S(2)}) %collective-permute-start.22) | collective-permute-done | bytes 294944 | tf_op jit(solution)/shard_map/ppermute | solution.py:704
  81.0 0.1 collective-permute-start.25
  81.1 0.4 collective-permute-start.26
  81.5 0.4 collective-permute-start.29
  81.9 0.2 collective-permute-start.27
  82.1 0.9 collective-permute-done.21
  83.0 0.1 collective-permute-start.28
  83.1 1.0 %collective-permute-start.24 = (bf16[8,144,128]{2,1,0:T(8,128)(2,1)S(1)}, bf16[8,144,128]{2,1,0:T(8,128)(2,1)S(1)}, u32[]{:S(2)}, u32[]{:S(2)}) collective-permute-start(bf16[8,144,128]{2,1,0:T(8,128)(2,1)S(1)} %constant_dynamic-update-slice_fusion.10.refs_6_), channel_id=1, source_target_pairs={{0,1},{1,0},{2,3},{3,2},{4,5},{5,4},{6,7},{7,6},{8,9},{9,8},{10,11... | collective-permute-start | bytes 884744 | tf_op jit(solution)/shard_map/ppermute | solution.py:704
  84.1 0.1 class_gradients.1
  84.2 4.0 %collective-permute-done.29.refs_8_ = bf16[4,288,128]{2,1,0:T(8,128)(2,1)S(1)} collective-permute-done((bf16[4,288,128]{2,1,0:T(8,128)(2,1)S(1)}, bf16[4,288,128]{2,1,0:T(8,128)(2,1)S(1)}, u32[]{:S(2)}, u32[]{:S(2)}) %collective-permute-start.29) | collective-permute-done | bytes 294944 | tf_op jit(solution)/shard_map/ppermute | solution.py:704
  88.2 3.1 %first_outputs.1 = (f32[384,1152]{1,0:T(8,128)}, f32[384,384]{1,0:T(8,128)}, f32[384,1536]{1,0:T(8,128)}, f32[1536,384]{1,0:T(8,128)}) custom-call(bf16[4,288,128]{2,1,0:T(8,128)(2,1)S(1)} %constant_dynamic-update-slice_fusion.8.refs_0_, ...), custom_call_target="tpu_custom_call", output_to_operand_aliasing={{0}: (9, {}), {1}: (10, {}), {2}: (11, {}), {3}: (12, {})} | custom-call | bytes 1 | tf_op jit(solution)/shard_map/first_outputs/pallas_call | solution.py:683
  91.3 0.1 collective-permute-start.30
  91.4 0.5 collective-permute-start.31
  91.8 1.1 %collective-permute-done.30.refs_1_ = bf16[4,288,128]{2,1,0:T(8,128)(2,1)S(1)} collective-permute-done((bf16[4,288,128]{2,1,0:T(8,128)(2,1)S(1)}, bf16[4,288,128]{2,1,0:T(8,128)(2,1)S(1)}, u32[]{:S(2)}, u32[]{:S(2)}) %collective-permute-start.30) | collective-permute-done | bytes 294944 | tf_op jit(solution)/shard_map/ppermute | solution.py:698
  92.9 0.4 collective-permute-done.31.refs_2_
  93.3 1.4 %last_outputs.1 = (f32[384,1152]{1,0:T(8,128)}, f32[384,384]{1,0:T(8,128)}, f32[384,1536]{1,0:T(8,128)}, f32[1536,384]{1,0:T(8,128)}) custom-call(bf16[8,144,128]{2,1,0:T(8,128)(2,1)S(1)} %collective-permute-done.24.refs_0_, ...), custom_call_target="tpu_custom_call", output_to_operand_aliasing={{0}: (3, {}), {1}: (4, {}), {2}: (5, {}), {3}: (6, {})} | custom-call | bytes 1 | tf_op jit(solution)/shard_map/last_outputs/pallas_call | solution.py:683
  (91 shorter events, 0.9 us)
Async XLA Ops:
  0.7 3.9 %copy-start.1 = (bf16[1,384,1536]{2,1,0:T(8,128)(2,1)S(1)}, bf16[1,384,1536]{2,1,0:T(8,128)(2,1)}, u32[]{:S(2)}) copy-start(bf16[1,384,1536]{2,1,0:T(8,128)(2,1)} %param.37) | copy-start | bytes 3538948
  0.7 4.4 %copy-start.3 = (bf16[1,384,384]{2,1,0:T(8,128)(2,1)S(1)}, bf16[1,384,384]{2,1,0:T(8,128)(2,1)}, u32[]{:S(2)}) copy-start(bf16[1,384,384]{2,1,0:T(8,128)(2,1)} %param.32) | copy-start | bytes 884740
  0.7 3.8 %collective-permute-start.1 = (bf16[384,1152]{1,0:T(8,128)(2,1)}, bf16[384,1152]{1,0:T(8,128)(2,1)S(1)}, u32[]{:S(2)}, u32[]{:S(2)}) collective-permute-start(bf16[384,1152]{1,0:T(8,128)(2,1)} %bitcast.28), channel_id=1, source_target_pairs={{0,16},{16,0},{1,17},{17,1},{2,18},{18,2},{3,19},{19,3},{4,20},{20... | collective-permute-start | bytes 2654216 | tf_op jit(solution)/shard_map/ppermute | solution.py:698
  1.2 4.2 %copy-start.11 = (bf16[8,8]{1,0:T(8,128)(2,1)S(1)}, bf16[8,8]{1,0:T(8,128)(2,1)}, u32[]{:S(2)}) copy-start(bf16[8,8]{1,0:T(8,128)(2,1)} %refs_11_.1) | copy-start | bytes 388
  1.2 4.2 %copy-start.12 = (bf16[8,8]{1,0:T(8,128)(2,1)S(1)}, bf16[8,8]{1,0:T(8,128)(2,1)}, u32[]{:S(2)}) copy-start(bf16[8,8]{1,0:T(8,128)(2,1)} %refs_10_.1) | copy-start | bytes 388
  2.9 2.5 %copy-start = (bf16[1,384,1152]{2,1,0:T(8,128)(2,1)S(1)}, bf16[1,384,1152]{2,1,0:T(8,128)(2,1)}, u32[]{:S(2)}) copy-start(bf16[1,384,1152]{2,1,0:T(8,128)(2,1)} %param.27) | copy-start | bytes 2654212
  2.9 2.5 %copy-start.4 = (bf16[16,384]{1,0:T(8,128)(2,1)S(1)}, bf16[16,384]{1,0:T(8,128)(2,1)}, u32[]{:S(2)}) copy-start(bf16[16,384]{1,0:T(8,128)(2,1)} %get-tuple-element.129.vec_own.refs_7_.refs_6_) | copy-start | bytes 36868
  2.9 2.5 %copy-start.5 = (s32[4,196]{1,0:T(4,128)S(1)}, s32[4,196]{1,0:T(4,128)}, u32[]{:S(2)}) copy-start(s32[4,196]{1,0:T(4,128)} %refs_2_.5) | copy-start | bytes 9412
  3.0 2.5 %copy-start.8 = (f32[1,384]{1,0:T(1,128)S(1)}, f32[1,384]{1,0:T(1,128)}, u32[]{:S(2)}) copy-start(f32[1,384]{1,0:T(1,128)} %get-tuple-element.130.bias_ref.refs_11_) | copy-start | bytes 4612
  3.0 1.5 %collective-permute-start = (bf16[16,384]{1,0:T(8,128)(2,1)}, bf16[16,384]{1,0:T(8,128)(2,1)S(1)}, u32[]{:S(2)}, u32[]{:S(2)}) collective-permute-start(bf16[16,384]{1,0:T(8,128)(2,1)} %get-tuple-element.129.vec_own.refs_7_.refs_6_), channel_id=1, source_target_pairs={{0,16},{16,0},{1,17},{17,1},{2,18},{18,2},{3,19},{19,3},{4,20},{20... | collective-permute-start | bytes 36872 | tf_op jit(solution)/shard_map/ppermute | solution.py:698
  4.5 5.3 %copy-start.2 = (bf16[1,1536,384]{2,1,0:T(8,128)(2,1)S(1)}, bf16[1,1536,384]{2,1,0:T(8,128)(2,1)}, u32[]{:S(2)}) copy-start(bf16[1,1536,384]{2,1,0:T(8,128)(2,1)} %param.39) | copy-start | bytes 3538948
  4.5 5.3 %copy-start.9 = (bf16[4,384]{1,0:T(4,128)(2,1)S(1)}, bf16[4,384]{1,0:T(4,128)(2,1)}, u32[]{:S(2)}) copy-start(bf16[4,384]{1,0:T(4,128)(2,1)} %class_ref.1) | copy-start | bytes 9220
  4.5 5.3 %copy-start.10 = (bf16[4,384]{1,0:T(4,128)(2,1)S(1)}, bf16[4,384]{1,0:T(4,128)(2,1)}, u32[]{:S(2)}) copy-start(bf16[4,384]{1,0:T(4,128)(2,1)} %cot_ref.1) | copy-start | bytes 9220
  4.5 5.2 %collective-permute-start.3 = (bf16[384,1536]{1,0:T(8,128)(2,1)S(1)}, bf16[384,1536]{1,0:T(8,128)(2,1)S(1)}, u32[]{:S(2)}, u32[]{:S(2)}) collective-permute-start(bf16[384,1536]{1,0:T(8,128)(2,1)S(1)} %bitcast.33), channel_id=1, source_target_pairs={{0,16},{16,0},{1,17},{17,1},{2,18},{18,2},{3,19},{19,3},{4,20},{20... | collective-permute-start | bytes 3538952 | tf_op jit(solution)/shard_map/ppermute | solution.py:698
  4.9 4.9 %collective-permute-start.4 = (bf16[1536,384]{1,0:T(8,128)(2,1)}, bf16[1536,384]{1,0:T(8,128)(2,1)S(1)}, u32[]{:S(2)}, u32[]{:S(2)}) collective-permute-start(bf16[1536,384]{1,0:T(8,128)(2,1)} %bitcast.36), channel_id=1, source_target_pairs={{0,16},{16,0},{1,17},{17,1},{2,18},{18,2},{3,19},{19,3},{4,20},{20... | collective-permute-start | bytes 3538952 | tf_op jit(solution)/shard_map/ppermute | solution.py:698
  5.1 4.6 %collective-permute-start.2 = (bf16[384,384]{1,0:T(8,128)(2,1)S(1)}, bf16[384,384]{1,0:T(8,128)(2,1)S(1)}, u32[]{:S(2)}, u32[]{:S(2)}) collective-permute-start(bf16[384,384]{1,0:T(8,128)(2,1)S(1)} %bitcast.39), channel_id=1, source_target_pairs={{0,16},{16,0},{1,17},{17,1},{2,18},{18,2},{3,19},{19,3},{4,20},{20... | collective-permute-start | bytes 884744 | tf_op jit(solution)/shard_map/ppermute | solution.py:698
  9.8 12.6 %copy-start.6 = (f32[8,384]{1,0:T(8,128)S(1)}, f32[8,384]{1,0:T(8,128)}, u32[]{:S(2)}) copy-start(f32[8,384]{1,0:T(8,128)} %get-tuple-element.142.refs_12_) | copy-start | bytes 36868
  9.8 12.6 %copy-start.7 = (f32[8,384]{1,0:T(8,128)S(1)}, f32[8,384]{1,0:T(8,128)}, u32[]{:S(2)}) copy-start(f32[8,384]{1,0:T(8,128)} %get-tuple-element.143.refs_13_) | copy-start | bytes 36868
  22.0 4.2 %collective-permute-start.5 = (bf16[17,288,128]{2,1,0:T(8,128)(2,1)S(1)}, bf16[17,288,128]{2,1,0:T(8,128)(2,1)S(1)}, u32[]{:S(2)}, u32[]{:S(2)}) collective-permute-start(bf16[17,288,128]{2,1,0:T(8,128)(2,1)S(1)} %get-tuple-element.137), channel_id=1, source_target_pairs={{0,16},{16,0},{1,17},{17,1},{2,18},{18,2},{3,19},{19,3},{4,20},{20... | collective-permute-start | bytes 3760136 | tf_op jit(solution)/shard_map/ppermute | solution.py:698
  26.4 10.6 %collective-permute-start.7 = (bf16[8,288,128]{2,1,0:T(8,128)(2,1)S(1)}, bf16[8,288,128]{2,1,0:T(8,128)(2,1)S(1)}, u32[]{:S(2)}, u32[]{:S(2)}) collective-permute-start(bf16[8,288,128]{2,1,0:T(8,128)(2,1)S(1)} %add_convert_fusion), channel_id=1, source_target_pairs={{0,1},{1,0},{2,3},{3,2},{4,5},{5,4},{6,7},{7,6},{8,9},{9,8},{10,11... | collective-permute-start | bytes 1769480 | tf_op jit(solution)/shard_map/ppermute | solution.py:704
  35.9 3.4 %collective-permute-start.9 = (bf16[17,144,128]{2,1,0:T(8,128)(2,1)S(1)}, bf16[17,144,128]{2,1,0:T(8,128)(2,1)S(1)}, u32[]{:S(2)}, u32[]{:S(2)}) collective-permute-start(bf16[17,144,128]{2,1,0:T(8,128)(2,1)S(1)} %get-tuple-element.164), channel_id=1, source_target_pairs={{0,16},{16,0},{1,17},{17,1},{2,18},{18,2},{3,19},{19,3},{4,20},{20... | collective-permute-start | bytes 1880072 | tf_op jit(solution)/shard_map/ppermute | solution.py:698
  36.0 5.1 %collective-permute-start.6 = (bf16[2,208,208]{2,1,0:T(8,128)(2,1)S(1)}, bf16[2,208,208]{2,1,0:T(8,128)(2,1)S(1)}, u32[]{:S(2)}, u32[]{:S(2)}) collective-permute-start(bf16[2,208,208]{2,1,0:T(8,128)(2,1)S(1)} %get-tuple-element.157), channel_id=1, source_target_pairs={{0,16},{16,0},{1,17},{17,1},{2,18},{18,2},{3,19},{19,3},{4,20},{20... | collective-permute-start | bytes 519176 | tf_op jit(solution)/shard_map/ppermute | solution.py:698
  37.2 9.7 %collective-permute-start.8 = (bf16[4,288,128]{2,1,0:T(8,128)(2,1)S(1)}, bf16[4,288,128]{2,1,0:T(8,128)(2,1)S(1)}, u32[]{:S(2)}, u32[]{:S(2)}) collective-permute-start(bf16[4,288,128]{2,1,0:T(8,128)(2,1)S(1)} %add_convert_fusion.2), channel_id=1, source_target_pairs={{0,2},{1,3},{2,0},{3,1},{4,6},{5,7},{6,4},{7,5},{8,10},{9,11},{10,... | collective-permute-start | bytes 884744 | tf_op jit(solution)/shard_map/ppermute | solution.py:704
  39.5 9.9 %collective-permute-start.12 = (bf16[1280,128]{1,0:T(8,128)(2,1)S(1)}, bf16[1280,128]{1,0:T(8,128)(2,1)S(1)}, u32[]{:S(2)}, u32[]{:S(2)}) collective-permute-start(bf16[1280,128]{1,0:T(8,128)(2,1)S(1)} %pad_maximum_fusion), channel_id=1, source_target_pairs={{0,1},{1,0},{2,3},{3,2},{4,5},{5,4},{6,7},{7,6},{8,9},{9,8},{10,11... | collective-permute-start | bytes 983048 | tf_op jit(solution)/shard_map/ppermute | solution.py:704
  41.0 10.1 %collective-permute-start.11 = (bf16[2,144,128]{2,1,0:T(8,128)(2,1)S(1)}, bf16[2,144,128]{2,1,0:T(8,128)(2,1)S(1)}, u32[]{:S(2)}, u32[]{:S(2)}) collective-permute-start(bf16[2,144,128]{2,1,0:T(8,128)(2,1)S(1)} %constant_dynamic-update-slice_fusion), channel_id=1, source_target_pairs={{16,24},{17,25},{18,26},{19,27},{20,28},{21,29},{22,30},{23,31},{2... | collective-permute-start | bytes 221192 | tf_op jit(solution)/shard_map/ppermute | solution.py:704
  46.9 5.6 %collective-permute-start.10 = (bf16[2,288,128]{2,1,0:T(8,128)(2,1)S(1)}, bf16[2,288,128]{2,1,0:T(8,128)(2,1)S(1)}, u32[]{:S(2)}, u32[]{:S(2)}) collective-permute-start(bf16[2,288,128]{2,1,0:T(8,128)(2,1)S(1)} %add_convert_fusion.8), channel_id=1, source_target_pairs={{0,4},{1,5},{2,6},{3,7},{4,0},{5,1},{6,2},{7,3},{8,12},{9,13},{10,... | collective-permute-start | bytes 442376 | tf_op jit(solution)/shard_map/ppermute | solution.py:704
  49.6 6.2 %collective-permute-start.15 = (bf16[704,128]{1,0:T(8,128)(2,1)S(1)}, bf16[704,128]{1,0:T(8,128)(2,1)S(1)}, u32[]{:S(2)}, u32[]{:S(2)}) collective-permute-start(bf16[704,128]{1,0:T(8,128)(2,1)S(1)} %pad_maximum_fusion.1), channel_id=1, source_target_pairs={{0,2},{1,3},{2,0},{3,1},{4,6},{5,7},{6,4},{7,5},{8,10},{9,11},{10,... | collective-permute-start | bytes 540680 | tf_op jit(solution)/shard_map/ppermute | solution.py:704
  51.2 6.4 %collective-permute-start.14 = (bf16[4,144,128]{2,1,0:T(8,128)(2,1)S(1)}, bf16[4,144,128]{2,1,0:T(8,128)(2,1)S(1)}, u32[]{:S(2)}, u32[]{:S(2)}) collective-permute-start(bf16[4,144,128]{2,1,0:T(8,128)(2,1)S(1)} %constant_dynamic-update-slice_fusion.2), channel_id=1, source_target_pairs={{16,20},{17,21},{18,22},{19,23},{20,16},{21,17},{22,18},{23,19},{2... | collective-permute-start | bytes 442376 | tf_op jit(solution)/shard_map/ppermute | solution.py:704
  52.7 9.7 %collective-permute-start.13 = (bf16[2,288,128]{2,1,0:T(8,128)(2,1)S(1)}, bf16[2,288,128]{2,1,0:T(8,128)(2,1)S(1)}, u32[]{:S(2)}, u32[]{:S(2)}) collective-permute-start(bf16[2,288,128]{2,1,0:T(8,128)(2,1)S(1)} %pad_maximum_fusion.4), channel_id=1, source_target_pairs={{0,8},{1,9},{2,10},{3,11},{4,12},{5,13},{6,14},{7,15},{8,0},{9,1},... | collective-permute-start | bytes 442376 | tf_op jit(solution)/shard_map/ppermute | solution.py:704
  56.0 7.4 %collective-permute-start.18 = (bf16[704,128]{1,0:T(8,128)(2,1)S(1)}, bf16[704,128]{1,0:T(8,128)(2,1)S(1)}, u32[]{:S(2)}, u32[]{:S(2)}) collective-permute-start(bf16[704,128]{1,0:T(8,128)(2,1)S(1)} %pad_maximum_fusion.2), channel_id=1, source_target_pairs={{0,4},{1,5},{2,6},{3,7},{4,0},{5,1},{6,2},{7,3},{8,12},{9,13},{10,... | collective-permute-start | bytes 540680 | tf_op jit(solution)/shard_map/ppermute | solution.py:704
  57.6 5.8 %collective-permute-start.16 = (bf16[8,144,128]{2,1,0:T(8,128)(2,1)S(1)}, bf16[8,144,128]{2,1,0:T(8,128)(2,1)S(1)}, u32[]{:S(2)}, u32[]{:S(2)}) collective-permute-start(bf16[8,144,128]{2,1,0:T(8,128)(2,1)S(1)} %constant_dynamic-update-slice_fusion.4), channel_id=1, source_target_pairs={{16,17},{17,16},{18,19},{19,18},{20,21},{21,20},{22,23},{23,22},{2... | collective-permute-start | bytes 884744 | tf_op jit(solution)/shard_map/ppermute | solution.py:704
  63.5 14.2 %collective-permute-start.20 = (bf16[16,144,128]{2,1,0:T(8,128)(2,1)S(1)}, bf16[16,144,128]{2,1,0:T(8,128)(2,1)S(1)}, u32[]{:S(2)}, u32[]{:S(2)}) collective-permute-start(bf16[16,144,128]{2,1,0:T(8,128)(2,1)S(1)} %constant_dynamic-update-slice_fusion.6.refs_0_), channel_id=1, source_target_pairs={{16,18},{17,19},{18,16},{19,17},{20,22},{21,23},{22,20},{23,21},{2... | collective-permute-start | bytes 1769480 | tf_op jit(solution)/shard_map/ppermute | solution.py:704
  64.2 6.9 %collective-permute-start.17 = (bf16[2,288,128]{2,1,0:T(8,128)(2,1)S(1)}, bf16[2,288,128]{2,1,0:T(8,128)(2,1)S(1)}, u32[]{:S(2)}, u32[]{:S(2)}) collective-permute-start(bf16[2,288,128]{2,1,0:T(8,128)(2,1)S(1)} %add_convert_fusion.5), channel_id=1, source_target_pairs={{0,4},{1,5},{2,6},{3,7},{4,0},{5,1},{6,2},{7,3},{8,12},{9,13},{10,... | collective-permute-start | bytes 442376 | tf_op jit(solution)/shard_map/ppermute | solution.py:704
  65.7 11.9 %collective-permute-start.19 = (bf16[704,128]{1,0:T(8,128)(2,1)S(1)}, bf16[704,128]{1,0:T(8,128)(2,1)S(1)}, u32[]{:S(2)}, u32[]{:S(2)}) collective-permute-start(bf16[704,128]{1,0:T(8,128)(2,1)S(1)} %pad_maximum_fusion.3), channel_id=1, source_target_pairs={{0,8},{1,9},{2,10},{3,11},{4,12},{5,13},{6,14},{7,15},{8,0},{9,1},... | collective-permute-start | bytes 540680 | tf_op jit(solution)/shard_map/ppermute | solution.py:704
  71.2 9.8 %collective-permute-start.22 = (bf16[4,288,128]{2,1,0:T(8,128)(2,1)S(1)}, bf16[4,288,128]{2,1,0:T(8,128)(2,1)S(1)}, u32[]{:S(2)}, u32[]{:S(2)}) collective-permute-start(bf16[4,288,128]{2,1,0:T(8,128)(2,1)S(1)} %constant_dynamic-update-slice_fusion.8.refs_0_), channel_id=1, source_target_pairs={{0,2},{1,3},{2,0},{3,1},{4,6},{5,7},{6,4},{7,5},{8,10},{9,11},{10,... | collective-permute-start | bytes 884744 | tf_op jit(solution)/shard_map/ppermute | solution.py:704
  71.2 9.7 %collective-permute-start.23 = (bf16[4,288,128]{2,1,0:T(8,128)(2,1)S(1)}, bf16[4,288,128]{2,1,0:T(8,128)(2,1)S(1)}, u32[]{:S(2)}, u32[]{:S(2)}) collective-permute-start(bf16[4,288,128]{2,1,0:T(8,128)(2,1)S(1)} %constant_dynamic-update-slice_fusion.8.refs_0_), channel_id=1, source_target_pairs={{0,1},{1,0},{2,3},{3,2},{4,5},{5,4},{6,7},{7,6},{8,9},{9,8},{10,11... | collective-permute-start | bytes 884744 | tf_op jit(solution)/shard_map/ppermute | solution.py:704
  77.8 5.2 %collective-permute-start.21 = (bf16[4,144,128]{2,1,0:T(8,128)(2,1)S(1)}, bf16[4,144,128]{2,1,0:T(8,128)(2,1)S(1)}, u32[]{:S(2)}, u32[]{:S(2)}) collective-permute-start(bf16[4,144,128]{2,1,0:T(8,128)(2,1)S(1)} %fusion), channel_id=1, source_target_pairs={{0,2},{1,3},{2,0},{3,1},{4,6},{5,7},{6,4},{7,5},{8,10},{9,11},{10,... | collective-permute-start | bytes 442376 | tf_op jit(solution)/shard_map/ppermute | solution.py:704
  81.0 2.1 %collective-permute-start.25 = (bf16[4,288,128]{2,1,0:T(8,128)(2,1)S(1)}, bf16[4,288,128]{2,1,0:T(8,128)(2,1)S(1)}, u32[]{:S(2)}, u32[]{:S(2)}) collective-permute-start(bf16[4,288,128]{2,1,0:T(8,128)(2,1)S(1)} %constant_dynamic-update-slice_fusion.8.refs_0_), channel_id=1, source_target_pairs={{0,16},{16,0},{1,17},{17,1},{2,18},{18,2},{3,19},{19,3},{4,20},{20... | collective-permute-start | bytes 884744 | tf_op jit(solution)/shard_map/ppermute | solution.py:698
  81.1 3.2 %collective-permute-start.26 = (bf16[4,288,128]{2,1,0:T(8,128)(2,1)S(1)}, bf16[4,288,128]{2,1,0:T(8,128)(2,1)S(1)}, u32[]{:S(2)}, u32[]{:S(2)}) collective-permute-start(bf16[4,288,128]{2,1,0:T(8,128)(2,1)S(1)} %collective-permute-done.22.refs_2_), channel_id=1, source_target_pairs={{0,16},{16,0},{1,17},{17,1},{2,18},{18,2},{3,19},{19,3},{4,20},{20... | collective-permute-start | bytes 884744 | tf_op jit(solution)/shard_map/ppermute | solution.py:698
  81.5 6.7 %collective-permute-start.29 = (bf16[4,288,128]{2,1,0:T(8,128)(2,1)S(1)}, bf16[4,288,128]{2,1,0:T(8,128)(2,1)S(1)}, u32[]{:S(2)}, u32[]{:S(2)}) collective-permute-start(bf16[4,288,128]{2,1,0:T(8,128)(2,1)S(1)} %collective-permute-done.22.refs_2_), channel_id=1, source_target_pairs={{0,1},{1,0},{2,3},{3,2},{4,5},{5,4},{6,7},{7,6},{8,9},{9,8},{10,11... | collective-permute-start | bytes 884744 | tf_op jit(solution)/shard_map/ppermute | solution.py:704
  81.9 2.3 %collective-permute-start.27 = (bf16[4,288,128]{2,1,0:T(8,128)(2,1)S(1)}, bf16[4,288,128]{2,1,0:T(8,128)(2,1)S(1)}, u32[]{:S(2)}, u32[]{:S(2)}) collective-permute-start(bf16[4,288,128]{2,1,0:T(8,128)(2,1)S(1)} %collective-permute-done.23.refs_4_), channel_id=1, source_target_pairs={{0,16},{16,0},{1,17},{17,1},{2,18},{18,2},{3,19},{19,3},{4,20},{20... | collective-permute-start | bytes 884744 | tf_op jit(solution)/shard_map/ppermute | solution.py:698
  83.0 5.2 %collective-permute-start.28 = (bf16[8,144,128]{2,1,0:T(8,128)(2,1)S(1)}, bf16[8,144,128]{2,1,0:T(8,128)(2,1)S(1)}, u32[]{:S(2)}, u32[]{:S(2)}) collective-permute-start(bf16[8,144,128]{2,1,0:T(8,128)(2,1)S(1)} %constant_dynamic-update-slice_fusion.10.refs_6_), channel_id=1, source_target_pairs={{0,16},{16,0},{1,17},{17,1},{2,18},{18,2},{3,19},{19,3},{4,20},{20... | collective-permute-start | bytes 884744 | tf_op jit(solution)/shard_map/ppermute | solution.py:698
  83.1 8.2 %collective-permute-start.24 = (bf16[8,144,128]{2,1,0:T(8,128)(2,1)S(1)}, bf16[8,144,128]{2,1,0:T(8,128)(2,1)S(1)}, u32[]{:S(2)}, u32[]{:S(2)}) collective-permute-start(bf16[8,144,128]{2,1,0:T(8,128)(2,1)S(1)} %constant_dynamic-update-slice_fusion.10.refs_6_), channel_id=1, source_target_pairs={{0,1},{1,0},{2,3},{3,2},{4,5},{5,4},{6,7},{7,6},{8,9},{9,8},{10,11... | collective-permute-start | bytes 884744 | tf_op jit(solution)/shard_map/ppermute | solution.py:704
  91.3 1.6 %collective-permute-start.30 = (bf16[4,288,128]{2,1,0:T(8,128)(2,1)S(1)}, bf16[4,288,128]{2,1,0:T(8,128)(2,1)S(1)}, u32[]{:S(2)}, u32[]{:S(2)}) collective-permute-start(bf16[4,288,128]{2,1,0:T(8,128)(2,1)S(1)} %collective-permute-done.29.refs_8_), channel_id=1, source_target_pairs={{0,16},{16,0},{1,17},{17,1},{2,18},{18,2},{3,19},{19,3},{4,20},{20... | collective-permute-start | bytes 884744 | tf_op jit(solution)/shard_map/ppermute | solution.py:698
  91.4 2.0 %collective-permute-start.31 = (bf16[8,144,128]{2,1,0:T(8,128)(2,1)S(1)}, bf16[8,144,128]{2,1,0:T(8,128)(2,1)S(1)}, u32[]{:S(2)}, u32[]{:S(2)}) collective-permute-start(bf16[8,144,128]{2,1,0:T(8,128)(2,1)S(1)} %collective-permute-done.24.refs_0_), channel_id=1, source_target_pairs={{0,16},{16,0},{1,17},{17,1},{2,18},{18,2},{3,19},{19,3},{4,20},{20... | collective-permute-start | bytes 884744 | tf_op jit(solution)/shard_map/ppermute | solution.py:698
